TPU v7x, 32 devices: a whole 2x2x4 slice. The times are simulated.
32 devices in a mesh: dp: 4 (over z), seq: 4 (over y, x), tensor: 2 (over core).
Axes of the slice: x: 2, y: 2, z: 4, core: 2. Of those that a mesh axis runs over, the one named last changes fastest.
Arguments:
- hidden_in: bfloat16 [4, 1536, 2048], P('dp', 'seq'), may hold values from -6 to 6
- teacher: bfloat16 [4, 1536, 2048], P('dp', 'seq'), may hold values from -6 to 6
- segment_ids: int32 [4, 1536], P('dp'), may hold values from 0 to 2, as said below
- valid_mask: int32 [4, 1536], replicated, may hold values from 0 to 1, as said below
- norm1_gain: bfloat16 [2048], P(('dp', 'seq')), may hold values from 0.5 to 1.5
- w_z: bfloat16 [2048, 3072], P(('dp', 'seq'), 'tensor'), may hold values from -0.125 to 0.125
- w_x: bfloat16 [2048, 3072], P(('dp', 'seq'), 'tensor'), may hold values from -0.125 to 0.125
- w_bc: bfloat16 [2048, 512], replicated, may hold values from -0.125 to 0.125
- w_dt: bfloat16 [2048, 48], P(('dp', 'seq'), 'tensor'), may hold values from -0.125 to 0.125
- conv_weight: float32 [3584, 4], replicated, may hold values from -3 to 3
- conv_bias: float32 [3584], replicated, may hold values from -3 to 3
- dt_bias: float32 [48], replicated, may hold values from -3 to 0
- a_log: float32 [48], replicated, may hold values from -11 to -2
- d_skip: float32 [48], replicated, may hold values from 0.5 to 1.5
- group_gain: float32 [48, 64], replicated, may hold values from 0.5 to 1.5
- w_mamba_out: bfloat16 [3072, 2048], P('tensor', ('dp', 'seq')), may hold values from -0.109375 to 0.109375
- w_query: bfloat16 [2048, 1024], P(('dp', 'seq'), 'tensor'), may hold values from -0.125 to 0.125
- w_key: bfloat16 [2048, 256], P(('dp', 'seq'), 'tensor'), may hold values from -0.125 to 0.125
- w_value: bfloat16 [2048, 256], P(('dp', 'seq'), 'tensor'), may hold values from -0.125 to 0.125
- w_attn_out: bfloat16 [1024, 2048], P('tensor', ('dp', 'seq')), may hold values from -0.75 to 0.75
- norm2_gain: bfloat16 [2048], P(('dp', 'seq')), may hold values from 0.5 to 1.5
- w_gate: bfloat16 [2048, 4096], P(('dp', 'seq'), 'tensor'), may hold values from -0.125 to 0.125
- w_up: bfloat16 [2048, 4096], P(('dp', 'seq'), 'tensor'), may hold values from -0.125 to 0.125
- w_down: bfloat16 [4096, 2048], P('tensor', ('dp', 'seq')), may hold values from -0.09375 to 0.09375
Outputs:
- block_output: bfloat16 [4, 1536, 2048], P('dp', 'seq')
- grad_input: float32 [4, 1536, 2048], P('dp', 'seq')
- grad_norm1_gain: float32 [2048], P(('dp', 'seq'))
- grad_w_z: float32 [2048, 3072], P(('dp', 'seq'), 'tensor')
- grad_w_x: float32 [2048, 3072], P(('dp', 'seq'), 'tensor')
- grad_w_bc: float32 [2048, 512], replicated
- grad_w_dt: float32 [2048, 48], P(('dp', 'seq'), 'tensor')
- grad_conv_weight: float32 [3584, 4], replicated
- grad_conv_bias: float32 [3584], replicated
- grad_dt_bias: float32 [48], replicated
- grad_a_log: float32 [48], replicated
- grad_d_skip: float32 [48], replicated
- grad_group_gain: float32 [48, 64], replicated
- grad_w_mamba_out: float32 [3072, 2048], P('tensor', ('dp', 'seq'))
- grad_w_query: float32 [2048, 1024], P(('dp', 'seq'), 'tensor')
- grad_w_key: float32 [2048, 256], P(('dp', 'seq'), 'tensor')
- grad_w_value: float32 [2048, 256], P(('dp', 'seq'), 'tensor')
- grad_w_attn_out: float32 [1024, 2048], P('tensor', ('dp', 'seq'))
- grad_norm2_gain: float32 [2048], P(('dp', 'seq'))
- grad_w_gate: float32 [2048, 4096], P(('dp', 'seq'), 'tensor')
- grad_w_up: float32 [2048, 4096], P(('dp', 'seq'), 'tensor')
- grad_w_down: float32 [4096, 2048], P('tensor', ('dp', 'seq'))
Inputs may be any that keep to these rules, and one draw needn't show every extreme that they name: `segment_ids`: ids never fall along a row and start at 0; segment 1 begins within the first 192 positions of the row and segment 2 within its last 192. `valid_mask`: the last position of every row is valid.
All inputs are finite; a program needn't handle non-finite values.
Results may differ from a plain program's by a relative error of at most 0.012.
The roundings to bfloat16 on the way count: a program that leaves them out, or rounds other values in their place, can miss the bound.
Values may be sent and summed in bfloat16 or wider, within the bound.
A program may use at most 256 MiB of HBM per device.

v0:
```python
from functools import partial

import jax
import jax.numpy as jnp
from jax import lax
from jax.sharding import PartitionSpec as P

MH = 48
HP = 64
NS = 256
KC = 4
HD = 128


EPSILON = 1e-06
GROUP_EPSILON = 1e-05
ROPE_BASE = 10000.0
HIGHEST = lax.Precision.HIGHEST


def shifted(block, axis, distance):
    devices = range(lax.axis_size(axis))
    route = [(i - distance, i) for i in devices if i - distance in devices]
    return lax.ppermute(block, axis, route)


def carried_in(part, axis, combine, identity, reverse):
    count = lax.axis_size(axis)
    place = lax.axis_index(axis)
    ahead = count - 1 - place if reverse else place
    gathered = jax.tree.map(lambda a: lax.all_gather(a, axis), part)
    state = jax.tree.map(lambda a, e: jnp.zeros_like(a) + jnp.asarray(e, a.dtype), part, identity)

    def one(lap, state):
        source = count - 1 - lap if reverse else lap
        return combine(
            state, jax.tree.map(lambda a: lax.dynamic_index_in_dim(a, source, 0, False), gathered)
        )

    return lax.fori_loop(0, ahead, one, state)


def mat_dot(left_side, right_side):
    return jnp.dot(left_side, right_side, preferred_element_type=jnp.float32)


def dot_left_t(left_side, right_side):
    return lax.dot_general(
        left_side, right_side, (((0,), (0,)), ((), ())), preferred_element_type=jnp.float32
    )


def dot_right_t(left_side, right_side):
    return lax.dot_general(
        left_side, right_side, (((1,), (1,)), ((), ())), preferred_element_type=jnp.float32
    )


def rms_norm(values, gain_row):
    scale_row = lax.rsqrt(jnp.mean(values * values, axis=-1, keepdims=True) + EPSILON)
    return values * scale_row * gain_row


def rotate(positions, values):
    half_dim = values.shape[-1] // 2
    frequency = ROPE_BASE ** (-2.0 * jnp.arange(half_dim).astype(jnp.float32) / values.shape[-1])
    angles = positions.astype(jnp.float32)[:, None] * frequency[None, :]
    cosine = jnp.cos(angles)[:, None, :]
    sine_part = jnp.sin(angles)[:, None, :]
    first_half = values[..., :half_dim]
    second = values[..., half_dim:]
    return jnp.concatenate(
        [first_half * cosine - second * sine_part, second * cosine + first_half * sine_part],
        axis=-1,
    )


def conv_silu(seg_ext, seg_rows, extended, weights, bias_row):
    size_rows = seg_rows.shape[0]
    summed = jnp.zeros((size_rows, weights.shape[0]), jnp.float32) + bias_row[None, :]
    for tap_index in range(weights.shape[1]):
        window = lax.slice_in_dim(extended, tap_index, tap_index + size_rows, axis=0)
        keep_mask = (
            lax.slice_in_dim(seg_ext, tap_index, tap_index + size_rows) == seg_rows
        ).astype(jnp.float32)
        summed = summed + window * weights[:, tap_index][None, :] * keep_mask[:, None]
    return jax.nn.silu(summed)


def group_gate(ssm_out, gate_z, group_gain):
    mixed_val = ssm_out * jax.nn.silu(gate_z)
    return (
        mixed_val
        * lax.rsqrt(jnp.mean(mixed_val * mixed_val, axis=-1, keepdims=True) + GROUP_EPSILON)
        * group_gain[None]
    )


def swiglu(gate_pre, up_pre):
    return jax.nn.silu(gate_pre) * up_pre


def split_mixed(mixed_in, heads_local):
    size_rows = mixed_in.shape[0]
    width_x = heads_local * HP
    heads_x = mixed_in[:, :width_x].reshape(size_rows, heads_local, HP)
    return (heads_x, mixed_in[:, width_x : width_x + NS], mixed_in[:, width_x + NS :])


def ssd_main(seg_rows, seg_before, mixed_in, dt_raw, dt_bias_row, a_log_row, d_skip_row):
    size_rows = seg_rows.shape[0]
    heads_x, b_rows, c_rows = split_mixed(mixed_in, dt_raw.shape[1])
    dt_rows = jax.nn.softplus(dt_raw + dt_bias_row[None, :])
    cumul = jnp.cumsum(-jnp.exp(a_log_row)[None, :] * dt_rows, axis=0)
    order_pos = jnp.arange(size_rows)
    allowed = (seg_rows[:, None] == seg_rows[None, :]) & (order_pos[:, None] >= order_pos[None, :])
    differ = cumul[:, None, :] - cumul[None, :, :]
    decay = jnp.exp(jnp.where(allowed[:, :, None], differ, -jnp.inf))
    gram = jnp.dot(c_rows, b_rows.T, precision=HIGHEST, preferred_element_type=jnp.float32)
    mixing = gram[:, :, None] * decay * dt_rows[None, :, :]
    outputs = jnp.einsum("tsh,shp->thp", mixing, heads_x, precision=HIGHEST)
    outputs = outputs + d_skip_row[None, :, None] * heads_x
    tail_keep = (seg_rows == seg_rows[-1]).astype(jnp.float32)
    tail_weight = jnp.exp(cumul[-1][None, :] - cumul) * tail_keep[:, None] * dt_rows
    local_state = jnp.einsum("sh,shp,sn->hpn", tail_weight, heads_x, b_rows, precision=HIGHEST)
    carry_factor = jnp.exp(cumul[-1]) * (seg_rows[-1] == seg_before).astype(jnp.float32)
    return (outputs, carry_factor, local_state)


def ssd_state(seg_rows, seg_before, mixed_in, dt_raw, dt_bias_row, a_log_row, entry_state):
    heads_x, b_rows, c_rows = split_mixed(mixed_in, dt_raw.shape[1])
    dt_rows = jax.nn.softplus(dt_raw + dt_bias_row[None, :])
    cumul = jnp.cumsum(-jnp.exp(a_log_row)[None, :] * dt_rows, axis=0)
    entry_keep = (seg_rows == seg_before).astype(jnp.float32)
    entry_part = jnp.einsum("tn,hpn->thp", c_rows, entry_state, precision=HIGHEST)
    return jnp.exp(cumul)[:, :, None] * entry_keep[:, None, None] * entry_part


def chain_states(earlier, later):
    return (earlier[0] * later[0], later[0][:, None, None] * earlier[1] + later[1])


def block_scores(queries, keys_all, vals_all, seg_full, query_pos, seg_query, block_index, key_len):
    key_blk = keys_all[block_index * key_len : (block_index + 1) * key_len]
    val_blk = vals_all[block_index * key_len : (block_index + 1) * key_len]
    seg_key = seg_full[block_index * key_len : (block_index + 1) * key_len]
    key_pos = block_index * key_len + jnp.arange(key_len)
    scores = jnp.einsum(
        "tkgd,skd->kgts", queries, key_blk, preferred_element_type=jnp.float32
    ) * HD ** (-0.5)
    allowed = (query_pos[:, None] >= key_pos[None, :]) & (seg_query[:, None] == seg_key[None, :])
    return (key_blk, val_blk, jnp.where(allowed[None, None], scores, -jnp.inf))


def attend_forward(queries, keys_all, vals_all, seg_full, query_pos, seg_query, block_count):
    key_len = keys_all.shape[0] // block_count
    stat_shape = (queries.shape[1], queries.shape[2], queries.shape[0])
    running_max = jnp.full(stat_shape, -1e30, jnp.float32)
    running_sum = jnp.zeros(stat_shape, jnp.float32)
    for block_index in range(block_count):
        needed = block_index * key_len <= query_pos[-1]

        def stat_step(stats, block_index=block_index):
            old_max, old_sum = stats
            key_blk, val_blk, scores = block_scores(
                queries, keys_all, vals_all, seg_full, query_pos, seg_query, block_index, key_len
            )
            new_max = jnp.maximum(old_max, jnp.max(scores, axis=-1))
            new_sum = old_sum * jnp.exp(old_max - new_max) + jnp.sum(
                jnp.exp(scores - new_max[..., None]), axis=-1
            )
            return (new_max, new_sum)

        running_max, running_sum = lax.cond(
            needed, stat_step, lambda stats: stats, (running_max, running_sum)
        )
    log_total = running_max + jnp.log(running_sum)
    attended = jnp.zeros(queries.shape, jnp.float32)
    for block_index in range(block_count):
        needed = block_index * key_len <= query_pos[-1]

        def value_step(total, block_index=block_index):
            key_blk, val_blk, scores = block_scores(
                queries, keys_all, vals_all, seg_full, query_pos, seg_query, block_index, key_len
            )
            probs = jnp.exp(scores - log_total[..., None]).astype(jnp.bfloat16)
            return total + jnp.einsum(
                "kgts,skd->tkgd", probs, val_blk, preferred_element_type=jnp.float32
            )

        attended = lax.cond(needed, value_step, lambda total: total, attended)
    return (log_total, attended)


def attend_backward(
    queries, keys_all, vals_all, seg_full, query_pos, seg_query, block_count, grad_out, log_total
):
    key_len = keys_all.shape[0] // block_count
    delta = jnp.zeros(log_total.shape, jnp.float32)
    for block_index in range(block_count):
        needed = block_index * key_len <= query_pos[-1]

        def delta_step(total, block_index=block_index):
            key_blk, val_blk, scores = block_scores(
                queries, keys_all, vals_all, seg_full, query_pos, seg_query, block_index, key_len
            )
            probs = jnp.exp(scores - log_total[..., None])
            grad_probs = jnp.einsum(
                "tkgd,skd->kgts", grad_out, val_blk, preferred_element_type=jnp.float32
            )
            return total + jnp.sum(probs * grad_probs, axis=-1)

        delta = lax.cond(needed, delta_step, lambda total: total, delta)
    grad_query = jnp.zeros(queries.shape, jnp.float32)
    empty_part = jnp.zeros((key_len, keys_all.shape[1], keys_all.shape[2]), jnp.float32)
    key_parts = []
    val_parts = []
    for block_index in range(block_count):
        needed = block_index * key_len <= query_pos[-1]

        def grad_step(total, block_index=block_index):
            key_blk, val_blk, scores = block_scores(
                queries, keys_all, vals_all, seg_full, query_pos, seg_query, block_index, key_len
            )
            probs = jnp.exp(scores - log_total[..., None])
            grad_probs = jnp.einsum(
                "tkgd,skd->kgts", grad_out, val_blk, preferred_element_type=jnp.float32
            )
            grad_scores = (probs * (grad_probs - delta[..., None])).astype(jnp.bfloat16)
            new_total = total + jnp.einsum(
                "kgts,skd->tkgd", grad_scores, key_blk, preferred_element_type=jnp.float32
            ) * HD ** (-0.5)
            key_part = jnp.einsum(
                "kgts,tkgd->skd", grad_scores, queries, preferred_element_type=jnp.float32
            ) * HD ** (-0.5)
            val_part = jnp.einsum(
                "kgts,tkgd->skd",
                probs.astype(jnp.bfloat16),
                grad_out,
                preferred_element_type=jnp.float32,
            )
            return (new_total, key_part, val_part)

        grad_query, key_part, val_part = lax.cond(
            needed, grad_step, lambda total: (total, empty_part, empty_part), grad_query
        )
        key_parts.append(key_part)
        val_parts.append(val_part)
    return (grad_query, jnp.concatenate(key_parts, axis=0), jnp.concatenate(val_parts, axis=0))


def local(
    hidden_in,
    teacher,
    segment_ids,
    valid_mask,
    norm1_gain,
    w_z,
    w_x,
    w_bc,
    w_dt,
    conv_weight,
    conv_bias,
    dt_bias,
    a_log,
    d_skip,
    group_gain,
    w_mamba_out,
    w_query,
    w_key,
    w_value,
    w_attn_out,
    norm2_gain,
    w_gate,
    w_up,
    w_down,
):
    tensor_rank = lax.axis_index("tensor")
    seq_rank = lax.axis_index("seq")
    data_rank = lax.axis_index("dp")
    seq_count = lax.axis_size("seq")
    tensor_count = lax.axis_size("tensor")
    size_rows = hidden_in.shape[1]
    full_length = segment_ids.shape[1]
    row_start = seq_rank * size_rows
    seg_full = segment_ids[0]
    seg_local = lax.dynamic_slice_in_dim(seg_full, row_start, size_rows)
    seg_padded = jnp.concatenate([jnp.full((KC - 1,), -1, jnp.int32), seg_full])
    seg_ext = lax.dynamic_slice_in_dim(seg_padded, row_start, size_rows + KC - 1)
    seg_prev = lax.dynamic_index_in_dim(seg_padded, row_start + KC - 2, keepdims=False)
    token_count = jnp.sum(valid_mask).astype(jnp.float32)
    mask_rows = lax.dynamic_slice(valid_mask, (data_rank, row_start), (1, size_rows))[0].astype(
        jnp.float32
    )
    total_tokens = float(valid_mask.shape[0] * valid_mask.shape[1])
    (
        gain_one,
        full_z,
        full_x,
        full_dt,
        full_mo,
        full_q,
        full_k,
        full_v,
        full_ao,
        gain_two,
        full_gate,
        full_up,
        full_down,
    ) = (
        lax.all_gather(norm1_gain, ("dp", "seq"), axis=0, tiled=True),
        lax.all_gather(w_z, ("dp", "seq"), axis=0, tiled=True),
        lax.all_gather(w_x, ("dp", "seq"), axis=0, tiled=True),
        lax.all_gather(w_dt, ("dp", "seq"), axis=0, tiled=True),
        lax.all_gather(w_mamba_out, ("dp", "seq"), axis=1, tiled=True),
        lax.all_gather(w_query, ("dp", "seq"), axis=0, tiled=True),
        lax.all_gather(w_key, ("dp", "seq"), axis=0, tiled=True),
        lax.all_gather(w_value, ("dp", "seq"), axis=0, tiled=True),
        lax.all_gather(w_attn_out, ("dp", "seq"), axis=1, tiled=True),
        lax.all_gather(norm2_gain, ("dp", "seq"), axis=0, tiled=True),
        lax.all_gather(w_gate, ("dp", "seq"), axis=0, tiled=True),
        lax.all_gather(w_up, ("dp", "seq"), axis=0, tiled=True),
        lax.all_gather(w_down, ("dp", "seq"), axis=1, tiled=True),
    )
    heads_local = MH // tensor_count
    width_x = heads_local * HP
    head_start = tensor_rank * heads_local
    hidden = hidden_in[0].astype(jnp.float32)
    normed_f, norm_one_pull = jax.vjp(rms_norm, hidden, gain_one.astype(jnp.float32))
    normed = normed_f.astype(jnp.bfloat16)
    gate_z = mat_dot(normed, full_z)
    pre_x = mat_dot(normed, full_x).astype(jnp.bfloat16)
    pre_bc = mat_dot(normed, w_bc).astype(jnp.bfloat16)
    dt_raw = mat_dot(normed, full_dt)
    pre_all = jnp.concatenate([pre_x, pre_bc], axis=1)
    rim_rows = shifted(pre_all[size_rows - (KC - 1) :], "seq", 1)
    extended = jnp.concatenate([rim_rows, pre_all], axis=0).astype(jnp.float32)
    conv_local = jnp.concatenate(
        [
            lax.dynamic_slice_in_dim(conv_weight, head_start * HP, width_x, 0),
            conv_weight[MH * HP :],
        ],
        axis=0,
    )
    bias_local = jnp.concatenate(
        [lax.dynamic_slice_in_dim(conv_bias, head_start * HP, width_x, 0), conv_bias[MH * HP :]],
        axis=0,
    )
    mixed_f, conv_pull = jax.vjp(
        partial(conv_silu, seg_ext, seg_local), extended, conv_local, bias_local
    )
    mixed_in = lax.optimization_barrier(mixed_f.astype(jnp.bfloat16)).astype(jnp.float32)
    dt_bias_loc = lax.dynamic_slice_in_dim(dt_bias, head_start, heads_local)
    a_log_loc = lax.dynamic_slice_in_dim(a_log, head_start, heads_local)
    d_skip_loc = lax.dynamic_slice_in_dim(d_skip, head_start, heads_local)
    group_loc = lax.dynamic_slice_in_dim(group_gain, head_start, heads_local, 0)
    (ssm_local, carry_dev, state_dev), main_pull = jax.vjp(
        partial(ssd_main, seg_local, seg_prev), mixed_in, dt_raw, dt_bias_loc, a_log_loc, d_skip_loc
    )
    identity = (jnp.ones_like(carry_dev), jnp.zeros_like(state_dev))
    entry_state = carried_in((carry_dev, state_dev), "seq", chain_states, identity, False)[1]
    ssm_entry, state_pull = jax.vjp(
        partial(ssd_state, seg_local, seg_prev),
        mixed_in,
        dt_raw,
        dt_bias_loc,
        a_log_loc,
        entry_state,
    )
    ssm_out = ssm_local + ssm_entry
    gated_f, gate_pull = jax.vjp(
        group_gate, ssm_out, gate_z.reshape(size_rows, heads_local, HP), group_loc
    )
    gated = gated_f.reshape(size_rows, width_x).astype(jnp.bfloat16)
    mamba_part = mat_dot(gated, full_mo)
    positions = row_start + jnp.arange(size_rows)
    heads_q = full_q.shape[1] // HD
    heads_kv = full_k.shape[1] // HD
    groups = heads_q // heads_kv
    query_rot, query_pull = jax.vjp(
        partial(rotate, positions), mat_dot(normed, full_q).reshape(size_rows, heads_q, HD)
    )
    queries = query_rot.astype(jnp.bfloat16).reshape(size_rows, heads_kv, groups, HD)
    key_rot, key_pull = jax.vjp(
        partial(rotate, positions), mat_dot(normed, full_k).reshape(size_rows, heads_kv, HD)
    )
    keys_local = key_rot.astype(jnp.bfloat16).reshape(size_rows, heads_kv * HD)
    vals_local = mat_dot(normed, full_v).astype(jnp.bfloat16)
    keys_all, vals_all = (
        lax.all_gather(keys_local, "seq", axis=0, tiled=True),
        lax.all_gather(vals_local, "seq", axis=0, tiled=True),
    )
    keys_all = keys_all.reshape(full_length, heads_kv, HD)
    vals_all = vals_all.reshape(full_length, heads_kv, HD)
    block_count = seq_count // 4
    log_total, attended_f = attend_forward(
        queries, keys_all, vals_all, seg_full, positions, seg_local, block_count
    )
    attended = attended_f.reshape(size_rows, heads_q * HD).astype(jnp.bfloat16)
    branch = lax.psum(mamba_part + mat_dot(attended, full_ao), "tensor")
    middle = hidden + branch
    normed_two_f, norm_two_pull = jax.vjp(rms_norm, middle, gain_two.astype(jnp.float32))
    normed_two = normed_two_f.astype(jnp.bfloat16)
    act_f, glu_pull = jax.vjp(swiglu, mat_dot(normed_two, full_gate), mat_dot(normed_two, full_up))
    activated = act_f.astype(jnp.bfloat16)
    block_out = middle + lax.psum(mat_dot(activated, full_down), "tensor")
    (
        back_z,
        back_x,
        back_dt,
        back_mo,
        back_q,
        back_k,
        back_v,
        back_ao,
        back_gate,
        back_up,
        back_down,
    ) = (
        lax.all_gather(w_z, ("dp", "seq"), axis=0, tiled=True),
        lax.all_gather(w_x, ("dp", "seq"), axis=0, tiled=True),
        lax.all_gather(w_dt, ("dp", "seq"), axis=0, tiled=True),
        lax.all_gather(w_mamba_out, ("dp", "seq"), axis=1, tiled=True),
        lax.all_gather(w_query, ("dp", "seq"), axis=0, tiled=True),
        lax.all_gather(w_key, ("dp", "seq"), axis=0, tiled=True),
        lax.all_gather(w_value, ("dp", "seq"), axis=0, tiled=True),
        lax.all_gather(w_attn_out, ("dp", "seq"), axis=1, tiled=True),
        lax.all_gather(w_gate, ("dp", "seq"), axis=0, tiled=True),
        lax.all_gather(w_up, ("dp", "seq"), axis=0, tiled=True),
        lax.all_gather(w_down, ("dp", "seq"), axis=1, tiled=True),
    )
    d_out = (
        2.0
        * total_tokens
        / token_count
        * mask_rows[:, None]
        * (block_out - teacher[0].astype(jnp.float32))
    )
    d_mlp = d_out.astype(jnp.bfloat16)
    grad_down = dot_left_t(activated, d_mlp)
    d_gate_f, d_up_f = glu_pull(dot_right_t(d_mlp, back_down))
    d_gate = d_gate_f.astype(jnp.bfloat16)
    d_up = d_up_f.astype(jnp.bfloat16)
    grad_gate = dot_left_t(normed_two, d_gate)
    grad_up = dot_left_t(normed_two, d_up)
    d_normed_two = lax.psum(dot_right_t(d_gate, back_gate) + dot_right_t(d_up, back_up), "tensor")
    d_middle_n, grad_gain_two = norm_two_pull(d_normed_two)
    d_middle = d_out + d_middle_n
    d_branch = d_middle.astype(jnp.bfloat16)
    grad_ao = dot_left_t(attended, d_branch)
    grad_mo = dot_left_t(gated, d_branch)
    d_attended = (
        dot_right_t(d_branch, back_ao).astype(jnp.bfloat16).reshape(size_rows, heads_kv, groups, HD)
    )
    d_gated = dot_right_t(d_branch, back_mo).reshape(size_rows, heads_local, HP)
    d_ssm, d_gate_z_f, grad_group = gate_pull(d_gated)
    d_gate_z = d_gate_z_f.reshape(size_rows, width_x).astype(jnp.bfloat16)
    d_mixed_s, d_dt_s, d_dtb_s, d_alog_s, d_entry = state_pull(d_ssm)
    state_grad = carried_in((carry_dev, d_entry), "seq", chain_states, identity, True)[1]
    d_carry = jnp.sum(state_grad * entry_state, axis=(1, 2))
    d_mixed_m, d_dt_m, d_dtb_m, d_alog_m, grad_skip = main_pull((d_ssm, d_carry, state_grad))
    d_dt_raw = (d_dt_s + d_dt_m).astype(jnp.bfloat16)
    d_ext, grad_conv_loc, grad_bias_loc = conv_pull(d_mixed_s + d_mixed_m)
    rim_grad = shifted(d_ext[: KC - 1], "seq", -1)
    d_pre = d_ext[KC - 1 :] + jnp.pad(rim_grad, ((size_rows - (KC - 1), 0), (0, 0)))
    d_pre_x = d_pre[:, :width_x].astype(jnp.bfloat16)
    d_pre_bc = d_pre[:, width_x:]
    grad_query_rot, key_grads_all, val_grads_all = attend_backward(
        queries,
        keys_all,
        vals_all,
        seg_full,
        positions,
        seg_local,
        block_count,
        d_attended,
        log_total,
    )
    key_grad, val_grad = (
        lax.psum_scatter(
            key_grads_all.reshape(full_length, heads_kv * HD).astype(jnp.bfloat16),
            "seq",
            scatter_dimension=0,
            tiled=True,
        ).astype(jnp.float32),
        lax.psum_scatter(
            val_grads_all.reshape(full_length, heads_kv * HD).astype(jnp.bfloat16),
            "seq",
            scatter_dimension=0,
            tiled=True,
        ).astype(jnp.float32),
    )
    d_query = (
        query_pull(grad_query_rot.reshape(size_rows, heads_q, HD))[0]
        .reshape(size_rows, heads_q * HD)
        .astype(jnp.bfloat16)
    )
    d_key = (
        key_pull(key_grad.reshape(size_rows, heads_kv, HD))[0]
        .reshape(size_rows, heads_kv * HD)
        .astype(jnp.bfloat16)
    )
    d_value = val_grad.astype(jnp.bfloat16)
    grad_z = dot_left_t(normed, d_gate_z)
    grad_x = dot_left_t(normed, d_pre_x)
    grad_dt = dot_left_t(normed, d_dt_raw)
    grad_q = dot_left_t(normed, d_query)
    grad_k = dot_left_t(normed, d_key)
    grad_v = dot_left_t(normed, d_value)
    normed_wide = normed.astype(jnp.float32)
    bc_weight = w_bc.astype(jnp.float32)
    grad_bc = jnp.dot(
        normed_wide.T, d_pre_bc, precision=HIGHEST, preferred_element_type=jnp.float32
    )
    d_normed_part = (
        dot_right_t(d_gate_z, back_z)
        + dot_right_t(d_pre_x, back_x)
        + dot_right_t(d_dt_raw, back_dt)
        + dot_right_t(d_query, back_q)
        + dot_right_t(d_key, back_k)
        + dot_right_t(d_value, back_v)
        + jnp.dot(d_pre_bc, bc_weight.T, precision=HIGHEST, preferred_element_type=jnp.float32)
    )
    d_normed = lax.psum(d_normed_part.astype(jnp.bfloat16), "tensor").astype(jnp.float32)
    d_hidden_n, grad_gain_one = norm_one_pull(d_normed)
    grad_input = d_middle + d_hidden_n
    conv_x_full = lax.dynamic_update_slice_in_dim(
        jnp.zeros((MH * HP, KC), jnp.float32), grad_conv_loc[:width_x], head_start * HP, 0
    )
    grad_conv_full = jnp.concatenate([conv_x_full, grad_conv_loc[width_x:]], axis=0)
    bias_x_full = lax.dynamic_update_slice_in_dim(
        jnp.zeros((MH * HP,), jnp.float32), grad_bias_loc[:width_x], head_start * HP, 0
    )
    grad_bias_full = jnp.concatenate([bias_x_full, grad_bias_loc[width_x:]], axis=0)
    grad_dtb_full = lax.dynamic_update_slice_in_dim(
        jnp.zeros((MH,), jnp.float32), d_dtb_s + d_dtb_m, head_start, 0
    )
    grad_alog_full = lax.dynamic_update_slice_in_dim(
        jnp.zeros((MH,), jnp.float32), d_alog_s + d_alog_m, head_start, 0
    )
    grad_skip_full = lax.dynamic_update_slice_in_dim(
        jnp.zeros((MH,), jnp.float32), grad_skip, head_start, 0
    )
    grad_group_full = lax.dynamic_update_slice_in_dim(
        jnp.zeros((MH, HP), jnp.float32), grad_group, head_start, 0
    )
    sum_bc, sum_conv, sum_bias, sum_dtb, sum_alog, sum_skip, sum_group = lax.psum(
        (
            grad_bc,
            grad_conv_full,
            grad_bias_full,
            grad_dtb_full,
            grad_alog_full,
            grad_skip_full,
            grad_group_full,
        ),
        ("dp", "seq", "tensor"),
    )
    (
        out_gain_one,
        out_z,
        out_x,
        out_dt,
        out_mo,
        out_q,
        out_k,
        out_v,
        out_ao,
        out_gain_two,
        out_gate,
        out_up,
        out_down,
    ) = (
        lax.psum_scatter(grad_gain_one, ("dp", "seq"), scatter_dimension=0, tiled=True),
        lax.psum_scatter(grad_z, ("dp", "seq"), scatter_dimension=0, tiled=True),
        lax.psum_scatter(grad_x, ("dp", "seq"), scatter_dimension=0, tiled=True),
        lax.psum_scatter(grad_dt, ("dp", "seq"), scatter_dimension=0, tiled=True),
        lax.psum_scatter(grad_mo, ("dp", "seq"), scatter_dimension=1, tiled=True),
        lax.psum_scatter(grad_q, ("dp", "seq"), scatter_dimension=0, tiled=True),
        lax.psum_scatter(grad_k, ("dp", "seq"), scatter_dimension=0, tiled=True),
        lax.psum_scatter(grad_v, ("dp", "seq"), scatter_dimension=0, tiled=True),
        lax.psum_scatter(grad_ao, ("dp", "seq"), scatter_dimension=1, tiled=True),
        lax.psum_scatter(grad_gain_two, ("dp", "seq"), scatter_dimension=0, tiled=True),
        lax.psum_scatter(grad_gate, ("dp", "seq"), scatter_dimension=0, tiled=True),
        lax.psum_scatter(grad_up, ("dp", "seq"), scatter_dimension=0, tiled=True),
        lax.psum_scatter(grad_down, ("dp", "seq"), scatter_dimension=1, tiled=True),
    )
    return (
        block_out.astype(jnp.bfloat16)[None],
        grad_input[None],
        out_gain_one,
        out_z,
        out_x,
        sum_bc,
        out_dt,
        sum_conv,
        sum_bias,
        sum_dtb,
        sum_alog,
        sum_skip,
        sum_group,
        out_mo,
        out_q,
        out_k,
        out_v,
        out_ao,
        out_gain_two,
        out_gate,
        out_up,
        out_down,
    )


def solution(mesh):
    placed = (
        P("dp", "seq", None),
        P("dp", "seq", None),
        P("dp", None),
        P(),
        P(("dp", "seq")),
        P(("dp", "seq"), "tensor"),
        P(("dp", "seq"), "tensor"),
        P(),
        P(("dp", "seq"), "tensor"),
        P(),
        P(),
        P(),
        P(),
        P(),
        P(),
        P("tensor", ("dp", "seq")),
        P(("dp", "seq"), "tensor"),
        P(("dp", "seq"), "tensor"),
        P(("dp", "seq"), "tensor"),
        P("tensor", ("dp", "seq")),
        P(("dp", "seq")),
        P(("dp", "seq"), "tensor"),
        P(("dp", "seq"), "tensor"),
        P("tensor", ("dp", "seq")),
    )
    return jax.shard_map(
        local,
        mesh=mesh,
        in_specs=placed,
        out_specs=(
            P("dp", "seq", None),
            P("dp", "seq", None),
            P(("dp", "seq")),
            P(("dp", "seq"), "tensor"),
            P(("dp", "seq"), "tensor"),
            P(),
            P(("dp", "seq"), "tensor"),
            P(),
            P(),
            P(),
            P(),
            P(),
            P(),
            P("tensor", ("dp", "seq")),
            P(("dp", "seq"), "tensor"),
            P(("dp", "seq"), "tensor"),
            P(("dp", "seq"), "tensor"),
            P("tensor", ("dp", "seq")),
            P(("dp", "seq")),
            P(("dp", "seq"), "tensor"),
            P(("dp", "seq"), "tensor"),
            P("tensor", ("dp", "seq")),
        ),
        check_vma=False,
    )
```

profile of v0, /device:TPU:0, one launch (start us, length us, event | category | flops | bytes accessed | tf_op | source)
XLA Modules:
  0.0 3712.2 jit_solution(11683682886177756026)
XLA Ops:
  9.5 42.5 %all-gather.2 = bf16[16,1,128]{2,1,0:T(2,128)(2,1)S(1)} all-gather(bf16[1,1,128]{2,1,0:T(2,128)(2,1)} %bitcast.629), channel_id=1, replica_groups=mesh['dp'=4,'seq'=4,'tensor'=2] {'dp','seq'}, dimensions={0}, use_global_device_ids=true | all-gather | bytes 4352 | tf_op jit(solution)/shard_map/all_gather | solution.py:311
  57.4 37.4 %all_gather.76 = bf16[2048,24]{0,1:T(8,128)(2,1)S(1)} all-gather(bf16[128,24]{0,1:T(8,128)(2,1)} %param.45), channel_id=1, replica_groups=mesh['dp'=4,'seq'=4,'tensor'=2] {'dp','seq'}, dimensions={0}, use_global_device_ids=true | all-gather | bytes 104448 | tf_op jit(solution)/shard_map/all_gather | solution.py:314
  134.3 44.1 %all_gather.82 = bf16[2048,128]{1,0:T(8,128)(2,1)S(1)} all-gather(bf16[128,128]{1,0:T(8,128)(2,1)S(1)} %copy-done.108), channel_id=1, replica_groups=mesh['dp'=4,'seq'=4,'tensor'=2] {'dp','seq'}, dimensions={0}, use_global_device_ids=true | all-gather | bytes 557056 | tf_op jit(solution)/shard_map/all_gather | solution.py:317
  194.5 41.7 %all_gather.85 = bf16[2048,128]{1,0:T(8,128)(2,1)S(1)} all-gather(bf16[128,128]{1,0:T(8,128)(2,1)} %param.55), channel_id=1, replica_groups=mesh['dp'=4,'seq'=4,'tensor'=2] {'dp','seq'}, dimensions={0}, use_global_device_ids=true | all-gather | bytes 557056 | tf_op jit(solution)/shard_map/all_gather | solution.py:318
  236.9 12.8 all_gather.86
  297.8 50.2 %all-gather.32.cloned.1.call-done = f32[96,64,256]{2,1,0:T(8,128)} async-done(((f32[24,64,256]{2,1,0:T(8,128)}), f32[96,64,256]{2,1,0:T(8,128)}) %all-gather.32.cloned.1.call-update) | async-done | bytes 6291472 | tf_op jit(solution)/shard_map/all_gather | solution.py:31
  353.0 12.5 multiply_reduce_fusion.11
  367.3 98.9 %all-gather.20.cloned.1.call-done = bf16[1536,2048]{1,0:T(8,128)(2,1)} async-done(((bf16[1536,128]{1,0:T(8,128)(2,1)}), bf16[1536,2048]{1,0:T(8,128)(2,1)}) %all-gather.20.cloned.1.call-update) | async-done | bytes 6291472 | tf_op jit(solution)/shard_map/all_gather | solution.py:315
  473.2 57.0 %all-gather.24.cloned.1.call-done = bf16[512,2048]{1,0:T(8,128)(2,1)} async-done(((bf16[512,128]{1,0:T(8,128)(2,1)}), bf16[512,2048]{1,0:T(8,128)(2,1)}) %all-gather.24.cloned.1.call-update) | async-done | bytes 2097168 | tf_op jit(solution)/shard_map/all_gather | solution.py:319
  537.7 37.8 %all-gather.4 = bf16[16,1,128]{2,1,0:T(2,128)(2,1)S(1)} all-gather(bf16[1,1,128]{2,1,0:T(2,128)(2,1)S(1)} %bitcast.630), channel_id=1, replica_groups=mesh['dp'=4,'seq'=4,'tensor'=2] {'dp','seq'}, dimensions={0}, use_global_device_ids=true | all-gather | bytes 4352 | tf_op jit(solution)/shard_map/all_gather | solution.py:320
  581.5 92.8 %all-gather.26.cloned.1.call-done = bf16[2048,2048]{1,0:T(8,128)(2,1)} async-done(((bf16[128,2048]{1,0:T(8,128)(2,1)}), bf16[2048,2048]{1,0:T(8,128)(2,1)}) %all-gather.26.cloned.1.call-update) | async-done | bytes 8388624 | tf_op jit(solution)/shard_map/all_gather | solution.py:321
  683.3 105.2 %all-gather.28.cloned.1.call-done = bf16[2048,2048]{1,0:T(8,128)(2,1)} async-done(((bf16[128,2048]{1,0:T(8,128)(2,1)}), bf16[2048,2048]{1,0:T(8,128)(2,1)}) %all-gather.28.cloned.1.call-update) | async-done | bytes 8388624 | tf_op jit(solution)/shard_map/all_gather | solution.py:322
  799.3 132.7 %all-gather.30.cloned.1.call-done = bf16[2048,2048]{1,0:T(8,128)(2,1)} async-done(((bf16[2048,128]{1,0:T(8,128)(2,1)}), bf16[2048,2048]{1,0:T(8,128)(2,1)}) %all-gather.30.cloned.1.call-update) | async-done | bytes 8388624 | tf_op jit(solution)/shard_map/all_gather | solution.py:323
  943.2 19.4 all-reduce.33.cloned.1.call-done
  991.3 24.1 all-reduce.35.cloned.1.call-done
  1041.2 19.0 conditional.7
  1083.3 16.8 fusion.85
  1126.0 62.0 %all-gather.34.cloned.1.call-done = f32[96,64,256]{2,1,0:T(8,128)} async-done(((f32[24,64,256]{2,1,0:T(8,128)}), f32[96,64,256]{2,1,0:T(8,128)}) %all-gather.34.cloned.1.call-update) | async-done | bytes 6291472 | tf_op jit(solution)/shard_map/all_gather | solution.py:31
  1226.0 15.0 bitcast_add_fusion.3
  1347.9 12.3 fusion.270
  1375.6 73.9 %all-reduce.23 = (f32[2048]{0:T(1024)S(1)}, f32[2048]{0:T(1024)S(1)}) all-reduce(f32[2048]{0:T(1024)S(1)} %get-tuple-element.388, f32[2048]{0:T(1024)S(1)} %copy-done.107), channel_id=6, replica_groups=mesh['dp'=4,'seq'=4,'tensor'=2] {'dp','seq'}, use_global_device_ids=true, to_apply=%region_42.44.clone | all-reduce | flops 4096 | bytes 32768
  1456.0 92.8 %reduce-scatter.32.cloned.1.call-done = f32[512,128]{1,0:T(8,128)} async-done(((f32[512,2048]{1,0:T(8,128)}), f32[512,128]{1,0:T(8,128)}) %reduce-scatter.32.cloned.1.call-update) | async-done | bytes 262160 | tf_op jit(solution)/shard_map/reduce_scatter | solution.py:582
  1548.8 97.4 %reduce-scatter.26.cloned.1.call-done = f32[128,512]{1,0:T(8,128)} async-done(((f32[2048,512]{1,0:T(8,128)}), f32[128,512]{1,0:T(8,128)}) %reduce-scatter.26.cloned.1.call-update) | async-done | bytes 262160 | tf_op jit(solution)/shard_map/reduce_scatter | solution.py:579
  1646.2 130.5 %all-reduce.41.cloned.1.call-done = (f32[3584,4]{0,1:T(4,128)}, f32[3584]{0:T(1024)}, f32[48]{0:T(128)}, f32[48]{0:T(128)}, f32[48]{0:T(128)}, /*index=5*/f32[48,64]{1,0:T(8,128)}) async-done(((f32[3584,4]{0,1:T(4,128)}, f32[3584]{0:T(1024)}, f32[48]{0:T(128)}, f32[48]{0:T(128)}, f32[48]{0:T(128)}, /*index=5*/f32[48,64]{1,0:T(8,128)}), (f32[3584,4]{0,1:T(4,128)}, f32[3584]{0:T(1024)}, f32[48]{0:T(128)}, ...) | async-done | bytes 84560 | tf_op jit(solution)/shard_map/psum | solution.py:547
  1776.8 80.0 %reduce-scatter.22.cloned.1.call-done = f32[128,24]{0,1:T(8,128)} async-done(((f32[2048,24]{0,1:T(8,128)}), f32[128,24]{0,1:T(8,128)}) %reduce-scatter.22.cloned.1.call-update) | async-done | bytes 12304 | tf_op jit(solution)/shard_map/reduce_scatter | solution.py:577
  1856.7 145.1 %all-reduce.39.cloned.1.call-done = f32[2048,512]{1,0:T(8,128)} async-done(((f32[2048,512]{1,0:T(8,128)}), f32[2048,512]{1,0:T(8,128)}) %all-reduce.39.cloned.1.call-update) | async-done | bytes 4194320 | tf_op jit(solution)/shard_map/psum | solution.py:547
  2001.9 209.8 %reduce-scatter.24.cloned.1.call-done = f32[1536,128]{1,0:T(8,128)} async-done(((f32[1536,2048]{1,0:T(8,128)}), f32[1536,128]{1,0:T(8,128)}) %reduce-scatter.24.cloned.1.call-update) | async-done | bytes 786448 | tf_op jit(solution)/shard_map/reduce_scatter | solution.py:578
  2211.7 209.8 %reduce-scatter.18.cloned.1.call-done = f32[128,1536]{1,0:T(8,128)} async-done(((f32[2048,1536]{1,0:T(8,128)}), f32[128,1536]{1,0:T(8,128)}) %reduce-scatter.18.cloned.1.call-update) | async-done | bytes 786448 | tf_op jit(solution)/shard_map/reduce_scatter | solution.py:575
  2421.6 348.9 %reduce-scatter.38.cloned.1.call-done = f32[2048,128]{1,0:T(8,128)} async-done(((f32[2048,2048]{1,0:T(8,128)}), f32[2048,128]{1,0:T(8,128)}) %reduce-scatter.38.cloned.1.call-update) | async-done | bytes 1048592 | tf_op jit(solution)/shard_map/reduce_scatter | solution.py:586
  2770.4 354.8 %reduce-scatter.34.cloned.1.call-done = f32[128,2048]{1,0:T(8,128)} async-done(((f32[2048,2048]{1,0:T(8,128)}), f32[128,2048]{1,0:T(8,128)}) %reduce-scatter.34.cloned.1.call-update) | async-done | bytes 1048592 | tf_op jit(solution)/shard_map/reduce_scatter | solution.py:584
  3125.3 355.0 %reduce-scatter.36.cloned.1.call-done = f32[128,2048]{1,0:T(8,128)} async-done(((f32[2048,2048]{1,0:T(8,128)}), f32[128,2048]{1,0:T(8,128)}) %reduce-scatter.36.cloned.1.call-update) | async-done | bytes 1048592 | tf_op jit(solution)/shard_map/reduce_scatter | solution.py:585
  3480.3 216.9 %reduce-scatter.20.cloned.1.call-done = f32[128,1536]{1,0:T(8,128)} async-done(((f32[2048,1536]{1,0:T(8,128)}), f32[128,1536]{1,0:T(8,128)}) %reduce-scatter.20.cloned.1.call-update) | async-done | bytes 786448 | tf_op jit(solution)/shard_map/reduce_scatter | solution.py:576
  (575 shorter events, 498.2 us)
Async XLA Ops:
  7.2 101.3 %all-gather.16.cloned.1.call-start = ((), (), s32[]{:S(2)}) async-start(), calls=%async_computation.13 | async-start | bytes 6684672 | tf_op jit(solution)/shard_map/all_gather | solution.py:313
  7.9 249.8 %all-gather.22.cloned.1.call-start = ((), (), s32[]{:S(2)}) async-start(), calls=%async_computation.16 | async-start | bytes 2228224 | tf_op jit(solution)/shard_map/all_gather | solution.py:316
  8.7 269.5 %all-gather.18.cloned.1.call-start = ((), (), s32[]{:S(2)}) async-start(), calls=%async_computation.14 | async-start | bytes 6684672 | tf_op jit(solution)/shard_map/all_gather | solution.py:312
  9.4 338.6 %all-gather.32.cloned.1.call-start = ((), (), s32[]{:S(2)}) async-start(), calls=%async_computation.38 | async-start | bytes 7864320 | tf_op jit(solution)/shard_map/all_gather | solution.py:31
  52.0 235.0 %copy-start.55 = (f32[16,1,128]{2,1,0:T(1,128)}, f32[16,1,128]{2,1,0:T(1,128)S(1)}, u32[]{:S(2)}) copy-start(f32[16,1,128]{2,1,0:T(1,128)S(1)} %convert_element_type.295) | copy-start | bytes 24580
  114.5 4.7 collective-permute-start
  132.2 333.9 %all-gather.20.cloned.1.call-start = ((), (), s32[]{:S(2)}) async-start(), calls=%async_computation.15 | async-start | bytes 6684672 | tf_op jit(solution)/shard_map/all_gather | solution.py:315
  132.8 397.4 %all-gather.24.cloned.1.call-start = ((), (), s32[]{:S(2)}) async-start(), calls=%async_computation.17 | async-start | bytes 2228224 | tf_op jit(solution)/shard_map/all_gather | solution.py:319
  133.4 442.1 %all-reduce.31.cloned.1.call-start = ((), (), s32[]{:S(2)}) async-start(), calls=%async_computation.18 | async-start | bytes 6291456 | tf_op jit(solution)/shard_map/psum | solution.py:400
  535.5 138.7 %all-gather.26.cloned.1.call-start = ((), (), s32[]{:S(2)}) async-start(), calls=%async_computation.19 | async-start | bytes 8912896 | tf_op jit(solution)/shard_map/all_gather | solution.py:321
  536.3 252.2 %all-gather.28.cloned.1.call-start = ((), (), s32[]{:S(2)}) async-start(), calls=%async_computation.20 | async-start | bytes 8912896 | tf_op jit(solution)/shard_map/all_gather | solution.py:322
  537.0 395.0 %all-gather.30.cloned.1.call-start = ((), (), s32[]{:S(2)}) async-start(), calls=%async_computation.21 | async-start | bytes 8912896 | tf_op jit(solution)/shard_map/all_gather | solution.py:323
  537.6 425.0 %all-reduce.33.cloned.1.call-start = ((), (), s32[]{:S(2)}) async-start(), calls=%async_computation.22 | async-start | bytes 6291456 | tf_op jit(solution)/shard_map/psum | solution.py:406
  941.1 74.3 %all-reduce.35.cloned.1.call-start = ((), (), s32[]{:S(2)}) async-start(), calls=%async_computation.23 | async-start | bytes 6291456 | tf_op jit(solution)/shard_map/psum | solution.py:446
  990.8 126.4 %reduce-scatter.40.cloned.1.call-start = ((), (), s32[]{:S(2)}) async-start(), calls=%async_computation.40 | async-start | bytes 491520
  1062.3 60.3 %reduce-scatter.16.cloned.1.call-start = ((), (), s32[]{:S(2)}) async-start(), calls=%async_computation.24 | async-start | bytes 491520 | tf_op jit(solution)/shard_map/reduce_scatter | solution.py:486
  1070.1 117.9 %all-gather.34.cloned.1.call-start = ((), (), s32[]{:S(2)}) async-start(), calls=%async_computation.39 | async-start | bytes 7864320 | tf_op jit(solution)/shard_map/all_gather | solution.py:31
  1080.6 291.9 %all-reduce.37.cloned.1.call-start = ((), (), s32[]{:S(2)}) async-start(), calls=%async_computation.25 | async-start | bytes 3145728 | tf_op jit(solution)/shard_map/psum | solution.py:524
  1255.8 5.9 collective-permute-start.1
  1274.5 181.5 %reduce-scatter.28.cloned.1.call-start = ((), (), s32[]{:S(2)}) async-start(), calls=%async_computation.32 | async-start | bytes 1114112 | tf_op jit(solution)/shard_map/reduce_scatter | solution.py:580
  1277.8 178.2 %reduce-scatter.30.cloned.1.call-start = ((), (), s32[]{:S(2)}) async-start(), calls=%async_computation.33 | async-start | bytes 1114112 | tf_op jit(solution)/shard_map/reduce_scatter | solution.py:581
  1280.9 267.9 %reduce-scatter.32.cloned.1.call-start = ((), (), s32[]{:S(2)}) async-start(), calls=%async_computation.34 | async-start | bytes 4456448 | tf_op jit(solution)/shard_map/reduce_scatter | solution.py:582
  1285.8 360.5 %reduce-scatter.26.cloned.1.call-start = ((), (), s32[]{:S(2)}) async-start(), calls=%async_computation.31 | async-start | bytes 4456448 | tf_op jit(solution)/shard_map/reduce_scatter | solution.py:579
  1291.7 485.1 %all-reduce.41.cloned.1.call-start = ((), (), s32[]{:S(2)}) async-start(), calls=%async_computation.41 | async-start | bytes 199680 | tf_op jit(solution)/shard_map/psum | solution.py:547
  1294.6 562.1 %reduce-scatter.22.cloned.1.call-start = ((), (), s32[]{:S(2)}) async-start(), calls=%async_computation.29 | async-start | bytes 208896 | tf_op jit(solution)/shard_map/reduce_scatter | solution.py:577
  1297.1 704.7 %all-reduce.39.cloned.1.call-start = ((), (), s32[]{:S(2)}) async-start(), calls=%async_computation.28 | async-start | bytes 8388608 | tf_op jit(solution)/shard_map/psum | solution.py:547
  1304.5 907.2 %reduce-scatter.24.cloned.1.call-start = ((), (), s32[]{:S(2)}) async-start(), calls=%async_computation.30 | async-start | bytes 13369344 | tf_op jit(solution)/shard_map/reduce_scatter | solution.py:578
  1313.6 1107.9 %reduce-scatter.18.cloned.1.call-start = ((), (), s32[]{:S(2)}) async-start(), calls=%async_computation.26 | async-start | bytes 13369344 | tf_op jit(solution)/shard_map/reduce_scatter | solution.py:575
  1323.0 1447.4 %reduce-scatter.38.cloned.1.call-start = ((), (), s32[]{:S(2)}) async-start(), calls=%async_computation.37 | async-start | bytes 17825792 | tf_op jit(solution)/shard_map/reduce_scatter | solution.py:586
  1335.3 1789.9 %reduce-scatter.34.cloned.1.call-start = ((), (), s32[]{:S(2)}) async-start(), calls=%async_computation.35 | async-start | bytes 17825792 | tf_op jit(solution)/shard_map/reduce_scatter | solution.py:584
  1347.8 2132.5 %reduce-scatter.36.cloned.1.call-start = ((), (), s32[]{:S(2)}) async-start(), calls=%async_computation.36 | async-start | bytes 17825792 | tf_op jit(solution)/shard_map/reduce_scatter | solution.py:585
  1360.2 2337.0 %reduce-scatter.20.cloned.1.call-start = ((), (), s32[]{:S(2)}) async-start(), calls=%async_computation.27 | async-start | bytes 13369344 | tf_op jit(solution)/shard_map/reduce_scatter | solution.py:576
  (149 other events, 2266.4 us)
Sparse Core Ops, SparseCore 0:
  10.8 97.6 all-gather.15
  111.3 63.6 all-gather.21
  177.8 98.6 all-gather.17
  278.8 69.1 all-gather.31
  350.6 115.5 all-gather.19
  468.7 61.4 all-gather.23
  535.6 21.3 all-reduce.30
  560.2 113.9 all-gather.25
  677.4 111.0 all-gather.27
  791.4 140.5 all-gather.29
  941.2 21.3 all-reduce.32
  990.9 24.3 all-reduce.34
  1062.4 25.6 reduce-scatter.39
  1091.5 24.4 reduce-scatter.15
  1117.8 70.1 all-gather.33
  1274.7 20.9 all-reduce.36
  1298.3 79.0 reduce-scatter.27
  1380.2 74.1 reduce-scatter.29
  1457.2 91.5 reduce-scatter.31
  1551.5 94.6 reduce-scatter.25
  1653.8 122.9 all-reduce.40
  1779.6 77.1 reduce-scatter.21
  1863.8 138.0 all-reduce.38
  2008.9 202.7 reduce-scatter.23
  2217.9 203.5 reduce-scatter.17
  2424.4 345.9 reduce-scatter.37
  2773.2 351.9 reduce-scatter.33
  3128.2 352.0 reduce-scatter.35
  3487.5 209.6 reduce-scatter.19
where the time goes:
time: 3720 us; the launch traced here: 3710 us
  waiting for transfers between devices  2890 us (78%)
  matrix products  326 us (9%)
  blocking collectives  310 us (8%)
  other arithmetic  93.4 us (3%)
  local copies, waits for them, and re-layouts  62.1 us (2%)
    reduce_scatter x1, waiting for transfers between devices, local(): lax.psum_scatter(grad_up, ('dp', 'seq'), scatter_dimension=0, tiled=True)  355 us
    reduce_scatter x1, waiting for transfers between devices, local(): lax.psum_scatter(grad_gate, ('dp', 'seq'), scatter_dimension=0, tiled=True)  355 us
    reduce_scatter x1, waiting for transfers between devices, local(): lax.psum_scatter(grad_down, ('dp', 'seq'), scatter_dimension=1, tiled=True)  349 us
    psum x2, waiting for transfers between devices, local(): lax.psum((grad_bc, grad_conv_full, grad_bias_full, grad_dtb_full, grad_al...  276 us
    reduce_scatter x1, waiting for transfers between devices, local(): lax.psum_scatter(grad_x, ('dp', 'seq'), scatter_dimension=0, tiled=True)  217 us
    reduce_scatter x1, waiting for transfers between devices, local(): lax.psum_scatter(grad_z, ('dp', 'seq'), scatter_dimension=0, tiled=True)  210 us
    reduce_scatter x1, waiting for transfers between devices, local(): lax.psum_scatter(grad_mo, ('dp', 'seq'), scatter_dimension=1, tiled=True)  210 us
    all_gather x1, waiting for transfers between devices, local(): lax.all_gather(w_down, ('dp', 'seq'), axis=1, tiled=True)  133 us
  transfers between devices with their start and end apart: 31, of which 23 were waited for; matrix products, arithmetic and copies ran while one was open for 8% of the time, Pallas kernels for 0%

commit v1 on v0

--- a/solution.py
+++ b/solution.py
@@ -3,6 +3,8 @@
 import jax
 import jax.numpy as jnp
 from jax import lax
+from jax.experimental import pallas as pl
+from jax.experimental.pallas import tpu as pltpu
 from jax.sharding import PartitionSpec as P
 
 MH = 48
@@ -611,6 +613,1168 @@
     )
 
 
+GROUP = 4
+CHUNK = 128
+HEADS = 6
+MESH_ID = pl.DeviceIdType.MESH
+VMEM_BYTES = 56 * 1024 * 1024
+
+
+def dot_f32(left_side, right_side, left_dim, right_dim):
+    return lax.dot_general(
+        left_side,
+        right_side,
+        (((left_dim,), (right_dim,)), ((), ())),
+        preferred_element_type=jnp.float32,
+    )
+
+
+def halves(values):
+    high = values.astype(jnp.bfloat16)
+    return (high, (values - high.astype(jnp.float32)).astype(jnp.bfloat16))
+
+
+def dot_split(exact, parts, left_dim, right_dim):
+    high, low = parts
+    return dot_f32(exact, high, left_dim, right_dim) + dot_f32(exact, low, left_dim, right_dim)
+
+
+def dot_split_left(parts, exact, left_dim, right_dim):
+    high, low = parts
+    return dot_f32(high, exact, left_dim, right_dim) + dot_f32(low, exact, left_dim, right_dim)
+
+
+def dot_splits(left_parts, right_parts, left_dim, right_dim):
+    left_high, left_low = left_parts
+    right_high, right_low = right_parts
+    return dot_f32(left_high, right_high, left_dim, right_dim) + (
+        dot_f32(left_high, right_low, left_dim, right_dim)
+        + dot_f32(left_low, right_high, left_dim, right_dim)
+    )
+
+
+def plane_place():
+    data, place, core = lax.axis_index("dp"), lax.axis_index("seq"), lax.axis_index("tensor")
+    along_x = place + 1 - 2 * lax.rem(place, 2)
+    along_y = lax.rem(place + 2, GROUP)
+    across = GROUP - 1 - place
+    return (data, place, core, along_x, along_y, across)
+
+
+def meet(devices):
+    barrier = pltpu.get_barrier_semaphore()
+    for device in devices:
+        pl.semaphore_signal(barrier, inc=1, device_id=device, device_id_type=MESH_ID)
+    pl.semaphore_wait(barrier, len(devices))
+
+
+def remote(source, target, send_sem, recv_sem, device):
+    return pltpu.make_async_remote_copy(
+        src_ref=source,
+        dst_ref=target,
+        send_sem=send_sem,
+        recv_sem=recv_sem,
+        device_id=device,
+        device_id_type=MESH_ID,
+    )
+
+
+def any_specs(count):
+    return [pl.BlockSpec(memory_space=pl.ANY)] * count
+
+
+def vmem_specs(count):
+    return [pl.BlockSpec(memory_space=pltpu.VMEM)] * count
+
+
+def gather_kernel(own_ref, all_ref, local_sem, send_sems, recv_sems):
+    data, place, core, along_x, along_y, across = plane_place()
+    half = own_ref.shape[0] // 2
+    to_x, to_y, partner = (data, along_x, core), (data, along_y, core), (data, place, 1 - core)
+
+    def block(chip, part):
+        return all_ref.at[2 * chip + core, pl.ds(part * half, half)]
+
+    meet((to_x, to_y, partner))
+    own = pltpu.make_async_copy(own_ref, all_ref.at[2 * place + core], local_sem)
+    own.start()
+
+    def push(index, source, target, device):
+        copy = remote(source, target, send_sems.at[index], recv_sems.at[index], device)
+        copy.start()
+        return copy
+
+    first, second = own_ref.at[pl.ds(0, half)], own_ref.at[pl.ds(half, half)]
+    x_first = push(0, first, block(place, 0), to_x)
+    y_second = push(1, second, block(place, 1), to_y)
+    x_second = push(2, second, block(place, 1), to_x)
+    y_first = push(3, first, block(place, 0), to_y)
+    pair_own = push(4, own_ref, all_ref.at[2 * place + core], partner)
+    x_first.wait_recv()
+    over_y = push(5, block(along_x, 0), block(along_x, 0), to_y)
+    y_second.wait_recv()
+    over_x = push(6, block(along_y, 1), block(along_y, 1), to_x)
+    x_second.wait_recv()
+    mine_x = all_ref.at[2 * along_x + core]
+    pair_x = push(7, mine_x, mine_x, partner)
+    y_first.wait_recv()
+    mine_y = all_ref.at[2 * along_y + core]
+    pair_y = push(8, mine_y, mine_y, partner)
+    over_y.wait_recv()
+    pair_a = push(9, block(across, 0), block(across, 0), partner)
+    over_x.wait_recv()
+    pair_b = push(10, block(across, 1), block(across, 1), partner)
+    own.wait()
+    for copy in (pair_own, pair_x, pair_y, pair_a, pair_b):
+        copy.wait_recv()
+    for copy in (
+        x_first,
+        y_second,
+        x_second,
+        y_first,
+        pair_own,
+        over_y,
+        over_x,
+        pair_x,
+        pair_y,
+        pair_a,
+        pair_b,
+    ):
+        copy.wait_send()
+
+
+def gather_plane(own):
+    rows, width = own.shape
+    gathered = pl.pallas_call(
+        gather_kernel,
+        out_shape=jax.ShapeDtypeStruct((2 * GROUP, rows, width), own.dtype),
+        in_specs=any_specs(1),
+        out_specs=any_specs(1)[0],
+        scratch_shapes=[
+            pltpu.SemaphoreType.DMA,
+            pltpu.SemaphoreType.DMA((11,)),
+            pltpu.SemaphoreType.DMA((11,)),
+        ],
+        compiler_params=pltpu.CompilerParams(collective_id=1, has_side_effects=True),
+    )(own)
+    return gathered.reshape(2 * GROUP * rows, width)
+
+
+def scatter_kernel(part_ref, sum_ref, pair_in, outgoing, arrived, pair_s, pair_r, send_s, recv_s):
+    data, place, core, along_x, along_y, across = plane_place()
+    partner = (data, place, 1 - core)
+    others = (across, along_x, along_y)
+    step = 16
+    laps = part_ref.shape[1] // step
+    meet([partner] + [(data, chip, core) for chip in others])
+    pair = []
+    for index, chip in enumerate(others + (place,)):
+        copy = remote(
+            part_ref.at[2 * chip + 1 - core],
+            pair_in.at[index],
+            pair_s.at[index],
+            pair_r.at[index],
+            partner,
+        )
+        copy.start()
+        pair.append(copy)
+    sends = []
+    for index, chip in enumerate(others):
+        pair[index].wait_recv()
+
+        def add_pair(lap, carry, index=index, chip=chip):
+            rows = pl.ds(lap * step, step)
+            outgoing[index, rows] = (
+                part_ref[2 * chip + core, rows].astype(jnp.float32)
+                + pair_in[index, rows].astype(jnp.float32)
+            ).astype(jnp.bfloat16)
+            return carry
+
+        lax.fori_loop(0, laps, add_pair, 0)
+        copy = remote(
+            outgoing.at[index],
+            arrived.at[index],
+            send_s.at[index],
+            recv_s.at[index],
+            (data, chip, core),
+        )
+        copy.start()
+        sends.append(copy)
+    pair[3].wait_recv()
+    for copy in sends:
+        copy.wait_recv()
+
+    def add_all(lap, carry):
+        rows = pl.ds(lap * step, step)
+        total = part_ref[2 * place + core, rows].astype(jnp.float32)
+        total = total + pair_in[3, rows].astype(jnp.float32)
+        for index in range(3):
+            total = total + arrived[index, rows].astype(jnp.float32)
+        sum_ref[rows] = total
+        return carry
+
+    lax.fori_loop(0, laps, add_all, 0)
+    for copy in pair + sends:
+        copy.wait_send()
+
+
+def scatter_plane(part):
+    rows, width = part.shape[0] // (2 * GROUP), part.shape[1]
+    return pl.pallas_call(
+        scatter_kernel,
+        out_shape=jax.ShapeDtypeStruct((rows, width), jnp.float32),
+        in_specs=vmem_specs(1),
+        out_specs=vmem_specs(1)[0],
+        scratch_shapes=[
+            pltpu.VMEM((4, rows, width), jnp.bfloat16),
+            pltpu.VMEM((3, rows, width), jnp.bfloat16),
+            pltpu.VMEM((3, rows, width), jnp.bfloat16),
+            pltpu.SemaphoreType.DMA((4,)),
+            pltpu.SemaphoreType.DMA((4,)),
+            pltpu.SemaphoreType.DMA((3,)),
+            pltpu.SemaphoreType.DMA((3,)),
+        ],
+        compiler_params=pltpu.CompilerParams(
+            collective_id=2, has_side_effects=True, vmem_limit_bytes=VMEM_BYTES
+        ),
+    )(part.reshape(2 * GROUP, rows, width))
+
+
+def exchange_kernel(moves, count_in, *refs):
+    data, place, core, along_x, along_y, across = plane_place()
+    sources, targets = refs[:count_in], refs[count_in:-3]
+    local_sems, send_sems, recv_sems = refs[-3:]
+    others = (across, along_x, along_y)
+    meet([(data, chip, core) for chip in others])
+    copies = []
+    for index, chip in enumerate(others):
+        for at, move in enumerate(moves):
+            source, target = move(sources, targets, place, chip)
+            copy = remote(
+                source,
+                target,
+                send_sems.at[index, at],
+                recv_sems.at[index, at],
+                (data, chip, core),
+            )
+            copy.start()
+            copies.append(copy)
+    own = []
+    for at, move in enumerate(moves):
+        source, target = move(sources, targets, place, place)
+        copy = pltpu.make_async_copy(source, target, local_sems.at[at])
+        copy.start()
+        own.append(copy)
+    for copy in own:
+        copy.wait()
+    for copy in copies:
+        copy.wait()
+
+
+def exchange_plane(moves, arrays, out_shapes, identity):
+    shapes = tuple(jax.ShapeDtypeStruct(shape, jnp.bfloat16) for shape in out_shapes)
+    return pl.pallas_call(
+        partial(exchange_kernel, moves, len(arrays)),
+        out_shape=shapes,
+        in_specs=any_specs(len(arrays)),
+        out_specs=any_specs(len(shapes)),
+        scratch_shapes=[
+            pltpu.SemaphoreType.DMA((len(moves),)),
+            pltpu.SemaphoreType.DMA((3, len(moves))),
+            pltpu.SemaphoreType.DMA((3, len(moves))),
+        ],
+        compiler_params=pltpu.CompilerParams(collective_id=identity, has_side_effects=True),
+    )(*arrays)
+
+
+def column_move(source, target, start, width):
+    def move(sources, targets, place, chip):
+        columns = pl.ds(pl.multiple_of(chip * width, 128), width)
+        return (
+            sources[source].at[:, columns],
+            targets[target].at[place, :, pl.ds(start, width)],
+        )
+
+    return move
+
+
+def row_move(source, target, start, height):
+    def move(sources, targets, place, chip):
+        rows = pl.ds(pl.multiple_of(chip * height, 16), height)
+        return (
+            sources[source].at[rows],
+            targets[target].at[place, pl.ds(start, height)],
+        )
+
+    return move
+
+
+def block_move(source, target):
+    def move(sources, targets, place, chip):
+        return (sources[source].at[chip], targets[target].at[place])
+
+    return move
+
+
+def misc_move(source, target, start):
+    def move(sources, targets, place, chip):
+        return (
+            sources[source].at[chip],
+            targets[target].at[place, :, pl.ds(start, 128)],
+        )
+
+    return move
+
+
+def lane_masks():
+    lane = lax.broadcasted_iota(jnp.int32, (1, 2 * HP), 1)
+    return (lane < HP, lane >= HP)
+
+
+def pair_columns(ref, pair):
+    low, high = lane_masks()
+    return jnp.where(low, ref[:, 2 * pair : 2 * pair + 1], ref[:, 2 * pair + 1 : 2 * pair + 2])
+
+
+def head_sums(values):
+    low, high = lane_masks()
+    first = jnp.sum(jnp.where(low, values, 0.0), axis=1, keepdims=True)
+    second = jnp.sum(jnp.where(high, values, 0.0), axis=1, keepdims=True)
+    return (first, second)
+
+
+def head_means(values):
+    low, high = lane_masks()
+    first, second = head_sums(values)
+    return jnp.where(low, first, second) * (1.0 / HP)
+
+
+def stack_heads(values):
+    low, high = lane_masks()
+    zero = jnp.zeros_like(values)
+    return jnp.concatenate([jnp.where(low, values, zero), jnp.where(high, values, zero)], axis=0)
+
+
+def allowed_in(segc_ref, segr_ref):
+    size = segc_ref.shape[0]
+    row = lax.broadcasted_iota(jnp.int32, (size, size), 0)
+    column = lax.broadcasted_iota(jnp.int32, (size, size), 1)
+    return (segc_ref[...] == segr_ref[0]) & (row >= column)
+
+
+def head_decay(allowed, cumc_ref, cumr_ref, head):
+    differ = cumc_ref[:, head : head + 1] - cumr_ref[0, head : head + 1, :]
+    return jnp.exp(jnp.where(allowed, differ, -jnp.inf))
+
+
+def ssd_forward_kernel(
+    x_ref,
+    b_ref,
+    c_ref,
+    z_ref,
+    dtr_ref,
+    cumc_ref,
+    cumr_ref,
+    enter_ref,
+    leave_ref,
+    segc_ref,
+    segr_ref,
+    skip_ref,
+    gain_ref,
+    gated_ref,
+    ssm_ref,
+    states_ref,
+    state,
+):
+    @pl.when(pl.program_id(0) == 0)
+    def _():
+        state[...] = jnp.zeros_like(state)
+
+    size = x_ref.shape[0]
+    entry = state[...]
+    states_ref[0] = entry
+    b_rows, c_rows = b_ref[...], c_ref[...]
+    gram = dot_f32(c_rows, b_rows, 1, 1)
+    allowed = allowed_in(segc_ref, segr_ref)
+    entered = dot_split(c_rows, halves(entry), 1, 0)
+    for pair in range(HEADS // 2):
+        lanes = slice(2 * HP * pair, 2 * HP * (pair + 1))
+        heads_x = x_ref[:, lanes]
+        mixing = [
+            gram * head_decay(allowed, cumc_ref, cumr_ref, head) * dtr_ref[0, head : head + 1, :]
+            for head in (2 * pair, 2 * pair + 1)
+        ]
+        out = dot_split_left(
+            halves(jnp.concatenate(mixing, axis=1)), stack_heads(heads_x), 1, 0
+        )
+        wide_x = heads_x.astype(jnp.float32)
+        enter = pair_columns(enter_ref, pair)
+        out = out + enter * entered[:, lanes] + skip_ref[:, lanes] * wide_x
+        ssm_ref[:, lanes] = out
+        gate = z_ref[:, lanes]
+        value = out * (gate * jax.nn.sigmoid(gate))
+        scale = lax.rsqrt(head_means(value * value) + GROUP_EPSILON)
+        gated_ref[:, lanes] = (value * scale * gain_ref[:, lanes]).astype(jnp.bfloat16)
+        weighted = halves(pair_columns(leave_ref, pair) * wide_x)
+        state[:, lanes] = enter[size - 1 :, :] * entry[:, lanes] + dot_split(
+            b_rows, weighted, 0, 0
+        )
+
+
+def ssd_backward_kernel(
+    x_ref,
+    b_ref,
+    c_ref,
+    z_ref,
+    dtr_ref,
+    cumc_ref,
+    cumr_ref,
+    enter_ref,
+    leave_ref,
+    segc_ref,
+    segr_ref,
+    skip_ref,
+    gain_ref,
+    ssm_ref,
+    states_ref,
+    dgated_ref,
+    dx_ref,
+    db_ref,
+    dc_ref,
+    dz_ref,
+    rowsum_ref,
+    dleave_ref,
+    denter_ref,
+    colsum_ref,
+    carry_ref,
+    dskip_ref,
+    dgain_ref,
+    state,
+):
+    @pl.when(pl.program_id(0) == 0)
+    def _():
+        state[...] = jnp.zeros_like(state)
+        dskip_ref[...] = jnp.zeros_like(dskip_ref)
+        dgain_ref[...] = jnp.zeros_like(dgain_ref)
+
+    size = x_ref.shape[0]
+    later = state[...]
+    later_parts = halves(later)
+    entry = states_ref[0]
+    entry_parts = halves(entry)
+    carry_ref[0] = jnp.sum(later * entry, axis=0, keepdims=True)
+    b_rows, c_rows = b_ref[...], c_ref[...]
+    gram = dot_f32(c_rows, b_rows, 1, 1)
+    allowed = allowed_in(segc_ref, segr_ref)
+    entered = dot_split(c_rows, entry_parts, 1, 0)
+    d_weighted = dot_split(b_rows, later_parts, 1, 0)
+    d_gram = jnp.zeros((size, size), jnp.float32)
+    d_c = jnp.zeros(c_rows.shape, jnp.float32)
+    d_b = jnp.zeros(b_rows.shape, jnp.float32)
+    low, high = lane_masks()
+    rowsum_ref[...] = jnp.zeros_like(rowsum_ref)
+    dleave_ref[...] = jnp.zeros_like(dleave_ref)
+    denter_ref[...] = jnp.zeros_like(denter_ref)
+    colsum_ref[...] = jnp.zeros_like(colsum_ref)
+    for pair in range(HEADS // 2):
+        lanes = slice(2 * HP * pair, 2 * HP * (pair + 1))
+        heads_x = x_ref[:, lanes]
+        wide_x = heads_x.astype(jnp.float32)
+        ssm, gate, gain = ssm_ref[:, lanes], z_ref[:, lanes], gain_ref[:, lanes]
+        d_gated = dgated_ref[:, lanes]
+        sigmoid = jax.nn.sigmoid(gate)
+        silu = gate * sigmoid
+        value = ssm * silu
+        scale = lax.rsqrt(head_means(value * value) + GROUP_EPSILON)
+        dgain_ref[:, lanes] += jnp.sum(d_gated * value * scale, axis=0, keepdims=True)
+        d_scaled = d_gated * gain
+        d_value = scale * d_scaled - value * (scale * scale * scale) * head_means(d_scaled * value)
+        d_out = d_value * silu
+        dz_ref[:, lanes] = (d_value * ssm * (sigmoid * (1.0 + gate * (1.0 - sigmoid)))).astype(
+            jnp.bfloat16
+        )
+        dskip_ref[:, lanes] += jnp.sum(d_out * wide_x, axis=0, keepdims=True)
+        enter, leave = pair_columns(enter_ref, pair), pair_columns(leave_ref, pair)
+        d_out_parts = [stack_heads(half) for half in halves(d_out)]
+        mixing = []
+        for side in range(2):
+            head = 2 * pair + side
+            d_mixing = dot_split_left(
+                [half[size * side : size * (side + 1)] for half in d_out_parts], heads_x, 1, 1
+            )
+            decay = head_decay(allowed, cumc_ref, cumr_ref, head)
+            dt_row = dtr_ref[0, head : head + 1, :]
+            weighted_gram = gram * decay
+            mixing.append(weighted_gram * dt_row)
+            d_gram = d_gram + d_mixing * (decay * dt_row)
+            product = d_mixing * weighted_gram
+            colsum_ref[0, head : head + 1, :] = jnp.sum(product, axis=0, keepdims=True)
+            rowsum_ref[:, head : head + 1] = jnp.sum(product * dt_row, axis=1, keepdims=True)
+        d_x = dot_splits(halves(jnp.concatenate(mixing, axis=0)), d_out_parts, 0, 0)
+        first, second = head_sums(d_out * entered[:, lanes])
+        denter_ref[:, 2 * pair : 2 * pair + 1] = first
+        denter_ref[:, 2 * pair + 1 : 2 * pair + 2] = second
+        first, second = head_sums(d_weighted[:, lanes] * wide_x)
+        dleave_ref[:, 2 * pair : 2 * pair + 1] = first
+        dleave_ref[:, 2 * pair + 1 : 2 * pair + 2] = second
+        dx_ref[:, lanes] = d_x + skip_ref[:, lanes] * d_out + leave * d_weighted[:, lanes]
+        d_entered = halves(enter * d_out)
+        weighted = halves(leave * wide_x)
+        d_c = d_c + dot_splits(d_entered, [half[:, lanes] for half in entry_parts], 1, 1)
+        d_b = d_b + dot_splits(weighted, [half[:, lanes] for half in later_parts], 1, 1)
+        state[:, lanes] = enter[size - 1 :, :] * later[:, lanes] + dot_split(
+            c_rows, d_entered, 0, 0
+        )
+    d_gram_parts = halves(d_gram)
+    dc_ref[...] = d_c + dot_split_left(d_gram_parts, b_rows, 1, 0)
+    db_ref[...] = d_b + dot_split_left(d_gram_parts, c_rows, 0, 0)
+
+
+def ssd_specs(length, reverse):
+    laps = length // CHUNK
+
+    def at(lap):
+        return laps - 1 - lap if reverse else lap
+
+    def tall(width):
+        return pl.BlockSpec((CHUNK, width), lambda lap: (at(lap), 0))
+
+    def flat(height):
+        return pl.BlockSpec((1, height, CHUNK), lambda lap: (at(lap), 0, 0))
+
+    def whole(width):
+        return pl.BlockSpec((1, width), lambda lap: (0, 0))
+
+    def slab(height, width):
+        return pl.BlockSpec((1, height, width), lambda lap: (at(lap), 0, 0))
+
+    return (laps, tall, flat, whole, slab)
+
+
+def ssd_forward(arrays):
+    length, width = arrays[0].shape
+    laps, tall, flat, whole, slab = ssd_specs(length, False)
+    return pl.pallas_call(
+        ssd_forward_kernel,
+        grid=(laps,),
+        in_specs=[
+            tall(width),
+            tall(NS),
+            tall(NS),
+            tall(width),
+            flat(8),
+            tall(8),
+            flat(8),
+            tall(8),
+            tall(8),
+            tall(1),
+            flat(1),
+            whole(width),
+            whole(width),
+        ],
+        out_specs=[tall(width), tall(width), slab(NS, width)],
+        out_shape=[
+            jax.ShapeDtypeStruct((length, width), jnp.bfloat16),
+            jax.ShapeDtypeStruct((length, width), jnp.float32),
+            jax.ShapeDtypeStruct((laps, NS, width), jnp.float32),
+        ],
+        scratch_shapes=[pltpu.VMEM((NS, width), jnp.float32)],
+        compiler_params=pltpu.CompilerParams(vmem_limit_bytes=VMEM_BYTES),
+    )(*arrays)
+
+
+def ssd_backward(arrays, ssm, states, d_gated):
+    length, width = arrays[0].shape
+    laps, tall, flat, whole, slab = ssd_specs(length, True)
+    shaped = jax.ShapeDtypeStruct
+    return pl.pallas_call(
+        ssd_backward_kernel,
+        grid=(laps,),
+        in_specs=[
+            tall(width),
+            tall(NS),
+            tall(NS),
+            tall(width),
+            flat(8),
+            tall(8),
+            flat(8),
+            tall(8),
+            tall(8),
+            tall(1),
+            flat(1),
+            whole(width),
+            whole(width),
+            tall(width),
+            slab(NS, width),
+            tall(width),
+        ],
+        out_specs=[
+            tall(width),
+            tall(NS),
+            tall(NS),
+            tall(width),
+            tall(8),
+            tall(8),
+            tall(8),
+            flat(8),
+            slab(1, width),
+            whole(width),
+            whole(width),
+        ],
+        out_shape=[
+            shaped((length, width), jnp.float32),
+            shaped((length, NS), jnp.float32),
+            shaped((length, NS), jnp.float32),
+            shaped((length, width), jnp.bfloat16),
+            shaped((length, 8), jnp.float32),
+            shaped((length, 8), jnp.float32),
+            shaped((length, 8), jnp.float32),
+            shaped((laps, 8, CHUNK), jnp.float32),
+            shaped((laps, 1, width), jnp.float32),
+            shaped((1, width), jnp.float32),
+            shaped((1, width), jnp.float32),
+        ],
+        scratch_shapes=[pltpu.VMEM((NS, width), jnp.float32)],
+        compiler_params=pltpu.CompilerParams(vmem_limit_bytes=VMEM_BYTES),
+    )(*arrays, ssm, states, d_gated)
+
+
+QUERY_ROWS = 256
+
+
+def masked_scores(q_rows, k_ref, segc_ref, segr_ref, start, reach):
+    rows = q_rows.shape[0]
+    scores = dot_f32(q_rows, k_ref[:reach], 1, 1) * HD ** (-0.5)
+    row = lax.broadcasted_iota(jnp.int32, (rows, reach), 0) + start
+    column = lax.broadcasted_iota(jnp.int32, (rows, reach), 1)
+    allowed = (segc_ref[start : start + rows] == segr_ref[:, :reach]) & (row >= column)
+    return jnp.where(allowed, scores, -jnp.inf)
+
+
+def attend_forward_kernel(q_ref, k_ref, v_ref, segc_ref, segr_ref, out_ref, total_ref):
+    for start in range(0, q_ref.shape[0], QUERY_ROWS):
+        reach = start + QUERY_ROWS
+        rows = slice(start, reach)
+        scores = masked_scores(q_ref[rows], k_ref, segc_ref, segr_ref, start, reach)
+        top = jnp.max(scores, axis=1, keepdims=True)
+        powers = jnp.exp(scores - top)
+        total = jnp.sum(powers, axis=1, keepdims=True)
+        probs = (powers * (1.0 / total)).astype(jnp.bfloat16)
+        out_ref[rows] = dot_f32(probs, v_ref[:reach], 1, 0).astype(jnp.bfloat16)
+        total_ref[rows] = top + jnp.log(total)
+
+
+def attend_backward_kernel(
+    q_ref, k_ref, v_ref, segc_ref, segr_ref, total_ref, dout_ref, dq_ref, dk_ref, dv_ref
+):
+    dk_ref[...] = jnp.zeros_like(dk_ref)
+    dv_ref[...] = jnp.zeros_like(dv_ref)
+    for start in range(0, q_ref.shape[0], QUERY_ROWS):
+        reach = start + QUERY_ROWS
+        rows = slice(start, reach)
+        q_rows, d_out = q_ref[rows], dout_ref[rows]
+        scores = masked_scores(q_rows, k_ref, segc_ref, segr_ref, start, reach)
+        probs = jnp.exp(scores - total_ref[rows])
+        d_probs = dot_f32(d_out, v_ref[:reach], 1, 1)
+        delta = jnp.sum(probs * d_probs, axis=1, keepdims=True)
+        d_scores = (probs * (d_probs - delta)).astype(jnp.bfloat16)
+        dq_ref[rows] = dot_f32(d_scores, k_ref[:reach], 1, 0) * HD ** (-0.5)
+        dk_ref[:reach] += dot_f32(d_scores, q_rows, 0, 0) * HD ** (-0.5)
+        dv_ref[:reach] += dot_f32(probs.astype(jnp.bfloat16), d_out, 0, 0)
+
+
+def attend(kernel, arrays, out_shapes):
+    return pl.pallas_call(
+        kernel,
+        in_specs=vmem_specs(len(arrays)),
+        out_specs=vmem_specs(len(out_shapes)),
+        out_shape=[jax.ShapeDtypeStruct(shape, dtype) for shape, dtype in out_shapes],
+        compiler_params=pltpu.CompilerParams(vmem_limit_bytes=VMEM_BYTES),
+    )(*arrays)
+
+
+def turn(cosine, sine_part, first_half, second):
+    return (
+        first_half * cosine - second * sine_part,
+        second * cosine + first_half * sine_part,
+    )
+
+
+def over_chips(block):
+    place = lax.axis_index("seq")
+    count = lax.axis_size("seq")
+    stacked = jnp.zeros((count,) + block.shape, block.dtype)
+    stacked = lax.dynamic_update_index_in_dim(stacked, block, place, 0)
+    for mask in range(1, count):
+        moved = lax.ppermute(block, "seq", [(i, i ^ mask) for i in range(count)])
+        stacked = lax.dynamic_update_index_in_dim(stacked, moved, place ^ mask, 0)
+    return stacked
+
+
+def sum_from_chips(blocks):
+    place = lax.axis_index("seq")
+    count = lax.axis_size("seq")
+    total = lax.dynamic_index_in_dim(blocks, place, 0, False).astype(jnp.float32)
+    for mask in range(1, count):
+        block = lax.dynamic_index_in_dim(blocks, place ^ mask, 0, False)
+        moved = lax.ppermute(block, "seq", [(i, i ^ mask) for i in range(count)])
+        total = total + moved.astype(jnp.float32)
+    return total
+
+
+def both_cores(block):
+    core = lax.axis_index("tensor")
+    other = lax.ppermute(block, "tensor", [(0, 1), (1, 0)])
+    return jnp.where(
+        core == 0,
+        jnp.concatenate([block, other], axis=0),
+        jnp.concatenate([other, block], axis=0),
+    )
+
+
+def heads_local_plan(
+    hidden_in,
+    teacher,
+    segment_ids,
+    valid_mask,
+    norm1_gain,
+    w_z,
+    w_x,
+    w_bc,
+    w_dt,
+    conv_weight,
+    conv_bias,
+    dt_bias,
+    a_log,
+    d_skip,
+    group_gain,
+    w_mamba_out,
+    w_query,
+    w_key,
+    w_value,
+    w_attn_out,
+    norm2_gain,
+    w_gate,
+    w_up,
+    w_down,
+):
+    place, core, data_rank = (
+        lax.axis_index("seq"),
+        lax.axis_index("tensor"),
+        lax.axis_index("dp"),
+    )
+    data_count = lax.axis_size("dp")
+    chip_rows, width = hidden_in.shape[1:]
+    own_rows = chip_rows // 2
+    length = segment_ids.shape[1]
+    slice_rows = w_z.shape[0]
+    width_x = HEADS * HP
+    hidden_units = w_gate.shape[1] // GROUP
+    segment = segment_ids[0]
+    seg_column, seg_row = segment[:, None], segment[None, :]
+    own_start = place * chip_rows + core * own_rows
+    token_count = jnp.sum(valid_mask).astype(jnp.float32)
+    mask_rows = lax.dynamic_slice(valid_mask, (data_rank, own_start), (1, own_rows))[0]
+    total_tokens = float(valid_mask.shape[0] * valid_mask.shape[1])
+    bf16 = jnp.bfloat16
+
+    quarter = HD // (2 * GROUP)
+    misc = jnp.stack(
+        [
+            jnp.concatenate(
+                [
+                    w_key[:, quarter * chip : quarter * (chip + 1)],
+                    w_key[:, HD // 2 + quarter * chip : HD // 2 + quarter * (chip + 1)],
+                    w_value[:, 2 * quarter * chip : 2 * quarter * (chip + 1)],
+                    w_dt[:, HEADS * chip : HEADS * (chip + 1)],
+                    norm1_gain[:, None],
+                    norm2_gain[:, None],
+                    jnp.zeros((slice_rows, 128 - 4 * quarter - HEADS - 2), bf16),
+                ],
+                axis=1,
+            )
+            for chip in range(GROUP)
+        ]
+    )
+    width_in = 2 * width_x + HD + 128
+    (in_slices,) = exchange_plane(
+        (
+            column_move(0, 0, 0, width_x),
+            column_move(1, 0, width_x, width_x),
+            column_move(2, 0, 2 * width_x, HD),
+            misc_move(3, 0, 2 * width_x + HD),
+        ),
+        (w_z, w_x, w_query, misc),
+        [(GROUP, slice_rows, width_in)],
+        3,
+    )
+    full_in = lax.all_gather(in_slices, "dp", axis=0, tiled=True).reshape(width, width_in)
+    hidden_own = lax.dynamic_slice(hidden_in[0], (core * own_rows, 0), (own_rows, width))
+    hidden = gather_plane(hidden_own).astype(jnp.float32)
+    hidden_own = hidden_own.astype(jnp.float32)
+    out_rows = width_x + HD
+    out_slices, gu_slices, down_slices = exchange_plane(
+        (
+            row_move(0, 0, 0, width_x),
+            row_move(1, 0, width_x, HD),
+            column_move(2, 1, 0, hidden_units),
+            column_move(3, 1, hidden_units, hidden_units),
+            row_move(4, 2, 0, hidden_units),
+        ),
+        (w_mamba_out, w_attn_out, w_gate, w_up, w_down),
+        [
+            (GROUP, out_rows, slice_rows),
+            (GROUP, slice_rows, 2 * hidden_units),
+            (GROUP, hidden_units, slice_rows),
+        ],
+        4,
+    )
+    full_out = (
+        lax.all_gather(out_slices, "dp", axis=0, tiled=True)
+        .transpose(1, 0, 2)
+        .reshape(out_rows, width)
+    )
+    full_gu = lax.all_gather(gu_slices, "dp", axis=0, tiled=True).reshape(width, 2 * hidden_units)
+    full_down = (
+        lax.all_gather(down_slices, "dp", axis=0, tiled=True)
+        .transpose(1, 0, 2)
+        .reshape(hidden_units, width)
+    )
+    gain_column = 2 * width_x + HD + 4 * quarter + HEADS
+    gain_one = full_in[:, gain_column].astype(jnp.float32)
+    gain_two = full_in[:, gain_column + 1].astype(jnp.float32)
+
+    scale_one = lax.rsqrt(jnp.mean(hidden * hidden, axis=-1, keepdims=True) + EPSILON)
+    normed = (hidden * scale_one * gain_one).astype(bf16)
+    projected = mat_dot(normed, full_in)
+    gate_z = projected[:, :width_x]
+    pre_all = jnp.concatenate(
+        [projected[:, width_x : 2 * width_x].astype(bf16), mat_dot(normed, w_bc).astype(bf16)],
+        axis=1,
+    )
+    dt_raw = projected[:, 2 * width_x + HD + 4 * quarter :][:, :HEADS]
+    head_start = core * (MH // 2) + place * HEADS
+    positions = jnp.arange(length)
+    frequency = ROPE_BASE ** (-2.0 * jnp.arange(HD // 2).astype(jnp.float32) / HD)
+    angles = positions.astype(jnp.float32)[:, None] * frequency[None, :]
+    cosine, sine_part = jnp.cos(angles), jnp.sin(angles)
+    cos_part = lax.dynamic_slice_in_dim(cosine, quarter * place, quarter, 1)
+    sin_part = lax.dynamic_slice_in_dim(sine_part, quarter * place, quarter, 1)
+    query_raw = projected[:, 2 * width_x : 2 * width_x + HD]
+    queries = jnp.concatenate(
+        turn(cosine, sine_part, query_raw[:, : HD // 2], query_raw[:, HD // 2 :]), axis=1
+    ).astype(bf16)
+    kv_raw = projected[:, 2 * width_x + HD :][:, : 4 * quarter]
+    key_first, key_second = turn(
+        cos_part, sin_part, kv_raw[:, :quarter], kv_raw[:, quarter : 2 * quarter]
+    )
+    kv_all = over_chips(
+        jnp.concatenate([key_first, key_second, kv_raw[:, 2 * quarter :]], axis=1).astype(bf16)
+    )
+    keys = jnp.concatenate(
+        [kv_all[chip, :, :quarter] for chip in range(GROUP)]
+        + [kv_all[chip, :, quarter : 2 * quarter] for chip in range(GROUP)],
+        axis=1,
+    )
+    vals = jnp.concatenate([kv_all[chip, :, 2 * quarter :] for chip in range(GROUP)], axis=1)
+
+    seg_ext = jnp.concatenate([jnp.full((KC - 1,), -1, jnp.int32), segment])
+    extended = jnp.concatenate(
+        [jnp.zeros((KC - 1, pre_all.shape[1]), bf16), pre_all], axis=0
+    ).astype(jnp.float32)
+    conv_local = jnp.concatenate(
+        [
+            lax.dynamic_slice_in_dim(conv_weight, head_start * HP, width_x, 0),
+            conv_weight[MH * HP :],
+        ],
+        axis=0,
+    )
+    bias_local = jnp.concatenate(
+        [lax.dynamic_slice_in_dim(conv_bias, head_start * HP, width_x, 0), conv_bias[MH * HP :]],
+        axis=0,
+    )
+    mixed_f, conv_pull = jax.vjp(
+        partial(conv_silu, seg_ext, segment), extended, conv_local, bias_local
+    )
+    mixed = mixed_f.astype(bf16)
+    heads_x, b_rows, c_rows = (
+        mixed[:, :width_x],
+        mixed[:, width_x : width_x + NS],
+        mixed[:, width_x + NS :],
+    )
+    dt_bias_loc = lax.dynamic_slice_in_dim(dt_bias, head_start, HEADS)
+    rate = jnp.exp(lax.dynamic_slice_in_dim(a_log, head_start, HEADS))
+    skip_loc = lax.dynamic_slice_in_dim(d_skip, head_start, HEADS)
+    gain_loc = lax.dynamic_slice_in_dim(group_gain, head_start, HEADS, 0).reshape(1, width_x)
+    laps = length // CHUNK
+    dt_rows = jax.nn.softplus(dt_raw + dt_bias_loc[None, :])
+    dt_laps = dt_rows.reshape(laps, CHUNK, HEADS)
+    seg_laps = segment.reshape(laps, CHUNK)
+    seg_last = seg_laps[:, -1]
+    seg_before = jnp.concatenate([jnp.full((1,), -1, jnp.int32), seg_last[:-1]])
+    cumul = jnp.cumsum(-rate * dt_laps, axis=1)
+    keep_enter = (seg_laps == seg_before[:, None]).astype(jnp.float32)[:, :, None]
+    keep_leave = (seg_laps == seg_last[:, None]).astype(jnp.float32)[:, :, None]
+    enter = jnp.exp(cumul) * keep_enter
+    leave_bare = jnp.exp(cumul[:, -1:] - cumul) * keep_leave
+    leave = leave_bare * dt_laps
+
+    def tall(values):
+        return jnp.pad(values, ((0, 0), (0, 0), (0, 8 - HEADS))).reshape(length, 8)
+
+    def flat(values):
+        return jnp.pad(values, ((0, 0), (0, 0), (0, 8 - HEADS))).transpose(0, 2, 1)
+
+    ssd_arrays = (
+        heads_x,
+        b_rows,
+        c_rows,
+        gate_z,
+        flat(dt_laps),
+        tall(cumul),
+        flat(cumul),
+        tall(enter),
+        tall(leave),
+        seg_column,
+        seg_laps[:, None, :],
+        jnp.repeat(skip_loc, HP)[None, :],
+        gain_loc,
+    )
+    gated, ssm, states = ssd_forward(ssd_arrays)
+    attended, log_total = attend(
+        attend_forward_kernel,
+        (queries, keys, vals, seg_column, seg_row),
+        (((length, HD), bf16), ((length, 1), jnp.float32)),
+    )
+    outs = jnp.concatenate([gated, attended], axis=1)
+    middle = hidden_own + scatter_plane(mat_dot(outs, full_out).astype(bf16))
+
+    scale_two = lax.rsqrt(jnp.mean(middle * middle, axis=-1, keepdims=True) + EPSILON)
+    normed_two = gather_plane((middle * scale_two * gain_two).astype(bf16))
+    gate_up = mat_dot(normed_two, full_gu)
+    act_f, glu_pull = jax.vjp(swiglu, gate_up[:, :hidden_units], gate_up[:, hidden_units:])
+    activated = act_f.astype(bf16)
+    block_out = middle + scatter_plane(mat_dot(activated, full_down).astype(bf16))
+    teacher_own = lax.dynamic_slice(teacher[0], (core * own_rows, 0), (own_rows, width))
+    d_out = (
+        2.0
+        * total_tokens
+        / token_count
+        * mask_rows.astype(jnp.float32)[:, None]
+        * (block_out - teacher_own.astype(jnp.float32))
+    )
+    d_mlp = gather_plane(d_out.astype(bf16))
+
+    def sum_columns(grads):
+        chunks = grads.astype(bf16).reshape(grads.shape[0], data_count * GROUP, slice_rows)
+        return lax.psum_scatter(
+            chunks.transpose(1, 0, 2), "dp", scatter_dimension=0, tiled=True
+        )
+
+    def sum_rows(grads):
+        summed = lax.psum_scatter(grads.astype(bf16), "dp", scatter_dimension=0, tiled=True)
+        return summed.reshape(GROUP, slice_rows, grads.shape[1])
+
+    grad_down = sum_columns(dot_left_t(activated, d_mlp))
+    d_gate, d_up = glu_pull(dot_right_t(d_mlp, full_down))
+    d_gate_up = jnp.concatenate([d_gate.astype(bf16), d_up.astype(bf16)], axis=1)
+    grad_gate_up = sum_rows(dot_left_t(normed_two, d_gate_up))
+    d_normed_two = scatter_plane(dot_right_t(d_gate_up, full_gu).astype(bf16))
+    grad_gain_two = jnp.sum(d_normed_two * middle * scale_two, axis=0)
+    d_scaled = d_normed_two * gain_two
+    d_middle = (
+        d_out
+        + scale_two * d_scaled
+        - middle * scale_two**3 * jnp.mean(d_scaled * middle, axis=-1, keepdims=True)
+    )
+    d_branch = gather_plane(d_middle.astype(bf16))
+    grad_out = sum_columns(dot_left_t(outs, d_branch))
+    d_outs = dot_right_t(d_branch, full_out)
+    d_query_rot, d_key_part, d_val_part = attend(
+        attend_backward_kernel,
+        (
+            queries,
+            keys,
+            vals,
+            seg_column,
+            seg_row,
+            log_total,
+            d_outs[:, width_x:].astype(bf16),
+        ),
+        (((length, HD), jnp.float32),) * 3,
+    )
+    d_kv = sum_from_chips(
+        jnp.stack(
+            [
+                jnp.concatenate(
+                    [
+                        d_key_part[:, quarter * chip : quarter * (chip + 1)],
+                        d_key_part[:, HD // 2 + quarter * chip : HD // 2 + quarter * (chip + 1)],
+                        d_val_part[:, 2 * quarter * chip : 2 * quarter * (chip + 1)],
+                    ],
+                    axis=1,
+                ).astype(bf16)
+                for chip in range(GROUP)
+            ]
+        )
+    )
+    d_query = jnp.concatenate(
+        turn(cosine, -sine_part, d_query_rot[:, : HD // 2], d_query_rot[:, HD // 2 :]), axis=1
+    )
+    d_key_first, d_key_second = turn(
+        cos_part, -sin_part, d_kv[:, :quarter], d_kv[:, quarter : 2 * quarter]
+    )
+    (
+        d_heads_x,
+        d_b_rows,
+        d_c_rows,
+        d_gate_z,
+        row_sums,
+        d_leave,
+        d_enter,
+        column_sums,
+        d_carry,
+        d_skip_lanes,
+        d_gain_lanes,
+    ) = ssd_backward(ssd_arrays, ssm, states, d_outs[:, :width_x])
+
+    def untall(values):
+        return values.reshape(laps, CHUNK, 8)[:, :, :HEADS]
+
+    column_sums = column_sums.transpose(0, 2, 1)[:, :, :HEADS]
+    d_leave, d_enter = untall(d_leave), untall(d_enter)
+    d_left = d_leave * leave
+    d_cumul = untall(row_sums) - column_sums * dt_laps + d_enter * enter - d_left
+    d_carried = jnp.sum(d_carry.reshape(laps, HEADS, HP), axis=-1) * enter[:, -1]
+    d_cumul = d_cumul.at[:, -1].add(jnp.sum(d_left, axis=1) + d_carried)
+    d_log = lax.cumsum(d_cumul, axis=1, reverse=True)
+    d_dt = column_sums + d_leave * leave_bare - rate * d_log
+    d_dt_f = d_dt.reshape(length, HEADS) * jax.nn.sigmoid(dt_raw + dt_bias_loc[None, :])
+    grad_dtb = jnp.sum(d_dt_f, axis=0)
+    grad_alog = -rate * jnp.sum(d_log * dt_laps, axis=(0, 1))
+    grad_skip = jnp.sum(d_skip_lanes.reshape(HEADS, HP), axis=-1)
+    grad_group = d_gain_lanes.reshape(HEADS, HP)
+    d_ext, grad_conv_loc, grad_bias_loc = conv_pull(
+        jnp.concatenate([d_heads_x, d_b_rows, d_c_rows], axis=1)
+    )
+    d_pre = d_ext[KC - 1 :]
+    d_pre_bc = d_pre[:, width_x:]
+    d_projected = jnp.concatenate(
+        [
+            d_gate_z,
+            d_pre[:, :width_x].astype(bf16),
+            d_query.astype(bf16),
+            d_key_first.astype(bf16),
+            d_key_second.astype(bf16),
+            d_kv[:, 2 * quarter :].astype(bf16),
+            d_dt_f.astype(bf16),
+            jnp.zeros((length, 128 - 4 * quarter - HEADS), bf16),
+        ],
+        axis=1,
+    )
+    d_normed_part = dot_right_t(d_projected, full_in) + dot_right_t(d_pre_bc.astype(bf16), w_bc)
+    grad_in = sum_rows(dot_left_t(normed, d_projected))
+    d_normed = scatter_plane(d_normed_part.astype(bf16))
+    grad_gain_one = jnp.sum(d_normed * hidden_own * lax.rsqrt(jnp.mean(hidden_own * hidden_own, axis=-1, keepdims=True) + EPSILON), axis=0)
+    scale_own = lax.rsqrt(jnp.mean(hidden_own * hidden_own, axis=-1, keepdims=True) + EPSILON)
+    d_scaled_one = d_normed * gain_one
+    grad_input = (
+        d_middle
+        + scale_own * d_scaled_one
+        - hidden_own * scale_own**3 * jnp.mean(d_scaled_one * hidden_own, axis=-1, keepdims=True)
+    )
+
+    bc_cols = 2 * NS // (2 * GROUP)
+    d_bc_parts = d_pre_bc.reshape(length, 2 * GROUP, bc_cols).transpose(1, 0, 2)
+    d_bc = lax.psum_scatter(d_bc_parts, ("seq", "tensor"), scatter_dimension=0, tiled=True)[0]
+    grad_bc = lax.psum_scatter(
+        dot_left_t(normed, d_bc.astype(bf16)), "dp", scatter_dimension=0, tiled=True
+    )
+    grad_bc = lax.all_gather(grad_bc, "dp", axis=0, tiled=True)
+    grad_bc = lax.all_gather(grad_bc, ("seq", "tensor"), axis=1, tiled=True)
+
+    back_gu, back_down = exchange_plane(
+        (block_move(0, 0), block_move(1, 1)),
+        (grad_gate_up, grad_down),
+        [grad_gate_up.shape, grad_down.shape],
+        5,
+    )
+    back_in, back_out = exchange_plane(
+        (block_move(0, 0), block_move(1, 1)),
+        (grad_in, grad_out),
+        [grad_in.shape, grad_out.shape],
+        6,
+    )
+
+    def columns(back, start, size):
+        return jnp.concatenate(
+            [back[chip, :, start : start + size] for chip in range(GROUP)], axis=1
+        ).astype(jnp.float32)
+
+    def rows(back, start, size):
+        return back[:, start : start + size].reshape(GROUP * size, slice_rows).astype(jnp.float32)
+
+    start_kv = 2 * width_x + HD
+    grad_key = jnp.concatenate(
+        [columns(back_in, start_kv, quarter), columns(back_in, start_kv + quarter, quarter)], axis=1
+    )
+
+    def placed(values, rows_all, start):
+        return lax.dynamic_update_slice_in_dim(
+            jnp.zeros((rows_all,) + values.shape[1:], jnp.float32), values, start, 0
+        )
+
+    grad_conv = jnp.concatenate(
+        [placed(grad_conv_loc[:width_x], MH * HP, head_start * HP), grad_conv_loc[width_x:]], axis=0
+    )
+    grad_bias = jnp.concatenate(
+        [placed(grad_bias_loc[:width_x], MH * HP, head_start * HP), grad_bias_loc[width_x:]], axis=0
+    )
+    small = [
+        grad_gain_one,
+        grad_gain_two,
+        grad_conv.reshape(-1),
+        grad_bias,
+        placed(grad_dtb, MH, head_start),
+        placed(grad_alog, MH, head_start),
+        placed(grad_skip, MH, head_start),
+        placed(grad_group, MH, head_start).reshape(-1),
+    ]
+    sizes = [values.shape[0] for values in small]
+    summed = lax.psum(jnp.concatenate(small), ("dp", "seq", "tensor"))
+    parts = []
+    start = 0
+    for size in sizes:
+        parts.append(summed[start : start + size])
+        start += size
+    sum_one, sum_two, sum_conv, sum_bias, sum_dtb, sum_alog, sum_skip, sum_group = parts
+    gain_start = (data_rank * GROUP + place) * slice_rows
+    return (
+        both_cores(block_out.astype(bf16))[None],
+        both_cores(grad_input)[None],
+        lax.dynamic_slice_in_dim(sum_one, gain_start, slice_rows),
+        columns(back_in, 0, width_x),
+        columns(back_in, width_x, width_x),
+        grad_bc,
+        columns(back_in, start_kv + 4 * quarter, HEADS),
+        sum_conv.reshape(conv_weight.shape),
+        sum_bias,
+        sum_dtb,
+        sum_alog,
+        sum_skip,
+        sum_group.reshape(MH, HP),
+        rows(back_out, 0, width_x),
+        columns(back_in, 2 * width_x, HD),
+        grad_key,
+        columns(back_in, start_kv + 2 * quarter, 2 * quarter),
+        rows(back_out, width_x, HD),
+        lax.dynamic_slice_in_dim(sum_two, gain_start, slice_rows),
+        columns(back_gu, 0, hidden_units),
+        columns(back_gu, hidden_units, hidden_units),
+        rows(back_down, 0, hidden_units),
+    )
+
+
 def solution(mesh):
     placed = (
         P("dp", "seq", None),
@@ -638,8 +1802,9 @@
         P(("dp", "seq"), "tensor"),
         P("tensor", ("dp", "seq")),
     )
+    whole_row = mesh.shape["seq"] == GROUP and mesh.shape["tensor"] == 2
     return jax.shard_map(
-        local,
+        heads_local_plan if whole_row else local,
         mesh=mesh,
         in_specs=placed,
         out_specs=(

time: 3720 us -> 1250 us (0.34)
  waiting for transfers between devices: 2890 us -> 351 us
  Pallas kernels: 0 us -> 450 us
  blocking collectives: 310 us -> 18 us
  matrix products: 326 us -> 123 us
  local copies, waits for them, and re-layouts: 62.1 us -> 153 us
    reduce_scatter x12 -> x6, waiting for transfers between devices: 1970 us -> 205 us  [the longest x2 157 us: sum_rows(): lax.psum_scatter(grads.astype(bf16), 'dp', scatter_dimension=0, tiled=True)]
    all_gather x10 -> x5, waiting for transfers between devices: 600 us -> 101 us  [the longest x1 77.3 us: heads_local_plan(): lax.all_gather(in_slices, 'dp', axis=0, tiled=True).reshape(width, width_in)]
    pallas_call x0 -> x16, Pallas kernels: none -> 450 us  [the longest x4 179 us: scatter_plane(): pl.pallas_call(scatter_kernel, out_shape=jax.ShapeDtypeStruct((rows, widt...]
    psum x6 -> x1, waiting for transfers between devices: 319 us -> 43.9 us  [heads_local_plan(): summed = lax.psum(jnp.concatenate(small), ('dp', 'seq', 'tensor'))]
    all_gather x8 -> x1, blocking collectives: 236 us -> 18 us  [heads_local_plan(): grad_bc = lax.all_gather(grad_bc, 'dp', axis=0, tiled=True)]
    dot_general x23 -> x0, matrix products: 126 us -> none  [the longest x3 44.3 us: ssd_main(): outputs = jnp.einsum('tsh,shp->thp', mixing, heads_x, precision=HIGHEST)]
    unnamed x1 -> x0, blocking collectives: 73.9 us -> none
    dot_general x11 -> x5, matrix products: 81 us -> 43.3 us  [dot_left_t(): lax.dot_general(left_side, right_side, (((0,), (0,)), ((), ())), preferre...]
  transfers between devices with their start and end apart: 31 -> 20, of which waited for: 23 -> 7; matrix products, arithmetic and copies ran while one was open for 8% -> 23% of each run, Pallas kernels for 0% -> 19%
where the time goes in v1:
time: 1250 us; the launch traced here: 1240 us
  Pallas kernels  450 us (36%)
  waiting for transfers between devices  351 us (28%)
  local copies, waits for them, and re-layouts  153 us (12%)
  matrix products  123 us (10%)
  other arithmetic  119 us (10%)
  blocking collectives  18 us (1%)
  between operations  16.9 us (1%)
    pallas_call x4, Pallas kernels, scatter_plane(): pl.pallas_call(scatter_kernel, out_shape=jax.ShapeDtypeStruct((rows, widt...  179 us
    reduce_scatter x2, waiting for transfers between devices, sum_rows(): lax.psum_scatter(grads.astype(bf16), 'dp', scatter_dimension=0, tiled=True)  157 us
    pallas_call x4, Pallas kernels, gather_plane(): pl.pallas_call(gather_kernel, out_shape=jax.ShapeDtypeStruct((2 * GROUP,...  123 us
    pallas_call x4, Pallas kernels, exchange_plane(): pl.pallas_call(partial(exchange_kernel, moves, len(arrays)), out_shape=sh...  90.4 us
    all_gather x1, waiting for transfers between devices, heads_local_plan(): lax.all_gather(in_slices, 'dp', axis=0, tiled=True).reshape(width, width_in)  77.3 us
    reduce_scatter x2, waiting for transfers between devices, sum_columns(): lax.psum_scatter(chunks.transpose(1, 0, 2), 'dp', scatter_dimension=0, ti...  47.1 us
    dot_general x5, matrix products, dot_right_t(): lax.dot_general(left_side, right_side, (((1,), (1,)), ((), ())), preferre...  46.6 us
    psum x1, waiting for transfers between devices, heads_local_plan(): summed = lax.psum(jnp.concatenate(small), ('dp', 'seq', 'tensor'))  43.9 us
  transfers between devices with their start and end apart: 20, of which 7 were waited for; matrix products, arithmetic and copies ran while one was open for 23% of the time, Pallas kernels for 19%

profile of v1, /device:TPU:0, one launch (start us, length us, event | category | flops | bytes accessed | tf_op | source)
XLA Modules:
  0.0 1239.0 jit_solution(1389847583805791170)
XLA Ops:
  7.3 28.1 %shard_map.403 = (bf16[4,512,128]{2,1,0:T(8,128)(2,1)}, bf16[4,128,1024]{2,1,0:T(8,128)(2,1)}, bf16[4,512,128]{2,1,0:T(8,128)(2,1)}) custom-call(bf16[1536,128]{1,0:T(8,128)(2,1)} %refs_0_.3, bf16[512,128]{1,0:T(8,128)(2,1)} %refs_1_.3, bf16[128,2048]{1,0:T(8,128)(2,1)} %refs_2_.3, bf16[128,2048]{1,0:T(8,128)(2,1)} %refs_3_.1, bf16[2048,128]{1,0:T(8,128)(2,1)} %refs_4_.1), custom_call_target="tpu_custom_call" | custom-call | tf_op jit(solution)/shard_map/pallas_call | solution.py:876
  38.6 15.3 %shard_map.400 = bf16[4,128,1024]{2,1,0:T(8,128)(2,1)} custom-call(bf16[128,1536]{1,0:T(8,128)(2,1)} %refs_0_.2, bf16[128,1536]{1,0:T(8,128)(2,1)} %refs_1_.2, bf16[128,512]{1,0:T(8,128)(2,1)} %refs_2_.2, bf16[4,128,128]{2,1,0:T(8,128)(2,1)} %pad_maximum_fusion.6.refs_3_), custom_call_target="tpu_custom_call" | custom-call | tf_op jit(solution)/shard_map/pallas_call | solution.py:876
  57.2 30.6 %shard_map.399 = bf16[8,192,2048]{2,1,0:T(8,128)(2,1)} custom-call(bf16[192,2048]{1,0:T(8,128)(2,1)} %get-tuple-element.191.own_ref), custom_call_target="tpu_custom_call" | custom-call | tf_op jit(solution)/shard_map/pallas_call | solution.py:748
  104.6 23.4 %all-gather.12.cloned.1.call-done = bf16[16,512,128]{2,1,0:T(8,128)(2,1)} async-done(((bf16[4,512,128]{2,1,0:T(8,128)(2,1)}), bf16[16,512,128]{2,1,0:T(8,128)(2,1)}) %all-gather.12.cloned.1.call-update) | async-done | bytes 2097168 | tf_op jit(solution)/shard_map/all_gather | solution.py:1439
  131.9 77.3 %all-gather.6.cloned.1.call-done = bf16[16,128,1024]{2,1,0:T(8,128)(2,1)} async-done(((bf16[4,128,1024]{2,1,0:T(8,128)(2,1)}), bf16[16,128,1024]{2,1,0:T(8,128)(2,1)}) %all-gather.6.cloned.1.call-update) | async-done | bytes 4194320 | tf_op jit(solution)/shard_map/all_gather | solution.py:1411
  272.7 16.2 %shard_map.401 = (bf16[1536,384]{1,0:T(8,128)(2,1)}, f32[1536,384]{1,0:T(8,128)}, f32[12,256,384]{2,1,0:T(8,128)}) custom-call(bf16[1536,384]{1,0:T(8,128)(2,1)} %slice.626.x_ref, bf16[1536,256]{1,0:T(8,128)(2,1)} %get-tuple-element.214.b_ref, bf16[1536,256]{1,0:T(8,128)(2,1)} %get-tuple-element.213.c_ref, f32[1536,384]{1,0:T(8,128)} %slice.629.z_ref, ...), custom_call_target="tpu_custom_call" | custom-call | tf_op jit(solution)/shard_map/pallas_call | solution.py:1157
  321.6 44.6 %shard_map.404 = f32[192,2048]{1,0:T(8,128)} custom-call(bf16[8,192,2048]{2,1,0:T(8,128)(2,1)} %bitcast.287), custom_call_target="tpu_custom_call" | custom-call | tf_op jit(solution)/shard_map/pallas_call | solution.py:823
  370.2 30.8 %shard_map.405 = bf16[8,192,2048]{2,1,0:T(8,128)(2,1)} custom-call(bf16[192,2048]{1,0:T(8,128)(2,1)} %multiply_convert_fusion.4.own_ref), custom_call_target="tpu_custom_call" | custom-call | tf_op jit(solution)/shard_map/pallas_call | solution.py:748
  401.0 10.8 fusion.77
  420.5 44.8 %shard_map.406 = f32[192,2048]{1,0:T(8,128)} custom-call(bf16[8,192,2048]{2,1,0:T(8,128)(2,1)} %bitcast.288), custom_call_target="tpu_custom_call" | custom-call | tf_op jit(solution)/shard_map/pallas_call | solution.py:823
  467.8 30.7 %shard_map.407 = bf16[8,192,2048]{2,1,0:T(8,128)(2,1)} custom-call(bf16[192,2048]{1,0:T(8,128)(2,1)} %fusion.25.own_ref), custom_call_target="tpu_custom_call" | custom-call | tf_op jit(solution)/shard_map/pallas_call | solution.py:748
  498.6 10.1 fusion.8
  508.7 8.9 convolution_convert_fusion
  517.6 44.8 %shard_map.408 = f32[192,2048]{1,0:T(8,128)} custom-call(bf16[8,192,2048]{2,1,0:T(8,128)(2,1)} %bitcast.286), custom_call_target="tpu_custom_call" | custom-call | tf_op jit(solution)/shard_map/pallas_call | solution.py:823
  567.5 30.7 %shard_map.409 = bf16[8,192,2048]{2,1,0:T(8,128)(2,1)} custom-call(bf16[192,2048]{1,0:T(8,128)(2,1)} %get-tuple-element.192.own_ref), custom_call_target="tpu_custom_call" | custom-call | tf_op jit(solution)/shard_map/pallas_call | solution.py:748
  606.9 26.9 %shard_map.410 = (f32[1536,384]{1,0:T(8,128)}, f32[1536,256]{1,0:T(8,128)}, f32[1536,256]{1,0:T(8,128)}, bf16[1536,384]{1,0:T(8,128)(2,1)}, f32[1536,8]{1,0:T(8,...) custom-call(bf16[1536,384]{1,0:T(8,128)(2,1)} %slice.626.x_ref, ...), custom_call_target="tpu_custom_call" | custom-call | tf_op jit(solution)/shard_map/pallas_call | solution.py:1190
  647.1 8.4 shard_map.411
  721.9 8.3 fusion.19
  747.2 13.1 %add_convert_fusion = bf16[1536,2048]{1,0:T(8,128)(2,1)} fusion(f32[1536,2048]{1,0:T(8,128)} %fusion.19, bf16[1536,1024]{1,0:T(8,128)(2,1)} %concatenate.270, bf16[2048,1024]{1,0:T(8,128)(2,1)} %bitcast.302), kind=kOutput, calls=%fused_computation.3 | convolution fusion | flops 6448742400 | bytes 26214400 | tf_op jit(solution)/shard_map/dot_general | solution.py:56
  760.3 44.5 %shard_map.412 = f32[192,2048]{1,0:T(8,128)} custom-call(bf16[8,192,2048]{2,1,0:T(8,128)(2,1)} %bitcast.285), custom_call_target="tpu_custom_call" | custom-call | tf_op jit(solution)/shard_map/pallas_call | solution.py:823
  807.5 8.0 convolution_convert_fusion.5
  823.6 11.1 convolution_convert_fusion.3
  834.8 8.1 convolution_convert_fusion.6
  850.8 11.2 convolution_convert_fusion.4
  862.1 18.0 %all_gather.22 = f32[2048,64]{0,1:T(8,128)} all-gather(f32[512,64]{0,1:T(8,128)} %reduce-scatter.13.cloned.1.call-done), channel_id=1, replica_groups=mesh['dp'=4,'seq'=4,'tensor'=2] {'dp'}, dimensions={0}, use_global_device_ids=true | all-gather | bytes 655360 | tf_op jit(solution)/shard_map/all_gather | solution.py:1693
  884.2 43.9 %all-reduce.16.cloned.1.call-done = f32[25232]{0:T(1024)} async-done(((f32[25232]{0:T(1024)}), f32[25232]{0:T(1024)}) %all-reduce.16.cloned.1.call-update) | async-done | bytes 100944 | tf_op jit(solution)/shard_map/psum | solution.py:1744
  949.4 25.9 %reduce-scatter.17.cloned.1.call-done.refs_1_ = bf16[4,512,128]{2,1,0:T(8,128)(2,1)} async-done(((bf16[16,512,128]{2,1,0:T(8,128)(2,1)}), bf16[4,512,128]{2,1,0:T(8,128)(2,1)}) %reduce-scatter.17.cloned.1.call-update) | async-done | bytes 524304 | tf_op jit(solution)/shard_map/reduce_scatter | solution.py:1570
  975.3 78.4 %reduce-scatter.15.cloned.1.call-done = bf16[512,1024]{1,0:T(8,128)(2,1)} async-done(((bf16[2048,1024]{1,0:T(8,128)(2,1)}), bf16[512,1024]{1,0:T(8,128)(2,1)}) %reduce-scatter.15.cloned.1.call-update) | async-done | bytes 1048592 | tf_op jit(solution)/shard_map/reduce_scatter | solution.py:1575
  1053.7 20.7 %shard_map.414 = (bf16[4,128,1024]{2,1,0:T(8,128)(2,1)}, bf16[4,512,128]{2,1,0:T(8,128)(2,1)}) custom-call(bf16[4,128,1024]{2,1,0:T(8,128)(2,1)} %bitcast.297, bf16[4,512,128]{2,1,0:T(8,128)(2,1)} %reduce-scatter.17.cloned.1.call-done.refs_1_), custom_call_target="tpu_custom_call" | custom-call | tf_op jit(solution)/shard_map/pallas_call | solution.py:876
  1079.1 21.2 %reduce-scatter.9.cloned.1.call-done.refs_1_ = bf16[4,512,128]{2,1,0:T(8,128)(2,1)} async-done(((bf16[16,512,128]{2,1,0:T(8,128)(2,1)}), bf16[4,512,128]{2,1,0:T(8,128)(2,1)}) %reduce-scatter.9.cloned.1.call-update) | async-done | bytes 524304 | tf_op jit(solution)/shard_map/reduce_scatter | solution.py:1570
  1100.3 79.0 %reduce-scatter.7.cloned.1.call-done = bf16[512,1024]{1,0:T(8,128)(2,1)} async-done(((bf16[2048,1024]{1,0:T(8,128)(2,1)}), bf16[512,1024]{1,0:T(8,128)(2,1)}) %reduce-scatter.7.cloned.1.call-update) | async-done | bytes 1048592 | tf_op jit(solution)/shard_map/reduce_scatter | solution.py:1575
  1179.3 26.3 %shard_map.413 = (bf16[4,128,1024]{2,1,0:T(8,128)(2,1)}, bf16[4,512,128]{2,1,0:T(8,128)(2,1)}) custom-call(bf16[4,128,1024]{2,1,0:T(8,128)(2,1)} %bitcast.296, bf16[4,512,128]{2,1,0:T(8,128)(2,1)} %reduce-scatter.9.cloned.1.call-done.refs_1_), custom_call_target="tpu_custom_call" | custom-call | tf_op jit(solution)/shard_map/pallas_call | solution.py:876
  (465 shorter events, 321.9 us)
Async XLA Ops:
  7.2 244.5 %copy-start = (bf16[2048,512]{1,0:T(8,128)(2,1)S(1)}, bf16[2048,512]{1,0:T(8,128)(2,1)}, u32[]{:S(2)}) copy-start(bf16[2048,512]{1,0:T(8,128)(2,1)} %param.33) | copy-start | bytes 6291460
  7.3 93.4 %all-gather.8.cloned.1.call-start = ((), (), s32[]{:S(2)}) async-start(), calls=%async_computation.7 | async-start | bytes 2621440 | tf_op jit(solution)/shard_map/all_gather | solution.py:1433
  35.4 92.6 %all-gather.12.cloned.1.call-start = ((), (), s32[]{:S(2)}) async-start(), calls=%async_computation.9 | async-start | bytes 2621440 | tf_op jit(solution)/shard_map/all_gather | solution.py:1439
  36.1 173.0 %all-gather.6.cloned.1.call-start = ((), (), s32[]{:S(2)}) async-start(), calls=%async_computation.6 | async-start | bytes 5242880 | tf_op jit(solution)/shard_map/all_gather | solution.py:1411
  53.9 347.1 %all-gather.10.cloned.1.call-start = ((), (), s32[]{:S(2)}) async-start(), calls=%async_computation.8 | async-start | bytes 5242880 | tf_op jit(solution)/shard_map/all_gather | solution.py:1437
  54.5 687.7 %reduce-scatter.11.cloned.1.call-start = ((), (), s32[]{:S(2)}) async-start(), calls=%async_computation.13 | async-start | bytes 3538944 | tf_op jit(solution)/shard_map/reduce_scatter | solution.py:1689
  54.6 169.2 %copy-start.54 = (f32[1536]{0:T(1024)}, f32[1536]{0:T(1024)S(1)}, u32[]{:S(2)}) copy-start(f32[1536]{0:T(1024)S(1)} %iota_convert_fusion) | copy-start | bytes 18436
  54.6 169.1 %copy-start.82 = (f32[64]{0:T(128)}, f32[64]{0:T(128)S(1)}, u32[]{:S(2)}) copy-start(f32[64]{0:T(128)S(1)} %multiply_power_fusion) | copy-start | bytes 772
  55.0 200.8 %copy-start.48 = (f32[1536]{0:T(1024)}, f32[1536]{0:T(1024)S(1)}, u32[]{:S(2)}) copy-start(f32[1536]{0:T(1024)S(1)} %get-tuple-element.313) | copy-start | bytes 18436
  93.6 142.2 %copy-start.78 = (f32[6]{0:T(128)}, f32[6]{0:T(128)S(1)}, u32[]{:S(2)}) copy-start(f32[6]{0:T(128)S(1)} %dynamic_slice.58) | copy-start | bytes 76
  99.2 145.7 %copy-start.50 = (f32[12,128]{1,0:T(8,128)}, f32[12,128]{1,0:T(8,128)S(1)}, u32[]{:S(2)}) copy-start(f32[12,128]{1,0:T(8,128)S(1)} %get-tuple-element.309) | copy-start | bytes 18436
  99.3 156.5 %copy-start.56 = (f32[896]{0:T(1024)}, f32[896]{0:T(1024)S(1)}, u32[]{:S(2)}) copy-start(f32[896]{0:T(1024)S(1)} %get-tuple-element.183) | copy-start | bytes 10756
  99.3 156.5 %copy-start.58 = (f32[896]{0:T(1024)}, f32[896]{0:T(1024)S(1)}, u32[]{:S(2)}) copy-start(f32[896]{0:T(1024)S(1)} %get-tuple-element.184) | copy-start | bytes 10756
  99.3 156.5 %copy-start.60 = (f32[896]{0:T(1024)}, f32[896]{0:T(1024)S(1)}, u32[]{:S(2)}) copy-start(f32[896]{0:T(1024)S(1)} %get-tuple-element.185) | copy-start | bytes 10756
  99.3 156.5 %copy-start.62 = (f32[896]{0:T(1024)}, f32[896]{0:T(1024)S(1)}, u32[]{:S(2)}) copy-start(f32[896]{0:T(1024)S(1)} %get-tuple-element.186) | copy-start | bytes 10756
  232.3 61.2 %collective-permute-start = (bf16[1536,64]{1,0:T(8,128)(2,1)}, bf16[1536,64]{1,0:T(8,128)(2,1)}, u32[]{:S(2)}, u32[]{:S(2)}) collective-permute-start(bf16[1536,64]{1,0:T(8,128)(2,1)} %pad_maximum_fusion.4), channel_id=1, source_target_pairs={{0,2},{2,0},{4,6},{6,4},{1,3},{3,1},{5,7},{7,5},{8,10},{10,8},{12,... | collective-permute-start | bytes 589832 | tf_op jit(solution)/shard_map/ppermute | solution.py:1309
  233.8 60.7 %collective-permute-start.1 = (bf16[1536,64]{1,0:T(8,128)(2,1)}, bf16[1536,64]{1,0:T(8,128)(2,1)}, u32[]{:S(2)}, u32[]{:S(2)}) collective-permute-start(bf16[1536,64]{1,0:T(8,128)(2,1)} %pad_maximum_fusion.4), channel_id=1, source_target_pairs={{0,4},{2,6},{4,0},{6,2},{1,5},{3,7},{5,1},{7,3},{8,12},{10,14},{12... | collective-permute-start | bytes 589832 | tf_op jit(solution)/shard_map/ppermute | solution.py:1309
  235.3 60.3 %collective-permute-start.2 = (bf16[1536,64]{1,0:T(8,128)(2,1)}, bf16[1536,64]{1,0:T(8,128)(2,1)}, u32[]{:S(2)}, u32[]{:S(2)}) collective-permute-start(bf16[1536,64]{1,0:T(8,128)(2,1)} %pad_maximum_fusion.4), channel_id=1, source_target_pairs={{0,6},{2,4},{4,2},{6,0},{1,7},{3,5},{5,3},{7,1},{8,14},{10,12},{12... | collective-permute-start | bytes 589832 | tf_op jit(solution)/shard_map/ppermute | solution.py:1309
  517.6 47.4 %copy-start.37 = (bf16[1,384,2048]{2,1,0:T(8,128)(2,1)S(1)}, bf16[1,384,2048]{2,1,0:T(8,128)(2,1)}, u32[]{:S(2)}) copy-start(bf16[1,384,2048]{2,1,0:T(8,128)(2,1)} %param.27) | copy-start | bytes 4718596
  687.3 174.8 %reduce-scatter.13.cloned.1.call-start = ((), (), s32[]{:S(2)}) async-start(), calls=%async_computation.14 | async-start | bytes 655360 | tf_op jit(solution)/shard_map/reduce_scatter | solution.py:1690
  701.8 28.6 %collective-permute-start.4 = (bf16[1536,64]{1,0:T(8,128)(2,1)}, bf16[1536,64]{1,0:T(8,128)(2,1)}, u32[]{:S(2)}, u32[]{:S(2)}) collective-permute-start(bf16[1536,64]{1,0:T(8,128)(2,1)} %get-tuple-element.217), channel_id=1, source_target_pairs={{0,2},{2,0},{4,6},{6,4},{1,3},{3,1},{5,7},{7,5},{8,10},{10,8},{12,... | collective-permute-start | bytes 589832 | tf_op jit(solution)/shard_map/ppermute | solution.py:1320
  702.3 28.1 %collective-permute-start.5 = (bf16[1536,64]{1,0:T(8,128)(2,1)}, bf16[1536,64]{1,0:T(8,128)(2,1)}, u32[]{:S(2)}, u32[]{:S(2)}) collective-permute-start(bf16[1536,64]{1,0:T(8,128)(2,1)} %get-tuple-element.219), channel_id=1, source_target_pairs={{0,4},{2,6},{4,0},{6,2},{1,5},{3,7},{5,1},{7,3},{8,12},{10,14},{12... | collective-permute-start | bytes 589832 | tf_op jit(solution)/shard_map/ppermute | solution.py:1320
  703.6 26.8 %collective-permute-start.6 = (bf16[1536,64]{1,0:T(8,128)(2,1)S(1)}, bf16[1536,64]{1,0:T(8,128)(2,1)}, u32[]{:S(2)}, u32[]{:S(2)}) collective-permute-start(bf16[1536,64]{1,0:T(8,128)(2,1)S(1)} %get-tuple-element.218), channel_id=1, source_target_pairs={{0,6},{2,4},{4,2},{6,0},{1,7},{3,5},{5,3},{7,1},{8,14},{10,12},{12... | collective-permute-start | bytes 589832 | tf_op jit(solution)/shard_map/ppermute | solution.py:1320
  747.1 181.0 %all-reduce.16.cloned.1.call-start = ((), (), s32[]{:S(2)}) async-start(), calls=%async_computation.10 | async-start | bytes 204800 | tf_op jit(solution)/shard_map/psum | solution.py:1744
  760.3 46.4 %copy-start.64 = (f32[2048]{0:T(1024)S(1)}, f32[2048]{0:T(1024)}, u32[]{:S(2)}) copy-start(f32[2048]{0:T(1024)} %get-tuple-element.179) | copy-start | bytes 24580
  807.4 167.9 %reduce-scatter.17.cloned.1.call-start = ((), (), s32[]{:S(2)}) async-start(), calls=%async_computation.17 | async-start | bytes 2621440 | tf_op jit(solution)/shard_map/reduce_scatter | solution.py:1570
  823.4 230.3 %reduce-scatter.15.cloned.1.call-start = ((), (), s32[]{:S(2)}) async-start(), calls=%async_computation.16 | async-start | bytes 5242880 | tf_op jit(solution)/shard_map/reduce_scatter | solution.py:1575
  834.8 265.6 %reduce-scatter.9.cloned.1.call-start = ((), (), s32[]{:S(2)}) async-start(), calls=%async_computation.12 | async-start | bytes 2621440 | tf_op jit(solution)/shard_map/reduce_scatter | solution.py:1570
  850.8 328.6 %reduce-scatter.7.cloned.1.call-start = ((), (), s32[]{:S(2)}) async-start(), calls=%async_computation.11 | async-start | bytes 5242880 | tf_op jit(solution)/shard_map/reduce_scatter | solution.py:1575
  862.0 364.4 %all-gather.14.cloned.1.call-start = ((), (), s32[]{:S(2)}) async-start(), calls=%async_computation.15 | async-start | bytes 4718592 | tf_op jit(solution)/shard_map/all_gather | solution.py:1694
  883.7 60.2 %collective-permute-start.7 = (f32[192,2048]{1,0:T(8,128)}, f32[192,2048]{1,0:T(8,128)}, u32[]{:S(2)}, u32[]{:S(2)}) collective-permute-start(f32[192,2048]{1,0:T(8,128)} %fusion.14), channel_id=1, source_target_pairs={{0,1},{1,0},{2,3},{3,2},{4,5},{5,4},{6,7},{7,6},{8,9},{9,8},{10,11... | collective-permute-start | bytes 4718600 | tf_op jit(solution)/shard_map/ppermute | solution.py:1327
  883.7 57.0 %collective-permute-start.3 = (bf16[192,2048]{1,0:T(8,128)(2,1)}, bf16[192,2048]{1,0:T(8,128)(2,1)S(1)}, u32[]{:S(2)}, u32[]{:S(2)}) collective-permute-start(bf16[192,2048]{1,0:T(8,128)(2,1)} %get-tuple-element.212), channel_id=1, source_target_pairs={{0,1},{1,0},{2,3},{3,2},{4,5},{5,4},{6,7},{7,6},{8,9},{9,8},{10,11... | collective-permute-start | bytes 2359304 | tf_op jit(solution)/shard_map/ppermute | solution.py:1327
  (88 other events, 1024.1 us)
Sparse Core Ops, SparseCore 0:
  35.5 46.2 all-gather.7
  83.4 44.5 all-gather.11
  129.5 79.5 all-gather.5
  210.6 79.2 all-gather.9
  687.4 54.6 reduce-scatter.10
  747.2 21.5 reduce-scatter.12
  807.5 120.5 all-reduce.15
  930.5 44.7 reduce-scatter.16
  977.6 76.0 reduce-scatter.14
  1055.9 44.3 reduce-scatter.8
  1103.2 76.0 reduce-scatter.6
  1181.2 43.2 all-gather.13

commit v2 on v0

--- a/solution.py
+++ b/solution.py
@@ -3,6 +3,8 @@
 import jax
 import jax.numpy as jnp
 from jax import lax
+from jax.experimental import pallas as pl
+from jax.experimental.pallas import tpu as pltpu
 from jax.sharding import PartitionSpec as P
 
 MH = 48
@@ -611,6 +613,1644 @@
     )
 
 
+GROUP = 4
+CHUNK = 128
+HEADS = 6
+MESH_ID = pl.DeviceIdType.MESH
+VMEM_BYTES = 56 * 1024 * 1024
+
+
+def dot_f32(left_side, right_side, left_dim, right_dim):
+    return lax.dot_general(
+        left_side,
+        right_side,
+        (((left_dim,), (right_dim,)), ((), ())),
+        preferred_element_type=jnp.float32,
+    )
+
+
+def halves(values):
+    high = values.astype(jnp.bfloat16)
+    return (high, (values - high.astype(jnp.float32)).astype(jnp.bfloat16))
+
+
+def dot_split(exact, parts, left_dim, right_dim):
+    high, low = parts
+    return dot_f32(exact, high, left_dim, right_dim) + dot_f32(exact, low, left_dim, right_dim)
+
+
+def dot_split_left(parts, exact, left_dim, right_dim):
+    high, low = parts
+    return dot_f32(high, exact, left_dim, right_dim) + dot_f32(low, exact, left_dim, right_dim)
+
+
+def dot_splits(left_parts, right_parts, left_dim, right_dim):
+    left_high, left_low = left_parts
+    right_high, right_low = right_parts
+    return dot_f32(left_high, right_high, left_dim, right_dim) + (
+        dot_f32(left_high, right_low, left_dim, right_dim)
+        + dot_f32(left_low, right_high, left_dim, right_dim)
+    )
+
+
+def plane_place():
+    data, place, core = lax.axis_index("dp"), lax.axis_index("seq"), lax.axis_index("tensor")
+    along_x = place + 1 - 2 * lax.rem(place, 2)
+    along_y = lax.rem(place + 2, GROUP)
+    across = GROUP - 1 - place
+    return (data, place, core, along_x, along_y, across)
+
+
+def meet(devices):
+    barrier = pltpu.get_barrier_semaphore()
+    for device in devices:
+        pl.semaphore_signal(barrier, inc=1, device_id=device, device_id_type=MESH_ID)
+    pl.semaphore_wait(barrier, len(devices))
+
+
+def remote(source, target, send_sem, recv_sem, device):
+    return pltpu.make_async_remote_copy(
+        src_ref=source,
+        dst_ref=target,
+        send_sem=send_sem,
+        recv_sem=recv_sem,
+        device_id=device,
+        device_id_type=MESH_ID,
+    )
+
+
+def lasting(microseconds):
+    return pl.CostEstimate(
+        flops=int(microseconds * 9e8),
+        bytes_accessed=int(microseconds * 3e6),
+        transcendentals=0,
+    )
+
+
+def any_specs(count):
+    return [pl.BlockSpec(memory_space=pl.ANY)] * count
+
+
+def vmem_specs(count):
+    return [pl.BlockSpec(memory_space=pltpu.VMEM)] * count
+
+
+def gather_kernel(apply, count_in, count_out, own_ref, *refs):
+    inputs, all_ref = refs[:count_in], refs[count_in]
+    outputs = refs[count_in + 1 : count_in + 1 + count_out]
+    send_sems, recv_sems = refs[count_in + 1 + count_out :]
+    data, place, core, along_x, along_y, across = plane_place()
+    height = own_ref.shape[0]
+    half = height // 2
+    to_x, to_y, partner = (data, along_x, core), (data, along_y, core), (data, place, 1 - core)
+
+    def block(chip, part):
+        return all_ref.at[2 * chip + core, pl.ds(part * half, half)]
+
+    def work(chip, side):
+        if apply is not None:
+            index = 2 * chip + side
+            rows = pl.ds(pl.multiple_of(index * height, 16), height)
+            apply(all_ref[index], rows, inputs, outputs)
+
+    meet((to_x, to_y, partner))
+
+    def push(index, source, target, device):
+        copy = remote(source, target, send_sems.at[index], recv_sems.at[index], device)
+        copy.start()
+        return copy
+
+    first, second = own_ref.at[pl.ds(0, half)], own_ref.at[pl.ds(half, half)]
+    x_first = push(0, first, block(place, 0), to_x)
+    y_second = push(1, second, block(place, 1), to_y)
+    x_second = push(2, second, block(place, 1), to_x)
+    y_first = push(3, first, block(place, 0), to_y)
+    pair_own = push(4, own_ref, all_ref.at[2 * place + core], partner)
+    all_ref[2 * place + core] = own_ref[...]
+    work(place, core)
+    pair_own.wait_recv()
+    work(place, 1 - core)
+    x_first.wait_recv()
+    over_y = push(5, block(along_x, 0), block(along_x, 0), to_y)
+    y_second.wait_recv()
+    over_x = push(6, block(along_y, 1), block(along_y, 1), to_x)
+    x_second.wait_recv()
+    mine_x = all_ref.at[2 * along_x + core]
+    pair_x = push(7, mine_x, mine_x, partner)
+    y_first.wait_recv()
+    mine_y = all_ref.at[2 * along_y + core]
+    pair_y = push(8, mine_y, mine_y, partner)
+    work(along_x, core)
+    work(along_y, core)
+    pair_x.wait_recv()
+    work(along_x, 1 - core)
+    pair_y.wait_recv()
+    work(along_y, 1 - core)
+    over_y.wait_recv()
+    pair_a = push(9, block(across, 0), block(across, 0), partner)
+    over_x.wait_recv()
+    pair_b = push(10, block(across, 1), block(across, 1), partner)
+    work(across, core)
+    pair_a.wait_recv()
+    pair_b.wait_recv()
+    work(across, 1 - core)
+    for copy in (
+        x_first,
+        y_second,
+        x_second,
+        y_first,
+        pair_own,
+        over_y,
+        over_x,
+        pair_x,
+        pair_y,
+        pair_a,
+        pair_b,
+    ):
+        copy.wait_send()
+
+
+def gather_plane(own, identity=1, apply=None, inputs=(), outputs=()):
+    rows, width = own.shape
+    gathered, *results = pl.pallas_call(
+        partial(gather_kernel, apply, len(inputs), len(outputs)),
+        out_shape=[jax.ShapeDtypeStruct((2 * GROUP, rows, width), own.dtype)]
+        + [jax.ShapeDtypeStruct(shape, dtype) for shape, dtype in outputs],
+        in_specs=vmem_specs(1 + len(inputs)),
+        out_specs=vmem_specs(1 + len(outputs)),
+        scratch_shapes=[pltpu.SemaphoreType.DMA((11,)), pltpu.SemaphoreType.DMA((11,))],
+        cost_estimate=lasting(35),
+        compiler_params=pltpu.CompilerParams(
+            collective_id=identity, has_side_effects=True, vmem_limit_bytes=VMEM_BYTES
+        ),
+    )(own, *inputs)
+    gathered = gathered.reshape(2 * GROUP * rows, width)
+    return (gathered, *results) if results else gathered
+
+
+def apply_gate_up(block, rows, inputs, outputs):
+    weights, (both_ref, act_ref) = inputs[0], outputs
+    units = act_ref.shape[1]
+    both = jnp.dot(block, weights[...], preferred_element_type=jnp.float32)
+    both_ref[rows] = both
+    gate = both[:, :units]
+    act_ref[rows] = (gate * jax.nn.sigmoid(gate) * both[:, units:]).astype(jnp.bfloat16)
+
+
+def apply_down_back(block, rows, inputs, outputs):
+    weights, both_ref = inputs
+    units = weights.shape[1]
+    d_act = jnp.dot(block, weights[...], preferred_element_type=jnp.float32)
+    gate, up = both_ref[rows, :units], both_ref[rows, units:]
+    sigmoid = jax.nn.sigmoid(gate)
+    silu = gate * sigmoid
+    d_gate = d_act * up * (sigmoid * (1.0 + gate * (1.0 - sigmoid)))
+    outputs[0][rows, :units] = d_gate.astype(jnp.bfloat16)
+    outputs[0][rows, units:] = (d_act * silu).astype(jnp.bfloat16)
+
+
+def apply_out_back(block, rows, inputs, outputs):
+    outputs[0][rows] = jnp.dot(block, inputs[0][...], preferred_element_type=jnp.float32)
+
+
+def scatter_kernel(count, left_ref, right_ref, *refs):
+    data, place, core, along_x, along_y, across = plane_place()
+    partner = (data, place, 1 - core)
+    to_x, to_y = (data, along_x, core), (data, along_y, core)
+    order = (across, along_x, along_y, place)
+    extra, sums = refs[: count - 1], refs[count - 1 : 2 * count - 1]
+    parts, scratch = refs[2 * count - 1 : 3 * count - 1], refs[3 * count - 1 :]
+    step = 16
+    meet((partner, to_x, to_y))
+
+    def multiply(at, chip, side):
+        part = parts[at]
+        index = 2 * chip + side
+        height, columns = part.shape[1:]
+        if at == 0:
+            rows = pl.ds(pl.multiple_of(index * height, 16), height)
+            block = dot_f32(left_ref[rows], right_ref[...], 1, 1)
+        else:
+            start = left_ref.shape[1] - GROUP * height
+            turned = pl.ds(pl.multiple_of(start + chip * height, 128), height)
+            along = pl.ds(pl.multiple_of(side * columns, 128), columns)
+            block = dot_f32(left_ref[:, turned], extra[at - 1][:, along], 0, 0)
+        part[index] = block.astype(jnp.bfloat16)
+
+    def one_array(at, part_ref, sum_ref, own_refs):
+        pair_in, send_a, send_x, send_y, got_x, got_y, pair_s, pair_r, send_s, recv_s = own_refs
+        half = part_ref.shape[1] // 2
+        pair = []
+
+        def send_pair(index):
+            chip = order[index]
+            multiply(at, chip, 1 - core)
+            copy = remote(
+                part_ref.at[2 * chip + 1 - core],
+                pair_in.at[index],
+                pair_s.at[index],
+                pair_r.at[index],
+                partner,
+            )
+            copy.start()
+            pair.append(copy)
+            multiply(at, chip, core)
+
+        def own_rows(index, rows):
+            return part_ref[2 * order[index] + core, rows].astype(jnp.float32) + pair_in[
+                index, rows
+            ].astype(jnp.float32)
+
+        def fill(target, index, first, extra=None):
+            def one(lap, carry):
+                rows = pl.ds(pl.multiple_of(lap * step, step), step)
+                total = own_rows(index, pl.ds(pl.multiple_of(first + lap * step, step), step))
+                if extra is not None:
+                    total = total + extra[rows].astype(jnp.float32)
+                target[rows] = total.astype(jnp.bfloat16)
+                return carry
+
+            lax.fori_loop(0, half // step, one, 0)
+
+        def push(index, source, target, device):
+            copy = remote(source, target, send_s.at[index], recv_s.at[index], device)
+            copy.start()
+            return copy
+
+        send_pair(0)
+        pair[0].wait_recv()
+        fill(send_a.at[0], 0, 0)
+        far_x = push(0, send_a.at[0], got_x.at[0], to_x)
+        fill(send_a.at[1], 0, half)
+        far_y = push(1, send_a.at[1], got_y.at[0], to_y)
+        send_pair(1)
+        pair[1].wait_recv()
+        fill(send_x.at[0], 1, 0)
+        near_x = push(2, send_x.at[0], got_x.at[1], to_x)
+        send_pair(2)
+        pair[2].wait_recv()
+        fill(send_y.at[0], 2, half)
+        near_y = push(3, send_y.at[0], got_y.at[1], to_y)
+        send_pair(3)
+        yield
+        far_x.wait_recv()
+        fill(send_y.at[1], 2, 0, got_x.at[0])
+        last_y = push(4, send_y.at[1], got_y.at[2], to_y)
+        far_y.wait_recv()
+        fill(send_x.at[1], 1, half, got_y.at[0])
+        last_x = push(5, send_x.at[1], got_x.at[2], to_x)
+        yield
+        pair[3].wait_recv()
+        near_x.wait_recv()
+        near_y.wait_recv()
+        last_y.wait_recv()
+        last_x.wait_recv()
+
+        def finish(first, near, last):
+            def one(lap, carry):
+                rows = pl.ds(pl.multiple_of(lap * step, step), step)
+                place_rows = pl.ds(pl.multiple_of(first + lap * step, step), step)
+                sum_ref[place_rows] = (
+                    own_rows(3, place_rows)
+                    + near[rows].astype(jnp.float32)
+                    + last[rows].astype(jnp.float32)
+                )
+                return carry
+
+            lax.fori_loop(0, half // step, one, 0)
+
+        finish(0, got_x.at[1], got_y.at[2])
+        finish(half, got_y.at[1], got_x.at[2])
+        for copy in pair + [far_x, far_y, near_x, near_y, last_x, last_y]:
+            copy.wait_send()
+
+    each = len(scratch) // count
+    runs = [
+        one_array(at, parts[at], sums[at], scratch[each * at : each * (at + 1)]) for at in range(count)
+    ]
+    for run in runs:
+        next(run)
+    for run in runs:
+        next(run)
+    for run in runs:
+        for _ in run:
+            pass
+
+
+def scatter_plane(left, right, identity, extra=()):
+    height, width = left.shape[0] // (2 * GROUP), right.shape[0]
+    sizes = [(height, width)] + [size for _, *size in extra]
+    shapes = []
+    scratch = [pltpu.VMEM((2 * GROUP, *size), jnp.bfloat16) for size in sizes]
+    for rows, columns in sizes:
+        half = (rows // 2, columns)
+        shapes.append(jax.ShapeDtypeStruct((rows, columns), jnp.float32))
+        scratch += [
+            pltpu.VMEM((4, rows, columns), jnp.bfloat16),
+            pltpu.VMEM((2,) + half, jnp.bfloat16),
+            pltpu.VMEM((2,) + half, jnp.bfloat16),
+            pltpu.VMEM((2,) + half, jnp.bfloat16),
+            pltpu.VMEM((3,) + half, jnp.bfloat16),
+            pltpu.VMEM((3,) + half, jnp.bfloat16),
+            pltpu.SemaphoreType.DMA((4,)),
+            pltpu.SemaphoreType.DMA((4,)),
+            pltpu.SemaphoreType.DMA((6,)),
+            pltpu.SemaphoreType.DMA((6,)),
+        ]
+    count = 1 + len(extra)
+    return pl.pallas_call(
+        partial(scatter_kernel, count),
+        out_shape=shapes,
+        in_specs=vmem_specs(1 + count),
+        out_specs=vmem_specs(count),
+        scratch_shapes=scratch,
+        cost_estimate=lasting(35),
+        compiler_params=pltpu.CompilerParams(
+            collective_id=identity, has_side_effects=True, vmem_limit_bytes=VMEM_BYTES
+        ),
+    )(left, right, *[array for array, *_ in extra])
+
+
+def finish_kernel(count_bulk, *refs):
+    small_ref, bc_ref, own_ref, out_ref = refs[:4]
+    bulk = refs[4 : 4 + count_bulk]
+    small_sum, bc_all, both_ref, both_out = refs[4 + count_bulk : 8 + count_bulk]
+    bulk_back = refs[8 + count_bulk : 8 + 2 * count_bulk]
+    small_in, bc_send, bc_in, line_in, bc_line, own_sems, send_s, recv_s = refs[8 + 2 * count_bulk :]
+    data, place, core, along_x, along_y, across = plane_place()
+    count = lax.axis_size("dp")
+    mine = 2 * place + core
+    partner = (data, place, 1 - core)
+    others = (across, along_x, along_y)
+    plane = []
+    for turn_by in range(1, 2 * GROUP):
+        other = lax.rem(mine + turn_by, 2 * GROUP)
+        plane.append((other, (data, other // 2, lax.rem(other, 2))))
+    line = []
+    for turn_by in range(1, count):
+        other = lax.rem(data + turn_by, count)
+        line.append((other, (other, place, core)))
+    meet([device for _, device in plane + line])
+
+    sent = 0
+    started = []
+
+    def push(source, target, device):
+        nonlocal sent
+        copy = remote(source, target, send_s.at[sent], recv_s.at[sent], device)
+        copy.start()
+        sent += 1
+        started.append(copy)
+        return copy
+
+    piece = small_in.shape[2]
+    rows = bc_in.shape[1]
+
+    def piece_of(ref, index):
+        return ref.at[:, pl.ds(pl.multiple_of(index * piece, 128), piece)]
+
+    def rows_of(ref, index):
+        return ref.at[pl.ds(pl.multiple_of(index * rows, 16), rows)]
+
+    bc_send[...] = bc_ref[...].astype(jnp.bfloat16)
+    first = [push(rows_of(bc_send, other), bc_in.at[data], device) for other, device in line]
+    first += [push(piece_of(small_ref, other), small_in.at[mine], device) for other, device in plane]
+    late = []
+    for source, target in ((own_ref, both_ref), (out_ref, both_out)):
+        late.append(push(source, target.at[core], partner))
+    own = []
+    for index, (source, target) in enumerate(zip(bulk, bulk_back)):
+        for chip in others:
+            late.append(push(source.at[chip], target.at[place], (data, chip, core)))
+        copy = pltpu.make_async_copy(source.at[place], target.at[place], own_sems.at[index])
+        copy.start()
+        own.append(copy)
+    small_in[mine] = piece_of(small_ref, mine)[...]
+    bc_in[data] = rows_of(bc_send, data)[...]
+    both_ref[core] = own_ref[...]
+    both_out[core] = out_ref[...]
+    for copy in first:
+        copy.wait_recv()
+    total = small_in[0]
+    for index in range(1, 2 * GROUP):
+        total = total + small_in[index]
+    line_in[data] = total
+    total = bc_in[0].astype(jnp.float32)
+    for index in range(1, count):
+        total = total + bc_in[index].astype(jnp.float32)
+    bc_line[data] = total.astype(jnp.bfloat16)
+    second = [push(bc_line.at[data], bc_line.at[data], device) for _, device in line]
+    second += [push(line_in.at[data], line_in.at[data], device) for _, device in line]
+    for copy in second:
+        copy.wait_recv()
+    total = line_in[0]
+    for index in range(1, count):
+        total = total + line_in[index]
+    piece_of(small_sum, mine)[...] = total
+    third = [push(bc_line, bc_all.at[mine], (data, chip, core)) for chip in others]
+    late += [
+        push(piece_of(small_sum, mine), piece_of(small_sum, mine), device) for _, device in plane
+    ]
+    late.append(push(bc_line, bc_all.at[mine], partner))
+    bc_all[mine] = bc_line[...]
+    for copy, chip in zip(third, others):
+        copy.wait_recv()
+        held = bc_all.at[2 * chip + core]
+        late.append(push(held, held, partner))
+    for copy in late:
+        copy.wait_recv()
+    for copy in started:
+        copy.wait_send()
+    for copy in own:
+        copy.wait()
+
+
+def finish_all(small, bc_sum, own_rows, out_rows, bulk):
+    count = lax.axis_size("dp")
+    places = 2 * GROUP
+    pushes = (count - 1) * 4 + (places - 1) * 2 + 2 * GROUP + 1 + 3 * len(bulk)
+    shaped = jax.ShapeDtypeStruct
+    piece, line_rows = small.shape[1] // places, bc_sum.shape[0] // count
+    width = bc_sum.shape[1]
+    return pl.pallas_call(
+        partial(finish_kernel, len(bulk)),
+        out_shape=[
+            shaped(small.shape, jnp.float32),
+            shaped((places, count, line_rows, width), jnp.bfloat16),
+            shaped((2,) + own_rows.shape, own_rows.dtype),
+            shaped((2,) + out_rows.shape, out_rows.dtype),
+        ]
+        + [shaped(array.shape, array.dtype) for array in bulk],
+        in_specs=vmem_specs(4) + any_specs(len(bulk)),
+        out_specs=vmem_specs(4) + any_specs(len(bulk)),
+        scratch_shapes=[
+            pltpu.VMEM((places, 8, piece), jnp.float32),
+            pltpu.VMEM(bc_sum.shape, jnp.bfloat16),
+            pltpu.VMEM((count, line_rows, width), jnp.bfloat16),
+            pltpu.VMEM((count, 8, piece), jnp.float32),
+            pltpu.VMEM((count, line_rows, width), jnp.bfloat16),
+            pltpu.SemaphoreType.DMA((len(bulk),)),
+            pltpu.SemaphoreType.DMA((pushes,)),
+            pltpu.SemaphoreType.DMA((pushes,)),
+        ],
+        cost_estimate=lasting(45),
+        compiler_params=pltpu.CompilerParams(
+            collective_id=7, has_side_effects=True, vmem_limit_bytes=VMEM_BYTES
+        ),
+    )(small, bc_sum, own_rows, out_rows, *bulk)
+
+
+def unpack_kernel(
+    gu_ref,
+    down_ref,
+    out_ref,
+    in_ref,
+    bc_ref,
+    taps_ref,
+    gate_ref,
+    up_ref,
+    d_ref,
+    mo_ref,
+    ao_ref,
+    z_ref,
+    x_ref,
+    q_ref,
+    k_ref,
+    v_ref,
+    dt_ref,
+    grad_bc_ref,
+    grad_conv_ref,
+):
+    units, width, part = down_ref.shape[2], HEADS * HP, HD // 4
+    grad_conv_ref[...] = taps_ref[...].T[:, :KC]
+    for chip in range(GROUP):
+        columns = slice(units * chip, units * (chip + 1))
+        gate_ref[:, columns] = gu_ref[chip, :, :units].astype(jnp.float32)
+        up_ref[:, columns] = gu_ref[chip, :, units:].astype(jnp.float32)
+        d_ref[columns] = down_ref[chip].astype(jnp.float32).T
+        turned = out_ref[chip].astype(jnp.float32).T
+        mo_ref[width * chip : width * (chip + 1)] = turned[:width]
+        ao_ref[HD * chip : HD * (chip + 1)] = turned[width:]
+        high, wide = bc_ref.shape[1:]
+        for core in range(2):
+            grad_bc_ref[wide * core : wide * (core + 1), high * chip : high * (chip + 1)] = (
+                bc_ref[2 * chip + core].astype(jnp.float32).T
+            )
+    for chip in range(GROUP):
+        columns = slice(width * chip, width * (chip + 1))
+        z_ref[:, columns] = in_ref[chip, :, :width].astype(jnp.float32)
+        x_ref[:, columns] = in_ref[chip, :, width + HD : 2 * width + HD].astype(jnp.float32)
+        q_ref[:, HD * chip : HD * (chip + 1)] = in_ref[chip, :, width : width + HD].astype(
+            jnp.float32
+        )
+    held = [in_ref[chip, :, 2 * width + HD :].astype(jnp.float32) for chip in range(GROUP)]
+    k_ref[...] = jnp.concatenate(
+        [
+            held[0][:, :part],
+            held[1][:, :part],
+            held[0][:, part : 2 * part],
+            held[1][:, part : 2 * part],
+        ],
+        axis=1,
+    )
+    v_ref[...] = jnp.concatenate([held[2][:, : 2 * part], held[3][:, : 2 * part]], axis=1)
+    dt_ref[...] = jnp.concatenate(
+        [values[:, DT_LANE : DT_LANE + HEADS] for values in held], axis=1
+    )
+
+
+def exchange_kernel(moves, count_in, spread, *refs):
+    data, place, core, along_x, along_y, across = plane_place()
+    sources, targets = refs[:count_in], refs[count_in:-3]
+    local_sems, send_sems, recv_sems = refs[-3:]
+    count = lax.axis_size("dp")
+    others = (across, along_x, along_y)
+    devices = [(data, chip, core) for chip in others]
+    if spread:
+        mine = GROUP * data + place
+        all_places = GROUP * count
+        devices = []
+        for turn_by in range(1, all_places):
+            other = lax.rem(mine + turn_by, all_places)
+            devices.append((other // GROUP, lax.rem(other, GROUP), core))
+    meet(devices)
+    copies = []
+    for index, chip in enumerate(others):
+        for at, move in enumerate(moves):
+            source, target = move(sources, targets, place, chip)
+            slot = index * len(moves) + at
+            copy = remote(
+                source, target, send_sems.at[slot], recv_sems.at[slot], (data, chip, core)
+            )
+            copy.start()
+            copies.append(copy)
+    own = []
+    if spread:
+        first = 3 * len(moves)
+        for index, device in enumerate(devices):
+            copy = remote(
+                sources[-1],
+                targets[-1].at[mine],
+                send_sems.at[first + index],
+                recv_sems.at[first + index],
+                device,
+            )
+            copy.start()
+            copies.append(copy)
+        copy = pltpu.make_async_copy(sources[-1], targets[-1].at[mine], local_sems.at[len(moves)])
+        copy.start()
+        own.append(copy)
+    for at, move in enumerate(moves):
+        source, target = move(sources, targets, place, place)
+        copy = pltpu.make_async_copy(source, target, local_sems.at[at])
+        copy.start()
+        own.append(copy)
+    for copy in own:
+        copy.wait()
+    for copy in copies:
+        copy.wait()
+
+
+def exchange_plane(moves, arrays, out_shapes, identity, spread=False):
+    shapes = [jax.ShapeDtypeStruct(shape, jnp.bfloat16) for shape in out_shapes]
+    count = 3 * len(moves)
+    if spread:
+        places = GROUP * lax.axis_size("dp")
+        shapes.append(jax.ShapeDtypeStruct((places,) + arrays[-1].shape, arrays[-1].dtype))
+        count += places - 1
+    return pl.pallas_call(
+        partial(exchange_kernel, moves, len(arrays), spread),
+        out_shape=shapes,
+        in_specs=any_specs(len(arrays)),
+        out_specs=any_specs(len(shapes)),
+        scratch_shapes=[
+            pltpu.SemaphoreType.DMA((len(moves) + 1,)),
+            pltpu.SemaphoreType.DMA((count,)),
+            pltpu.SemaphoreType.DMA((count,)),
+        ],
+        cost_estimate=lasting(25),
+        compiler_params=pltpu.CompilerParams(collective_id=identity, has_side_effects=True),
+    )(*arrays)
+
+
+def column_move(source, target, start, width):
+    def move(sources, targets, place, chip):
+        columns = pl.ds(pl.multiple_of(chip * width, 128), width)
+        return (
+            sources[source].at[:, columns],
+            targets[target].at[place, :, pl.ds(start, width)],
+        )
+
+    return move
+
+
+def block_move(source, target):
+    def move(sources, targets, place, chip):
+        return (sources[source].at[chip], targets[target].at[place])
+
+    return move
+
+
+def misc_move(source, target, start):
+    def move(sources, targets, place, chip):
+        return (
+            sources[source].at[chip],
+            targets[target].at[place, :, pl.ds(start, 128)],
+        )
+
+    return move
+
+
+def lane_masks():
+    lane = lax.broadcasted_iota(jnp.int32, (1, 2 * HP), 1)
+    return (lane < HP, lane >= HP)
+
+
+DT_LANE = HP
+
+
+def at_lane(lane, values):
+    row = lax.broadcasted_iota(jnp.int32, (1, 2 * HP), 1)
+    return jnp.where(row == lane, values, 0.0)
+
+
+def at_row(row, values):
+    rows = lax.broadcasted_iota(jnp.int32, (values.shape[1], 1), 0)
+    return jnp.where(rows == row, values, 0.0)
+
+
+def pair_columns(values, pair):
+    low, high = lane_masks()
+    lane = DT_LANE + 2 * pair
+    return jnp.where(low, values[:, lane : lane + 1], values[:, lane + 1 : lane + 2])
+
+
+def head_sums(values):
+    low, high = lane_masks()
+    first = jnp.sum(jnp.where(low, values, 0.0), axis=1, keepdims=True)
+    second = jnp.sum(jnp.where(high, values, 0.0), axis=1, keepdims=True)
+    return (first, second)
+
+
+def head_means(values):
+    low, high = lane_masks()
+    first, second = head_sums(values)
+    return jnp.where(low, first, second) * (1.0 / HP)
+
+
+def stack_heads(values):
+    low, high = lane_masks()
+    zero = jnp.zeros_like(values)
+    return jnp.concatenate([jnp.where(low, values, zero), jnp.where(high, values, zero)], axis=0)
+
+
+def order_in(size):
+    row = lax.broadcasted_iota(jnp.int32, (size, size), 0)
+    column = lax.broadcasted_iota(jnp.int32, (size, size), 1)
+    return (row, column)
+
+
+def exact_sum(ones, values):
+    high = values.astype(jnp.bfloat16)
+    rest = values - high.astype(jnp.float32)
+    middle = rest.astype(jnp.bfloat16)
+    low = (rest - middle.astype(jnp.float32)).astype(jnp.bfloat16)
+    return dot_f32(ones, high, 1, 0) + (dot_f32(ones, middle, 1, 0) + dot_f32(ones, low, 1, 0))
+
+
+def chunk_decays(proj_ref, heads_ref, keeps_ref):
+    size, width = proj_ref.shape
+    raw = proj_ref[:, width - 2 * HP :] + heads_ref[0:1]
+    dt_rows = jnp.maximum(raw, 0.0) + jnp.log1p(jnp.exp(-jnp.abs(raw)))
+    row, column = order_in(size)
+    lower = jnp.where(row >= column, 1.0, 0.0).astype(jnp.bfloat16)
+    cumul = exact_sum(lower, -heads_ref[1:2] * dt_rows)
+    enter = jnp.exp(cumul) * keeps_ref[:, 0:1]
+    leave_bare = jnp.exp(cumul[size - 1 :] - cumul) * keeps_ref[:, 1:2]
+    return (raw, dt_rows, cumul, enter, leave_bare)
+
+
+def conv_windows(block, proj_ref, before_ref, bc_ref, bc_before_ref):
+    if block < HEADS // 2:
+        start = proj_ref.shape[1] - 2 * HP * (1 + HEADS // 2 - block)
+        lanes = slice(start, start + 2 * HP)
+        now, before = proj_ref[:, lanes], before_ref[:, lanes]
+        now, before = now.astype(jnp.bfloat16), before.astype(jnp.bfloat16)
+    else:
+        start = 2 * HP * (block - HEADS // 2)
+        lanes = slice(start, start + 2 * HP)
+        now, before = bc_ref[:, lanes], bc_before_ref[8:, lanes]
+    now, before = now.astype(jnp.float32), before.astype(jnp.float32)
+    size = now.shape[0]
+    extended = jnp.concatenate([before, now], axis=0)
+    return [now] + [extended[8 - back : 8 - back + size] for back in range(1, KC)]
+
+
+def conv_sum(windows, taps_ref, lanes, keeps_ref):
+    total = taps_ref[KC : KC + 1, lanes] + taps_ref[KC - 1 : KC, lanes] * windows[0]
+    for back in range(1, KC):
+        total = total + taps_ref[KC - 1 - back : KC - back, lanes] * (
+            windows[back] * keeps_ref[:, 1 + back : 2 + back]
+        )
+    return total
+
+
+def head_decay(allowed, cumul, cumul_t, head):
+    lane = DT_LANE + head
+    differ = cumul[:, lane : lane + 1] - cumul_t[lane : lane + 1, :]
+    return jnp.exp(jnp.where(allowed, differ, -jnp.inf))
+
+
+def ssd_forward_kernel(
+    proj_ref,
+    before_ref,
+    bc_ref,
+    bc_before_ref,
+    taps_ref,
+    heads_ref,
+    keeps_ref,
+    segc_ref,
+    segr_ref,
+    skip_ref,
+    gain_ref,
+    gated_ref,
+    ssm_ref,
+    states_ref,
+    mixed_ref,
+    state,
+):
+    @pl.when(pl.program_id(0) == 0)
+    def _():
+        state[...] = jnp.zeros_like(state)
+
+    size = proj_ref.shape[0]
+    width = HEADS * HP
+    for block in range(mixed_ref.shape[1] // (2 * HP)):
+        lanes = slice(2 * HP * block, 2 * HP * (block + 1))
+        windows = conv_windows(block, proj_ref, before_ref, bc_ref, bc_before_ref)
+        summed = conv_sum(windows, taps_ref, lanes, keeps_ref)
+        mixed_ref[:, lanes] = (summed * jax.nn.sigmoid(summed)).astype(jnp.bfloat16)
+    raw, dt_rows, cumul, enter_all, leave_bare = chunk_decays(proj_ref, heads_ref, keeps_ref)
+    leave_all = leave_bare * dt_rows
+    cumul_t, dt_t = cumul.T, dt_rows.T
+    entry = state[...]
+    states_ref[0] = entry
+    b_rows, c_rows = mixed_ref[:, width : width + NS], mixed_ref[:, width + NS :]
+    gram = dot_f32(c_rows, b_rows, 1, 1)
+    row, column = order_in(size)
+    allowed = (segc_ref[...] == segr_ref[0]) & (row >= column)
+    entered = dot_split(c_rows, halves(entry), 1, 0)
+    for pair in range(HEADS // 2):
+        lanes = slice(2 * HP * pair, 2 * HP * (pair + 1))
+        heads_x = mixed_ref[:, lanes]
+        mixing = []
+        for head in (2 * pair, 2 * pair + 1):
+            lane = DT_LANE + head
+            decay = head_decay(allowed, cumul, cumul_t, head)
+            mixing.append(gram * decay * dt_t[lane : lane + 1, :])
+        out = dot_split_left(
+            halves(jnp.concatenate(mixing, axis=1)), stack_heads(heads_x), 1, 0
+        )
+        wide_x = heads_x.astype(jnp.float32)
+        enter = pair_columns(enter_all, pair)
+        out = out + enter * entered[:, lanes] + skip_ref[:, lanes] * wide_x
+        ssm_ref[:, lanes] = out
+        gate = proj_ref[:, lanes]
+        value = out * (gate * jax.nn.sigmoid(gate))
+        scale = lax.rsqrt(head_means(value * value) + GROUP_EPSILON)
+        gated_ref[:, lanes] = (value * scale * gain_ref[:, lanes]).astype(jnp.bfloat16)
+        weighted = halves(pair_columns(leave_all, pair) * wide_x)
+        state[:, lanes] = enter[size - 1 :, :] * entry[:, lanes] + dot_split(
+            b_rows, weighted, 0, 0
+        )
+
+
+def ssd_backward_kernel(
+    proj_ref,
+    before_ref,
+    bc_ref,
+    bc_before_ref,
+    taps_ref,
+    heads_ref,
+    keeps_ref,
+    segc_ref,
+    segr_ref,
+    skip_ref,
+    gain_ref,
+    mixed_ref,
+    ssm_ref,
+    states_ref,
+    dgated_ref,
+    dq_ref,
+    dproj_ref,
+    dtaps_ref,
+    dheads_ref,
+    dskip_ref,
+    dgain_ref,
+    state,
+    d_mixed,
+    next_rows,
+):
+    @pl.when(pl.program_id(0) == 0)
+    def _():
+        state[...] = jnp.zeros_like(state)
+        next_rows[...] = jnp.zeros_like(next_rows)
+        dtaps_ref[...] = jnp.zeros_like(dtaps_ref)
+        dheads_ref[...] = jnp.zeros_like(dheads_ref)
+        dskip_ref[...] = jnp.zeros_like(dskip_ref)
+        dgain_ref[...] = jnp.zeros_like(dgain_ref)
+
+    size = proj_ref.shape[0]
+    width = HEADS * HP
+    raw, dt_rows, cumul, enter_all, leave_bare = chunk_decays(proj_ref, heads_ref, keeps_ref)
+    leave_all = leave_bare * dt_rows
+    cumul_t, dt_t = cumul.T, dt_rows.T
+    later = state[...]
+    later_parts = halves(later)
+    entry = states_ref[0]
+    entry_parts = halves(entry)
+    carried = jnp.sum(later * entry, axis=0, keepdims=True)
+    b_rows, c_rows = mixed_ref[:, width : width + NS], mixed_ref[:, width + NS :]
+    gram = dot_f32(c_rows, b_rows, 1, 1)
+    row, column = order_in(size)
+    allowed = (segc_ref[...] == segr_ref[0]) & (row >= column)
+    entered = dot_split(c_rows, entry_parts, 1, 0)
+    d_weighted = dot_split(b_rows, later_parts, 1, 0)
+    d_gram = jnp.zeros((size, size), jnp.float32)
+    d_c = jnp.zeros(c_rows.shape, jnp.float32)
+    d_b = jnp.zeros(b_rows.shape, jnp.float32)
+    row_sums = jnp.zeros((size, 2 * HP), jnp.float32)
+    d_leave = jnp.zeros((size, 2 * HP), jnp.float32)
+    d_enter = jnp.zeros((size, 2 * HP), jnp.float32)
+    column_sums = jnp.zeros((2 * HP, size), jnp.float32)
+    d_carried = jnp.zeros((1, 2 * HP), jnp.float32)
+    for pair in range(HEADS // 2):
+        lanes = slice(2 * HP * pair, 2 * HP * (pair + 1))
+        heads_x = mixed_ref[:, lanes]
+        wide_x = heads_x.astype(jnp.float32)
+        ssm, gate, gain = ssm_ref[:, lanes], proj_ref[:, lanes], gain_ref[:, lanes]
+        d_gated = dgated_ref[:, lanes]
+        sigmoid = jax.nn.sigmoid(gate)
+        silu = gate * sigmoid
+        value = ssm * silu
+        scale = lax.rsqrt(head_means(value * value) + GROUP_EPSILON)
+        dgain_ref[:, lanes] += jnp.sum(d_gated * value * scale, axis=0, keepdims=True)
+        d_scaled = d_gated * gain
+        d_value = scale * d_scaled - value * (scale * scale * scale) * head_means(d_scaled * value)
+        d_out = d_value * silu
+        dproj_ref[:, lanes] = (d_value * ssm * (sigmoid * (1.0 + gate * (1.0 - sigmoid)))).astype(
+            jnp.bfloat16
+        )
+        dskip_ref[:, lanes] += jnp.sum(d_out * wide_x, axis=0, keepdims=True)
+        enter, leave = pair_columns(enter_all, pair), pair_columns(leave_all, pair)
+        d_out_parts = [stack_heads(half) for half in halves(d_out)]
+        mixing = []
+        for side in range(2):
+            head = 2 * pair + side
+            lane = DT_LANE + head
+            d_mixing = dot_split_left(
+                [half[size * side : size * (side + 1)] for half in d_out_parts], heads_x, 1, 1
+            )
+            decay = head_decay(allowed, cumul, cumul_t, head)
+            dt_row = dt_t[lane : lane + 1, :]
+            weighted_gram = gram * decay
+            mixing.append(weighted_gram * dt_row)
+            d_gram = d_gram + d_mixing * (decay * dt_row)
+            product = d_mixing * weighted_gram
+            column_sums = column_sums + at_row(lane, jnp.sum(product, axis=0, keepdims=True))
+            row_sums = row_sums + at_lane(lane, jnp.sum(product * dt_row, axis=1, keepdims=True))
+        d_x = dot_splits(halves(jnp.concatenate(mixing, axis=0)), d_out_parts, 0, 0)
+        first_lane = DT_LANE + 2 * pair
+        first, second = head_sums(d_out * entered[:, lanes])
+        d_enter = d_enter + at_lane(first_lane, first) + at_lane(first_lane + 1, second)
+        first, second = head_sums(d_weighted[:, lanes] * wide_x)
+        d_leave = d_leave + at_lane(first_lane, first) + at_lane(first_lane + 1, second)
+        first, second = head_sums(carried[:, lanes])
+        d_carried = d_carried + at_lane(first_lane, first) + at_lane(first_lane + 1, second)
+        d_mixed[:, lanes] = d_x + skip_ref[:, lanes] * d_out + leave * d_weighted[:, lanes]
+        d_entered = halves(enter * d_out)
+        weighted = halves(leave * wide_x)
+        d_c = d_c + dot_splits(d_entered, [half[:, lanes] for half in entry_parts], 1, 1)
+        d_b = d_b + dot_splits(weighted, [half[:, lanes] for half in later_parts], 1, 1)
+        state[:, lanes] = enter[size - 1 :, :] * later[:, lanes] + dot_split(
+            c_rows, d_entered, 0, 0
+        )
+    d_gram_parts = halves(d_gram)
+    d_mixed[:, width : width + NS] = d_b + dot_split_left(d_gram_parts, c_rows, 0, 0)
+    d_mixed[:, width + NS :] = d_c + dot_split_left(d_gram_parts, b_rows, 1, 0)
+
+    column_sums = column_sums.T
+    d_left = d_leave * leave_all
+    d_cumul = row_sums - column_sums * dt_rows + d_enter * enter_all - d_left
+    at_last = jnp.sum(d_left, axis=0, keepdims=True) + d_carried * enter_all[size - 1 :]
+    last_row = lax.broadcasted_iota(jnp.int32, (size, 1), 0) == size - 1
+    d_cumul = d_cumul + jnp.where(last_row, at_last, 0.0)
+    upper = jnp.where(row <= column, 1.0, 0.0).astype(jnp.bfloat16)
+    d_log = exact_sum(upper, d_cumul)
+    rate = heads_ref[1:2]
+    d_raw = (column_sums + d_leave * leave_bare - rate * d_log) * jax.nn.sigmoid(raw)
+    lane_row = lax.broadcasted_iota(jnp.int32, (1, 2 * HP), 1)
+    d_raw = jnp.where((lane_row >= DT_LANE) & (lane_row < DT_LANE + HEADS), d_raw, 0.0)
+    dheads_ref[0:1] += jnp.sum(d_raw, axis=0, keepdims=True)
+    dheads_ref[1:2] += -rate * jnp.sum(d_log * dt_rows, axis=0, keepdims=True)
+    total = proj_ref.shape[1]
+    dproj_ref[:, total - 2 * HP : total] = jnp.concatenate(
+        [jnp.zeros((size, DT_LANE), jnp.bfloat16), d_raw[:, DT_LANE:].astype(jnp.bfloat16)], axis=1
+    )
+    dproj_ref[:, width : width + HD] = dq_ref[...]
+
+    for block in range(mixed_ref.shape[1] // (2 * HP)):
+        lanes = slice(2 * HP * block, 2 * HP * (block + 1))
+        windows = conv_windows(block, proj_ref, before_ref, bc_ref, bc_before_ref)
+        summed = conv_sum(windows, taps_ref, lanes, keeps_ref)
+        sigmoid = jax.nn.sigmoid(summed)
+        d_sum = d_mixed[:, lanes] * (sigmoid * (1.0 + summed * (1.0 - sigmoid)))
+        dtaps_ref[KC : KC + 1, lanes] += jnp.sum(d_sum, axis=0, keepdims=True)
+        dtaps_ref[KC - 1 : KC, lanes] += jnp.sum(d_sum * windows[0], axis=0, keepdims=True)
+        d_pre = taps_ref[KC - 1 : KC, lanes] * d_sum
+        for back in range(1, KC):
+            tap = KC - 1 - back
+            kept = d_sum * keeps_ref[:, 1 + back : 2 + back]
+            dtaps_ref[tap : tap + 1, lanes] += jnp.sum(
+                kept * windows[back], axis=0, keepdims=True
+            )
+            extended = jnp.concatenate([kept, next_rows[back - 1, :, lanes]], axis=0)
+            d_pre = d_pre + taps_ref[tap : tap + 1, lanes] * extended[back : back + size]
+            next_rows[back - 1, :, lanes] = kept[:8]
+        if block < HEADS // 2:
+            start = total - 2 * HP * (1 + HEADS // 2 - block)
+            dproj_ref[:, start : start + 2 * HP] = d_pre.astype(jnp.bfloat16)
+        else:
+            start = total + 2 * HP * (block - HEADS // 2)
+            dproj_ref[:, start : start + 2 * HP] = d_pre.astype(jnp.bfloat16)
+
+
+def ssd_specs(length, reverse, width_in, width_all, width):
+    laps = length // CHUNK
+
+    def at(lap):
+        return laps - 1 - lap if reverse else lap
+
+    def tall(columns):
+        return pl.BlockSpec((CHUNK, columns), lambda lap: (at(lap), 0))
+
+    def rim(rows, columns):
+        each = CHUNK // rows
+        return pl.BlockSpec((rows, columns), lambda lap: (jnp.maximum(each * at(lap) - 1, 0), 0))
+
+    def whole(rows, columns):
+        return pl.BlockSpec((rows, columns), lambda lap: (0, 0))
+
+    def slab(rows, columns):
+        return pl.BlockSpec((1, rows, columns), lambda lap: (at(lap), 0, 0))
+
+    specs = [
+        tall(width_in),
+        rim(8, width_in),
+        tall(2 * NS),
+        rim(16, 2 * NS),
+        whole(8, width_all),
+        whole(8, 2 * HP),
+        tall(8),
+        tall(1),
+        slab(1, CHUNK),
+        whole(1, width),
+        whole(1, width),
+    ]
+    return (laps, tall, whole, slab, specs)
+
+
+def ssd_forward(arrays):
+    length, width_in = arrays[0].shape
+    width, width_all = HEADS * HP, HEADS * HP + 2 * NS
+    laps, tall, whole, slab, specs = ssd_specs(length, False, width_in, width_all, width)
+    shaped = jax.ShapeDtypeStruct
+    return pl.pallas_call(
+        ssd_forward_kernel,
+        grid=(laps,),
+        in_specs=specs,
+        out_specs=[tall(width), tall(width), slab(NS, width), tall(width_all)],
+        out_shape=[
+            shaped((length, width), jnp.bfloat16),
+            shaped((length, width), jnp.float32),
+            shaped((laps, NS, width), jnp.float32),
+            shaped((length, width_all), jnp.bfloat16),
+        ],
+        scratch_shapes=[pltpu.VMEM((NS, width), jnp.float32)],
+        cost_estimate=lasting(6),
+        compiler_params=pltpu.CompilerParams(vmem_limit_bytes=VMEM_BYTES),
+    )(*arrays)
+
+
+def ssd_backward(arrays, mixed, ssm, states, d_outs, d_query):
+    length, width_in = arrays[0].shape
+    width, width_all = HEADS * HP, HEADS * HP + 2 * NS
+    laps, tall, whole, slab, specs = ssd_specs(length, True, width_in, width_all, width)
+    shaped = jax.ShapeDtypeStruct
+    return pl.pallas_call(
+        ssd_backward_kernel,
+        grid=(laps,),
+        in_specs=specs
+        + [
+            tall(width_all),
+            tall(width),
+            slab(NS, width),
+            tall(d_outs.shape[1]),
+            tall(HD),
+        ],
+        out_specs=[
+            tall(width_in + 2 * NS),
+            whole(8, width_all),
+            whole(8, 2 * HP),
+            whole(1, width),
+            whole(1, width),
+        ],
+        out_shape=[
+            shaped((length, width_in + 2 * NS), jnp.bfloat16),
+            shaped((8, width_all), jnp.float32),
+            shaped((8, 2 * HP), jnp.float32),
+            shaped((1, width), jnp.float32),
+            shaped((1, width), jnp.float32),
+        ],
+        scratch_shapes=[
+            pltpu.VMEM((NS, width), jnp.float32),
+            pltpu.VMEM((CHUNK, width_all), jnp.float32),
+            pltpu.VMEM((KC - 1, 8, width_all), jnp.float32),
+        ],
+        cost_estimate=lasting(48),
+        compiler_params=pltpu.CompilerParams(vmem_limit_bytes=VMEM_BYTES),
+    )(*arrays, mixed, ssm, states, d_outs, d_query)
+
+
+QUERY_ROWS = 256
+
+
+def masked_scores(q_rows, k_ref, segc_ref, segr_ref, start, reach):
+    rows = q_rows.shape[0]
+    scores = dot_f32(q_rows, k_ref[:reach], 1, 1) * HD ** (-0.5)
+    row = lax.broadcasted_iota(jnp.int32, (rows, reach), 0) + start
+    column = lax.broadcasted_iota(jnp.int32, (rows, reach), 1)
+    allowed = (segc_ref[start : start + rows] == segr_ref[:, :reach]) & (row >= column)
+    return jnp.where(allowed, scores, -jnp.inf)
+
+
+def rotate_rows(values, cos_ref, sin_ref, sign):
+    return values * cos_ref[...] + sign * (pltpu.roll(values, HD // 2, 1) * sin_ref[...])
+
+
+def swap_middle(values):
+    lane = lax.broadcasted_iota(jnp.int32, (1, HD), 1) // (HD // 4)
+    up = pltpu.roll(values, HD // 4, 1)
+    down = pltpu.roll(values, HD - HD // 4, 1)
+    return jnp.where(lane == 1, down, jnp.where(lane == 2, up, values))
+
+
+def join_halves(ref, first):
+    half = ref.shape[2] // 2
+    one, two = ref[first], ref[first + 1]
+    early = jnp.concatenate([one[:, :half], two[:, :half]], axis=1)
+    late = jnp.concatenate([one[:, half:], two[:, half:]], axis=1)
+    return jnp.concatenate([early, late], axis=0)
+
+
+def fold_rows(values):
+    rows = values.shape[0] // 2
+    return jnp.concatenate([values[:rows], values[rows:]], axis=1)
+
+
+def unfold_rows(values):
+    columns = values.shape[1] // 2
+    return jnp.concatenate([values[:, :columns], values[:, columns:]], axis=0)
+
+
+def attend_forward_kernel(
+    raw_ref, cos_ref, sin_ref, kv_ref, segc_ref, segr_ref, out_ref, total_ref, q_ref, k_ref, v_ref
+):
+    q_ref[...] = swap_middle(rotate_rows(raw_ref[...], cos_ref, sin_ref, 1.0)).astype(jnp.bfloat16)
+    k_ref[...] = join_halves(kv_ref, 0)
+    v_ref[...] = join_halves(kv_ref, 2)
+    for start in range(0, q_ref.shape[0], QUERY_ROWS):
+        reach = start + QUERY_ROWS
+        rows = slice(start, reach)
+        scores = masked_scores(q_ref[rows], k_ref, segc_ref, segr_ref, start, reach)
+        top = jnp.max(scores, axis=1, keepdims=True)
+        powers = jnp.exp(scores - top)
+        total = jnp.sum(powers, axis=1, keepdims=True)
+        probs = (powers * (1.0 / total)).astype(jnp.bfloat16)
+        out_ref[rows] = dot_f32(probs, v_ref[:reach], 1, 0).astype(jnp.bfloat16)
+        total_ref[rows] = top + jnp.log(total)
+
+
+def attend_backward_kernel(
+    q_ref,
+    k_ref,
+    v_ref,
+    cos_ref,
+    sin_ref,
+    segc_ref,
+    segr_ref,
+    total_ref,
+    dout_ref,
+    dq_ref,
+    dkv_ref,
+    dq_sum,
+    dk_sum,
+    dv_sum,
+):
+    dk_sum[...] = jnp.zeros_like(dk_sum)
+    dv_sum[...] = jnp.zeros_like(dv_sum)
+    for start in range(0, q_ref.shape[0], QUERY_ROWS):
+        reach = start + QUERY_ROWS
+        rows = slice(start, reach)
+        q_rows, d_out = q_ref[rows], dout_ref[rows].astype(jnp.bfloat16)
+        scores = masked_scores(q_rows, k_ref, segc_ref, segr_ref, start, reach)
+        probs = jnp.exp(scores - total_ref[rows])
+        d_probs = dot_f32(d_out, v_ref[:reach], 1, 1)
+        delta = jnp.sum(probs * d_probs, axis=1, keepdims=True)
+        d_scores = (probs * (d_probs - delta)).astype(jnp.bfloat16)
+        dq_sum[rows] = dot_f32(d_scores, k_ref[:reach], 1, 0) * HD ** (-0.5)
+        dk_sum[:reach] += dot_f32(d_scores, q_rows, 0, 0) * HD ** (-0.5)
+        dv_sum[:reach] += dot_f32(probs.astype(jnp.bfloat16), d_out, 0, 0)
+    dq_ref[...] = rotate_rows(swap_middle(dq_sum[...]), cos_ref, sin_ref, -1.0).astype(jnp.bfloat16)
+    half = HD // 2
+    dkv_ref[0] = fold_rows(dk_sum[:, :half]).astype(jnp.bfloat16)
+    dkv_ref[1] = fold_rows(dk_sum[:, half:]).astype(jnp.bfloat16)
+    dkv_ref[2] = fold_rows(dv_sum[:, :half]).astype(jnp.bfloat16)
+    dkv_ref[3] = fold_rows(dv_sum[:, half:]).astype(jnp.bfloat16)
+
+
+def place_kv_kernel(lane_ref, cos_ref, sin_ref, *refs):
+    parts, out_ref = refs[:-1], refs[-1]
+    total = parts[0][...].astype(jnp.float32)
+    for part in parts[1:]:
+        total = total + part[...].astype(jnp.float32)
+    total = unfold_rows(total)
+    part = cos_ref.shape[1]
+    turned = turn(cos_ref[...], -sin_ref[...], total[:, :part], total[:, part:])
+    out_ref[:, : 2 * part] = jnp.concatenate(turned, axis=1).astype(jnp.bfloat16)
+    out_ref[:, 2 * part :] = lane_ref[:, 2 * part :]
+
+
+def place_kv(d_projected, parts, cos_part, sin_part, width_in):
+    length = d_projected.shape[0]
+    lanes = pl.BlockSpec((length, HD), lambda step: (0, width_in // HD - 1))
+
+    def whole(array):
+        return pl.BlockSpec(array.shape, lambda step: (0, 0))
+
+    arrays = (cos_part, sin_part, *parts)
+    return pl.pallas_call(
+        place_kv_kernel,
+        grid=(1,),
+        in_specs=[lanes] + [whole(array) for array in arrays],
+        out_specs=lanes,
+        out_shape=jax.ShapeDtypeStruct(d_projected.shape, d_projected.dtype),
+        input_output_aliases={0: 0},
+        cost_estimate=lasting(3),
+        compiler_params=pltpu.CompilerParams(vmem_limit_bytes=VMEM_BYTES),
+    )(d_projected, *arrays)
+
+
+def attend(kernel, arrays, out_shapes, scratch=()):
+    return pl.pallas_call(
+        kernel,
+        in_specs=vmem_specs(len(arrays)),
+        out_specs=vmem_specs(len(out_shapes)),
+        out_shape=[jax.ShapeDtypeStruct(shape, dtype) for shape, dtype in out_shapes],
+        scratch_shapes=[pltpu.VMEM(shape, dtype) for shape, dtype in scratch],
+        cost_estimate=lasting(9),
+        compiler_params=pltpu.CompilerParams(vmem_limit_bytes=VMEM_BYTES),
+    )(*arrays)
+
+
+def turn(cosine, sine_part, first_half, second):
+    return (
+        first_half * cosine - second * sine_part,
+        second * cosine + first_half * sine_part,
+    )
+
+
+def after(value, *earlier):
+    return lax.optimization_barrier((value,) + earlier)[0]
+
+
+def over_chips(block):
+    place = lax.axis_index("seq")
+    count = lax.axis_size("seq")
+    stacked = jnp.zeros((count,) + block.shape, block.dtype)
+    stacked = lax.dynamic_update_index_in_dim(stacked, block, place, 0)
+    for mask in range(1, count):
+        moved = lax.ppermute(block, "seq", [(i, i ^ mask) for i in range(count)])
+        stacked = lax.dynamic_update_index_in_dim(stacked, moved, place ^ mask, 0)
+    return stacked
+
+
+def from_chips(blocks):
+    place = lax.axis_index("seq")
+    count = lax.axis_size("seq")
+    moved = [lax.dynamic_index_in_dim(blocks, place, 0, False)]
+    for mask in range(1, count):
+        block = lax.dynamic_index_in_dim(blocks, place ^ mask, 0, False)
+        moved.append(lax.ppermute(block, "seq", [(i, i ^ mask) for i in range(count)]))
+    return moved
+
+
+def heads_local_plan(
+    hidden_in,
+    teacher,
+    segment_ids,
+    valid_mask,
+    norm1_gain,
+    w_z,
+    w_x,
+    w_bc,
+    w_dt,
+    conv_weight,
+    conv_bias,
+    dt_bias,
+    a_log,
+    d_skip,
+    group_gain,
+    w_mamba_out,
+    w_query,
+    w_key,
+    w_value,
+    w_attn_out,
+    norm2_gain,
+    w_gate,
+    w_up,
+    w_down,
+):
+    place, core, data_rank = (
+        lax.axis_index("seq"),
+        lax.axis_index("tensor"),
+        lax.axis_index("dp"),
+    )
+    data_count = lax.axis_size("dp")
+    chip_rows, width = hidden_in.shape[1:]
+    own_rows = chip_rows // 2
+    length = segment_ids.shape[1]
+    slice_rows = w_z.shape[0]
+    width_x = HEADS * HP
+    hidden_units = w_gate.shape[1] // GROUP
+    segment = segment_ids[0]
+    seg_column, seg_row = segment[:, None], segment[None, :]
+    own_start = place * chip_rows + core * own_rows
+    token_count = jnp.sum(valid_mask).astype(jnp.float32)
+    mask_rows = lax.dynamic_slice(valid_mask, (data_rank, own_start), (1, own_rows))[0]
+    total_tokens = float(valid_mask.shape[0] * valid_mask.shape[1])
+    bf16 = jnp.bfloat16
+
+    half, part = HD // 2, HD // 4
+    kv_columns = (
+        (w_key[:, :part], w_key[:, half : half + part]),
+        (w_key[:, part:half], w_key[:, half + part :]),
+        (w_value[:, :half],),
+        (w_value[:, half:],),
+    )
+    misc = jnp.stack(
+        [
+            jnp.concatenate(
+                kv_columns[chip]
+                + (
+                    w_dt[:, HEADS * chip : HEADS * (chip + 1)],
+                    jnp.zeros((slice_rows, half - HEADS), bf16),
+                ),
+                axis=1,
+            )
+            for chip in range(GROUP)
+        ]
+    )
+    gains = jnp.concatenate(
+        [norm1_gain[None], norm2_gain[None], jnp.zeros((6, slice_rows), bf16)]
+    ).astype(jnp.float32)
+    width_in = 2 * width_x + 2 * HD
+    in_slices, gains_all = exchange_plane(
+        (
+            column_move(0, 0, 0, width_x),
+            column_move(1, 0, width_x, HD),
+            column_move(2, 0, width_x + HD, width_x),
+            misc_move(3, 0, 2 * width_x + HD),
+        ),
+        (w_z, w_query, w_x, misc, gains),
+        [(GROUP, slice_rows, width_in)],
+        3,
+        True,
+    )
+    gain_one, gain_two = gains_all[:, 0].reshape(width), gains_all[:, 1].reshape(width)
+    full_in = lax.all_gather(in_slices, "dp", axis=0, tiled=True).reshape(width, width_in)
+    hidden_own = lax.dynamic_slice(hidden_in[0], (core * own_rows, 0), (own_rows, width))
+    hidden_own = after(hidden_own, in_slices)
+    hidden_all = gather_plane(hidden_own)
+    hidden_own = hidden_own.astype(jnp.float32)
+    width_out = width_x + HD
+    out_slices, gu_slices, down_slices = exchange_plane(
+        (
+            column_move(0, 0, 0, width_x),
+            column_move(1, 0, width_x, HD),
+            column_move(2, 1, 0, hidden_units),
+            column_move(3, 1, hidden_units, hidden_units),
+            column_move(4, 2, 0, hidden_units),
+        ),
+        (after(w_mamba_out.T, hidden_all), w_attn_out.T, w_gate, w_up, w_down.T),
+        [
+            (GROUP, slice_rows, width_out),
+            (GROUP, slice_rows, 2 * hidden_units),
+            (GROUP, slice_rows, hidden_units),
+        ],
+        4,
+    )
+    hidden = after(hidden_all, out_slices).astype(jnp.float32)
+    out_gathered = lax.all_gather(after(out_slices, full_in), "dp", axis=0, tiled=True)
+    full_out = out_gathered.reshape(width, width_out)
+
+    scale_one = lax.rsqrt(jnp.mean(hidden * hidden, axis=-1, keepdims=True) + EPSILON)
+    normed = (hidden * scale_one * gain_one).astype(bf16)
+    pre_bc = mat_dot(normed, w_bc).astype(bf16)
+    positions = jnp.arange(length)
+    frequency = ROPE_BASE ** (-2.0 * jnp.arange(half).astype(jnp.float32) / HD)
+    angles = positions.astype(jnp.float32)[:, None] * frequency[None, :]
+    cosine, sine_part = jnp.cos(angles), jnp.sin(angles)
+    cos_wide = jnp.concatenate([cosine, cosine], axis=1)
+    sin_wide = jnp.concatenate([-sine_part, sine_part], axis=1)
+    on_key = place < 2
+    cos_part = lax.dynamic_slice_in_dim(cosine, part * lax.rem(place, 2), part, 1)
+    sin_part = lax.dynamic_slice_in_dim(sine_part, part * lax.rem(place, 2), part, 1)
+    cos_part = jnp.where(on_key, cos_part, 1.0)
+    sin_part = jnp.where(on_key, sin_part, 0.0)
+    head_start = core * (MH // 2) + place * HEADS
+
+    def local_rows(values, width_head):
+        return jnp.concatenate(
+            [
+                lax.dynamic_slice_in_dim(values, head_start * width_head, HEADS * width_head, 0),
+                values[MH * width_head :],
+            ],
+            axis=0,
+        )
+
+    taps = jnp.concatenate(
+        [local_rows(conv_weight, HP).T, local_rows(conv_bias, HP)[None]], axis=0
+    )
+    taps = jnp.pad(taps, ((0, 8 - KC - 1), (0, 0)))
+    rate = jnp.exp(local_rows(a_log, 1))
+    head_rows = jnp.zeros((8, HD), jnp.float32)
+    head_rows = head_rows.at[0, DT_LANE : DT_LANE + HEADS].set(local_rows(dt_bias, 1))
+    head_rows = head_rows.at[1, DT_LANE : DT_LANE + HEADS].set(rate)
+    skip_row = jnp.repeat(local_rows(d_skip, 1), HP)[None, :]
+    gain_row = lax.dynamic_slice_in_dim(group_gain, head_start, HEADS, 0).reshape(1, width_x)
+    laps = length // CHUNK
+    seg_laps = segment.reshape(laps, CHUNK)
+    seg_last = seg_laps[:, -1:]
+    seg_before = jnp.concatenate([jnp.full((1, 1), -1, jnp.int32), seg_last[:-1]])
+    seg_ext = jnp.concatenate([jnp.full((KC - 1,), -1, jnp.int32), segment])
+    keeps = [(seg_laps == seg_before).reshape(length), (seg_laps == seg_last).reshape(length)]
+    keeps += [seg_ext[KC - 1 - back : KC - 1 - back + length] == segment for back in range(1, KC)]
+    keeps = jnp.stack(keeps + [jnp.zeros((length,), bool)] * 3, axis=1).astype(jnp.float32)
+
+    normed_in, pre_bc = lax.optimization_barrier((normed, pre_bc, keeps, cos_wide, sin_wide))[:2]
+    projected = mat_dot(normed_in, full_in)
+    full_all = jnp.concatenate([full_in, w_bc], axis=1)
+    kv_raw = projected[:, 2 * width_x + HD : 2 * width_x + HD + half]
+    kv_own = jnp.concatenate(
+        turn(cos_part, sin_part, kv_raw[:, :part], kv_raw[:, part:]), axis=1
+    ).astype(bf16)
+    kv_all = over_chips(fold_rows(kv_own))
+
+    ssd_arrays = (
+        projected,
+        projected,
+        pre_bc,
+        pre_bc,
+        taps,
+        head_rows,
+        keeps,
+        seg_column,
+        seg_laps[:, None, :],
+        skip_row,
+        gain_row,
+    )
+    gated, ssm, states, mixed = ssd_forward(ssd_arrays)
+    gu_gathered = lax.all_gather(after(gu_slices, out_gathered, gated), "dp", axis=0, tiled=True)
+    down_gathered = lax.all_gather(after(down_slices, gu_gathered), "dp", axis=0, tiled=True)
+    full_gu = gu_gathered.reshape(width, 2 * hidden_units)
+    full_down = down_gathered.reshape(width, hidden_units)
+    attended, log_total, queries, keys, vals = attend(
+        attend_forward_kernel,
+        (
+            projected[:, width_x : width_x + HD],
+            cos_wide,
+            sin_wide,
+            after(kv_all, out_gathered),
+            seg_column,
+            seg_row,
+        ),
+        (
+            ((length, HD), bf16),
+            ((length, 1), jnp.float32),
+            ((length, HD), bf16),
+            ((length, HD), bf16),
+            ((length, HD), bf16),
+        ),
+    )
+    outs = jnp.concatenate([gated, attended], axis=1)
+    middle = hidden_own + scatter_plane(outs, full_out, 2)[0]
+
+    scale_two = lax.rsqrt(jnp.mean(middle * middle, axis=-1, keepdims=True) + EPSILON)
+    normed_two, gate_up, activated = gather_plane(
+        after((middle * scale_two * gain_two).astype(bf16), gu_gathered, full_all),
+        9,
+        apply_gate_up,
+        (full_gu,),
+        (((length, 2 * hidden_units), jnp.float32), ((length, hidden_units), bf16)),
+    )
+    block_out = middle + scatter_plane(activated, full_down, 2)[0]
+    teacher_own = lax.dynamic_slice(teacher[0], (core * own_rows, 0), (own_rows, width))
+    d_out = (
+        2.0
+        * total_tokens
+        / token_count
+        * mask_rows.astype(jnp.float32)[:, None]
+        * (block_out - teacher_own.astype(jnp.float32))
+    )
+    d_mlp, d_gate_up = gather_plane(
+        d_out.astype(bf16),
+        10,
+        apply_down_back,
+        (full_down, gate_up),
+        (((length, 2 * hidden_units), bf16),),
+    )
+
+    def sum_rows(grads):
+        summed = lax.psum_scatter(grads.astype(bf16), "dp", scatter_dimension=0, tiled=True)
+        return summed.reshape(GROUP, slice_rows, grads.shape[1])
+
+    grad_down = sum_rows(dot_left_t(d_mlp, activated))
+    d_normed_two = scatter_plane(d_gate_up, full_gu, 11)[0]
+    grad_gate_up = sum_rows(
+        after(dot_left_t(normed_two, d_gate_up).astype(bf16), grad_down, d_normed_two)
+    )
+    grad_gain_two = jnp.sum(d_normed_two * middle * scale_two, axis=0)
+    d_scaled = d_normed_two * gain_two
+    d_middle = (
+        d_out
+        + scale_two * d_scaled
+        - middle * scale_two**3 * jnp.mean(d_scaled * middle, axis=-1, keepdims=True)
+    )
+    d_branch, d_outs = gather_plane(
+        after(d_middle.astype(bf16), grad_down),
+        12,
+        apply_out_back,
+        (full_out,),
+        (((length, width_out), jnp.float32),),
+    )
+    d_query, d_kv = attend(
+        attend_backward_kernel,
+        (
+            queries,
+            keys,
+            vals,
+            cos_wide,
+            sin_wide,
+            seg_column,
+            seg_row,
+            log_total,
+            d_outs[:, width_x:],
+        ),
+        (((length, HD), bf16), ((GROUP, length // 2, HD), bf16)),
+        (((length, HD), jnp.float32),) * 3,
+    )
+    d_kv_parts = from_chips(d_kv)
+    grad_out = sum_rows(
+        after(dot_left_t(d_branch, outs).astype(bf16), grad_gate_up, d_query)
+    )
+    d_projected, grad_taps, grad_heads, d_skip_lanes, d_gain_lanes = ssd_backward(
+        ssd_arrays, mixed, ssm, states, after(d_outs, grad_gate_up), d_query
+    )
+    d_kv_parts = lax.optimization_barrier((d_projected, *d_kv_parts))[1:]
+    d_projected = place_kv(d_projected, d_kv_parts, cos_part, sin_part, width_in)
+    grad_skip = jnp.sum(d_skip_lanes.reshape(HEADS, HP), axis=-1)
+    grad_group = d_gain_lanes.reshape(HEADS, HP)
+    grad_in = sum_rows(
+        after(dot_left_t(normed, d_projected[:, :width_in]).astype(bf16), grad_out)
+    )
+    bc_cols = 2 * NS // GROUP
+    d_normed, bc_sum = scatter_plane(
+        after(d_projected, grad_out), full_all, 8, ((normed, bc_cols, width // 2),)
+    )
+    scale_own = lax.rsqrt(jnp.mean(hidden_own * hidden_own, axis=-1, keepdims=True) + EPSILON)
+    grad_gain_one = jnp.sum(d_normed * hidden_own * scale_own, axis=0)
+    d_scaled_one = d_normed * gain_one
+    grad_input = (
+        d_middle
+        + scale_own * d_scaled_one
+        - hidden_own * scale_own**3 * jnp.mean(d_scaled_one * hidden_own, axis=-1, keepdims=True)
+    )
+    taps_all = jnp.concatenate(
+        [
+            lax.dynamic_update_slice(
+                jnp.zeros((8, MH * HP), jnp.float32), grad_taps[:, :width_x], (0, head_start * HP)
+            ),
+            grad_taps[:, width_x:],
+        ],
+        axis=1,
+    )
+    heads_all = lax.dynamic_update_slice(
+        jnp.zeros((8, 128), jnp.float32),
+        jnp.concatenate([grad_heads[:2, DT_LANE : DT_LANE + HEADS], grad_skip[None]]),
+        (0, head_start),
+    )
+    group_all = lax.dynamic_update_slice(
+        jnp.zeros((MH, HP), jnp.float32), grad_group, (head_start, 0)
+    )
+    small = [taps_all, heads_all]
+    small += [
+        values.reshape(8, -1) for values in (grad_gain_one, grad_gain_two, group_all)
+    ]
+    small = jnp.concatenate(small, axis=1)
+    small_width = -(-small.shape[1] // (2 * GROUP * 128)) * 2 * GROUP * 128
+    small = jnp.pad(small, ((0, 0), (0, small_width - small.shape[1])))
+    summed, bc_all, both_input, both_output, *back = finish_all(
+        small,
+        bc_sum,
+        grad_input,
+        block_out.astype(bf16),
+        [grad_gate_up, grad_down, grad_out],
+    )
+    (back_in,) = exchange_plane(
+        (block_move(0, 0),), (after(grad_in, both_input),), [grad_in.shape], 6
+    )
+    width_taps = MH * HP + 2 * NS
+    sum_taps = summed[:, :width_taps]
+    sum_heads = summed[:, width_taps : width_taps + 128]
+    summed = summed[:, width_taps + 128 :]
+    sum_one = summed[:, : width // 8].reshape(width)
+    sum_two = summed[:, width // 8 : width // 4].reshape(width)
+    sum_group = summed[:, width // 4 :][:, : MH * HP // 8].reshape(MH, HP)
+    gain_start = (data_rank * GROUP + place) * slice_rows
+
+    (
+        grad_gate,
+        grad_up,
+        grad_down,
+        grad_mo,
+        grad_ao,
+        grad_z,
+        grad_x,
+        grad_q,
+        grad_k,
+        grad_v,
+        grad_dt,
+        grad_bc,
+        grad_conv,
+    ) = attend(
+        unpack_kernel,
+        (*back, back_in, bc_all.reshape(2 * GROUP, bc_cols, width // 2), sum_taps),
+        [
+            (array.shape, jnp.float32)
+            for array in (
+                w_gate,
+                w_up,
+                w_down,
+                w_mamba_out,
+                w_attn_out,
+                w_z,
+                w_x,
+                w_query,
+                w_key,
+                w_value,
+                w_dt,
+                w_bc,
+                conv_weight,
+            )
+        ],
+    )
+    return (
+        both_output.reshape(1, chip_rows, width),
+        both_input.reshape(1, chip_rows, width),
+        lax.dynamic_slice_in_dim(sum_one, gain_start, slice_rows),
+        grad_z,
+        grad_x,
+        grad_bc,
+        grad_dt,
+        grad_conv,
+        sum_taps[KC],
+        sum_heads[0, :MH],
+        sum_heads[1, :MH],
+        sum_heads[2, :MH],
+        sum_group,
+        grad_mo,
+        grad_q,
+        grad_k,
+        grad_v,
+        grad_ao,
+        lax.dynamic_slice_in_dim(sum_two, gain_start, slice_rows),
+        grad_gate,
+        grad_up,
+        grad_down,
+    )
+
+
 def solution(mesh):
     placed = (
         P("dp", "seq", None),
@@ -638,8 +2278,9 @@
         P(("dp", "seq"), "tensor"),
         P("tensor", ("dp", "seq")),
     )
+    whole_row = mesh.shape["seq"] == GROUP and mesh.shape["tensor"] == 2
     return jax.shard_map(
-        local,
+        heads_local_plan if whole_row else local,
         mesh=mesh,
         in_specs=placed,
         out_specs=(

time: 3720 us -> 740 us (0.20)
  waiting for transfers between devices: 2890 us -> 36.7 us
  Pallas kernels: 0 us -> 523 us
  blocking collectives: 310 us -> 0 us
  matrix products: 326 us -> 54.4 us
  other arithmetic: 93.4 us -> 46.2 us
    reduce_scatter x12 -> x4, waiting for transfers between devices: 1970 us -> 9.18 us  [sum_rows(): lax.psum_scatter(grads.astype(bf16), 'dp', scatter_dimension=0, tiled=True)]
    all_gather x10 -> x4, waiting for transfers between devices: 600 us -> 26.2 us  [the longest x1 18.4 us: heads_local_plan(): lax.all_gather(after(gu_slices, out_gathered, gated), 'dp', axis=0, tiled...]
    pallas_call x0 -> x18, Pallas kernels: none -> 523 us  [the longest x4 160 us: scatter_plane(): pl.pallas_call(partial(scatter_kernel, count), out_shape=shapes, in_specs...]
    psum x6 -> x0, waiting for transfers between devices: 319 us -> none  [the longest x2 276 us: local(): lax.psum((grad_bc, grad_conv_full, grad_bias_full, grad_dtb_full, grad_al...]
    all_gather x8 -> x0, blocking collectives: 236 us -> none  [the longest x1 44.1 us: local(): lax.all_gather(w_key, ('dp', 'seq'), axis=0, tiled=True)]
    dot_general x34 -> x0, matrix products: 181 us -> none  [the longest x11 54.8 us: dot_right_t(): lax.dot_general(left_side, right_side, (((1,), (1,)), ((), ())), preferre...]
    unnamed x1 -> x0, blocking collectives: 73.9 us -> none
    dot_general x12 -> x2, matrix products: 64.9 us -> 16.1 us  [mat_dot(): return jnp.dot(left_side, right_side, preferred_element_type=jnp.float32)]
  transfers between devices with their start and end apart: 31 -> 14, of which waited for: 23 -> 5; matrix products, arithmetic and copies ran while one was open for 8% -> 16% of each run, Pallas kernels for 0% -> 55%
where the time goes in v2:
time: 740 us; the launch traced here: 730 us
  Pallas kernels  523 us (71%)
  matrix products  54.4 us (7%)
  other arithmetic  46.2 us (6%)
  local copies, waits for them, and re-layouts  45.3 us (6%)
  waiting for transfers between devices  36.7 us (5%)
  between operations  16.2 us (2%)
  starting transfers between devices  8.39 us (1%)
    pallas_call x4, Pallas kernels, scatter_plane(): pl.pallas_call(partial(scatter_kernel, count), out_shape=shapes, in_specs...  160 us
    pallas_call x4, Pallas kernels, gather_plane(): pl.pallas_call(partial(gather_kernel, apply, len(inputs), len(outputs)),...  145 us
    pallas_call x3, Pallas kernels, exchange_plane(): pl.pallas_call(partial(exchange_kernel, moves, len(arrays), spread), out_...  63.3 us
    pallas_call x1, Pallas kernels, finish_all(): pl.pallas_call(partial(finish_kernel, len(bulk)), out_shape=[shaped(small...  51.5 us
    pallas_call x1, Pallas kernels, ssd_backward(): pl.pallas_call(ssd_backward_kernel, grid=(laps,), in_specs=specs + [tall(...  48.1 us
    dot_general x4, matrix products, dot_left_t(): lax.dot_general(left_side, right_side, (((0,), (0,)), ((), ())), preferre...  38.3 us
    pallas_call x3, Pallas kernels, attend(): pl.pallas_call(kernel, in_specs=vmem_specs(len(arrays)), out_specs=vmem_s...  26.2 us
    pallas_call x1, Pallas kernels, ssd_forward(): pl.pallas_call(ssd_forward_kernel, grid=(laps,), in_specs=specs, out_spec...  25.3 us
  transfers between devices with their start and end apart: 14, of which 5 were waited for; matrix products, arithmetic and copies ran while one was open for 16% of the time, Pallas kernels for 55%

profile of v2, /device:TPU:0, one launch (start us, length us, event | category | flops | bytes accessed | tf_op | source)
XLA Modules:
  0.0 730.1 jit_solution(16724951565815158213)
XLA Ops:
  12.8 20.7 %shard_map.399 = (bf16[4,128,1024]{2,1,0:T(8,128)(2,1)}, f32[16,8,128]{2,1,0:T(8,128)}) custom-call(bf16[128,1536]{1,0:T(8,128)(2,1)} %refs_0_.1, bf16[128,512]{1,0:T(8,128)(2,1)} %refs_1_.1, bf16[128,1536]{1,0:T(8,128)(2,1)} %refs_2_.2, bf16[4,128,128]{2,1,0:T(8,128)(2,1)} %pad_maximum_fusion.4.refs_3_, f32[8,128]{1,0:T(8,128)} %maximum_convert_fusion.refs_4_), custom_call_target="tpu_custom_call" | custom-call | flops 22499999744 | bytes 75000000 | tf_op jit(solution)/shard_map/pallas_call | solution.py:1221
  34.6 34.1 %shard_map.400 = bf16[8,192,2048]{2,1,0:T(8,128)(2,1)} custom-call(bf16[192,2048]{1,0:T(8,128)(2,1)} %dynamic-slice_bitcast_fusion.own_ref), custom_call_target="tpu_custom_call" | custom-call | flops 31499999232 | bytes 105000000 | tf_op jit(solution)/shard_map/pallas_call | solution.py:775
  71.5 27.0 %shard_map.401 = (bf16[4,128,512]{2,1,0:T(8,128)(2,1)}, bf16[4,128,1024]{2,1,0:T(8,128)(2,1)}, bf16[4,128,512]{2,1,0:T(8,128)(2,1)}) custom-call(bf16[128,1536]{1,0:T(8,128)(2,1)} %bitcast.113, bf16[128,512]{1,0:T(8,128)(2,1)} %bitcast.122, bf16[128,2048]{1,0:T(8,128)(2,1)} %refs_2_.3, bf16[128,2048]{1,0:T(8,128)(2,1)} %refs_3_.1, bf16[128,2048]{1,0:T(8,128)(2,1)} %bitcast.112), custom_call_target="tpu_custom_call" | custom-call | flops 22499999744 | bytes 75000000 | tf_op jit(solution)/shard_map/pallas_call | solution.py:1221
  100.6 4.1 fusion
  110.1 4.4 fusion.2.refs_0_
  114.6 4.5 convolution_convert_fusion.4.bc_ref.bc_before_ref
  128.8 11.7 %fusion.23.proj_ref.before_ref = f32[1536,1024]{1,0:T(8,128)} fusion(bf16[1536,2048]{1,0:T(8,128)(2,1)} %copy-done.6, bf16[2048,1024]{1,0:T(8,128)(2,1)} %bitcast.108), kind=kOutput, calls=%fused_computation.112 | convolution fusion | flops 6442450944 | bytes 16777216 | tf_op jit(solution)/shard_map/dot_general | solution.py:46
  140.5 25.3 %shard_map.402 = (bf16[1536,384]{1,0:T(8,128)(2,1)}, f32[1536,384]{1,0:T(8,128)}, f32[12,256,384]{2,1,0:T(8,128)}, bf16[1536,896]{1,0:T(8,128)(2,1)}) custom-call(f32[1536,1024]{1,0:T(8,128)} %fusion.23.proj_ref.before_ref, f32[1536,1024]{1,0:T(8,128)} %fusion.23.proj_ref.before_ref, bf16[1536,512]{1,0:T(8,128)(2,1)} %convolution_convert_fusion.4.bc_ref.bc_before_ref, ...), custom_call_target="tpu_custom_call" | custom-call | flops 5400000000 | bytes 18000000 | tf_op jit(solution)/shard_map/pallas_call | solution.py:1628
  178.2 5.1 pad_maximum_fusion.right_ref
  185.6 8.4 %shard_map.403 = (bf16[1536,128]{1,0:T(8,128)(2,1)}, f32[1536,1]{1,0:T(8,128)}, bf16[1536,128]{1,0:T(8,128)(2,1)}, bf16[1536,128]{1,0:T(8,128)(2,1)}, bf16[1536,128]{1,0:T(8,128)(2,1)}) custom-call(f32[1536,128]{1,0:T(8,128)} %slice.208.raw_ref, f32[1536,128]{1,0:T(8,128)} %get-tuple-element.310.cos_ref, f32[1536,128]{1,0:T(8,128)} %get-tuple-element.311.sin_ref, ...), custom_call_target="tpu_custom_call" | custom-call | flops 8099999744 | bytes 27000000 | tf_op jit(solution)/shard_map/pallas_call | solution.py:1815
  196.3 35.4 %shard_map.404 = f32[192,2048]{1,0:T(8,128)} custom-call(bf16[1536,512]{1,0:T(8,128)(2,1)} %copy-done.14, bf16[2048,512]{1,0:T(8,128)(2,1)} %bitcast.136), custom_call_target="tpu_custom_call" | custom-call | flops 31499999232 | bytes 105000000 | tf_op jit(solution)/shard_map/pallas_call | solution.py:961
  234.7 18.4 %all-gather.9.cloned.1.call-done = bf16[16,128,1024]{2,1,0:T(8,128)(2,1)} async-done(((bf16[4,128,1024]{2,1,0:T(8,128)(2,1)}), bf16[16,128,1024]{2,1,0:T(8,128)(2,1)}) %all-gather.9.cloned.1.call-update) | async-done | bytes 4194320 | tf_op jit(solution)/shard_map/all_gather | solution.py:2034
  254.6 38.3 %shard_map.405 = (bf16[8,192,2048]{2,1,0:T(8,128)(2,1)}, f32[1536,1024]{1,0:T(8,128)}, bf16[1536,512]{1,0:T(8,128)(2,1)}) custom-call(bf16[192,2048]{1,0:T(8,128)(2,1)} %multiply_convert_fusion.own_ref, bf16[2048,1024]{1,0:T(8,128)(2,1)} %bitcast.134), custom_call_target="tpu_custom_call" | custom-call | flops 31499999232 | bytes 105000000 | tf_op jit(solution)/shard_map/pallas_call | solution.py:775
  293.0 6.0 all-gather.11.cloned.1.call-done
  299.0 36.0 %shard_map.406 = f32[192,2048]{1,0:T(8,128)} custom-call(bf16[1536,512]{1,0:T(8,128)(2,1)} %get-tuple-element.135.left_ref, bf16[2048,512]{1,0:T(8,128)(2,1)} %bitcast.138), custom_call_target="tpu_custom_call" | custom-call | flops 31499999232 | bytes 105000000 | tf_op jit(solution)/shard_map/pallas_call | solution.py:961
  337.5 37.5 %shard_map.407 = (bf16[8,192,2048]{2,1,0:T(8,128)(2,1)}, bf16[1536,1024]{1,0:T(8,128)(2,1)}) custom-call(bf16[192,2048]{1,0:T(8,128)(2,1)} %fusion.11.own_ref, bf16[2048,512]{1,0:T(8,128)(2,1)} %bitcast.139, f32[1536,1024]{1,0:T(8,128)} %get-tuple-element.138.refs_1_), custom_call_target="tpu_custom_call" | custom-call | flops 31499999232 | bytes 105000000 | tf_op jit(solution)/shard_map/pallas_call | solution.py:775
  375.0 7.7 %convolution_convert_fusion.3 = bf16[2048,512]{1,0:T(8,128)(2,1)} fusion(bf16[1536,2048]{1,0:T(8,128)(2,1)} %bitcast.146, bf16[1536,512]{1,0:T(8,128)(2,1)S(1)} %copy-done.41), kind=kOutput, calls=%fused_computation.15 | convolution fusion | flops 3222274048 | bytes 9961472 | tf_op jit(solution)/shard_map/dot_general | solution.py:50
  382.8 11.4 %convolution_convert_fusion.1 = bf16[2048,1024]{1,0:T(8,128)(2,1)} fusion(bf16[1536,2048]{1,0:T(8,128)(2,1)} %bitcast.145, bf16[1536,1024]{1,0:T(8,128)(2,1)} %get-tuple-element.139.left_ref), kind=kOutput, calls=%fused_computation.7 | convolution fusion | flops 6444548096 | bytes 13631488 | tf_op jit(solution)/shard_map/dot_general | solution.py:50
  394.2 37.1 %shard_map.408 = f32[192,2048]{1,0:T(8,128)} custom-call(bf16[1536,1024]{1,0:T(8,128)(2,1)} %get-tuple-element.139.left_ref, bf16[2048,1024]{1,0:T(8,128)(2,1)} %bitcast.135), custom_call_target="tpu_custom_call" | custom-call | flops 31499999232 | bytes 105000000 | tf_op jit(solution)/shard_map/pallas_call | solution.py:961
  433.5 3.9 fusion.16
  437.4 35.3 %shard_map.409 = (bf16[8,192,2048]{2,1,0:T(8,128)(2,1)}, f32[1536,512]{1,0:T(8,128)}) custom-call(bf16[192,2048]{1,0:T(8,128)(2,1)} %get-tuple-element.141.own_ref, bf16[2048,512]{1,0:T(8,128)(2,1)} %bitcast.137), custom_call_target="tpu_custom_call" | custom-call | flops 31499999232 | bytes 105000000 | tf_op jit(solution)/shard_map/pallas_call | solution.py:775
  474.8 9.5 %shard_map.410 = (bf16[1536,128]{1,0:T(8,128)(2,1)}, bf16[4,768,128]{2,1,0:T(8,128)(2,1)}) custom-call(bf16[1536,128]{1,0:T(8,128)(2,1)} %get-tuple-element.146.q_ref, bf16[1536,128]{1,0:T(8,128)(2,1)} %get-tuple-element.147.k_ref, bf16[1536,128]{1,0:T(8,128)(2,1)} %get-tuple-element.148.v_ref, f32[1536,128]{1,0:T(8,128)} %get-tuple-element.310.cos_ref, ...), custom_call_target="tpu_custom_call" | custom-call | flops 8099999744 | bytes 27000000 | tf_op jit(solution)/shard_map/pallas_call | solution.py:1815
  489.8 7.6 %convolution_convert_fusion.2 = bf16[2048,512]{1,0:T(8,128)(2,1)} fusion(bf16[1536,2048]{1,0:T(8,128)(2,1)} %bitcast.144, bf16[1536,512]{1,0:T(8,128)(2,1)S(1)} %copy-done.15), kind=kOutput, calls=%fused_computation.14 | convolution fusion | flops 3222274048 | bytes 9961472 | tf_op jit(solution)/shard_map/dot_general | solution.py:50
  497.5 9.2 %reduce-scatter.7.cloned.1.call-done = bf16[512,1024]{1,0:T(8,128)(2,1)} async-done(((bf16[2048,1024]{1,0:T(8,128)(2,1)}), bf16[512,1024]{1,0:T(8,128)(2,1)}) %reduce-scatter.7.cloned.1.call-update) | async-done | bytes 1048592 | tf_op jit(solution)/shard_map/reduce_scatter | solution.py:2085
  506.7 48.1 %shard_map.411 = (bf16[1536,1536]{1,0:T(8,128)(2,1)}, f32[8,896]{1,0:T(8,128)}, f32[8,128]{1,0:T(8,128)}, f32[1,384]{1,0:T(1,128)}, f32[1,384]{1,0:T(1,128)}) custom-call(f32[1536,1024]{1,0:T(8,128)} %fusion.23.proj_ref.before_ref, f32[1536,1024]{1,0:T(8,128)} %fusion.23.proj_ref.before_ref, ...), custom_call_target="tpu_custom_call" | custom-call | flops 43200000000 | bytes 144000000 | tf_op jit(solution)/shard_map/pallas_call | solution.py:1650
  559.3 3.6 shard_map.412.left_ref
  562.8 11.6 %convolution_convert_fusion = bf16[2048,1024]{1,0:T(8,128)(2,1)} fusion(bf16[1536,2048]{1,0:T(8,128)(2,1)} %copy-done.6, bf16[1536,1536]{1,0:T(8,128)(2,1)} %shard_map.412.left_ref), kind=kOutput, calls=%fused_computation.6 | convolution fusion | flops 6444548096 | bytes 13631488 | tf_op jit(solution)/shard_map/dot_general | solution.py:50
  574.4 51.2 %shard_map.413 = (f32[192,2048]{1,0:T(8,128)}, f32[128,1024]{1,0:T(8,128)}) custom-call(bf16[1536,1536]{1,0:T(8,128)(2,1)} %shard_map.412.left_ref, bf16[2048,1536]{1,0:T(8,128)(2,1)} %pad_maximum_fusion.right_ref, bf16[1536,2048]{1,0:T(8,128)(2,1)} %copy-done.6), custom_call_target="tpu_custom_call" | custom-call | flops 31499999232 | bytes 105000000 | tf_op jit(solution)/shard_map/pallas_call | solution.py:961
  628.2 3.0 fusion.8.refs_2_
  631.2 51.5 %shard_map.414 = (f32[8,5120]{1,0:T(8,128)}, bf16[8,4,32,1024]{3,2,1,0:T(8,128)(2,1)}, f32[2,192,2048]{2,1,0:T(8,128)}, bf16[2,192,2048]{2,1,0:T(8,128)(2,1)}, b...) custom-call(f32[8,5120]{1,0:T(8,128)} %pad.16.refs_0_, ...), custom_call_target="tpu_custom_call" | custom-call | flops 40499998720 | bytes 135000000 | tf_op jit(solution)/shard_map/pallas_call | solution.py:1075
  690.4 15.6 %shard_map.415.in_ref = bf16[4,128,1024]{2,1,0:T(8,128)(2,1)} custom-call(bf16[4,128,1024]{2,1,0:T(8,128)(2,1)} %bitcast.141), custom_call_target="tpu_custom_call" | custom-call | flops 22499999744 | bytes 75000000 | tf_op jit(solution)/shard_map/pallas_call | solution.py:1221
  706.1 8.3 %shard_map.416 = (f32[128,2048]{1,0:T(8,128)}, f32[128,2048]{1,0:T(8,128)}, f32[2048,128]{1,0:T(8,128)}, f32[1536,128]{1,0:T(8,128)}, f32[512,128]{1,0:T(8,128)}...) custom-call(bf16[4,128,1024]{2,1,0:T(8,128)(2,1)} %get-tuple-element, ...), custom_call_target="tpu_custom_call" | custom-call | flops 8099999744 | bytes 27000000 | tf_op jit(solution)/shard_map/pallas_call | solution.py:1815
  (243 shorter events, 82.5 us)
Async XLA Ops:
  7.2 26.4 %copy-start = (bf16[1,384,2048]{2,1,0:T(8,128)(2,1)S(1)}, bf16[1,384,2048]{2,1,0:T(8,128)(2,1)}, u32[]{:S(2)}) copy-start(bf16[1,384,2048]{2,1,0:T(8,128)(2,1)} %param.28) | copy-start | bytes 4718596
  7.2 121.3 %all-gather.5.cloned.1.call-start = ((), (), s32[]{:S(2)}) async-start(), calls=%async_computation.4 | async-start | bytes 5242880 | tf_op jit(solution)/shard_map/all_gather | solution.py:1941
  33.6 138.4 %all-gather.7.cloned.1.call-start = ((), (), s32[]{:S(2)}) async-start(), calls=%async_computation.5 | async-start | bytes 2621440 | tf_op jit(solution)/shard_map/all_gather | solution.py:1964
  34.6 34.1 %copy-start.18 = (bf16[1536,128]{1,0:T(8,128)(2,1)S(1)}, bf16[1536,128]{1,0:T(8,128)(2,1)}, u32[]{:S(2)}) copy-start(bf16[1536,128]{1,0:T(8,128)(2,1)} %param.43) | copy-start | bytes 1179652
  34.6 35.1 %copy-start.17 = (bf16[2048,128]{1,0:T(8,128)(2,1)S(1)}, bf16[2048,128]{1,0:T(8,128)(2,1)}, u32[]{:S(2)}) copy-start(bf16[2048,128]{1,0:T(8,128)(2,1)} %param.51) | copy-start | bytes 1572868
  105.6 147.9 %copy-start.24 = (f32[16,1,128]{2,1,0:T(1,128)}, f32[16,1,128]{2,1,0:T(1,128)S(1)}, u32[]{:S(2)}) copy-start(f32[16,1,128]{2,1,0:T(1,128)S(1)} %get-tuple-element.278) | copy-start | bytes 24580
  114.6 8.0 %copy-start.30 = (s32[4,1536]{1,0:T(4,128)S(1)}, s32[4,1536]{1,0:T(4,128)}, u32[]{:S(2)}) copy-start(s32[4,1536]{1,0:T(4,128)} %param.31) | copy-start | bytes 73732
  114.6 9.3 %copy-start.40 = (s32[2]{0:T(128)S(1)}, s32[2]{0:T(128)}, u32[]{:S(2)}) copy-start(s32[2]{0:T(128)} %constant.143.clone.1) | copy-start | bytes 28
  114.6 9.9 %copy-start.37 = (f32[48]{0:T(128)S(1)}, f32[48]{0:T(128)}, u32[]{:S(2)}) copy-start(f32[48]{0:T(128)} %param.39) | copy-start | bytes 580
  114.6 12.8 %copy-start.39 = (f32[48]{0:T(128)S(1)}, f32[48]{0:T(128)}, u32[]{:S(2)}) copy-start(f32[48]{0:T(128)} %param.40) | copy-start | bytes 580
  114.6 13.3 %copy-start.29 = (f32[3584,4]{0,1:T(4,128)S(1)}, f32[3584,4]{0,1:T(4,128)}, u32[]{:S(2)}) copy-start(f32[3584,4]{0,1:T(4,128)} %param.37) | copy-start | bytes 172036
  114.6 13.2 %slice-start = ((f32[3584,4]{0,1:T(4,128)}), f32[512,4]{0,1:T(4,128)S(1)}, s32[]{:S(2)}) async-start(f32[3584,4]{0,1:T(4,128)} %param.37), calls=%async_computation.12 | async-start | bytes 16384 | tf_op jit(solution)/shard_map/slice | solution.py:1987
  127.7 12.8 %copy-start.36 = (f32[8,128]{1,0:T(8,128)}, f32[8,128]{1,0:T(8,128)S(1)}, u32[]{:S(2)}) copy-start(f32[8,128]{1,0:T(8,128)S(1)} %scatter.9.heads_ref) | copy-start | bytes 12292
  128.5 124.5 %all-gather.9.cloned.1.call-start = ((), (), s32[]{:S(2)}) async-start(), calls=%async_computation.6 | async-start | bytes 5242880 | tf_op jit(solution)/shard_map/all_gather | solution.py:2034
  172.0 127.0 %all-gather.11.cloned.1.call-start = ((), (), s32[]{:S(2)}) async-start(), calls=%async_computation.7 | async-start | bytes 2621440 | tf_op jit(solution)/shard_map/all_gather | solution.py:2035
  172.0 6.1 copy-start.8
  172.5 10.9 %collective-permute-start = (bf16[768,128]{1,0:T(8,128)(2,1)S(1)}, bf16[768,128]{1,0:T(8,128)(2,1)S(1)}, u32[]{:S(2)}, u32[]{:S(2)}) collective-permute-start(bf16[768,128]{1,0:T(8,128)(2,1)S(1)} %get-tuple-element.263), channel_id=1, source_target_pairs={{0,2},{2,0},{4,6},{6,4},{1,3},{3,1},{5,7},{7,5},{8,10},{10,8},{12,... | collective-permute-start | bytes 589832 | tf_op jit(solution)/shard_map/ppermute | solution.py:1843
  174.1 10.6 %collective-permute-start.1 = (bf16[768,128]{1,0:T(8,128)(2,1)S(1)}, bf16[768,128]{1,0:T(8,128)(2,1)S(1)}, u32[]{:S(2)}, u32[]{:S(2)}) collective-permute-start(bf16[768,128]{1,0:T(8,128)(2,1)S(1)} %get-tuple-element.263), channel_id=1, source_target_pairs={{0,4},{2,6},{4,0},{6,2},{1,5},{3,7},{5,1},{7,3},{8,12},{10,14},{12... | collective-permute-start | bytes 589832 | tf_op jit(solution)/shard_map/ppermute | solution.py:1843
  175.6 9.2 %collective-permute-start.2 = (bf16[768,128]{1,0:T(8,128)(2,1)S(1)}, bf16[768,128]{1,0:T(8,128)(2,1)S(1)}, u32[]{:S(2)}, u32[]{:S(2)}) collective-permute-start(bf16[768,128]{1,0:T(8,128)(2,1)S(1)} %get-tuple-element.263), channel_id=1, source_target_pairs={{0,6},{2,4},{4,2},{6,0},{1,7},{3,5},{5,3},{7,1},{8,14},{10,12},{12... | collective-permute-start | bytes 589832 | tf_op jit(solution)/shard_map/ppermute | solution.py:1843
  196.3 35.4 %copy-start.2 = (bf16[192,2048]{1,0:T(8,128)(2,1)S(1)}, bf16[192,2048]{1,0:T(8,128)(2,1)}, u32[]{:S(2)}) copy-start(bf16[192,2048]{1,0:T(8,128)(2,1)} %dynamic-slice_bitcast_fusion.own_ref) | copy-start | bytes 2359300
  234.7 58.3 %copy-start.31 = (f32[192]{0:T(256)}, f32[192]{0:T(256)S(1)}, u32[]{:S(2)}) copy-start(f32[192]{0:T(256)S(1)} %get-tuple-element.301) | copy-start | bytes 2308
  253.1 178.2 %reduce-scatter.5.cloned.1.call-start = ((), (), s32[]{:S(2)}) async-start(), calls=%async_computation.8 | async-start | bytes 2621440 | tf_op jit(solution)/shard_map/reduce_scatter | solution.py:2085
  299.0 36.0 %copy-start.12 = (bf16[1,384,2048]{2,1,0:T(8,128)(2,1)S(1)}, bf16[1,384,2048]{2,1,0:T(8,128)(2,1)}, u32[]{:S(2)}) copy-start(bf16[1,384,2048]{2,1,0:T(8,128)(2,1)} %param.29) | copy-start | bytes 4718596
  337.5 37.5 %copy-start.41 = (bf16[1536,512]{1,0:T(8,128)(2,1)S(1)}, bf16[1536,512]{1,0:T(8,128)(2,1)}, u32[]{:S(2)}) copy-start(bf16[1536,512]{1,0:T(8,128)(2,1)} %get-tuple-element.135.left_ref) | copy-start | bytes 4718596
  382.7 123.9 %reduce-scatter.7.cloned.1.call-start = ((), (), s32[]{:S(2)}) async-start(), calls=%async_computation.9 | async-start | bytes 5242880 | tf_op jit(solution)/shard_map/reduce_scatter | solution.py:2085
  431.4 143.0 %reduce-scatter.9.cloned.1.call-start = ((), (), s32[]{:S(2)}) async-start(), calls=%async_computation.10 | async-start | bytes 2621440 | tf_op jit(solution)/shard_map/reduce_scatter | solution.py:2085
  486.3 68.4 %collective-permute-start.3 = (bf16[768,128]{1,0:T(8,128)(2,1)S(1)}, bf16[768,128]{1,0:T(8,128)(2,1)S(1)}, u32[]{:S(2)}, u32[]{:S(2)}) collective-permute-start(bf16[768,128]{1,0:T(8,128)(2,1)S(1)} %get-tuple-element.271), channel_id=1, source_target_pairs={{0,2},{2,0},{4,6},{6,4},{1,3},{3,1},{5,7},{7,5},{8,10},{10,8},{12,... | collective-permute-start | bytes 589832 | tf_op jit(solution)/shard_map/ppermute | solution.py:1854
  487.4 67.4 %collective-permute-start.4 = (bf16[768,128]{1,0:T(8,128)(2,1)S(1)}, bf16[768,128]{1,0:T(8,128)(2,1)S(1)}, u32[]{:S(2)}, u32[]{:S(2)}) collective-permute-start(bf16[768,128]{1,0:T(8,128)(2,1)S(1)} %get-tuple-element.270), channel_id=1, source_target_pairs={{0,4},{2,6},{4,0},{6,2},{1,5},{3,7},{5,1},{7,3},{8,12},{10,14},{12... | collective-permute-start | bytes 589832 | tf_op jit(solution)/shard_map/ppermute | solution.py:1854
  488.3 66.5 %collective-permute-start.5 = (bf16[768,128]{1,0:T(8,128)(2,1)S(1)}, bf16[768,128]{1,0:T(8,128)(2,1)S(1)}, u32[]{:S(2)}, u32[]{:S(2)}) collective-permute-start(bf16[768,128]{1,0:T(8,128)(2,1)S(1)} %get-tuple-element.269), channel_id=1, source_target_pairs={{0,6},{2,4},{4,2},{6,0},{1,7},{3,5},{5,3},{7,1},{8,14},{10,12},{12... | collective-permute-start | bytes 589832 | tf_op jit(solution)/shard_map/ppermute | solution.py:1854
  506.6 183.8 %reduce-scatter.11.cloned.1.call-start = ((), (), s32[]{:S(2)}) async-start(), calls=%async_computation.11 | async-start | bytes 5242880 | tf_op jit(solution)/shard_map/reduce_scatter | solution.py:2085
  574.4 51.2 %copy-start.3 = (bf16[192,2048]{1,0:T(8,128)(2,1)S(1)}, bf16[192,2048]{1,0:T(8,128)(2,1)}, u32[]{:S(2)}) copy-start(bf16[192,2048]{1,0:T(8,128)(2,1)} %dynamic-slice_bitcast_fusion.own_ref) | copy-start | bytes 2359300
  574.4 51.2 %copy-start.23 = (f32[16,1,128]{2,1,0:T(1,128)S(1)}, f32[16,1,128]{2,1,0:T(1,128)}, u32[]{:S(2)}) copy-start(f32[16,1,128]{2,1,0:T(1,128)} %copy-done.22) | copy-start | bytes 24580
  (26 other events, 79.7 us)
Sparse Core Ops, SparseCore 0:
  33.7 78.9 all-gather.4
  128.7 43.2 all-gather.6
  173.5 79.4 all-gather.8
  254.5 44.4 all-gather.10
  382.9 42.7 reduce-scatter.4
  431.6 75.0 reduce-scatter.6
  508.9 44.3 reduce-scatter.8
  574.5 85.5 reduce-scatter.10

commit v3 on v2

--- a/solution.py
+++ b/solution.py
@@ -2,6 +2,7 @@
 
 import jax
 import jax.numpy as jnp
+import numpy as np
 from jax import lax
 from jax.experimental import pallas as pl
 from jax.experimental.pallas import tpu as pltpu
@@ -614,7 +615,7 @@
 
 
 GROUP = 4
-CHUNK = 128
+CHUNK = 256
 HEADS = 6
 MESH_ID = pl.DeviceIdType.MESH
 VMEM_BYTES = 56 * 1024 * 1024
@@ -632,25 +633,6 @@
 def halves(values):
     high = values.astype(jnp.bfloat16)
     return (high, (values - high.astype(jnp.float32)).astype(jnp.bfloat16))
-
-
-def dot_split(exact, parts, left_dim, right_dim):
-    high, low = parts
-    return dot_f32(exact, high, left_dim, right_dim) + dot_f32(exact, low, left_dim, right_dim)
-
-
-def dot_split_left(parts, exact, left_dim, right_dim):
-    high, low = parts
-    return dot_f32(high, exact, left_dim, right_dim) + dot_f32(low, exact, left_dim, right_dim)
-
-
-def dot_splits(left_parts, right_parts, left_dim, right_dim):
-    left_high, left_low = left_parts
-    right_high, right_low = right_parts
-    return dot_f32(left_high, right_high, left_dim, right_dim) + (
-        dot_f32(left_high, right_low, left_dim, right_dim)
-        + dot_f32(left_low, right_high, left_dim, right_dim)
-    )
 
 
 def plane_place():
@@ -810,7 +792,21 @@
 
 
 def apply_out_back(block, rows, inputs, outputs):
-    outputs[0][rows] = jnp.dot(block, inputs[0][...], preferred_element_type=jnp.float32)
+    both = jnp.dot(block, inputs[0][...], preferred_element_type=jnp.float32)
+    width = outputs[0].shape[1]
+    outputs[0][rows] = both[:, :width]
+    outputs[1][rows] = both[:, width:].astype(jnp.bfloat16)
+
+
+def apply_norm(block, rows, inputs, outputs):
+    gain_ref, weights = inputs
+    values = block.astype(jnp.float32)
+    scale = lax.rsqrt(jnp.mean(values * values, axis=-1, keepdims=True) + EPSILON)
+    normed = (values * scale * gain_ref[...]).astype(jnp.bfloat16)
+    outputs[0][rows] = normed
+    outputs[1][rows] = jnp.dot(normed, weights[...], preferred_element_type=jnp.float32).astype(
+        jnp.bfloat16
+    )
 
 
 def scatter_kernel(count, left_ref, right_ref, *refs):
@@ -818,8 +814,9 @@
     partner = (data, place, 1 - core)
     to_x, to_y = (data, along_x, core), (data, along_y, core)
     order = (across, along_x, along_y, place)
-    extra, sums = refs[: count - 1], refs[count - 1 : 2 * count - 1]
-    parts, scratch = refs[2 * count - 1 : 3 * count - 1], refs[3 * count - 1 :]
+    count_in = 0 if count == 1 else count
+    extra, sums = refs[:count_in], refs[count_in : count_in + count]
+    parts, scratch = refs[count_in + count : count_in + 2 * count], refs[count_in + 2 * count :]
     step = 16
     meet((partner, to_x, to_y))
 
@@ -829,7 +826,10 @@
         height, columns = part.shape[1:]
         if at == 0:
             rows = pl.ds(pl.multiple_of(index * height, 16), height)
-            block = dot_f32(left_ref[rows], right_ref[...], 1, 1)
+            depth = right_ref.shape[1]
+            block = dot_f32(left_ref[rows, :depth], right_ref[...], 1, 1)
+            if count > 1:
+                block = block + dot_f32(left_ref[rows, depth:], extra[-1][...], 1, 1)
         else:
             start = left_ref.shape[1] - GROUP * height
             turned = pl.ds(pl.multiple_of(start + chip * height, 128), height)
@@ -937,7 +937,7 @@
             pass
 
 
-def scatter_plane(left, right, identity, extra=()):
+def scatter_plane(left, right, identity, extra=(), beside=()):
     height, width = left.shape[0] // (2 * GROUP), right.shape[0]
     sizes = [(height, width)] + [size for _, *size in extra]
     shapes = []
@@ -961,96 +961,159 @@
     return pl.pallas_call(
         partial(scatter_kernel, count),
         out_shape=shapes,
-        in_specs=vmem_specs(1 + count),
+        in_specs=vmem_specs(2 if count == 1 else 2 + count),
         out_specs=vmem_specs(count),
         scratch_shapes=scratch,
         cost_estimate=lasting(35),
         compiler_params=pltpu.CompilerParams(
             collective_id=identity, has_side_effects=True, vmem_limit_bytes=VMEM_BYTES
         ),
-    )(left, right, *[array for array, *_ in extra])
-
-
-def finish_kernel(count_bulk, *refs):
-    small_ref, bc_ref, own_ref, out_ref = refs[:4]
-    bulk = refs[4 : 4 + count_bulk]
-    small_sum, bc_all, both_ref, both_out = refs[4 + count_bulk : 8 + count_bulk]
-    bulk_back = refs[8 + count_bulk : 8 + 2 * count_bulk]
-    small_in, bc_send, bc_in, line_in, bc_line, own_sems, send_s, recv_s = refs[8 + 2 * count_bulk :]
+    )(left, right, *[array for array, *_ in extra], *beside)
+
+
+def plane_sum_kernel(
+    small_ref, own_ref, out_ref, bulk, sum_ref, both_ref, both_out, back, small_in, own_sem, send_s, recv_s
+):
+    data, place, core, along_x, along_y, across = plane_place()
+    mine = 2 * place + core
+    partner = (data, place, 1 - core)
+    plane = []
+    for turn_by in range(1, 2 * GROUP):
+        other = lax.rem(mine + turn_by, 2 * GROUP)
+        plane.append((other, (data, other // 2, lax.rem(other, 2))))
+    meet([device for _, device in plane])
+    started = []
+
+    def push(source, target, device):
+        slot = len(started)
+        copy = remote(source, target, send_s.at[slot], recv_s.at[slot], device)
+        copy.start()
+        started.append(copy)
+
+    piece = small_in.shape[2]
+
+    def piece_of(index):
+        return small_ref.at[:, pl.ds(pl.multiple_of(index * piece, 128), piece)]
+
+    for other, device in plane:
+        push(piece_of(other), small_in.at[mine], device)
+    for source, target in ((own_ref, both_ref), (out_ref, both_out)):
+        push(source, target.at[core], partner)
+    for chip in (across, along_x, along_y):
+        push(bulk.at[chip], back.at[place], (data, chip, core))
+    own = pltpu.make_async_copy(bulk.at[place], back.at[place], own_sem)
+    own.start()
+    small_in[mine] = piece_of(mine)[...]
+    both_ref[core] = own_ref[...]
+    both_out[core] = out_ref[...]
+    for copy in started:
+        copy.wait()
+    own.wait()
+    total = small_in[0]
+    for index in range(1, 2 * GROUP):
+        total = total + small_in[index]
+    sum_ref[...] = total
+
+
+def plane_sum(small, own_rows, out_rows, bulk):
+    places = 2 * GROUP
+    pushes = places - 1 + 2 + 3
+    shaped = jax.ShapeDtypeStruct
+    piece = small.shape[1] // places
+    return pl.pallas_call(
+        plane_sum_kernel,
+        out_shape=[
+            shaped((8, piece), jnp.float32),
+            shaped((2,) + own_rows.shape, own_rows.dtype),
+            shaped((2,) + out_rows.shape, out_rows.dtype),
+            shaped(bulk.shape, bulk.dtype),
+        ],
+        in_specs=vmem_specs(3) + any_specs(1),
+        out_specs=vmem_specs(3) + any_specs(1),
+        scratch_shapes=[
+            pltpu.VMEM((places, 8, piece), jnp.float32),
+            pltpu.SemaphoreType.DMA,
+            pltpu.SemaphoreType.DMA((pushes,)),
+            pltpu.SemaphoreType.DMA((pushes,)),
+        ],
+        cost_estimate=lasting(20),
+        compiler_params=pltpu.CompilerParams(
+            collective_id=7, has_side_effects=True, vmem_limit_bytes=VMEM_BYTES
+        ),
+    )(small, own_rows, out_rows, bulk)
+
+
+def finish_kernel(
+    piece_ref,
+    bc_ref,
+    bulk,
+    small_all,
+    bc_all,
+    back,
+    bc_send,
+    bc_in,
+    bc_line,
+    line_in,
+    own_sem,
+    send_s,
+    recv_s,
+):
     data, place, core, along_x, along_y, across = plane_place()
     count = lax.axis_size("dp")
     mine = 2 * place + core
     partner = (data, place, 1 - core)
     others = (across, along_x, along_y)
+    chips = [(data, chip, core) for chip in others]
     plane = []
     for turn_by in range(1, 2 * GROUP):
         other = lax.rem(mine + turn_by, 2 * GROUP)
-        plane.append((other, (data, other // 2, lax.rem(other, 2))))
+        plane.append((data, other // 2, lax.rem(other, 2)))
     line = []
     for turn_by in range(1, count):
         other = lax.rem(data + turn_by, count)
         line.append((other, (other, place, core)))
-    meet([device for _, device in plane + line])
-
-    sent = 0
+    meet(plane + [device for _, device in line])
     started = []
 
     def push(source, target, device):
-        nonlocal sent
-        copy = remote(source, target, send_s.at[sent], recv_s.at[sent], device)
+        slot = len(started)
+        copy = remote(source, target, send_s.at[slot], recv_s.at[slot], device)
         copy.start()
-        sent += 1
         started.append(copy)
         return copy
 
-    piece = small_in.shape[2]
     rows = bc_in.shape[1]
 
-    def piece_of(ref, index):
-        return ref.at[:, pl.ds(pl.multiple_of(index * piece, 128), piece)]
-
-    def rows_of(ref, index):
-        return ref.at[pl.ds(pl.multiple_of(index * rows, 16), rows)]
+    def rows_of(index):
+        return bc_send.at[pl.ds(pl.multiple_of(index * rows, 16), rows)]
 
     bc_send[...] = bc_ref[...].astype(jnp.bfloat16)
-    first = [push(rows_of(bc_send, other), bc_in.at[data], device) for other, device in line]
-    first += [push(piece_of(small_ref, other), small_in.at[mine], device) for other, device in plane]
+    first = [push(rows_of(other), bc_in.at[data], device) for other, device in line]
+    small = [push(piece_ref, line_in.at[data], device) for _, device in line]
     late = []
-    for source, target in ((own_ref, both_ref), (out_ref, both_out)):
-        late.append(push(source, target.at[core], partner))
-    own = []
-    for index, (source, target) in enumerate(zip(bulk, bulk_back)):
-        for chip in others:
-            late.append(push(source.at[chip], target.at[place], (data, chip, core)))
-        copy = pltpu.make_async_copy(source.at[place], target.at[place], own_sems.at[index])
-        copy.start()
-        own.append(copy)
-    small_in[mine] = piece_of(small_ref, mine)[...]
-    bc_in[data] = rows_of(bc_send, data)[...]
-    both_ref[core] = own_ref[...]
-    both_out[core] = out_ref[...]
+    for chip, device in zip(others, chips):
+        late.append(push(bulk.at[chip], back.at[place], device))
+    own = pltpu.make_async_copy(bulk.at[place], back.at[place], own_sem)
+    own.start()
+    bc_in[data] = rows_of(data)[...]
+    line_in[data] = piece_ref[...]
     for copy in first:
         copy.wait_recv()
-    total = small_in[0]
-    for index in range(1, 2 * GROUP):
-        total = total + small_in[index]
-    line_in[data] = total
     total = bc_in[0].astype(jnp.float32)
     for index in range(1, count):
         total = total + bc_in[index].astype(jnp.float32)
     bc_line[data] = total.astype(jnp.bfloat16)
     second = [push(bc_line.at[data], bc_line.at[data], device) for _, device in line]
-    second += [push(line_in.at[data], line_in.at[data], device) for _, device in line]
-    for copy in second:
+    for copy in small:
         copy.wait_recv()
     total = line_in[0]
     for index in range(1, count):
         total = total + line_in[index]
-    piece_of(small_sum, mine)[...] = total
-    third = [push(bc_line, bc_all.at[mine], (data, chip, core)) for chip in others]
-    late += [
-        push(piece_of(small_sum, mine), piece_of(small_sum, mine), device) for _, device in plane
-    ]
+    small_all[mine] = total
+    late += [push(small_all.at[mine], small_all.at[mine], device) for device in plane]
+    for copy in second:
+        copy.wait_recv()
+    third = [push(bc_line, bc_all.at[mine], device) for device in chips]
     late.append(push(bc_line, bc_all.at[mine], partner))
     bc_all[mine] = bc_line[...]
     for copy, chip in zip(third, others):
@@ -1061,43 +1124,38 @@
         copy.wait_recv()
     for copy in started:
         copy.wait_send()
-    for copy in own:
-        copy.wait()
-
-
-def finish_all(small, bc_sum, own_rows, out_rows, bulk):
+    own.wait()
+
+
+def finish_all(piece, bc_sum, bulk):
     count = lax.axis_size("dp")
     places = 2 * GROUP
-    pushes = (count - 1) * 4 + (places - 1) * 2 + 2 * GROUP + 1 + 3 * len(bulk)
+    pushes = 3 * (count - 1) + (places - 1) + 2 * (GROUP - 1) + GROUP
     shaped = jax.ShapeDtypeStruct
-    piece, line_rows = small.shape[1] // places, bc_sum.shape[0] // count
-    width = bc_sum.shape[1]
+    blocks = (count, bc_sum.shape[0] // count, bc_sum.shape[1])
     return pl.pallas_call(
-        partial(finish_kernel, len(bulk)),
+        finish_kernel,
         out_shape=[
-            shaped(small.shape, jnp.float32),
-            shaped((places, count, line_rows, width), jnp.bfloat16),
-            shaped((2,) + own_rows.shape, own_rows.dtype),
-            shaped((2,) + out_rows.shape, out_rows.dtype),
-        ]
-        + [shaped(array.shape, array.dtype) for array in bulk],
-        in_specs=vmem_specs(4) + any_specs(len(bulk)),
-        out_specs=vmem_specs(4) + any_specs(len(bulk)),
+            shaped((places,) + piece.shape, jnp.float32),
+            shaped((places,) + blocks, jnp.bfloat16),
+            shaped(bulk.shape, bulk.dtype),
+        ],
+        in_specs=vmem_specs(2) + any_specs(1),
+        out_specs=vmem_specs(2) + any_specs(1),
         scratch_shapes=[
-            pltpu.VMEM((places, 8, piece), jnp.float32),
             pltpu.VMEM(bc_sum.shape, jnp.bfloat16),
-            pltpu.VMEM((count, line_rows, width), jnp.bfloat16),
-            pltpu.VMEM((count, 8, piece), jnp.float32),
-            pltpu.VMEM((count, line_rows, width), jnp.bfloat16),
-            pltpu.SemaphoreType.DMA((len(bulk),)),
+            pltpu.VMEM(blocks, jnp.bfloat16),
+            pltpu.VMEM(blocks, jnp.bfloat16),
+            pltpu.VMEM((count,) + piece.shape, jnp.float32),
+            pltpu.SemaphoreType.DMA,
             pltpu.SemaphoreType.DMA((pushes,)),
             pltpu.SemaphoreType.DMA((pushes,)),
         ],
-        cost_estimate=lasting(45),
+        cost_estimate=lasting(30),
         compiler_params=pltpu.CompilerParams(
-            collective_id=7, has_side_effects=True, vmem_limit_bytes=VMEM_BYTES
+            collective_id=6, has_side_effects=True, vmem_limit_bytes=VMEM_BYTES
         ),
-    )(small, bc_sum, own_rows, out_rows, *bulk)
+    )(piece, bc_sum, bulk)
 
 
 def unpack_kernel(
@@ -1106,7 +1164,8 @@
     out_ref,
     in_ref,
     bc_ref,
-    taps_ref,
+    misc_ref,
+    pieces_ref,
     gate_ref,
     up_ref,
     d_ref,
@@ -1115,116 +1174,238 @@
     z_ref,
     x_ref,
     q_ref,
+    grad_bc_ref,
     k_ref,
     v_ref,
     dt_ref,
-    grad_bc_ref,
-    grad_conv_ref,
+    conv_ref,
+    bias_ref,
+    dtb_ref,
+    alog_ref,
+    skip_ref,
+    group_ref,
+    one_ref,
+    two_ref,
+    sums_ref,
 ):
     units, width, part = down_ref.shape[2], HEADS * HP, HD // 4
-    grad_conv_ref[...] = taps_ref[...].T[:, :KC]
-    for chip in range(GROUP):
-        columns = slice(units * chip, units * (chip + 1))
-        gate_ref[:, columns] = gu_ref[chip, :, :units].astype(jnp.float32)
-        up_ref[:, columns] = gu_ref[chip, :, units:].astype(jnp.float32)
-        d_ref[columns] = down_ref[chip].astype(jnp.float32).T
-        turned = out_ref[chip].astype(jnp.float32).T
-        mo_ref[width * chip : width * (chip + 1)] = turned[:width]
-        ao_ref[HD * chip : HD * (chip + 1)] = turned[width:]
-        high, wide = bc_ref.shape[1:]
-        for core in range(2):
-            grad_bc_ref[wide * core : wide * (core + 1), high * chip : high * (chip + 1)] = (
-                bc_ref[2 * chip + core].astype(jnp.float32).T
-            )
-    for chip in range(GROUP):
-        columns = slice(width * chip, width * (chip + 1))
-        z_ref[:, columns] = in_ref[chip, :, :width].astype(jnp.float32)
-        x_ref[:, columns] = in_ref[chip, :, width + HD : 2 * width + HD].astype(jnp.float32)
-        q_ref[:, HD * chip : HD * (chip + 1)] = in_ref[chip, :, width : width + HD].astype(
-            jnp.float32
+    gate_ref[...] = gu_ref[0, :, :units].astype(jnp.float32)
+    up_ref[...] = gu_ref[0, :, units:].astype(jnp.float32)
+    d_ref[...] = down_ref[0].astype(jnp.float32).T
+    turned = out_ref[0].astype(jnp.float32).T
+    mo_ref[...] = turned[:width]
+    ao_ref[...] = turned[width:]
+    z_ref[...] = in_ref[0, :, :width].astype(jnp.float32)
+    q_ref[...] = in_ref[0, :, width : width + HD].astype(jnp.float32)
+    x_ref[...] = in_ref[0, :, width + HD : 2 * width + HD].astype(jnp.float32)
+    wide = bc_ref.shape[2]
+    for core in range(2):
+        grad_bc_ref[wide * core : wide * (core + 1)] = bc_ref[core].astype(jnp.float32).T
+
+    @pl.when(pl.program_id(0) == 0)
+    def _():
+        for index in range(2 * GROUP):
+            piece = pieces_ref.shape[2]
+            sums_ref[:, piece * index : piece * (index + 1)] = pieces_ref[index]
+        held = [misc_ref[chip].astype(jnp.float32) for chip in range(GROUP)]
+        k_ref[...] = jnp.concatenate(
+            [
+                held[0][:, :part],
+                held[1][:, :part],
+                held[0][:, part : 2 * part],
+                held[1][:, part : 2 * part],
+            ],
+            axis=1,
         )
-    held = [in_ref[chip, :, 2 * width + HD :].astype(jnp.float32) for chip in range(GROUP)]
-    k_ref[...] = jnp.concatenate(
-        [
-            held[0][:, :part],
-            held[1][:, :part],
-            held[0][:, part : 2 * part],
-            held[1][:, part : 2 * part],
+        v_ref[...] = jnp.concatenate([held[2][:, : 2 * part], held[3][:, : 2 * part]], axis=1)
+        dt_ref[...] = jnp.concatenate(
+            [values[:, DT_LANE : DT_LANE + HEADS] for values in held], axis=1
+        ).T
+        taps = bias_ref.shape[1]
+        conv_ref[...] = sums_ref[:KC, :taps]
+        bias_ref[...] = sums_ref[KC : KC + 1, :taps]
+        dtb_ref[...] = sums_ref[0:1, taps : taps + MH]
+        alog_ref[...] = sums_ref[1:2, taps : taps + MH]
+        skip_ref[...] = sums_ref[2:3, taps : taps + MH]
+        start = taps + 128
+        mine = GROUP * lax.axis_index("dp") + lax.axis_index("seq")
+        slice_rows = one_ref.shape[1]
+        each = slice_rows * GROUP * lax.axis_size("dp") // 8
+        for ref in (one_ref, two_ref):
+            gains = sums_ref[:, start : start + each]
+            row = lax.broadcasted_iota(jnp.int32, (8, 1), 0)
+            total = jnp.zeros((1, slice_rows), jnp.float32)
+            for at in range(each // slice_rows):
+                block = gains[:, slice_rows * at : slice_rows * (at + 1)]
+                wanted = row * (each // slice_rows) + at == mine
+                total = total + jnp.sum(jnp.where(wanted, block, 0.0), axis=0, keepdims=True)
+            ref[...] = total
+            start += each
+        per_row = MH // 8
+        for head in range(MH):
+            row, lane = head // per_row, start + HP * (head % per_row)
+            group_ref[head : head + 1, :] = sums_ref[row : row + 1, lane : lane + HP]
+
+
+def unpack_all(back, bc_all, sums, shapes):
+    gu, down, out, in_all = back
+
+    def per_chip(array, rows=1):
+        return pl.BlockSpec((rows,) + array.shape[1:], lambda chip: (chip, 0, 0))
+
+    def across(shape):
+        return pl.BlockSpec((shape[0], shape[1] // GROUP), lambda chip: (0, chip))
+
+    def down_along(shape):
+        return pl.BlockSpec((shape[0] // GROUP, shape[1]), lambda chip: (chip, 0))
+
+    def once(shape):
+        return pl.BlockSpec(shape, lambda chip: (0,) * len(shape))
+
+    misc_block = (GROUP, in_all.shape[1], HD)
+    kinds = [across, across, down_along, down_along, down_along, across, across, across, across]
+    kinds += [once] * (len(shapes) - len(kinds))
+    return pl.pallas_call(
+        unpack_kernel,
+        grid=(GROUP,),
+        in_specs=[
+            per_chip(gu),
+            per_chip(down),
+            per_chip(out),
+            per_chip(in_all),
+            per_chip(bc_all, 2),
+            pl.BlockSpec(misc_block, lambda chip: (0, 0, in_all.shape[2] // HD - 1)),
+            once(sums.shape),
         ],
-        axis=1,
-    )
-    v_ref[...] = jnp.concatenate([held[2][:, : 2 * part], held[3][:, : 2 * part]], axis=1)
-    dt_ref[...] = jnp.concatenate(
-        [values[:, DT_LANE : DT_LANE + HEADS] for values in held], axis=1
-    )
-
-
-def exchange_kernel(moves, count_in, spread, *refs):
+        out_specs=[kind(shape) for kind, shape in zip(kinds, shapes)],
+        out_shape=[jax.ShapeDtypeStruct(shape, jnp.float32) for shape in shapes],
+        scratch_shapes=[pltpu.VMEM((8, 2 * GROUP * sums.shape[2]), jnp.float32)],
+        cost_estimate=lasting(8),
+        compiler_params=pltpu.CompilerParams(vmem_limit_bytes=VMEM_BYTES),
+    )(gu, down, out, in_all, bc_all, in_all, sums)
+
+
+def push_moves(moves, sources, targets, local_sems, send_sems, recv_sems, first=0):
     data, place, core, along_x, along_y, across = plane_place()
-    sources, targets = refs[:count_in], refs[count_in:-3]
-    local_sems, send_sems, recv_sems = refs[-3:]
-    count = lax.axis_size("dp")
-    others = (across, along_x, along_y)
-    devices = [(data, chip, core) for chip in others]
-    if spread:
-        mine = GROUP * data + place
-        all_places = GROUP * count
-        devices = []
-        for turn_by in range(1, all_places):
-            other = lax.rem(mine + turn_by, all_places)
-            devices.append((other // GROUP, lax.rem(other, GROUP), core))
-    meet(devices)
     copies = []
-    for index, chip in enumerate(others):
+    for index, chip in enumerate((across, along_x, along_y)):
         for at, move in enumerate(moves):
             source, target = move(sources, targets, place, chip)
-            slot = index * len(moves) + at
+            slot = first + index * len(moves) + at
             copy = remote(
                 source, target, send_sems.at[slot], recv_sems.at[slot], (data, chip, core)
             )
             copy.start()
             copies.append(copy)
-    own = []
-    if spread:
-        first = 3 * len(moves)
-        for index, device in enumerate(devices):
-            copy = remote(
-                sources[-1],
-                targets[-1].at[mine],
-                send_sems.at[first + index],
-                recv_sems.at[first + index],
-                device,
-            )
-            copy.start()
-            copies.append(copy)
-        copy = pltpu.make_async_copy(sources[-1], targets[-1].at[mine], local_sems.at[len(moves)])
-        copy.start()
-        own.append(copy)
     for at, move in enumerate(moves):
         source, target = move(sources, targets, place, place)
         copy = pltpu.make_async_copy(source, target, local_sems.at[at])
         copy.start()
-        own.append(copy)
-    for copy in own:
+        copies.append(copy)
+    return copies
+
+
+def plane_peers():
+    data, place, core, along_x, along_y, across = plane_place()
+    return [(data, chip, core) for chip in (across, along_x, along_y)]
+
+
+def exchange_kernel(moves, count_in, *refs):
+    sources, targets = refs[:count_in], refs[count_in:-3]
+    meet(plane_peers())
+    for copy in push_moves(moves, sources, targets, *refs[-3:]):
         copy.wait()
+
+
+def first_exchange_kernel(
+    moves,
+    z_ref,
+    q_ref,
+    x_ref,
+    key_ref,
+    value_ref,
+    dt_ref,
+    one_ref,
+    two_ref,
+    in_ref,
+    gains_ref,
+    misc,
+    gains,
+    local_sems,
+    send_sems,
+    recv_sems,
+):
+    data, place, core, along_x, along_y, across = plane_place()
+    places = GROUP * lax.axis_size("dp")
+    mine = GROUP * data + place
+    devices = []
+    for turn_by in range(1, places):
+        other = lax.rem(mine + turn_by, places)
+        devices.append((other // GROUP, lax.rem(other, GROUP), core))
+    meet(devices)
+    half, part = HD // 2, HD // 4
+    keys, values = key_ref[...], value_ref[...]
+    steps = dt_ref[...].astype(jnp.float32).T.astype(keys.dtype)
+    columns = (
+        (keys[:, :part], keys[:, half : half + part]),
+        (keys[:, part:half], keys[:, half + part :]),
+        (values[:, :half],),
+        (values[:, half:],),
+    )
+    for chip in range(GROUP):
+        heads = steps[:, HEADS * chip : HEADS * (chip + 1)]
+        rest = jnp.zeros((keys.shape[0], half - HEADS), keys.dtype)
+        misc[chip] = jnp.concatenate([*columns[chip], heads, rest], axis=1)
+    gains[...] = jnp.zeros_like(gains)
+    gains[0:1] = one_ref[...].astype(jnp.float32)
+    gains[1:2] = two_ref[...].astype(jnp.float32)
+    sources = (z_ref, q_ref, x_ref, misc)
+    copies = push_moves(moves, sources, (in_ref,), local_sems, send_sems, recv_sems)
+    for index, device in enumerate(devices):
+        slot = 3 * len(moves) + index
+        copy = remote(
+            gains, gains_ref.at[mine], send_sems.at[slot], recv_sems.at[slot], device
+        )
+        copy.start()
+        copies.append(copy)
+    gains_ref[mine] = gains[...]
     for copy in copies:
         copy.wait()
 
 
-def exchange_plane(moves, arrays, out_shapes, identity, spread=False):
-    shapes = [jax.ShapeDtypeStruct(shape, jnp.bfloat16) for shape in out_shapes]
+def first_exchange(moves, arrays, width_in):
+    places = GROUP * lax.axis_size("dp")
+    slice_rows = arrays[0].shape[0]
+    count = 3 * len(moves) + places - 1
+    return pl.pallas_call(
+        partial(first_exchange_kernel, moves),
+        out_shape=[
+            jax.ShapeDtypeStruct((GROUP, slice_rows, width_in), jnp.bfloat16),
+            jax.ShapeDtypeStruct((places, 8, slice_rows), jnp.float32),
+        ],
+        in_specs=any_specs(3) + vmem_specs(5),
+        out_specs=any_specs(1) + vmem_specs(1),
+        scratch_shapes=[
+            pltpu.VMEM((GROUP, slice_rows, HD), jnp.bfloat16),
+            pltpu.VMEM((8, slice_rows), jnp.float32),
+            pltpu.SemaphoreType.DMA((len(moves),)),
+            pltpu.SemaphoreType.DMA((count,)),
+            pltpu.SemaphoreType.DMA((count,)),
+        ],
+        cost_estimate=lasting(20),
+        compiler_params=pltpu.CompilerParams(collective_id=3, has_side_effects=True),
+    )(*arrays)
+
+
+def exchange_plane(moves, arrays, out_shapes, identity):
     count = 3 * len(moves)
-    if spread:
-        places = GROUP * lax.axis_size("dp")
-        shapes.append(jax.ShapeDtypeStruct((places,) + arrays[-1].shape, arrays[-1].dtype))
-        count += places - 1
     return pl.pallas_call(
-        partial(exchange_kernel, moves, len(arrays), spread),
-        out_shape=shapes,
+        partial(exchange_kernel, moves, len(arrays)),
+        out_shape=[jax.ShapeDtypeStruct(shape, jnp.bfloat16) for shape in out_shapes],
         in_specs=any_specs(len(arrays)),
-        out_specs=any_specs(len(shapes)),
+        out_specs=any_specs(len(out_shapes)),
         scratch_shapes=[
-            pltpu.SemaphoreType.DMA((len(moves) + 1,)),
+            pltpu.SemaphoreType.DMA((len(moves),)),
             pltpu.SemaphoreType.DMA((count,)),
             pltpu.SemaphoreType.DMA((count,)),
         ],
@@ -1274,15 +1455,40 @@
     return jnp.where(row == lane, values, 0.0)
 
 
-def at_row(row, values):
-    rows = lax.broadcasted_iota(jnp.int32, (values.shape[1], 1), 0)
-    return jnp.where(rows == row, values, 0.0)
-
-
-def pair_columns(values, pair):
-    low, high = lane_masks()
-    lane = DT_LANE + 2 * pair
-    return jnp.where(low, values[:, lane : lane + 1], values[:, lane + 1 : lane + 2])
+def dot_beside(exact, values, left_dim):
+    width = values.shape[1]
+    both = dot_f32(exact, jnp.concatenate(halves(values), axis=1), left_dim, 0)
+    return both[:, :width] + both[:, width:]
+
+
+def dot_along(left, right):
+    left_high, left_low = halves(left)
+    right_high, right_low = halves(right)
+    return dot_f32(
+        jnp.concatenate([left_high, left_high, left_low], axis=1),
+        jnp.concatenate([right_high, right_low, right_high], axis=1),
+        1,
+        1,
+    )
+
+
+def spread_heads(*columns):
+    width = HEADS * HP
+    row = lax.rem(lax.broadcasted_iota(jnp.int32, (4 * HP, width), 0), 2 * HP)
+    head = lax.broadcasted_iota(jnp.int32, (4 * HP, width), 1) // HP
+    pick = jnp.where(row == DT_LANE + head, 1.0, 0.0).astype(jnp.bfloat16)
+    parts = [jnp.concatenate(halves(values), axis=1) for values in columns]
+    wide = dot_f32(jnp.concatenate(parts, axis=0), pick, 1, 0)
+    size = columns[0].shape[0]
+    return [wide[size * at : size * (at + 1)] for at in range(len(columns))]
+
+
+def wide_keeps(keeps_ref):
+    size = keeps_ref.shape[0]
+    return [None] + [
+        jnp.broadcast_to(keeps_ref[:, 1 + back : 2 + back], (size, 2 * HP))
+        for back in range(1, KC)
+    ]
 
 
 def head_sums(values):
@@ -1346,11 +1552,11 @@
     return [now] + [extended[8 - back : 8 - back + size] for back in range(1, KC)]
 
 
-def conv_sum(windows, taps_ref, lanes, keeps_ref):
+def conv_sum(windows, taps_ref, lanes, keeps):
     total = taps_ref[KC : KC + 1, lanes] + taps_ref[KC - 1 : KC, lanes] * windows[0]
     for back in range(1, KC):
         total = total + taps_ref[KC - 1 - back : KC - back, lanes] * (
-            windows[back] * keeps_ref[:, 1 + back : 2 + back]
+            windows[back] * keeps[back]
         )
     return total
 
@@ -1373,10 +1579,13 @@
     segr_ref,
     skip_ref,
     gain_ref,
+    cos_ref,
+    sin_ref,
     gated_ref,
     ssm_ref,
     states_ref,
     mixed_ref,
+    kv_ref,
     state,
 ):
     @pl.when(pl.program_id(0) == 0)
@@ -1385,13 +1594,14 @@
 
     size = proj_ref.shape[0]
     width = HEADS * HP
+    keeps = wide_keeps(keeps_ref)
     for block in range(mixed_ref.shape[1] // (2 * HP)):
         lanes = slice(2 * HP * block, 2 * HP * (block + 1))
         windows = conv_windows(block, proj_ref, before_ref, bc_ref, bc_before_ref)
-        summed = conv_sum(windows, taps_ref, lanes, keeps_ref)
+        summed = conv_sum(windows, taps_ref, lanes, keeps)
         mixed_ref[:, lanes] = (summed * jax.nn.sigmoid(summed)).astype(jnp.bfloat16)
     raw, dt_rows, cumul, enter_all, leave_bare = chunk_decays(proj_ref, heads_ref, keeps_ref)
-    leave_all = leave_bare * dt_rows
+    enter_all, leave_all = spread_heads(enter_all, leave_bare * dt_rows)
     cumul_t, dt_t = cumul.T, dt_rows.T
     entry = state[...]
     states_ref[0] = entry
@@ -1399,7 +1609,8 @@
     gram = dot_f32(c_rows, b_rows, 1, 1)
     row, column = order_in(size)
     allowed = (segc_ref[...] == segr_ref[0]) & (row >= column)
-    entered = dot_split(c_rows, halves(entry), 1, 0)
+    entered = dot_beside(c_rows, entry, 1)
+    weighted = []
     for pair in range(HEADS // 2):
         lanes = slice(2 * HP * pair, 2 * HP * (pair + 1))
         heads_x = mixed_ref[:, lanes]
@@ -1408,24 +1619,31 @@
             lane = DT_LANE + head
             decay = head_decay(allowed, cumul, cumul_t, head)
             mixing.append(gram * decay * dt_t[lane : lane + 1, :])
-        out = dot_split_left(
-            halves(jnp.concatenate(mixing, axis=1)), stack_heads(heads_x), 1, 0
+        stacked = stack_heads(heads_x)
+        out = dot_f32(
+            jnp.concatenate(halves(jnp.concatenate(mixing, axis=1)), axis=1),
+            jnp.concatenate([stacked, stacked], axis=0),
+            1,
+            0,
         )
         wide_x = heads_x.astype(jnp.float32)
-        enter = pair_columns(enter_all, pair)
+        enter = enter_all[:, lanes]
         out = out + enter * entered[:, lanes] + skip_ref[:, lanes] * wide_x
         ssm_ref[:, lanes] = out
         gate = proj_ref[:, lanes]
         value = out * (gate * jax.nn.sigmoid(gate))
         scale = lax.rsqrt(head_means(value * value) + GROUP_EPSILON)
         gated_ref[:, lanes] = (value * scale * gain_ref[:, lanes]).astype(jnp.bfloat16)
-        weighted = halves(pair_columns(leave_all, pair) * wide_x)
-        state[:, lanes] = enter[size - 1 :, :] * entry[:, lanes] + dot_split(
-            b_rows, weighted, 0, 0
-        )
+        weighted.append(leave_all[:, lanes] * wide_x)
+        state[:, lanes] = enter[size - 1 :, :] * entry[:, lanes]
+    state[...] += dot_beside(b_rows, jnp.concatenate(weighted, axis=1), 0)
+    kv = proj_ref[:, proj_ref.shape[1] - 2 * HP :][:, :HP]
+    kv = jnp.concatenate([kv[: size // 2], kv[size // 2 :]], axis=1)
+    kv_ref[...] = turn_folded(kv, cos_ref[...], sin_ref[...]).astype(jnp.bfloat16)
 
 
 def ssd_backward_kernel(
+    moves,
     proj_ref,
     before_ref,
     bc_ref,
@@ -1442,17 +1660,41 @@
     states_ref,
     dgated_ref,
     dq_ref,
+    gu_ref,
+    down_ref,
     dproj_ref,
     dtaps_ref,
     dheads_ref,
     dskip_ref,
     dgain_ref,
+    gu_back,
+    down_back,
     state,
     d_mixed,
     next_rows,
+    *sems,
 ):
+    def transfers(act):
+        data, place, core, along_x, along_y, across = plane_place()
+        sources, targets = (gu_ref, down_ref), (gu_back, down_back)
+        local_sems, send_sems, recv_sems = sems
+        for index, chip in enumerate((across, along_x, along_y)):
+            for at, move in enumerate(moves):
+                source, target = move(sources, targets, place, chip)
+                slot = index * len(moves) + at
+                act(
+                    remote(
+                        source, target, send_sems.at[slot], recv_sems.at[slot], (data, chip, core)
+                    )
+                )
+        for at, move in enumerate(moves):
+            source, target = move(sources, targets, place, place)
+            act(pltpu.make_async_copy(source, target, local_sems.at[at]))
+
     @pl.when(pl.program_id(0) == 0)
     def _():
+        meet(plane_peers())
+        transfers(lambda copy: copy.start())
         state[...] = jnp.zeros_like(state)
         next_rows[...] = jnp.zeros_like(next_rows)
         dtaps_ref[...] = jnp.zeros_like(dtaps_ref)
@@ -1463,27 +1705,21 @@
     size = proj_ref.shape[0]
     width = HEADS * HP
     raw, dt_rows, cumul, enter_all, leave_bare = chunk_decays(proj_ref, heads_ref, keeps_ref)
-    leave_all = leave_bare * dt_rows
     cumul_t, dt_t = cumul.T, dt_rows.T
     later = state[...]
-    later_parts = halves(later)
     entry = states_ref[0]
-    entry_parts = halves(entry)
     carried = jnp.sum(later * entry, axis=0, keepdims=True)
     b_rows, c_rows = mixed_ref[:, width : width + NS], mixed_ref[:, width + NS :]
     gram = dot_f32(c_rows, b_rows, 1, 1)
     row, column = order_in(size)
     allowed = (segc_ref[...] == segr_ref[0]) & (row >= column)
-    entered = dot_split(c_rows, entry_parts, 1, 0)
-    d_weighted = dot_split(b_rows, later_parts, 1, 0)
+    d_weighted = dot_beside(b_rows, later, 1)
+    enter_all, bare_all, dt_all = spread_heads(enter_all, leave_bare, dt_rows)
     d_gram = jnp.zeros((size, size), jnp.float32)
-    d_c = jnp.zeros(c_rows.shape, jnp.float32)
-    d_b = jnp.zeros(b_rows.shape, jnp.float32)
     row_sums = jnp.zeros((size, 2 * HP), jnp.float32)
-    d_leave = jnp.zeros((size, 2 * HP), jnp.float32)
-    d_enter = jnp.zeros((size, 2 * HP), jnp.float32)
-    column_sums = jnp.zeros((2 * HP, size), jnp.float32)
-    d_carried = jnp.zeros((1, 2 * HP), jnp.float32)
+    column_sums = jnp.zeros((size, 2 * HP), jnp.float32)
+    at_last = jnp.zeros((1, 2 * HP), jnp.float32)
+    d_entered, weighted = [], []
     for pair in range(HEADS // 2):
         lanes = slice(2 * HP * pair, 2 * HP * (pair + 1))
         heads_x = mixed_ref[:, lanes]
@@ -1502,53 +1738,65 @@
             jnp.bfloat16
         )
         dskip_ref[:, lanes] += jnp.sum(d_out * wide_x, axis=0, keepdims=True)
-        enter, leave = pair_columns(enter_all, pair), pair_columns(leave_all, pair)
-        d_out_parts = [stack_heads(half) for half in halves(d_out)]
-        mixing = []
+        enter, bare, dt_pair = enter_all[:, lanes], bare_all[:, lanes], dt_all[:, lanes]
+        high, low = [stack_heads(half) for half in halves(d_out)]
+        d_mixing = dot_f32(jnp.concatenate([high, low], axis=0), heads_x, 1, 1)
+        grams = []
         for side in range(2):
             head = 2 * pair + side
             lane = DT_LANE + head
-            d_mixing = dot_split_left(
-                [half[size * side : size * (side + 1)] for half in d_out_parts], heads_x, 1, 1
-            )
             decay = head_decay(allowed, cumul, cumul_t, head)
-            dt_row = dt_t[lane : lane + 1, :]
-            weighted_gram = gram * decay
-            mixing.append(weighted_gram * dt_row)
-            d_gram = d_gram + d_mixing * (decay * dt_row)
-            product = d_mixing * weighted_gram
-            column_sums = column_sums + at_row(lane, jnp.sum(product, axis=0, keepdims=True))
-            row_sums = row_sums + at_lane(lane, jnp.sum(product * dt_row, axis=1, keepdims=True))
-        d_x = dot_splits(halves(jnp.concatenate(mixing, axis=0)), d_out_parts, 0, 0)
+            grams.append(gram * decay)
+            first = size * side
+            d_mix = d_mixing[first : first + size] + d_mixing[2 * size + first : 3 * size + first]
+            d_gram = d_gram + d_mix * (decay * dt_t[lane : lane + 1, :])
+        gram_high, gram_low = halves(jnp.concatenate(grams, axis=0))
+        bare_x = dot_f32(
+            jnp.concatenate([gram_high, gram_high, gram_low], axis=0),
+            jnp.concatenate([high, low, high], axis=0),
+            0,
+            0,
+        )
+        left = bare * d_weighted[:, lanes]
+        d_x = bare_x + left
         first_lane = DT_LANE + 2 * pair
-        first, second = head_sums(d_out * entered[:, lanes])
-        d_enter = d_enter + at_lane(first_lane, first) + at_lane(first_lane + 1, second)
-        first, second = head_sums(d_weighted[:, lanes] * wide_x)
-        d_leave = d_leave + at_lane(first_lane, first) + at_lane(first_lane + 1, second)
-        first, second = head_sums(carried[:, lanes])
-        d_carried = d_carried + at_lane(first_lane, first) + at_lane(first_lane + 1, second)
-        d_mixed[:, lanes] = d_x + skip_ref[:, lanes] * d_out + leave * d_weighted[:, lanes]
-        d_entered = halves(enter * d_out)
-        weighted = halves(leave * wide_x)
-        d_c = d_c + dot_splits(d_entered, [half[:, lanes] for half in entry_parts], 1, 1)
-        d_b = d_b + dot_splits(weighted, [half[:, lanes] for half in later_parts], 1, 1)
-        state[:, lanes] = enter[size - 1 :, :] * later[:, lanes] + dot_split(
-            c_rows, d_entered, 0, 0
-        )
+        first, second = head_sums(d_out * (ssm - skip_ref[:, lanes] * wide_x))
+        row_sums = row_sums + at_lane(first_lane, first) + at_lane(first_lane + 1, second)
+        first, second = head_sums(d_x * wide_x)
+        column_sums = column_sums + at_lane(first_lane, first) + at_lane(first_lane + 1, second)
+        last = jnp.sum(dt_pair * left * wide_x, axis=0, keepdims=True)
+        last = last + carried[:, lanes] * enter[size - 1 :]
+        first, second = head_sums(last)
+        at_last = at_last + at_lane(first_lane, first) + at_lane(first_lane + 1, second)
+        d_mixed[:, lanes] = dt_pair * d_x + skip_ref[:, lanes] * d_out
+        d_entered.append(enter * d_out)
+        weighted.append(bare * dt_pair * wide_x)
+        state[:, lanes] = enter[size - 1 :, :] * later[:, lanes]
+    d_entered = jnp.concatenate(d_entered, axis=1)
+    state[...] += dot_beside(c_rows, d_entered, 0)
     d_gram_parts = halves(d_gram)
-    d_mixed[:, width : width + NS] = d_b + dot_split_left(d_gram_parts, c_rows, 0, 0)
-    d_mixed[:, width + NS :] = d_c + dot_split_left(d_gram_parts, b_rows, 1, 0)
-
-    column_sums = column_sums.T
-    d_left = d_leave * leave_all
-    d_cumul = row_sums - column_sums * dt_rows + d_enter * enter_all - d_left
-    at_last = jnp.sum(d_left, axis=0, keepdims=True) + d_carried * enter_all[size - 1 :]
+    d_b = dot_along(jnp.concatenate(weighted, axis=1), later)
+    d_mixed[:, width : width + NS] = d_b + dot_f32(
+        jnp.concatenate(d_gram_parts, axis=0),
+        jnp.concatenate([c_rows, c_rows], axis=0),
+        0,
+        0,
+    )
+    d_c = dot_along(d_entered, entry)
+    d_mixed[:, width + NS :] = d_c + dot_f32(
+        jnp.concatenate(d_gram_parts, axis=1),
+        jnp.concatenate([b_rows, b_rows], axis=0),
+        1,
+        0,
+    )
+
+    d_cumul = row_sums - column_sums * dt_rows
     last_row = lax.broadcasted_iota(jnp.int32, (size, 1), 0) == size - 1
     d_cumul = d_cumul + jnp.where(last_row, at_last, 0.0)
     upper = jnp.where(row <= column, 1.0, 0.0).astype(jnp.bfloat16)
     d_log = exact_sum(upper, d_cumul)
     rate = heads_ref[1:2]
-    d_raw = (column_sums + d_leave * leave_bare - rate * d_log) * jax.nn.sigmoid(raw)
+    d_raw = (column_sums - rate * d_log) * jax.nn.sigmoid(raw)
     lane_row = lax.broadcasted_iota(jnp.int32, (1, 2 * HP), 1)
     d_raw = jnp.where((lane_row >= DT_LANE) & (lane_row < DT_LANE + HEADS), d_raw, 0.0)
     dheads_ref[0:1] += jnp.sum(d_raw, axis=0, keepdims=True)
@@ -1559,10 +1807,11 @@
     )
     dproj_ref[:, width : width + HD] = dq_ref[...]
 
+    keeps = wide_keeps(keeps_ref)
     for block in range(mixed_ref.shape[1] // (2 * HP)):
         lanes = slice(2 * HP * block, 2 * HP * (block + 1))
         windows = conv_windows(block, proj_ref, before_ref, bc_ref, bc_before_ref)
-        summed = conv_sum(windows, taps_ref, lanes, keeps_ref)
+        summed = conv_sum(windows, taps_ref, lanes, keeps)
         sigmoid = jax.nn.sigmoid(summed)
         d_sum = d_mixed[:, lanes] * (sigmoid * (1.0 + summed * (1.0 - sigmoid)))
         dtaps_ref[KC : KC + 1, lanes] += jnp.sum(d_sum, axis=0, keepdims=True)
@@ -1570,7 +1819,7 @@
         d_pre = taps_ref[KC - 1 : KC, lanes] * d_sum
         for back in range(1, KC):
             tap = KC - 1 - back
-            kept = d_sum * keeps_ref[:, 1 + back : 2 + back]
+            kept = d_sum * keeps[back]
             dtaps_ref[tap : tap + 1, lanes] += jnp.sum(
                 kept * windows[back], axis=0, keepdims=True
             )
@@ -1584,6 +1833,10 @@
             start = total + 2 * HP * (block - HEADS // 2)
             dproj_ref[:, start : start + 2 * HP] = d_pre.astype(jnp.bfloat16)
 
+    @pl.when(pl.program_id(0) == pl.num_programs(0) - 1)
+    def _():
+        transfers(lambda copy: copy.wait())
+
 
 def ssd_specs(length, reverse, width_in, width_all, width):
     laps = length // CHUNK
@@ -1596,7 +1849,7 @@
 
     def rim(rows, columns):
         each = CHUNK // rows
-        return pl.BlockSpec((rows, columns), lambda lap: (jnp.maximum(each * at(lap) - 1, 0), 0))
+        return pl.BlockSpec((rows, columns), lambda lap: (lax.rem(each * (at(lap) + laps) - 1, each * laps), 0))
 
     def whole(rows, columns):
         return pl.BlockSpec((rows, columns), lambda lap: (0, 0))
@@ -1620,66 +1873,83 @@
     return (laps, tall, whole, slab, specs)
 
 
-def ssd_forward(arrays):
+def ssd_forward(arrays, cos_part, sin_part):
     length, width_in = arrays[0].shape
     width, width_all = HEADS * HP, HEADS * HP + 2 * NS
     laps, tall, whole, slab, specs = ssd_specs(length, False, width_in, width_all, width)
     shaped = jax.ShapeDtypeStruct
+    fold = pl.BlockSpec((CHUNK // 2, 2 * HP), lambda lap: (lap, 0))
     return pl.pallas_call(
         ssd_forward_kernel,
         grid=(laps,),
-        in_specs=specs,
-        out_specs=[tall(width), tall(width), slab(NS, width), tall(width_all)],
+        in_specs=specs + [fold, fold],
+        out_specs=[
+            tall(width),
+            tall(width),
+            slab(NS, width),
+            tall(width_all),
+            fold,
+        ],
         out_shape=[
             shaped((length, width), jnp.bfloat16),
             shaped((length, width), jnp.float32),
             shaped((laps, NS, width), jnp.float32),
             shaped((length, width_all), jnp.bfloat16),
+            shaped((length // 2, 2 * HP), jnp.bfloat16),
         ],
         scratch_shapes=[pltpu.VMEM((NS, width), jnp.float32)],
         cost_estimate=lasting(6),
         compiler_params=pltpu.CompilerParams(vmem_limit_bytes=VMEM_BYTES),
-    )(*arrays)
-
-
-def ssd_backward(arrays, mixed, ssm, states, d_outs, d_query):
+    )(*arrays, cos_part, sin_part)
+
+
+def ssd_backward(arrays, mixed, ssm, states, d_outs, d_query, grads):
     length, width_in = arrays[0].shape
     width, width_all = HEADS * HP, HEADS * HP + 2 * NS
     laps, tall, whole, slab, specs = ssd_specs(length, True, width_in, width_all, width)
     shaped = jax.ShapeDtypeStruct
+    moves = (block_move(0, 0), block_move(1, 1))
     return pl.pallas_call(
-        ssd_backward_kernel,
+        partial(ssd_backward_kernel, moves),
         grid=(laps,),
         in_specs=specs
         + [
             tall(width_all),
             tall(width),
             slab(NS, width),
-            tall(d_outs.shape[1]),
+            tall(width),
             tall(HD),
-        ],
+        ]
+        + any_specs(2),
         out_specs=[
             tall(width_in + 2 * NS),
             whole(8, width_all),
             whole(8, 2 * HP),
             whole(1, width),
             whole(1, width),
-        ],
+        ]
+        + any_specs(2),
         out_shape=[
             shaped((length, width_in + 2 * NS), jnp.bfloat16),
             shaped((8, width_all), jnp.float32),
             shaped((8, 2 * HP), jnp.float32),
             shaped((1, width), jnp.float32),
             shaped((1, width), jnp.float32),
-        ],
+        ]
+        + [shaped(array.shape, array.dtype) for array in grads],
         scratch_shapes=[
             pltpu.VMEM((NS, width), jnp.float32),
             pltpu.VMEM((CHUNK, width_all), jnp.float32),
             pltpu.VMEM((KC - 1, 8, width_all), jnp.float32),
+            pltpu.SemaphoreType.DMA((len(moves),)),
+            pltpu.SemaphoreType.DMA((3 * len(moves),)),
+            pltpu.SemaphoreType.DMA((3 * len(moves),)),
         ],
         cost_estimate=lasting(48),
-        compiler_params=pltpu.CompilerParams(vmem_limit_bytes=VMEM_BYTES),
-    )(*arrays, mixed, ssm, states, d_outs, d_query)
+        compiler_params=pltpu.CompilerParams(
+            collective_id=13, has_side_effects=True, vmem_limit_bytes=VMEM_BYTES
+        ),
+    )(*arrays, mixed, ssm, states, d_outs, d_query, *grads)
 
 
 QUERY_ROWS = 256
@@ -1705,30 +1975,42 @@
     return jnp.where(lane == 1, down, jnp.where(lane == 2, up, values))
 
 
-def join_halves(ref, first):
-    half = ref.shape[2] // 2
-    one, two = ref[first], ref[first + 1]
-    early = jnp.concatenate([one[:, :half], two[:, :half]], axis=1)
-    late = jnp.concatenate([one[:, half:], two[:, half:]], axis=1)
-    return jnp.concatenate([early, late], axis=0)
-
-
-def fold_rows(values):
-    rows = values.shape[0] // 2
-    return jnp.concatenate([values[:rows], values[rows:]], axis=1)
-
-
-def unfold_rows(values):
-    columns = values.shape[1] // 2
-    return jnp.concatenate([values[:, :columns], values[:, columns:]], axis=0)
+def unfold_rows(values, write):
+    step, columns = CHUNK // 2, values.shape[1] // 2
+    for start in range(0, values.shape[0], step):
+        rows = values[start : start + step]
+        write(2 * start, rows[:, :columns])
+        write(2 * start + step, rows[:, columns:])
+
+
+def fold_rows(ref, index, values):
+    step = CHUNK // 2
+    for start in range(0, values.shape[0] // 2, step):
+        ref[index, start : start + step] = jnp.concatenate(
+            [values[2 * start : 2 * start + step], values[2 * start + step : 2 * start + 2 * step]],
+            axis=1,
+        ).astype(ref.dtype)
+
+
+def join_halves(ref, first, target):
+    half = HD // 2
+
+    def write_at(lanes):
+        def write(start, rows):
+            target[start : start + rows.shape[0], lanes] = rows
+
+        return write
+
+    unfold_rows(ref[first], write_at(slice(0, half)))
+    unfold_rows(ref[first + 1], write_at(slice(half, HD)))
 
 
 def attend_forward_kernel(
     raw_ref, cos_ref, sin_ref, kv_ref, segc_ref, segr_ref, out_ref, total_ref, q_ref, k_ref, v_ref
 ):
     q_ref[...] = swap_middle(rotate_rows(raw_ref[...], cos_ref, sin_ref, 1.0)).astype(jnp.bfloat16)
-    k_ref[...] = join_halves(kv_ref, 0)
-    v_ref[...] = join_halves(kv_ref, 2)
+    join_halves(kv_ref, 0, k_ref)
+    join_halves(kv_ref, 2, v_ref)
     for start in range(0, q_ref.shape[0], QUERY_ROWS):
         reach = start + QUERY_ROWS
         rows = slice(start, reach)
@@ -1762,7 +2044,7 @@
     for start in range(0, q_ref.shape[0], QUERY_ROWS):
         reach = start + QUERY_ROWS
         rows = slice(start, reach)
-        q_rows, d_out = q_ref[rows], dout_ref[rows].astype(jnp.bfloat16)
+        q_rows, d_out = q_ref[rows], dout_ref[rows]
         scores = masked_scores(q_rows, k_ref, segc_ref, segr_ref, start, reach)
         probs = jnp.exp(scores - total_ref[rows])
         d_probs = dot_f32(d_out, v_ref[:reach], 1, 1)
@@ -1773,10 +2055,48 @@
         dv_sum[:reach] += dot_f32(probs.astype(jnp.bfloat16), d_out, 0, 0)
     dq_ref[...] = rotate_rows(swap_middle(dq_sum[...]), cos_ref, sin_ref, -1.0).astype(jnp.bfloat16)
     half = HD // 2
-    dkv_ref[0] = fold_rows(dk_sum[:, :half]).astype(jnp.bfloat16)
-    dkv_ref[1] = fold_rows(dk_sum[:, half:]).astype(jnp.bfloat16)
-    dkv_ref[2] = fold_rows(dv_sum[:, :half]).astype(jnp.bfloat16)
-    dkv_ref[3] = fold_rows(dv_sum[:, half:]).astype(jnp.bfloat16)
+    fold_rows(dkv_ref, 0, dk_sum[:, :half])
+    fold_rows(dkv_ref, 1, dk_sum[:, half:])
+    fold_rows(dkv_ref, 2, dv_sum[:, :half])
+    fold_rows(dkv_ref, 3, dv_sum[:, half:])
+
+
+def rotation_tables(length):
+    half, part = HD // 2, HD // 4
+    frequency = np.float32(ROPE_BASE) ** (
+        np.float32(-2.0) * np.arange(half).astype(np.float32) / np.float32(HD)
+    )
+    angles = np.arange(length).astype(np.float32)[:, None] * frequency[None, :]
+    cosine, sine_part = np.cos(angles), np.sin(angles)
+
+    def folded(values):
+        rows = values.reshape(length // CHUNK, 2, CHUNK // 2, half)
+        return rows.transpose(0, 2, 1, 3).reshape(length // 2, HD)
+
+    cos_kinds, sin_kinds = [], []
+    for start in (0, part):
+        columns = slice(start, start + part)
+        cos_part, sin_part = cosine[:, columns], sine_part[:, columns]
+        cos_kinds.append(folded(np.concatenate([cos_part, cos_part], axis=1)))
+        sin_kinds.append(folded(np.concatenate([-sin_part, sin_part], axis=1)))
+    cos_kinds.append(np.ones_like(cos_kinds[0]))
+    sin_kinds.append(np.zeros_like(sin_kinds[0]))
+    tables = (
+        np.concatenate([cosine, cosine], axis=1),
+        np.concatenate([-sine_part, sine_part], axis=1),
+        np.stack(cos_kinds),
+        np.stack(sin_kinds),
+    )
+    return [jnp.asarray(table.astype(np.float32)) for table in tables]
+
+
+def turn_folded(values, cosine, sine_part):
+    lane = lax.rem(lax.broadcasted_iota(jnp.int32, (1, HD), 1), HD // 2)
+    quarter = HD // 4
+    other = jnp.where(
+        lane < quarter, pltpu.roll(values, HD - quarter, 1), pltpu.roll(values, quarter, 1)
+    )
+    return values * cosine + other * sine_part
 
 
 def place_kv_kernel(lane_ref, cos_ref, sin_ref, *refs):
@@ -1784,11 +2104,14 @@
     total = parts[0][...].astype(jnp.float32)
     for part in parts[1:]:
         total = total + part[...].astype(jnp.float32)
-    total = unfold_rows(total)
-    part = cos_ref.shape[1]
-    turned = turn(cos_ref[...], -sin_ref[...], total[:, :part], total[:, part:])
-    out_ref[:, : 2 * part] = jnp.concatenate(turned, axis=1).astype(jnp.bfloat16)
-    out_ref[:, 2 * part :] = lane_ref[:, 2 * part :]
+    half = HD // 2
+    total = turn_folded(total, cos_ref[...], -sin_ref[...])
+
+    def write(start, values):
+        out_ref[start : start + values.shape[0], :half] = values.astype(jnp.bfloat16)
+
+    unfold_rows(total, write)
+    out_ref[:, half:] = lane_ref[:, half:]
 
 
 def place_kv(d_projected, parts, cos_part, sin_part, width_in):
@@ -1811,23 +2134,24 @@
     )(d_projected, *arrays)
 
 
-def attend(kernel, arrays, out_shapes, scratch=()):
+def whole_block(shape):
+    return pl.BlockSpec(shape, lambda step: (0,) * len(shape))
+
+
+def attend(kernel, arrays, out_shapes, scratch=(), blocks=None):
     return pl.pallas_call(
         kernel,
-        in_specs=vmem_specs(len(arrays)),
-        out_specs=vmem_specs(len(out_shapes)),
+        grid=(1,),
+        in_specs=[
+            whole_block(array.shape) if blocks is None or blocks[at] is None else blocks[at]
+            for at, array in enumerate(arrays)
+        ],
+        out_specs=[whole_block(shape) for shape, _ in out_shapes],
         out_shape=[jax.ShapeDtypeStruct(shape, dtype) for shape, dtype in out_shapes],
         scratch_shapes=[pltpu.VMEM(shape, dtype) for shape, dtype in scratch],
         cost_estimate=lasting(9),
         compiler_params=pltpu.CompilerParams(vmem_limit_bytes=VMEM_BYTES),
     )(*arrays)
-
-
-def turn(cosine, sine_part, first_half, second):
-    return (
-        first_half * cosine - second * sine_part,
-        second * cosine + first_half * sine_part,
-    )
 
 
 def after(value, *earlier):
@@ -1894,7 +2218,6 @@
     width_x = HEADS * HP
     hidden_units = w_gate.shape[1] // GROUP
     segment = segment_ids[0]
-    seg_column, seg_row = segment[:, None], segment[None, :]
     own_start = place * chip_rows + core * own_rows
     token_count = jnp.sum(valid_mask).astype(jnp.float32)
     mask_rows = lax.dynamic_slice(valid_mask, (data_rank, own_start), (1, own_rows))[0]
@@ -1902,46 +2225,28 @@
     bf16 = jnp.bfloat16
 
     half, part = HD // 2, HD // 4
-    kv_columns = (
-        (w_key[:, :part], w_key[:, half : half + part]),
-        (w_key[:, part:half], w_key[:, half + part :]),
-        (w_value[:, :half],),
-        (w_value[:, half:],),
-    )
-    misc = jnp.stack(
-        [
-            jnp.concatenate(
-                kv_columns[chip]
-                + (
-                    w_dt[:, HEADS * chip : HEADS * (chip + 1)],
-                    jnp.zeros((slice_rows, half - HEADS), bf16),
-                ),
-                axis=1,
-            )
-            for chip in range(GROUP)
-        ]
-    )
-    gains = jnp.concatenate(
-        [norm1_gain[None], norm2_gain[None], jnp.zeros((6, slice_rows), bf16)]
-    ).astype(jnp.float32)
     width_in = 2 * width_x + 2 * HD
-    in_slices, gains_all = exchange_plane(
+    in_slices, gains_all = first_exchange(
         (
             column_move(0, 0, 0, width_x),
             column_move(1, 0, width_x, HD),
             column_move(2, 0, width_x + HD, width_x),
             misc_move(3, 0, 2 * width_x + HD),
         ),
-        (w_z, w_query, w_x, misc, gains),
-        [(GROUP, slice_rows, width_in)],
-        3,
-        True,
+        (w_z, w_query, w_x, w_key, w_value, w_dt.T, norm1_gain[None], norm2_gain[None]),
+        width_in,
     )
     gain_one, gain_two = gains_all[:, 0].reshape(width), gains_all[:, 1].reshape(width)
     full_in = lax.all_gather(in_slices, "dp", axis=0, tiled=True).reshape(width, width_in)
     hidden_own = lax.dynamic_slice(hidden_in[0], (core * own_rows, 0), (own_rows, width))
     hidden_own = after(hidden_own, in_slices)
-    hidden_all = gather_plane(hidden_own)
+    hidden_all, normed, pre_bc = gather_plane(
+        hidden_own,
+        1,
+        apply_norm,
+        (gain_one[None], w_bc),
+        (((length, width), bf16), ((length, 2 * NS), bf16)),
+    )
     hidden_own = hidden_own.astype(jnp.float32)
     width_out = width_x + HD
     out_slices, gu_slices, down_slices = exchange_plane(
@@ -1952,7 +2257,7 @@
             column_move(3, 1, hidden_units, hidden_units),
             column_move(4, 2, 0, hidden_units),
         ),
-        (after(w_mamba_out.T, hidden_all), w_attn_out.T, w_gate, w_up, w_down.T),
+        (after(w_mamba_out.T, normed), w_attn_out.T, w_gate, w_up, w_down.T),
         [
             (GROUP, slice_rows, width_out),
             (GROUP, slice_rows, 2 * hidden_units),
@@ -1960,24 +2265,19 @@
         ],
         4,
     )
-    hidden = after(hidden_all, out_slices).astype(jnp.float32)
     out_gathered = lax.all_gather(after(out_slices, full_in), "dp", axis=0, tiled=True)
     full_out = out_gathered.reshape(width, width_out)
 
-    scale_one = lax.rsqrt(jnp.mean(hidden * hidden, axis=-1, keepdims=True) + EPSILON)
-    normed = (hidden * scale_one * gain_one).astype(bf16)
-    pre_bc = mat_dot(normed, w_bc).astype(bf16)
-    positions = jnp.arange(length)
-    frequency = ROPE_BASE ** (-2.0 * jnp.arange(half).astype(jnp.float32) / HD)
-    angles = positions.astype(jnp.float32)[:, None] * frequency[None, :]
-    cosine, sine_part = jnp.cos(angles), jnp.sin(angles)
-    cos_wide = jnp.concatenate([cosine, cosine], axis=1)
-    sin_wide = jnp.concatenate([-sine_part, sine_part], axis=1)
-    on_key = place < 2
-    cos_part = lax.dynamic_slice_in_dim(cosine, part * lax.rem(place, 2), part, 1)
-    sin_part = lax.dynamic_slice_in_dim(sine_part, part * lax.rem(place, 2), part, 1)
-    cos_part = jnp.where(on_key, cos_part, 1.0)
-    sin_part = jnp.where(on_key, sin_part, 0.0)
+    segment, conv_weight, conv_bias, dt_bias, a_log, d_skip, group_gain = (
+        lax.optimization_barrier(
+            (segment, conv_weight, conv_bias, dt_bias, a_log, d_skip, group_gain, out_slices)
+        )[:7]
+    )
+    seg_column, seg_row = segment[:, None], segment[None, :]
+    cos_wide, sin_wide, cos_folded, sin_folded = rotation_tables(length)
+    kind = jnp.minimum(place, 2)
+    cos_folded = lax.dynamic_index_in_dim(cos_folded, kind, 0, False)
+    sin_folded = lax.dynamic_index_in_dim(sin_folded, kind, 0, False)
     head_start = core * (MH // 2) + place * HEADS
 
     def local_rows(values, width_head):
@@ -1994,9 +2294,8 @@
     )
     taps = jnp.pad(taps, ((0, 8 - KC - 1), (0, 0)))
     rate = jnp.exp(local_rows(a_log, 1))
-    head_rows = jnp.zeros((8, HD), jnp.float32)
-    head_rows = head_rows.at[0, DT_LANE : DT_LANE + HEADS].set(local_rows(dt_bias, 1))
-    head_rows = head_rows.at[1, DT_LANE : DT_LANE + HEADS].set(rate)
+    head_rows = jnp.stack([local_rows(dt_bias, 1), rate])
+    head_rows = jnp.pad(head_rows, ((0, 6), (DT_LANE, HD - DT_LANE - HEADS)))
     skip_row = jnp.repeat(local_rows(d_skip, 1), HP)[None, :]
     gain_row = lax.dynamic_slice_in_dim(group_gain, head_start, HEADS, 0).reshape(1, width_x)
     laps = length // CHUNK
@@ -2008,14 +2307,7 @@
     keeps += [seg_ext[KC - 1 - back : KC - 1 - back + length] == segment for back in range(1, KC)]
     keeps = jnp.stack(keeps + [jnp.zeros((length,), bool)] * 3, axis=1).astype(jnp.float32)
 
-    normed_in, pre_bc = lax.optimization_barrier((normed, pre_bc, keeps, cos_wide, sin_wide))[:2]
-    projected = mat_dot(normed_in, full_in)
-    full_all = jnp.concatenate([full_in, w_bc], axis=1)
-    kv_raw = projected[:, 2 * width_x + HD : 2 * width_x + HD + half]
-    kv_own = jnp.concatenate(
-        turn(cos_part, sin_part, kv_raw[:, :part], kv_raw[:, part:]), axis=1
-    ).astype(bf16)
-    kv_all = over_chips(fold_rows(kv_own))
+    projected = mat_dot(normed, full_in)
 
     ssd_arrays = (
         projected,
@@ -2030,7 +2322,8 @@
         skip_row,
         gain_row,
     )
-    gated, ssm, states, mixed = ssd_forward(ssd_arrays)
+    gated, ssm, states, mixed, kv_own = ssd_forward(ssd_arrays, cos_folded, sin_folded)
+    kv_all = over_chips(kv_own)
     gu_gathered = lax.all_gather(after(gu_slices, out_gathered, gated), "dp", axis=0, tiled=True)
     down_gathered = lax.all_gather(after(down_slices, gu_gathered), "dp", axis=0, tiled=True)
     full_gu = gu_gathered.reshape(width, 2 * hidden_units)
@@ -2038,7 +2331,7 @@
     attended, log_total, queries, keys, vals = attend(
         attend_forward_kernel,
         (
-            projected[:, width_x : width_x + HD],
+            projected,
             cos_wide,
             sin_wide,
             after(kv_all, out_gathered),
@@ -2052,13 +2345,14 @@
             ((length, HD), bf16),
             ((length, HD), bf16),
         ),
+        blocks=[pl.BlockSpec((length, HD), lambda step: (0, width_x // HD))] + [None] * 5,
     )
     outs = jnp.concatenate([gated, attended], axis=1)
     middle = hidden_own + scatter_plane(outs, full_out, 2)[0]
 
     scale_two = lax.rsqrt(jnp.mean(middle * middle, axis=-1, keepdims=True) + EPSILON)
     normed_two, gate_up, activated = gather_plane(
-        after((middle * scale_two * gain_two).astype(bf16), gu_gathered, full_all),
+        after((middle * scale_two * gain_two).astype(bf16), gu_gathered),
         9,
         apply_gate_up,
         (full_gu,),
@@ -2097,12 +2391,12 @@
         + scale_two * d_scaled
         - middle * scale_two**3 * jnp.mean(d_scaled * middle, axis=-1, keepdims=True)
     )
-    d_branch, d_outs = gather_plane(
+    d_branch, d_gated, d_attended = gather_plane(
         after(d_middle.astype(bf16), grad_down),
         12,
         apply_out_back,
         (full_out,),
-        (((length, width_out), jnp.float32),),
+        (((length, width_x), jnp.float32), ((length, HD), bf16)),
     )
     d_query, d_kv = attend(
         attend_backward_kernel,
@@ -2115,7 +2409,7 @@
             seg_column,
             seg_row,
             log_total,
-            d_outs[:, width_x:],
+            d_attended,
         ),
         (((length, HD), bf16), ((GROUP, length // 2, HD), bf16)),
         (((length, HD), jnp.float32),) * 3,
@@ -2124,11 +2418,19 @@
     grad_out = sum_rows(
         after(dot_left_t(d_branch, outs).astype(bf16), grad_gate_up, d_query)
     )
-    d_projected, grad_taps, grad_heads, d_skip_lanes, d_gain_lanes = ssd_backward(
-        ssd_arrays, mixed, ssm, states, after(d_outs, grad_gate_up), d_query
+    (
+        d_projected,
+        grad_taps,
+        grad_heads,
+        d_skip_lanes,
+        d_gain_lanes,
+        back_gate_up,
+        back_down,
+    ) = ssd_backward(
+        ssd_arrays, mixed, ssm, states, d_gated, d_query, (grad_gate_up, grad_down)
     )
     d_kv_parts = lax.optimization_barrier((d_projected, *d_kv_parts))[1:]
-    d_projected = place_kv(d_projected, d_kv_parts, cos_part, sin_part, width_in)
+    d_projected = place_kv(d_projected, d_kv_parts, cos_folded, sin_folded, width_in)
     grad_skip = jnp.sum(d_skip_lanes.reshape(HEADS, HP), axis=-1)
     grad_group = d_gain_lanes.reshape(HEADS, HP)
     grad_in = sum_rows(
@@ -2136,7 +2438,7 @@
     )
     bc_cols = 2 * NS // GROUP
     d_normed, bc_sum = scatter_plane(
-        after(d_projected, grad_out), full_all, 8, ((normed, bc_cols, width // 2),)
+        after(d_projected, grad_out), full_in, 8, ((normed, bc_cols, width // 2),), (w_bc,)
     )
     scale_own = lax.rsqrt(jnp.mean(hidden_own * hidden_own, axis=-1, keepdims=True) + EPSILON)
     grad_gain_one = jnp.sum(d_normed * hidden_own * scale_own, axis=0)
@@ -2170,25 +2472,30 @@
     small = jnp.concatenate(small, axis=1)
     small_width = -(-small.shape[1] // (2 * GROUP * 128)) * 2 * GROUP * 128
     small = jnp.pad(small, ((0, 0), (0, small_width - small.shape[1])))
-    summed, bc_all, both_input, both_output, *back = finish_all(
-        small,
-        bc_sum,
-        grad_input,
-        block_out.astype(bf16),
-        [grad_gate_up, grad_down, grad_out],
-    )
-    (back_in,) = exchange_plane(
-        (block_move(0, 0),), (after(grad_in, both_input),), [grad_in.shape], 6
-    )
-    width_taps = MH * HP + 2 * NS
-    sum_taps = summed[:, :width_taps]
-    sum_heads = summed[:, width_taps : width_taps + 128]
-    summed = summed[:, width_taps + 128 :]
-    sum_one = summed[:, : width // 8].reshape(width)
-    sum_two = summed[:, width // 8 : width // 4].reshape(width)
-    sum_group = summed[:, width // 4 :][:, : MH * HP // 8].reshape(MH, HP)
-    gain_start = (data_rank * GROUP + place) * slice_rows
-
+    piece, both_input, both_output, back_out = plane_sum(
+        small, grad_input, block_out.astype(bf16), grad_out
+    )
+    small_all, bc_all, back_in = finish_all(piece, bc_sum, grad_in)
+    bc_all = bc_all.reshape(2 * GROUP, bc_cols, width // 2)
+    shapes = [
+        array.shape
+        for array in (
+            w_gate,
+            w_up,
+            w_down,
+            w_mamba_out,
+            w_attn_out,
+            w_z,
+            w_x,
+            w_query,
+            w_bc,
+            w_key,
+            w_value,
+            w_dt.T,
+            conv_weight.T,
+        )
+    ]
+    shapes += [(1, conv_bias.shape[0])] + [(1, MH)] * 3 + [(MH, HP)] + [(1, slice_rows)] * 2
     (
         grad_gate,
         grad_up,
@@ -2198,53 +2505,41 @@
         grad_z,
         grad_x,
         grad_q,
+        grad_bc,
         grad_k,
         grad_v,
         grad_dt,
-        grad_bc,
         grad_conv,
-    ) = attend(
-        unpack_kernel,
-        (*back, back_in, bc_all.reshape(2 * GROUP, bc_cols, width // 2), sum_taps),
-        [
-            (array.shape, jnp.float32)
-            for array in (
-                w_gate,
-                w_up,
-                w_down,
-                w_mamba_out,
-                w_attn_out,
-                w_z,
-                w_x,
-                w_query,
-                w_key,
-                w_value,
-                w_dt,
-                w_bc,
-                conv_weight,
-            )
-        ],
+        grad_bias,
+        grad_dtb,
+        grad_alog,
+        grad_skip,
+        grad_group,
+        grad_one,
+        grad_two,
+    ) = unpack_all(
+        (back_gate_up, back_down, back_out, back_in), bc_all, small_all, shapes
     )
     return (
         both_output.reshape(1, chip_rows, width),
         both_input.reshape(1, chip_rows, width),
-        lax.dynamic_slice_in_dim(sum_one, gain_start, slice_rows),
+        grad_one[0],
         grad_z,
         grad_x,
         grad_bc,
-        grad_dt,
-        grad_conv,
-        sum_taps[KC],
-        sum_heads[0, :MH],
-        sum_heads[1, :MH],
-        sum_heads[2, :MH],
-        sum_group,
+        grad_dt.T,
+        grad_conv.T,
+        grad_bias[0],
+        grad_dtb[0],
+        grad_alog[0],
+        grad_skip[0],
+        grad_group,
         grad_mo,
         grad_q,
         grad_k,
         grad_v,
         grad_ao,
-        lax.dynamic_slice_in_dim(sum_two, gain_start, slice_rows),
+        grad_two[0],
         grad_gate,
         grad_up,
         grad_down,

time: 740 us -> 683 us (0.923)
  Pallas kernels: 523 us -> 493 us
  other arithmetic: 46.2 us -> 19.6 us
  waiting for transfers between devices: 36.7 us -> 58.4 us
  local copies, waits for them, and re-layouts: 45.3 us -> 31.2 us
    pallas_call x9, Pallas kernels: 214 us -> 183 us  [the longest x1 39.4 us: ssd_backward(): pl.pallas_call(partial(ssd_backward_kernel, moves), grid=(laps,), in_spec...]
    slice x13 -> x1, local copies, waits for them, and re-layouts: 12.1 us -> 1.53 us  [heads_local_plan(): gains_all[:, 0].reshape(width)]
    dot_general x2 -> x1, matrix products: 16.1 us -> 11.7 us  [mat_dot(): return jnp.dot(left_side, right_side, preferred_element_type=jnp.float32)]
    unnamed x103 -> x87, local copies, waits for them, and re-layouts: 16.3 us -> 15.2 us
  transfers between devices with their start and end apart: 14 -> 14, of which waited for: 5 -> 8; matrix products, arithmetic and copies ran while one was open for 16% -> 12% of each run, Pallas kernels for 55% -> 52%
where the time goes in v3:
time: 683 us; the launch traced here: 677 us
  Pallas kernels  493 us (72%)
  waiting for transfers between devices  58.4 us (9%)
  matrix products  50.4 us (7%)
  local copies, waits for them, and re-layouts  31.2 us (5%)
  other arithmetic  19.6 us (3%)
  between operations  15.9 us (2%)
  starting transfers between devices  8.45 us (1%)
    pallas_call x4, Pallas kernels, scatter_plane(): pl.pallas_call(partial(scatter_kernel, count), out_shape=shapes, in_specs...  159 us
    pallas_call x4, Pallas kernels, gather_plane(): pl.pallas_call(partial(gather_kernel, apply, len(inputs), len(outputs)),...  148 us
    pallas_call x1, Pallas kernels, ssd_backward(): pl.pallas_call(partial(ssd_backward_kernel, moves), grid=(laps,), in_spec...  39.4 us
    dot_general x4, matrix products, dot_left_t(): lax.dot_general(left_side, right_side, (((0,), (0,)), ((), ())), preferre...  38.7 us
    pallas_call x1, Pallas kernels, finish_all(): pl.pallas_call(finish_kernel, out_shape=[shaped((places,) + piece.shape,...  35.7 us
    pallas_call x1, Pallas kernels, exchange_plane(): pl.pallas_call(partial(exchange_kernel, moves, len(arrays)), out_shape=[j...  27.6 us
    pallas_call x1, Pallas kernels, first_exchange(): pl.pallas_call(partial(first_exchange_kernel, moves), out_shape=[jax.Shap...  22.4 us
    pallas_call x2, Pallas kernels, attend(): pl.pallas_call(kernel, grid=(1,), in_specs=[whole_block(array.shape) if b...  18.2 us
  transfers between devices with their start and end apart: 14, of which 8 were waited for; matrix products, arithmetic and copies ran while one was open for 12% of the time, Pallas kernels for 52%

profile of v3, /device:TPU:0, one launch (start us, length us, event | category | flops | bytes accessed | tf_op | source)
XLA Modules:
  0.0 676.8 jit_solution(5860819301165210433)
XLA Ops:
  7.3 22.4 %shard_map.435 = (bf16[4,128,1024]{2,1,0:T(8,128)(2,1)}, f32[16,8,128]{2,1,0:T(8,128)}) custom-call(bf16[128,1536]{1,0:T(8,128)(2,1)} %z_ref.1, bf16[128,512]{1,0:T(8,128)(2,1)} %q_ref.1, bf16[128,1536]{1,0:T(8,128)(2,1)} %x_ref.1, bf16[128,128]{1,0:T(8,128)(2,1)} %key_ref.1, bf16[128,128]{1,0:T(8,128)(2,1)} %value_ref.1, bf16[24,128]{1,0:T(8,128)(2,1)} %bitcast.102, ...), custom_call_target="tpu_custom_call" | custom-call | flops 17999998976 | bytes 60000000 | tf_op jit(solution)/shard_map/pallas_call | solution.py:1380
  33.2 37.2 %shard_map.436 = (bf16[8,192,2048]{2,1,0:T(8,128)(2,1)}, bf16[1536,2048]{1,0:T(8,128)(2,1)}, bf16[1536,512]{1,0:T(8,128)(2,1)}) custom-call(bf16[192,2048]{1,0:T(8,128)(2,1)} %dynamic-slice_bitcast_fusion.own_ref, f32[1,2048]{1,0:T(1,128)} %get-tuple-element.209.refs_0_, bf16[2048,512]{1,0:T(8,128)(2,1)} %refs_1_.3), custom_call_target="tpu_custom_call" | custom-call | flops 31499999232 | bytes 105000000 | tf_op jit(solution)/shard_map/pallas_call | solution.py:757
  72.3 27.6 %shard_map.437 = (bf16[4,128,512]{2,1,0:T(8,128)(2,1)}, bf16[4,128,1024]{2,1,0:T(8,128)(2,1)}, bf16[4,128,512]{2,1,0:T(8,128)(2,1)}) custom-call(bf16[128,1536]{1,0:T(8,128)(2,1)} %bitcast.80, bf16[128,512]{1,0:T(8,128)(2,1)} %bitcast.84, bf16[128,2048]{1,0:T(8,128)(2,1)} %refs_2_.1, bf16[128,2048]{1,0:T(8,128)(2,1)} %refs_3_.1, bf16[128,2048]{1,0:T(8,128)(2,1)} %bitcast.79), custom_call_target="tpu_custom_call" | custom-call | flops 22499999744 | bytes 75000000 | tf_op jit(solution)/shard_map/pallas_call | solution.py:1402
  101.4 7.3 %all-gather.5.cloned.1.call-done = bf16[16,128,1024]{2,1,0:T(8,128)(2,1)} async-done(((bf16[4,128,1024]{2,1,0:T(8,128)(2,1)}), bf16[16,128,1024]{2,1,0:T(8,128)(2,1)}) %all-gather.5.cloned.1.call-update) | async-done | bytes 4194320 | tf_op jit(solution)/shard_map/all_gather | solution.py:2240
  117.4 11.7 %fusion.13.proj_ref.before_ref.raw_ref = f32[1536,1024]{1,0:T(8,128)} fusion(bf16[1536,2048]{1,0:T(8,128)(2,1)} %get-tuple-element.111.refs_0_, bf16[2048,1024]{1,0:T(8,128)(2,1)} %bitcast.90), kind=kOutput, calls=%fused_computation.75 | convolution fusion | flops 6442450944 | bytes 16777216 | tf_op jit(solution)/shard_map/dot_general | solution.py:47
  129.1 16.8 %shard_map.438 = (bf16[1536,384]{1,0:T(8,128)(2,1)}, f32[1536,384]{1,0:T(8,128)}, f32[6,256,384]{2,1,0:T(8,128)}, bf16[1536,896]{1,0:T(8,128)(2,1)}, bf16[768,128]{1,0:T(8,128)(2,1)}) custom-call(f32[1536,1024]{1,0:T(8,128)} %fusion.13.proj_ref.before_ref.raw_ref, f32[1536,1024]{1,0:T(8,128)} %fusion.13.proj_ref.before_ref.raw_ref, ...), custom_call_target="tpu_custom_call" | custom-call | flops 5400000000 | bytes 18000000 | tf_op jit(solution)/shard_map/pallas_call | solution.py:1882
  145.9 8.8 %all-gather.7.cloned.1.call-done = bf16[16,128,512]{2,1,0:T(8,128)(2,1)} async-done(((bf16[4,128,512]{2,1,0:T(8,128)(2,1)}), bf16[16,128,512]{2,1,0:T(8,128)(2,1)}) %all-gather.7.cloned.1.call-update) | async-done | bytes 2097168 | tf_op jit(solution)/shard_map/all_gather | solution.py:2268
  162.2 2.8 collective-permute-done
  165.1 4.2 collective-permute-done.1
  170.3 9.0 %shard_map.439 = (bf16[1536,128]{1,0:T(8,128)(2,1)}, f32[1536,1]{1,0:T(8,128)}, bf16[1536,128]{1,0:T(8,128)(2,1)}, bf16[1536,128]{1,0:T(8,128)(2,1)}, bf16[1536,128]{1,0:T(8,128)(2,1)}) custom-call(f32[1536,1024]{1,0:T(8,128)} %fusion.13.proj_ref.before_ref.raw_ref, f32[1536,128]{1,0:T(8,128)} %constant.102.clone.cos_ref, ...), custom_call_target="tpu_custom_call" | custom-call | flops 8099999744 | bytes 27000000 | tf_op jit(solution)/shard_map/pallas_call | solution.py:2142
  181.5 35.4 %shard_map.440 = f32[192,2048]{1,0:T(8,128)} custom-call(bf16[1536,512]{1,0:T(8,128)(2,1)} %copy-done.10, bf16[2048,512]{1,0:T(8,128)(2,1)} %bitcast.94), custom_call_target="tpu_custom_call" | custom-call | flops 31499999232 | bytes 105000000 | tf_op jit(solution)/shard_map/pallas_call | solution.py:961
  220.0 15.9 %all-gather.9.cloned.1.call-done = bf16[16,128,1024]{2,1,0:T(8,128)(2,1)} async-done(((bf16[4,128,1024]{2,1,0:T(8,128)(2,1)}), bf16[16,128,1024]{2,1,0:T(8,128)(2,1)}) %all-gather.9.cloned.1.call-update) | async-done | bytes 4194320 | tf_op jit(solution)/shard_map/all_gather | solution.py:2327
  237.2 38.3 %shard_map.441 = (bf16[8,192,2048]{2,1,0:T(8,128)(2,1)}, f32[1536,1024]{1,0:T(8,128)}, bf16[1536,512]{1,0:T(8,128)(2,1)}) custom-call(bf16[192,2048]{1,0:T(8,128)(2,1)} %multiply_convert_fusion.own_ref, bf16[2048,1024]{1,0:T(8,128)(2,1)} %bitcast.92), custom_call_target="tpu_custom_call" | custom-call | flops 31499999232 | bytes 105000000 | tf_op jit(solution)/shard_map/pallas_call | solution.py:757
  275.5 6.2 all-gather.11.cloned.1.call-done
  281.8 36.3 %shard_map.442 = f32[192,2048]{1,0:T(8,128)} custom-call(bf16[1536,512]{1,0:T(8,128)(2,1)} %get-tuple-element.133.left_ref, bf16[2048,512]{1,0:T(8,128)(2,1)} %bitcast.96), custom_call_target="tpu_custom_call" | custom-call | flops 31499999232 | bytes 105000000 | tf_op jit(solution)/shard_map/pallas_call | solution.py:961
  320.6 37.6 %shard_map.443 = (bf16[8,192,2048]{2,1,0:T(8,128)(2,1)}, bf16[1536,1024]{1,0:T(8,128)(2,1)}) custom-call(bf16[192,2048]{1,0:T(8,128)(2,1)} %fusion.8.own_ref, bf16[2048,512]{1,0:T(8,128)(2,1)} %bitcast.97, f32[1536,1024]{1,0:T(8,128)} %get-tuple-element.136.refs_1_), custom_call_target="tpu_custom_call" | custom-call | flops 31499999232 | bytes 105000000 | tf_op jit(solution)/shard_map/pallas_call | solution.py:757
  358.1 7.7 %convolution_convert_fusion.3 = bf16[2048,512]{1,0:T(8,128)(2,1)} fusion(bf16[1536,2048]{1,0:T(8,128)(2,1)} %bitcast.107, bf16[1536,512]{1,0:T(8,128)(2,1)S(1)} %copy-done.37), kind=kOutput, calls=%fused_computation.9 | convolution fusion | flops 3222274048 | bytes 9961472 | tf_op jit(solution)/shard_map/dot_general | solution.py:51
  365.9 11.3 %convolution_convert_fusion.1 = bf16[2048,1024]{1,0:T(8,128)(2,1)} fusion(bf16[1536,2048]{1,0:T(8,128)(2,1)} %bitcast.106, bf16[1536,1024]{1,0:T(8,128)(2,1)} %get-tuple-element.137.left_ref), kind=kOutput, calls=%fused_computation.1 | convolution fusion | flops 6444548096 | bytes 13631488 | tf_op jit(solution)/shard_map/dot_general | solution.py:51
  377.2 37.1 %shard_map.444 = f32[192,2048]{1,0:T(8,128)} custom-call(bf16[1536,1024]{1,0:T(8,128)(2,1)} %get-tuple-element.137.left_ref, bf16[2048,1024]{1,0:T(8,128)(2,1)} %bitcast.93), custom_call_target="tpu_custom_call" | custom-call | flops 31499999232 | bytes 105000000 | tf_op jit(solution)/shard_map/pallas_call | solution.py:961
  417.7 3.0 fusion.11
  420.8 35.0 %shard_map.445 = (bf16[8,192,2048]{2,1,0:T(8,128)(2,1)}, f32[1536,384]{1,0:T(8,128)}, bf16[1536,128]{1,0:T(8,128)(2,1)}) custom-call(bf16[192,2048]{1,0:T(8,128)(2,1)} %get-tuple-element.139.own_ref, bf16[2048,512]{1,0:T(8,128)(2,1)} %bitcast.95), custom_call_target="tpu_custom_call" | custom-call | flops 31499999232 | bytes 105000000 | tf_op jit(solution)/shard_map/pallas_call | solution.py:757
  455.8 9.2 %shard_map.446 = (bf16[1536,128]{1,0:T(8,128)(2,1)}, bf16[4,768,128]{2,1,0:T(8,128)(2,1)}) custom-call(bf16[1536,128]{1,0:T(8,128)(2,1)} %get-tuple-element.141.q_ref, bf16[1536,128]{1,0:T(8,128)(2,1)} %get-tuple-element.142.k_ref, bf16[1536,128]{1,0:T(8,128)(2,1)} %get-tuple-element.143.v_ref, f32[1536,128]{1,0:T(8,128)} %constant.102.clone.cos_ref, ...), custom_call_target="tpu_custom_call" | custom-call | flops 8099999744 | bytes 27000000 | tf_op jit(solution)/shard_map/pallas_call | solution.py:2142
  470.6 8.1 %convolution_convert_fusion.2 = bf16[2048,512]{1,0:T(8,128)(2,1)} fusion(bf16[1536,2048]{1,0:T(8,128)(2,1)} %bitcast.105, bf16[1536,512]{1,0:T(8,128)(2,1)S(1)} %copy-done.11), kind=kOutput, calls=%fused_computation.8 | convolution fusion | flops 3222274048 | bytes 9961472 | tf_op jit(solution)/shard_map/dot_general | solution.py:51
  478.7 10.9 %reduce-scatter.7.cloned.1.call-done = bf16[512,1024]{1,0:T(8,128)(2,1)} async-done(((bf16[2048,1024]{1,0:T(8,128)(2,1)}), bf16[512,1024]{1,0:T(8,128)(2,1)}) %reduce-scatter.7.cloned.1.call-update) | async-done | bytes 1048592 | tf_op jit(solution)/shard_map/reduce_scatter | solution.py:2379
  489.7 39.4 %shard_map.447 = (bf16[1536,1536]{1,0:T(8,128)(2,1)}, f32[8,896]{1,0:T(8,128)}, f32[8,128]{1,0:T(8,128)}, f32[1,384]{1,0:T(1,128)}, f32[1,384]{1,0:T(1,128)}, /*...) custom-call(f32[1536,1024]{1,0:T(8,128)} %fusion.13.proj_ref.before_ref.raw_ref, ...), custom_call_target="tpu_custom_call" | custom-call | flops 43200000000 | bytes 144000000 | tf_op jit(solution)/shard_map/pallas_call | solution.py:1912
  529.9 2.7 shard_map.448.left_ref
  532.6 11.6 %convolution_convert_fusion = bf16[2048,1024]{1,0:T(8,128)(2,1)} fusion(bf16[1536,2048]{1,0:T(8,128)(2,1)} %get-tuple-element.111.refs_0_, bf16[1536,1536]{1,0:T(8,128)(2,1)} %shard_map.448.left_ref), kind=kOutput, calls=%fused_computation | convolution fusion | flops 6444548096 | bytes 13631488 | tf_op jit(solution)/shard_map/dot_general | solution.py:51
  546.9 50.6 %shard_map.449 = (f32[192,2048]{1,0:T(8,128)}, f32[128,1024]{1,0:T(8,128)}) custom-call(bf16[1536,1536]{1,0:T(8,128)(2,1)} %shard_map.448.left_ref, bf16[2048,1024]{1,0:T(8,128)(2,1)} %bitcast.91, bf16[1536,2048]{1,0:T(8,128)(2,1)} %get-tuple-element.111.refs_0_, bf16[2048,512]{1,0:T(8,128)(2,1)} %refs_1_.3), custom_call_target="tpu_custom_call" | custom-call | flops 31499999232 | bytes 105000000 | tf_op jit(solution)/shard_map/pallas_call | solution.py:961
  600.0 3.0 fusion.5.own_ref
  603.0 14.8 %shard_map.450 = (f32[8,640]{1,0:T(8,128)}, f32[2,192,2048]{2,1,0:T(8,128)}, bf16[2,192,2048]{2,1,0:T(8,128)(2,1)}, bf16[4,128,512]{2,1,0:T(8,128)(2,1)}) custom-call(f32[8,5120]{1,0:T(8,128)} %pad.15.small_ref, f32[192,2048]{1,0:T(8,128)} %fusion.5.own_ref, bf16[192,2048]{1,0:T(8,128)(2,1)} %get-tuple-element.202.out_ref, bf16[4,128,512]{2,1,0:T(8,128)(2,1)} %bitcast.100), custom_call_target="tpu_custom_call" | custom-call | flops 17999998976 | bytes 60000000 | tf_op jit(solution)/shard_map/pallas_call | solution.py:1023
  619.9 35.7 %shard_map.451 = (f32[8,8,640]{2,1,0:T(8,128)}, bf16[8,4,32,1024]{3,2,1,0:T(8,128)(2,1)}, bf16[4,128,1024]{2,1,0:T(8,128)(2,1)}) custom-call(f32[8,640]{1,0:T(8,128)} %get-tuple-element.168.piece_ref, f32[128,1024]{1,0:T(8,128)} %get-tuple-element.169.bc_ref, bf16[4,128,1024]{2,1,0:T(8,128)(2,1)} %bitcast.98), custom_call_target="tpu_custom_call" | custom-call | flops 27000000512 | bytes 90000000 | tf_op jit(solution)/shard_map/pallas_call | solution.py:1136
  655.6 7.7 %shard_map.452 = (f32[128,2048]{1,0:T(8,128)}, f32[128,2048]{1,0:T(8,128)}, f32[2048,128]{1,0:T(8,128)}, f32[1536,128]{1,0:T(8,128)}, f32[512,128]{1,0:T(8,128)}...) custom-call(bf16[4,128,1024]{2,1,0:T(8,128)(2,1)} %get-tuple-element, ...), custom_call_target="tpu_custom_call" | custom-call | flops 7200000000 | bytes 24000000 | tf_op jit(solution)/shard_map/pallas_call | solution.py:1268
  (197 shorter events, 55.5 us)
Async XLA Ops:
  7.2 22.5 %copy-start = (bf16[1,384,2048]{2,1,0:T(8,128)(2,1)S(1)}, bf16[1,384,2048]{2,1,0:T(8,128)(2,1)}, u32[]{:S(2)}) copy-start(bf16[1,384,2048]{2,1,0:T(8,128)(2,1)} %param.28) | copy-start | bytes 4718596
  7.2 101.5 %all-gather.5.cloned.1.call-start = ((), (), s32[]{:S(2)}) async-start(), calls=%async_computation.4 | async-start | bytes 5242880 | tf_op jit(solution)/shard_map/all_gather | solution.py:2240
  29.7 125.1 %all-gather.7.cloned.1.call-start = ((), (), s32[]{:S(2)}) async-start(), calls=%async_computation.5 | async-start | bytes 2621440 | tf_op jit(solution)/shard_map/all_gather | solution.py:2268
  33.2 203.0 %copy-start.19 = (f32[16,1,128]{2,1,0:T(1,128)}, f32[16,1,128]{2,1,0:T(1,128)S(1)}, u32[]{:S(2)}) copy-start(f32[16,1,128]{2,1,0:T(1,128)S(1)} %get-tuple-element.210) | copy-start | bytes 24580
  33.2 37.2 %copy-start.13 = (bf16[2048,128]{1,0:T(8,128)(2,1)S(1)}, bf16[2048,128]{1,0:T(8,128)(2,1)}, u32[]{:S(2)}) copy-start(bf16[2048,128]{1,0:T(8,128)(2,1)} %param.51) | copy-start | bytes 1572868
  33.2 38.2 %copy-start.21 = (bf16[512,128]{1,0:T(8,128)(2,1)S(1)}, bf16[512,128]{1,0:T(8,128)(2,1)}, u32[]{:S(2)}) copy-start(bf16[512,128]{1,0:T(8,128)(2,1)} %param.47) | copy-start | bytes 393220
  33.2 39.0 %copy-start.29 = (s32[1,1536]{1,0:T(1,128)S(1)}, s32[1,1536]{1,0:T(1,128)}, u32[]{:S(2)}) copy-start(s32[1,1536]{1,0:T(1,128)} %param.30) | copy-start | bytes 18436
  72.2 28.3 %copy-start.28 = (f32[3584]{0:T(1024)S(1)}, f32[3584]{0:T(1024)}, u32[]{:S(2)}) copy-start(f32[3584]{0:T(1024)} %param.38) | copy-start | bytes 43012
  72.2 28.3 %copy-start.34 = (f32[48]{0:T(128)S(1)}, f32[48]{0:T(128)}, u32[]{:S(2)}) copy-start(f32[48]{0:T(128)} %param.40) | copy-start | bytes 580
  72.2 28.3 %copy-start.35 = (f32[48]{0:T(128)S(1)}, f32[48]{0:T(128)}, u32[]{:S(2)}) copy-start(f32[48]{0:T(128)} %param.39) | copy-start | bytes 580
  72.2 29.1 %slice-start.1 = ((f32[3584]{0:T(1024)}), f32[512]{0:T(512)S(1)}, s32[]{:S(2)}) async-start(f32[3584]{0:T(1024)} %param.38), calls=%async_computation.13 | async-start | bytes 4096 | tf_op jit(solution)/shard_map/slice | solution.py:2287
  72.2 29.1 %copy-start.23 = (f32[3584,4]{0,1:T(4,128)S(1)}, f32[3584,4]{0,1:T(4,128)}, u32[]{:S(2)}) copy-start(f32[3584,4]{0,1:T(4,128)} %param.37) | copy-start | bytes 172036
  99.8 14.8 %slice-start = ((f32[3584,4]{0,1:T(4,128)}), f32[512,4]{0,1:T(4,128)S(1)}, s32[]{:S(2)}) async-start(f32[3584,4]{0,1:T(4,128)} %param.37), calls=%async_computation.12 | async-start | bytes 16384 | tf_op jit(solution)/shard_map/slice | solution.py:2287
  108.7 127.1 %all-gather.9.cloned.1.call-start = ((), (), s32[]{:S(2)}) async-start(), calls=%async_computation.6 | async-start | bytes 5242880 | tf_op jit(solution)/shard_map/all_gather | solution.py:2327
  129.1 26.5 %copy-start.25 = (s32[4,1536]{1,0:T(4,128)S(1)}, s32[4,1536]{1,0:T(4,128)}, u32[]{:S(2)}) copy-start(s32[4,1536]{1,0:T(4,128)} %param.31) | copy-start | bytes 73732
  154.8 127.0 %all-gather.11.cloned.1.call-start = ((), (), s32[]{:S(2)}) async-start(), calls=%async_computation.7 | async-start | bytes 2621440 | tf_op jit(solution)/shard_map/all_gather | solution.py:2328
  157.1 8.0 %collective-permute-start = (bf16[768,128]{1,0:T(8,128)(2,1)}, bf16[768,128]{1,0:T(8,128)(2,1)S(1)}, u32[]{:S(2)}, u32[]{:S(2)}) collective-permute-start(bf16[768,128]{1,0:T(8,128)(2,1)} %get-tuple-element.126), channel_id=1, source_target_pairs={{0,2},{2,0},{4,6},{6,4},{1,3},{3,1},{5,7},{7,5},{8,10},{10,8},{12,... | collective-permute-start | bytes 589832 | tf_op jit(solution)/shard_map/ppermute | solution.py:2167
  158.6 10.8 %collective-permute-start.1 = (bf16[768,128]{1,0:T(8,128)(2,1)}, bf16[768,128]{1,0:T(8,128)(2,1)S(1)}, u32[]{:S(2)}, u32[]{:S(2)}) collective-permute-start(bf16[768,128]{1,0:T(8,128)(2,1)} %get-tuple-element.126), channel_id=1, source_target_pairs={{0,4},{2,6},{4,0},{6,2},{1,5},{3,7},{5,1},{7,3},{8,12},{10,14},{12... | collective-permute-start | bytes 589832 | tf_op jit(solution)/shard_map/ppermute | solution.py:2167
  160.0 9.4 %collective-permute-start.2 = (bf16[768,128]{1,0:T(8,128)(2,1)}, bf16[768,128]{1,0:T(8,128)(2,1)S(1)}, u32[]{:S(2)}, u32[]{:S(2)}) collective-permute-start(bf16[768,128]{1,0:T(8,128)(2,1)} %get-tuple-element.126), channel_id=1, source_target_pairs={{0,6},{2,4},{4,2},{6,0},{1,7},{3,5},{5,3},{7,1},{8,14},{10,12},{12... | collective-permute-start | bytes 589832 | tf_op jit(solution)/shard_map/ppermute | solution.py:2167
  181.5 35.4 %copy-start.2 = (bf16[192,2048]{1,0:T(8,128)(2,1)S(1)}, bf16[192,2048]{1,0:T(8,128)(2,1)}, u32[]{:S(2)}) copy-start(bf16[192,2048]{1,0:T(8,128)(2,1)} %dynamic-slice_bitcast_fusion.own_ref) | copy-start | bytes 2359300
  220.0 55.5 %copy-start.26 = (f32[192]{0:T(256)}, f32[192]{0:T(256)S(1)}, u32[]{:S(2)}) copy-start(f32[192]{0:T(256)S(1)} %get-tuple-element.219) | copy-start | bytes 2308
  235.9 178.5 %reduce-scatter.5.cloned.1.call-start = ((), (), s32[]{:S(2)}) async-start(), calls=%async_computation.8 | async-start | bytes 2621440 | tf_op jit(solution)/shard_map/reduce_scatter | solution.py:2379
  281.8 36.3 %copy-start.9 = (bf16[1,384,2048]{2,1,0:T(8,128)(2,1)S(1)}, bf16[1,384,2048]{2,1,0:T(8,128)(2,1)}, u32[]{:S(2)}) copy-start(bf16[1,384,2048]{2,1,0:T(8,128)(2,1)} %param.29) | copy-start | bytes 4718596
  320.6 37.6 %copy-start.37 = (bf16[1536,512]{1,0:T(8,128)(2,1)S(1)}, bf16[1536,512]{1,0:T(8,128)(2,1)}, u32[]{:S(2)}) copy-start(bf16[1536,512]{1,0:T(8,128)(2,1)} %get-tuple-element.133.left_ref) | copy-start | bytes 4718596
  365.9 123.8 %reduce-scatter.7.cloned.1.call-start = ((), (), s32[]{:S(2)}) async-start(), calls=%async_computation.9 | async-start | bytes 5242880 | tf_op jit(solution)/shard_map/reduce_scatter | solution.py:2379
  414.5 129.8 %reduce-scatter.9.cloned.1.call-start = ((), (), s32[]{:S(2)}) async-start(), calls=%async_computation.10 | async-start | bytes 2621440 | tf_op jit(solution)/shard_map/reduce_scatter | solution.py:2379
  467.1 62.0 %collective-permute-start.3 = (bf16[768,128]{1,0:T(8,128)(2,1)S(1)}, bf16[768,128]{1,0:T(8,128)(2,1)S(1)}, u32[]{:S(2)}, u32[]{:S(2)}) collective-permute-start(bf16[768,128]{1,0:T(8,128)(2,1)S(1)} %get-tuple-element.206), channel_id=1, source_target_pairs={{0,2},{2,0},{4,6},{6,4},{1,3},{3,1},{5,7},{7,5},{8,10},{10,8},{12,... | collective-permute-start | bytes 589832 | tf_op jit(solution)/shard_map/ppermute | solution.py:2178
  468.2 60.9 %collective-permute-start.4 = (bf16[768,128]{1,0:T(8,128)(2,1)S(1)}, bf16[768,128]{1,0:T(8,128)(2,1)S(1)}, u32[]{:S(2)}, u32[]{:S(2)}) collective-permute-start(bf16[768,128]{1,0:T(8,128)(2,1)S(1)} %get-tuple-element.205), channel_id=1, source_target_pairs={{0,4},{2,6},{4,0},{6,2},{1,5},{3,7},{5,1},{7,3},{8,12},{10,14},{12... | collective-permute-start | bytes 589832 | tf_op jit(solution)/shard_map/ppermute | solution.py:2178
  469.1 60.0 %collective-permute-start.5 = (bf16[768,128]{1,0:T(8,128)(2,1)S(1)}, bf16[768,128]{1,0:T(8,128)(2,1)S(1)}, u32[]{:S(2)}, u32[]{:S(2)}) collective-permute-start(bf16[768,128]{1,0:T(8,128)(2,1)S(1)} %get-tuple-element.204), channel_id=1, source_target_pairs={{0,6},{2,4},{4,2},{6,0},{1,7},{3,5},{5,3},{7,1},{8,14},{10,12},{12... | collective-permute-start | bytes 589832 | tf_op jit(solution)/shard_map/ppermute | solution.py:2178
  489.7 130.2 %reduce-scatter.11.cloned.1.call-start = ((), (), s32[]{:S(2)}) async-start(), calls=%async_computation.11 | async-start | bytes 5242880 | tf_op jit(solution)/shard_map/reduce_scatter | solution.py:2379
  546.8 50.6 %copy-start.3 = (bf16[192,2048]{1,0:T(8,128)(2,1)S(1)}, bf16[192,2048]{1,0:T(8,128)(2,1)}, u32[]{:S(2)}) copy-start(bf16[192,2048]{1,0:T(8,128)(2,1)} %dynamic-slice_bitcast_fusion.own_ref) | copy-start | bytes 2359300
  546.9 50.6 %copy-start.22 = (f32[16,1,128]{2,1,0:T(1,128)S(1)}, f32[16,1,128]{2,1,0:T(1,128)}, u32[]{:S(2)}) copy-start(f32[16,1,128]{2,1,0:T(1,128)} %get-tuple-element.208) | copy-start | bytes 24580
  (22 other events, 58.3 us)
Sparse Core Ops, SparseCore 0:
  29.8 78.8 all-gather.4
  110.3 44.4 all-gather.6
  156.3 79.4 all-gather.8
  237.3 44.4 all-gather.10
  366.0 42.7 reduce-scatter.4
  414.6 74.9 reduce-scatter.6
  491.9 44.3 reduce-scatter.8
  544.4 75.4 reduce-scatter.10

commit v4 on v3

--- a/solution.py
+++ b/solution.py
@@ -615,7 +615,7 @@
 
 
 GROUP = 4
-CHUNK = 256
+CHUNK = 128
 HEADS = 6
 MESH_ID = pl.DeviceIdType.MESH
 VMEM_BYTES = 56 * 1024 * 1024
@@ -682,6 +682,13 @@
     outputs = refs[count_in + 1 : count_in + 1 + count_out]
     send_sems, recv_sems = refs[count_in + 1 + count_out :]
     data, place, core, along_x, along_y, across = plane_place()
+    to_x, to_y, partner = (data, along_x, core), (data, along_y, core), (data, place, 1 - core)
+    meet((to_x, to_y, partner))
+    gather_steps(apply, own_ref, inputs, all_ref, outputs, send_sems, recv_sems)
+
+
+def gather_steps(apply, own_ref, inputs, all_ref, outputs, send_sems, recv_sems, ready=None):
+    data, place, core, along_x, along_y, across = plane_place()
     height = own_ref.shape[0]
     half = height // 2
     to_x, to_y, partner = (data, along_x, core), (data, along_y, core), (data, place, 1 - core)
@@ -694,8 +701,6 @@
             index = 2 * chip + side
             rows = pl.ds(pl.multiple_of(index * height, 16), height)
             apply(all_ref[index], rows, inputs, outputs)
-
-    meet((to_x, to_y, partner))
 
     def push(index, source, target, device):
         copy = remote(source, target, send_sems.at[index], recv_sems.at[index], device)
@@ -712,6 +717,8 @@
     work(place, core)
     pair_own.wait_recv()
     work(place, 1 - core)
+    if ready is not None:
+        ready(place, 0)
     x_first.wait_recv()
     over_y = push(5, block(along_x, 0), block(along_x, 0), to_y)
     y_second.wait_recv()
@@ -726,8 +733,12 @@
     work(along_y, core)
     pair_x.wait_recv()
     work(along_x, 1 - core)
+    if ready is not None:
+        ready(along_x, 1)
     pair_y.wait_recv()
     work(along_y, 1 - core)
+    if ready is not None:
+        ready(along_y, 2)
     over_y.wait_recv()
     pair_a = push(9, block(across, 0), block(across, 0), partner)
     over_x.wait_recv()
@@ -736,6 +747,8 @@
     pair_a.wait_recv()
     pair_b.wait_recv()
     work(across, 1 - core)
+    if ready is not None:
+        ready(across, 3)
     for copy in (
         x_first,
         y_second,
@@ -809,7 +822,7 @@
     )
 
 
-def scatter_kernel(count, left_ref, right_ref, *refs):
+def scatter_kernel(count, left_ref, right_ref, *refs, store=None, between=None):
     data, place, core, along_x, along_y, across = plane_place()
     partner = (data, place, 1 - core)
     to_x, to_y = (data, along_x, core), (data, along_y, core)
@@ -910,11 +923,15 @@
             def one(lap, carry):
                 rows = pl.ds(pl.multiple_of(lap * step, step), step)
                 place_rows = pl.ds(pl.multiple_of(first + lap * step, step), step)
-                sum_ref[place_rows] = (
+                total = (
                     own_rows(3, place_rows)
                     + near[rows].astype(jnp.float32)
                     + last[rows].astype(jnp.float32)
                 )
+                if store is None:
+                    sum_ref[place_rows] = total
+                else:
+                    store(place_rows, total)
                 return carry
 
             lax.fori_loop(0, half // step, one, 0)
@@ -928,23 +945,130 @@
     runs = [
         one_array(at, parts[at], sums[at], scratch[each * at : each * (at + 1)]) for at in range(count)
     ]
-    for run in runs:
-        next(run)
-    for run in runs:
-        next(run)
+    for stage in range(2):
+        for run in runs:
+            next(run)
+        if between is not None:
+            between(stage)
     for run in runs:
         for _ in run:
             pass
 
 
-def scatter_plane(left, right, identity, extra=(), beside=()):
-    height, width = left.shape[0] // (2 * GROUP), right.shape[0]
-    sizes = [(height, width)] + [size for _, *size in extra]
-    shapes = []
+def down_and_back_kernel(
+    act_ref,
+    weights_ref,
+    middle_ref,
+    teacher_ref,
+    factor_ref,
+    both_ref,
+    out_ref,
+    d_out_ref,
+    d_mlp_ref,
+    d_both_ref,
+    grad_ref,
+    own_ref,
+    grad_sum,
+    gather_send,
+    gather_recv,
+    *scratch,
+):
+    def store(rows, total):
+        out = middle_ref[rows] + total
+        out_ref[rows] = out.astype(jnp.bfloat16)
+        d_out = factor_ref[rows] * (out - teacher_ref[rows].astype(jnp.float32))
+        d_out_ref[rows] = d_out
+        own_ref[rows] = d_out.astype(jnp.bfloat16)
+
+    def ready(chip, turn_at):
+        blocks = d_mlp_ref[pl.ds(2 * chip, 2)]
+        height = blocks.shape[0] * blocks.shape[1]
+        rows = pl.ds(pl.multiple_of(chip * height, 16), height)
+        part = dot_f32(blocks.reshape(height, blocks.shape[2]), act_ref[rows], 0, 0)
+        if turn_at == 0:
+            grad_sum[...] = part
+        elif turn_at < GROUP - 1:
+            grad_sum[...] += part
+        else:
+            grad_ref[...] = (grad_sum[...] + part).astype(jnp.bfloat16)
+
+    scatter_kernel(1, act_ref, weights_ref, None, *scratch, store=store)
+    gather_steps(
+        apply_down_back,
+        own_ref,
+        (weights_ref, both_ref),
+        d_mlp_ref,
+        (d_both_ref,),
+        gather_send,
+        gather_recv,
+        ready,
+    )
+
+
+def down_and_back(activated, full_down, middle, teacher_own, factor, gate_up):
+    rows, width = middle.shape
+    shaped = jax.ShapeDtypeStruct
+    return pl.pallas_call(
+        down_and_back_kernel,
+        out_shape=[
+            shaped((rows, width), jnp.bfloat16),
+            shaped((rows, width), jnp.float32),
+            shaped((2 * GROUP, rows, width), jnp.bfloat16),
+            shaped(gate_up.shape, jnp.bfloat16),
+            shaped(full_down.shape, jnp.bfloat16),
+        ],
+        in_specs=vmem_specs(6),
+        out_specs=vmem_specs(5),
+        scratch_shapes=[
+            pltpu.VMEM((rows, width), jnp.bfloat16),
+            pltpu.VMEM(full_down.shape, jnp.float32),
+            pltpu.SemaphoreType.DMA((11,)),
+            pltpu.SemaphoreType.DMA((11,)),
+        ]
+        + scatter_scratch([(rows, width)]),
+        cost_estimate=lasting(70),
+        compiler_params=pltpu.CompilerParams(
+            collective_id=10, has_side_effects=True, vmem_limit_bytes=VMEM_BYTES
+        ),
+    )(activated, full_down, middle, teacher_own, factor, gate_up)
+
+
+def up_back_kernel(d_both_ref, weights_ref, normed_ref, sum_ref, grad_ref, *scratch):
+    tiles = 4
+    width = normed_ref.shape[1] // tiles
+
+    def between(stage):
+        for tile in range(2 * stage, 2 * stage + 2):
+            columns = slice(width * tile, width * (tile + 1))
+            grad_ref[columns] = dot_f32(
+                normed_ref[:, columns], d_both_ref[...], 0, 0
+            ).astype(jnp.bfloat16)
+
+    scatter_kernel(1, d_both_ref, weights_ref, sum_ref, *scratch, between=between)
+
+
+def up_back(d_gate_up, full_gu, normed_two):
+    rows, width = d_gate_up.shape[0] // (2 * GROUP), full_gu.shape[0]
+    return pl.pallas_call(
+        up_back_kernel,
+        out_shape=[
+            jax.ShapeDtypeStruct((rows, width), jnp.float32),
+            jax.ShapeDtypeStruct(full_gu.shape, jnp.bfloat16),
+        ],
+        in_specs=vmem_specs(3),
+        out_specs=vmem_specs(2),
+        scratch_shapes=scatter_scratch([(rows, width)]),
+        cost_estimate=lasting(38),
+        compiler_params=pltpu.CompilerParams(
+            collective_id=11, has_side_effects=True, vmem_limit_bytes=VMEM_BYTES
+        ),
+    )(d_gate_up, full_gu, normed_two)
+
+
+def scatter_scratch(sizes):
     scratch = [pltpu.VMEM((2 * GROUP, *size), jnp.bfloat16) for size in sizes]
     for rows, columns in sizes:
         half = (rows // 2, columns)
-        shapes.append(jax.ShapeDtypeStruct((rows, columns), jnp.float32))
         scratch += [
             pltpu.VMEM((4, rows, columns), jnp.bfloat16),
             pltpu.VMEM((2,) + half, jnp.bfloat16),
@@ -957,13 +1081,20 @@
             pltpu.SemaphoreType.DMA((6,)),
             pltpu.SemaphoreType.DMA((6,)),
         ]
+    return scratch
+
+
+def scatter_plane(left, right, identity, extra=(), beside=()):
+    height, width = left.shape[0] // (2 * GROUP), right.shape[0]
+    sizes = [(height, width)] + [tuple(size) for _, *size in extra]
+    shapes = [jax.ShapeDtypeStruct(size, jnp.float32) for size in sizes]
     count = 1 + len(extra)
     return pl.pallas_call(
         partial(scatter_kernel, count),
         out_shape=shapes,
         in_specs=vmem_specs(2 if count == 1 else 2 + count),
         out_specs=vmem_specs(count),
-        scratch_shapes=scratch,
+        scratch_shapes=scatter_scratch(sizes),
         cost_estimate=lasting(35),
         compiler_params=pltpu.CompilerParams(
             collective_id=identity, has_side_effects=True, vmem_limit_bytes=VMEM_BYTES
@@ -1113,11 +1244,29 @@
     late += [push(small_all.at[mine], small_all.at[mine], device) for device in plane]
     for copy in second:
         copy.wait_recv()
-    third = [push(bc_line, bc_all.at[mine], device) for device in chips]
-    late.append(push(bc_line, bc_all.at[mine], partner))
+    half = count // 2
+
+    def half_of(chip, at):
+        return bc_all.at[2 * chip + core, pl.ds(at * half, half)]
+
+    def send_half(chip, at, device):
+        held = half_of(chip, at)
+        return push(held, held, device)
+
+    to_x, to_y = (data, along_x, core), (data, along_y, core)
     bc_all[mine] = bc_line[...]
-    for copy, chip in zip(third, others):
-        copy.wait_recv()
+    x_first = send_half(place, 0, to_x)
+    y_second = send_half(place, 1, to_y)
+    x_second = send_half(place, 1, to_x)
+    y_first = send_half(place, 0, to_y)
+    late.append(push(bc_all.at[mine], bc_all.at[mine], partner))
+    x_first.wait_recv()
+    over_y = send_half(along_x, 0, to_y)
+    y_second.wait_recv()
+    over_x = send_half(along_y, 1, to_x)
+    for copies, chip in (((x_second,), along_x), ((y_first,), along_y), ((over_x, over_y), across)):
+        for copy in copies:
+            copy.wait_recv()
         held = bc_all.at[2 * chip + core]
         late.append(push(held, held, partner))
     for copy in late:
@@ -1130,7 +1279,7 @@
 def finish_all(piece, bc_sum, bulk):
     count = lax.axis_size("dp")
     places = 2 * GROUP
-    pushes = 3 * (count - 1) + (places - 1) + 2 * (GROUP - 1) + GROUP
+    pushes = 3 * (count - 1) + (places - 1) + (GROUP - 1) + 6 + GROUP
     shaped = jax.ShapeDtypeStruct
     blocks = (count, bc_sum.shape[0] // count, bc_sum.shape[1])
     return pl.pallas_call(
@@ -1165,6 +1314,8 @@
     in_ref,
     bc_ref,
     misc_ref,
+    both_ref,
+    both_out,
     pieces_ref,
     gate_ref,
     up_ref,
@@ -1186,9 +1337,13 @@
     group_ref,
     one_ref,
     two_ref,
+    input_ref,
+    output_ref,
     sums_ref,
 ):
     units, width, part = down_ref.shape[2], HEADS * HP, HD // 4
+    input_ref[...] = both_ref[0]
+    output_ref[...] = both_out[0]
     gate_ref[...] = gu_ref[0, :, :units].astype(jnp.float32)
     up_ref[...] = gu_ref[0, :, units:].astype(jnp.float32)
     d_ref[...] = down_ref[0].astype(jnp.float32).T
@@ -1247,7 +1402,7 @@
             group_ref[head : head + 1, :] = sums_ref[row : row + 1, lane : lane + HP]
 
 
-def unpack_all(back, bc_all, sums, shapes):
+def unpack_all(back, bc_all, both, sums, shapes):
     gu, down, out, in_all = back
 
     def per_chip(array, rows=1):
@@ -1265,6 +1420,13 @@
     misc_block = (GROUP, in_all.shape[1], HD)
     kinds = [across, across, down_along, down_along, down_along, across, across, across, across]
     kinds += [once] * (len(shapes) - len(kinds))
+    out_shape = [jax.ShapeDtypeStruct(shape, jnp.float32) for shape in shapes]
+    rows, width = both[0].shape[1:]
+    step = 2 * rows // GROUP
+    rows_in = pl.BlockSpec((1, step, width), lambda chip: (chip // 2, lax.rem(chip, 2), 0))
+    out_shape += [jax.ShapeDtypeStruct((2 * rows, width), array.dtype) for array in both]
+    out_specs = [kind(shape) for kind, shape in zip(kinds, shapes)]
+    out_specs += [pl.BlockSpec((step, width), lambda chip: (chip, 0))] * 2
     return pl.pallas_call(
         unpack_kernel,
         grid=(GROUP,),
@@ -1275,14 +1437,16 @@
             per_chip(in_all),
             per_chip(bc_all, 2),
             pl.BlockSpec(misc_block, lambda chip: (0, 0, in_all.shape[2] // HD - 1)),
+            rows_in,
+            rows_in,
             once(sums.shape),
         ],
-        out_specs=[kind(shape) for kind, shape in zip(kinds, shapes)],
-        out_shape=[jax.ShapeDtypeStruct(shape, jnp.float32) for shape in shapes],
+        out_specs=out_specs,
+        out_shape=out_shape,
         scratch_shapes=[pltpu.VMEM((8, 2 * GROUP * sums.shape[2]), jnp.float32)],
         cost_estimate=lasting(8),
         compiler_params=pltpu.CompilerParams(vmem_limit_bytes=VMEM_BYTES),
-    )(gu, down, out, in_all, bc_all, in_all, sums)
+    )(gu, down, out, in_all, bc_all, in_all, *both, sums)
 
 
 def push_moves(moves, sources, targets, local_sems, send_sems, recv_sems, first=0):
@@ -1585,6 +1749,7 @@
     ssm_ref,
     states_ref,
     mixed_ref,
+    slope_ref,
     kv_ref,
     state,
 ):
@@ -1599,7 +1764,9 @@
         lanes = slice(2 * HP * block, 2 * HP * (block + 1))
         windows = conv_windows(block, proj_ref, before_ref, bc_ref, bc_before_ref)
         summed = conv_sum(windows, taps_ref, lanes, keeps)
-        mixed_ref[:, lanes] = (summed * jax.nn.sigmoid(summed)).astype(jnp.bfloat16)
+        sigmoid = jax.nn.sigmoid(summed)
+        mixed_ref[:, lanes] = (summed * sigmoid).astype(jnp.bfloat16)
+        slope_ref[:, lanes] = sigmoid * (1.0 + summed * (1.0 - sigmoid))
     raw, dt_rows, cumul, enter_all, leave_bare = chunk_decays(proj_ref, heads_ref, keeps_ref)
     enter_all, leave_all = spread_heads(enter_all, leave_bare * dt_rows)
     cumul_t, dt_t = cumul.T, dt_rows.T
@@ -1645,9 +1812,8 @@
 def ssd_backward_kernel(
     moves,
     proj_ref,
-    before_ref,
+    slope_ref,
     bc_ref,
-    bc_before_ref,
     taps_ref,
     heads_ref,
     keeps_ref,
@@ -1660,6 +1826,12 @@
     states_ref,
     dgated_ref,
     dq_ref,
+    kv_own_ref,
+    kv_x_ref,
+    kv_y_ref,
+    kv_a_ref,
+    cos_ref,
+    sin_ref,
     gu_ref,
     down_ref,
     dproj_ref,
@@ -1752,11 +1924,11 @@
             d_gram = d_gram + d_mix * (decay * dt_t[lane : lane + 1, :])
         gram_high, gram_low = halves(jnp.concatenate(grams, axis=0))
         bare_x = dot_f32(
+            jnp.concatenate([high, low, high], axis=0),
             jnp.concatenate([gram_high, gram_high, gram_low], axis=0),
-            jnp.concatenate([high, low, high], axis=0),
             0,
             0,
-        )
+        ).T
         left = bare * d_weighted[:, lanes]
         d_x = bare_x + left
         first_lane = DT_LANE + 2 * pair
@@ -1802,29 +1974,36 @@
     dheads_ref[0:1] += jnp.sum(d_raw, axis=0, keepdims=True)
     dheads_ref[1:2] += -rate * jnp.sum(d_log * dt_rows, axis=0, keepdims=True)
     total = proj_ref.shape[1]
+    d_kv = kv_own_ref[...].astype(jnp.float32)
+    for ref in (kv_x_ref, kv_y_ref, kv_a_ref):
+        d_kv = d_kv + ref[...].astype(jnp.float32)
+    d_kv = turn_folded(d_kv, cos_ref[...], -sin_ref[...])
+    d_kv = jnp.concatenate([d_kv[:, :DT_LANE], d_kv[:, DT_LANE:]], axis=0)
     dproj_ref[:, total - 2 * HP : total] = jnp.concatenate(
-        [jnp.zeros((size, DT_LANE), jnp.bfloat16), d_raw[:, DT_LANE:].astype(jnp.bfloat16)], axis=1
-    )
+        [d_kv, d_raw[:, DT_LANE:]], axis=1
+    ).astype(jnp.bfloat16)
     dproj_ref[:, width : width + HD] = dq_ref[...]
 
     keeps = wide_keeps(keeps_ref)
     for block in range(mixed_ref.shape[1] // (2 * HP)):
         lanes = slice(2 * HP * block, 2 * HP * (block + 1))
-        windows = conv_windows(block, proj_ref, before_ref, bc_ref, bc_before_ref)
-        summed = conv_sum(windows, taps_ref, lanes, keeps)
-        sigmoid = jax.nn.sigmoid(summed)
-        d_sum = d_mixed[:, lanes] * (sigmoid * (1.0 + summed * (1.0 - sigmoid)))
+        if block < HEADS // 2:
+            start = total - 2 * HP * (1 + HEADS // 2 - block)
+            pre = proj_ref[:, start : start + 2 * HP].astype(jnp.bfloat16).astype(jnp.float32)
+        else:
+            start = 2 * HP * (block - HEADS // 2)
+            pre = bc_ref[:, start : start + 2 * HP].astype(jnp.float32)
+        d_sum = d_mixed[:, lanes] * slope_ref[:, lanes]
         dtaps_ref[KC : KC + 1, lanes] += jnp.sum(d_sum, axis=0, keepdims=True)
-        dtaps_ref[KC - 1 : KC, lanes] += jnp.sum(d_sum * windows[0], axis=0, keepdims=True)
+        dtaps_ref[KC - 1 : KC, lanes] += jnp.sum(d_sum * pre, axis=0, keepdims=True)
         d_pre = taps_ref[KC - 1 : KC, lanes] * d_sum
         for back in range(1, KC):
             tap = KC - 1 - back
             kept = d_sum * keeps[back]
-            dtaps_ref[tap : tap + 1, lanes] += jnp.sum(
-                kept * windows[back], axis=0, keepdims=True
-            )
             extended = jnp.concatenate([kept, next_rows[back - 1, :, lanes]], axis=0)
-            d_pre = d_pre + taps_ref[tap : tap + 1, lanes] * extended[back : back + size]
+            later_rows = extended[back : back + size]
+            dtaps_ref[tap : tap + 1, lanes] += jnp.sum(later_rows * pre, axis=0, keepdims=True)
+            d_pre = d_pre + taps_ref[tap : tap + 1, lanes] * later_rows
             next_rows[back - 1, :, lanes] = kept[:8]
         if block < HEADS // 2:
             start = total - 2 * HP * (1 + HEADS // 2 - block)
@@ -1888,6 +2067,7 @@
             tall(width),
             slab(NS, width),
             tall(width_all),
+            tall(width_all),
             fold,
         ],
         out_shape=[
@@ -1895,6 +2075,7 @@
             shaped((length, width), jnp.float32),
             shaped((laps, NS, width), jnp.float32),
             shaped((length, width_all), jnp.bfloat16),
+            shaped((length, width_all), jnp.float32),
             shaped((length // 2, 2 * HP), jnp.bfloat16),
         ],
         scratch_shapes=[pltpu.VMEM((NS, width), jnp.float32)],
@@ -1903,16 +2084,17 @@
     )(*arrays, cos_part, sin_part)
 
 
-def ssd_backward(arrays, mixed, ssm, states, d_outs, d_query, grads):
+def ssd_backward(arrays, slope, mixed, ssm, states, d_outs, d_query, d_kv_parts, tables, grads):
     length, width_in = arrays[0].shape
     width, width_all = HEADS * HP, HEADS * HP + 2 * NS
     laps, tall, whole, slab, specs = ssd_specs(length, True, width_in, width_all, width)
     shaped = jax.ShapeDtypeStruct
     moves = (block_move(0, 0), block_move(1, 1))
+    fold = pl.BlockSpec((CHUNK // 2, 2 * HP), lambda lap: (laps - 1 - lap, 0))
     return pl.pallas_call(
         partial(ssd_backward_kernel, moves),
         grid=(laps,),
-        in_specs=specs
+        in_specs=[specs[0], tall(width_all), specs[2], *specs[4:]]
         + [
             tall(width_all),
             tall(width),
@@ -1920,6 +2102,7 @@
             tall(width),
             tall(HD),
         ]
+        + [fold] * 6
         + any_specs(2),
         out_specs=[
             tall(width_in + 2 * NS),
@@ -1949,7 +2132,7 @@
         compiler_params=pltpu.CompilerParams(
             collective_id=13, has_side_effects=True, vmem_limit_bytes=VMEM_BYTES
         ),
-    )(*arrays, mixed, ssm, states, d_outs, d_query, *grads)
+    )(arrays[0], slope, arrays[2], *arrays[4:], mixed, ssm, states, d_outs, d_query, *d_kv_parts, *tables, *grads)
 
 
 QUERY_ROWS = 256
@@ -2099,41 +2282,6 @@
     return values * cosine + other * sine_part
 
 
-def place_kv_kernel(lane_ref, cos_ref, sin_ref, *refs):
-    parts, out_ref = refs[:-1], refs[-1]
-    total = parts[0][...].astype(jnp.float32)
-    for part in parts[1:]:
-        total = total + part[...].astype(jnp.float32)
-    half = HD // 2
-    total = turn_folded(total, cos_ref[...], -sin_ref[...])
-
-    def write(start, values):
-        out_ref[start : start + values.shape[0], :half] = values.astype(jnp.bfloat16)
-
-    unfold_rows(total, write)
-    out_ref[:, half:] = lane_ref[:, half:]
-
-
-def place_kv(d_projected, parts, cos_part, sin_part, width_in):
-    length = d_projected.shape[0]
-    lanes = pl.BlockSpec((length, HD), lambda step: (0, width_in // HD - 1))
-
-    def whole(array):
-        return pl.BlockSpec(array.shape, lambda step: (0, 0))
-
-    arrays = (cos_part, sin_part, *parts)
-    return pl.pallas_call(
-        place_kv_kernel,
-        grid=(1,),
-        in_specs=[lanes] + [whole(array) for array in arrays],
-        out_specs=lanes,
-        out_shape=jax.ShapeDtypeStruct(d_projected.shape, d_projected.dtype),
-        input_output_aliases={0: 0},
-        cost_estimate=lasting(3),
-        compiler_params=pltpu.CompilerParams(vmem_limit_bytes=VMEM_BYTES),
-    )(d_projected, *arrays)
-
-
 def whole_block(shape):
     return pl.BlockSpec(shape, lambda step: (0,) * len(shape))
 
@@ -2322,7 +2470,7 @@
         skip_row,
         gain_row,
     )
-    gated, ssm, states, mixed, kv_own = ssd_forward(ssd_arrays, cos_folded, sin_folded)
+    gated, ssm, states, mixed, slope, kv_own = ssd_forward(ssd_arrays, cos_folded, sin_folded)
     kv_all = over_chips(kv_own)
     gu_gathered = lax.all_gather(after(gu_slices, out_gathered, gated), "dp", axis=0, tiled=True)
     down_gathered = lax.all_gather(after(down_slices, gu_gathered), "dp", axis=0, tiled=True)
@@ -2358,32 +2506,19 @@
         (full_gu,),
         (((length, 2 * hidden_units), jnp.float32), ((length, hidden_units), bf16)),
     )
-    block_out = middle + scatter_plane(activated, full_down, 2)[0]
     teacher_own = lax.dynamic_slice(teacher[0], (core * own_rows, 0), (own_rows, width))
-    d_out = (
-        2.0
-        * total_tokens
-        / token_count
-        * mask_rows.astype(jnp.float32)[:, None]
-        * (block_out - teacher_own.astype(jnp.float32))
-    )
-    d_mlp, d_gate_up = gather_plane(
-        d_out.astype(bf16),
-        10,
-        apply_down_back,
-        (full_down, gate_up),
-        (((length, 2 * hidden_units), bf16),),
+    factor = 2.0 * total_tokens / token_count * mask_rows.astype(jnp.float32)[:, None]
+    block_out, d_out, d_mlp, d_gate_up, grad_down = down_and_back(
+        activated, full_down, middle, teacher_own, factor, gate_up
     )
 
     def sum_rows(grads):
         summed = lax.psum_scatter(grads.astype(bf16), "dp", scatter_dimension=0, tiled=True)
         return summed.reshape(GROUP, slice_rows, grads.shape[1])
 
-    grad_down = sum_rows(dot_left_t(d_mlp, activated))
-    d_normed_two = scatter_plane(d_gate_up, full_gu, 11)[0]
-    grad_gate_up = sum_rows(
-        after(dot_left_t(normed_two, d_gate_up).astype(bf16), grad_down, d_normed_two)
-    )
+    grad_down = sum_rows(grad_down)
+    d_normed_two, grad_gate_up = up_back(d_gate_up, full_gu, normed_two)
+    grad_gate_up = sum_rows(after(grad_gate_up, grad_down))
     grad_gain_two = jnp.sum(d_normed_two * middle * scale_two, axis=0)
     d_scaled = d_normed_two * gain_two
     d_middle = (
@@ -2427,10 +2562,17 @@
         back_gate_up,
         back_down,
     ) = ssd_backward(
-        ssd_arrays, mixed, ssm, states, d_gated, d_query, (grad_gate_up, grad_down)
-    )
-    d_kv_parts = lax.optimization_barrier((d_projected, *d_kv_parts))[1:]
-    d_projected = place_kv(d_projected, d_kv_parts, cos_folded, sin_folded, width_in)
+        ssd_arrays,
+        slope,
+        mixed,
+        ssm,
+        states,
+        d_gated,
+        d_query,
+        d_kv_parts,
+        (cos_folded, sin_folded),
+        (grad_gate_up, grad_down),
+    )
     grad_skip = jnp.sum(d_skip_lanes.reshape(HEADS, HP), axis=-1)
     grad_group = d_gain_lanes.reshape(HEADS, HP)
     grad_in = sum_rows(
@@ -2472,9 +2614,7 @@
     small = jnp.concatenate(small, axis=1)
     small_width = -(-small.shape[1] // (2 * GROUP * 128)) * 2 * GROUP * 128
     small = jnp.pad(small, ((0, 0), (0, small_width - small.shape[1])))
-    piece, both_input, both_output, back_out = plane_sum(
-        small, grad_input, block_out.astype(bf16), grad_out
-    )
+    piece, both_input, both_output, back_out = plane_sum(small, grad_input, block_out, grad_out)
     small_all, bc_all, back_in = finish_all(piece, bc_sum, grad_in)
     bc_all = bc_all.reshape(2 * GROUP, bc_cols, width // 2)
     shapes = [
@@ -2517,19 +2657,25 @@
         grad_group,
         grad_one,
         grad_two,
+        grad_input,
+        block_out,
     ) = unpack_all(
-        (back_gate_up, back_down, back_out, back_in), bc_all, small_all, shapes
+        (back_gate_up, back_down, back_out, back_in),
+        bc_all,
+        (both_input, both_output),
+        small_all,
+        shapes,
     )
     return (
-        both_output.reshape(1, chip_rows, width),
-        both_input.reshape(1, chip_rows, width),
+        block_out[None],
+        grad_input[None],
         grad_one[0],
         grad_z,
         grad_x,
         grad_bc,
         grad_dt.T,
         grad_conv.T,
-        grad_bias[0],
+        grad_bias.reshape(-1),
         grad_dtb[0],
         grad_alog[0],
         grad_skip[0],

time: 683 us -> 663 us (0.971)
  matrix products: 50.4 us -> 31 us
    pallas_call x1 -> x2, Pallas kernels: 2.73 us -> 115 us  [the longest x1 73.4 us: down_and_back(): pl.pallas_call(down_and_back_kernel, out_shape=[shaped((rows, width), jnp...]
    pallas_call x4 -> x2, Pallas kernels: 159 us -> 86.3 us  [scatter_plane(): pl.pallas_call(partial(scatter_kernel, count), out_shape=shapes, in_specs...]
    pallas_call x4 -> x3, Pallas kernels: 148 us -> 111 us  [gather_plane(): pl.pallas_call(partial(gather_kernel, apply, len(inputs), len(outputs)),...]
    dot_general x4 -> x2, matrix products: 38.7 us -> 19.2 us  [dot_left_t(): lax.dot_general(left_side, right_side, (((0,), (0,)), ((), ())), preferre...]
    unnamed x87 -> x75, local copies, waits for them, and re-layouts: 15.2 us -> 9.38 us
  transfers between devices with their start and end apart: 14 -> 14, of which waited for: 8 -> 9; matrix products, arithmetic and copies ran while one was open for 12% -> 10% of each run, Pallas kernels for 52% -> 54%
where the time goes in v4:
time: 663 us; the launch traced here: 654 us
  Pallas kernels  494 us (75%)
  waiting for transfers between devices  63.3 us (10%)
  matrix products  31 us (5%)
  local copies, waits for them, and re-layouts  26.7 us (4%)
  between operations  16 us (2%)
  other arithmetic  14.9 us (2%)
  starting transfers between devices  8.31 us (1%)
    pallas_call x3, Pallas kernels, gather_plane(): pl.pallas_call(partial(gather_kernel, apply, len(inputs), len(outputs)),...  111 us
    pallas_call x2, Pallas kernels, scatter_plane(): pl.pallas_call(partial(scatter_kernel, count), out_shape=shapes, in_specs...  86.3 us
    pallas_call x1, Pallas kernels, down_and_back(): pl.pallas_call(down_and_back_kernel, out_shape=[shaped((rows, width), jnp...  73.4 us
    pallas_call x1, Pallas kernels, up_back(): pl.pallas_call(up_back_kernel, out_shape=[jax.ShapeDtypeStruct((rows, wid...  41.2 us
    pallas_call x1, Pallas kernels, ssd_backward(): pl.pallas_call(partial(ssd_backward_kernel, moves), grid=(laps,), in_spec...  36.8 us
    pallas_call x1, Pallas kernels, finish_all(): pl.pallas_call(finish_kernel, out_shape=[shaped((places,) + piece.shape,...  32.5 us
    pallas_call x1, Pallas kernels, exchange_plane(): pl.pallas_call(partial(exchange_kernel, moves, len(arrays)), out_shape=[j...  27.6 us
    pallas_call x1, Pallas kernels, first_exchange(): pl.pallas_call(partial(first_exchange_kernel, moves), out_shape=[jax.Shap...  22.4 us
  transfers between devices with their start and end apart: 14, of which 9 were waited for; matrix products, arithmetic and copies ran while one was open for 10% of the time, Pallas kernels for 54%

profile of v4, /device:TPU:0, one launch (start us, length us, event | category | flops | bytes accessed | tf_op | source)
XLA Modules:
  0.0 654.0 jit_solution(8767633850664609333)
XLA Ops:
  7.3 22.4 %shard_map.435 = (bf16[4,128,1024]{2,1,0:T(8,128)(2,1)}, f32[16,8,128]{2,1,0:T(8,128)}) custom-call(bf16[128,1536]{1,0:T(8,128)(2,1)} %z_ref.1, bf16[128,512]{1,0:T(8,128)(2,1)} %q_ref.1, bf16[128,1536]{1,0:T(8,128)(2,1)} %x_ref.1, bf16[128,128]{1,0:T(8,128)(2,1)} %key_ref.1, bf16[128,128]{1,0:T(8,128)(2,1)} %value_ref.1, bf16[24,128]{1,0:T(8,128)(2,1)} %bitcast.97, ...), custom_call_target="tpu_custom_call" | custom-call | flops 17999998976 | bytes 60000000 | tf_op jit(solution)/shard_map/pallas_call | solution.py:1544
  33.2 37.2 %shard_map.436 = (bf16[8,192,2048]{2,1,0:T(8,128)(2,1)}, bf16[1536,2048]{1,0:T(8,128)(2,1)}, bf16[1536,512]{1,0:T(8,128)(2,1)}) custom-call(bf16[192,2048]{1,0:T(8,128)(2,1)} %dynamic-slice_bitcast_fusion.1.own_ref, f32[1,2048]{1,0:T(1,128)} %get-tuple-element.214.refs_0_, bf16[2048,512]{1,0:T(8,128)(2,1)} %refs_1_.3), custom_call_target="tpu_custom_call" | custom-call | flops 31499999232 | bytes 105000000 | tf_op jit(solution)/shard_map/pallas_call | solution.py:770
  72.3 27.6 %shard_map.437 = (bf16[4,128,512]{2,1,0:T(8,128)(2,1)}, bf16[4,128,1024]{2,1,0:T(8,128)(2,1)}, bf16[4,128,512]{2,1,0:T(8,128)(2,1)}) custom-call(bf16[128,1536]{1,0:T(8,128)(2,1)} %bitcast.78, bf16[128,512]{1,0:T(8,128)(2,1)} %bitcast.82, bf16[128,2048]{1,0:T(8,128)(2,1)} %refs_2_.1, bf16[128,2048]{1,0:T(8,128)(2,1)} %refs_3_.1, bf16[128,2048]{1,0:T(8,128)(2,1)} %bitcast.75), custom_call_target="tpu_custom_call" | custom-call | flops 22499999744 | bytes 75000000 | tf_op jit(solution)/shard_map/pallas_call | solution.py:1566
  101.3 7.4 %all-gather.5.cloned.1.call-done = bf16[16,128,1024]{2,1,0:T(8,128)(2,1)} async-done(((bf16[4,128,1024]{2,1,0:T(8,128)(2,1)}), bf16[16,128,1024]{2,1,0:T(8,128)(2,1)}) %all-gather.5.cloned.1.call-update) | async-done | bytes 4194320 | tf_op jit(solution)/shard_map/all_gather | solution.py:2388
  114.8 2.1 dynamic-slice_bitcast_fusion.2
  116.9 11.8 %fusion.11.proj_ref.before_ref.raw_ref = f32[1536,1024]{1,0:T(8,128)} fusion(bf16[1536,2048]{1,0:T(8,128)(2,1)} %get-tuple-element.114.refs_0_, bf16[2048,1024]{1,0:T(8,128)(2,1)} %bitcast.86), kind=kOutput, calls=%fused_computation.72 | convolution fusion | flops 6442450944 | bytes 16777216 | tf_op jit(solution)/shard_map/dot_general | solution.py:47
  128.7 18.5 %shard_map.438 = (bf16[1536,384]{1,0:T(8,128)(2,1)}, f32[1536,384]{1,0:T(8,128)}, f32[12,256,384]{2,1,0:T(8,128)}, bf16[1536,896]{1,0:T(8,128)(2,1)}, f32[1536,896]{1,0:T(8,128)}, /*index=5*/bf16[768,128]{1,0:T(8,128)(2,1)}) custom-call(f32[1536,1024]{1,0:T(8,128)} %fusion.11.proj_ref.before_ref.raw_ref, f32[1536,1024]{1,0:T(8,128)} %fusion.11.proj_ref.before_ref.raw_ref, ...), custom_call_target="tpu_custom_call" | custom-call | flops 5400000000 | bytes 18000000 | tf_op jit(solution)/shard_map/pallas_call | solution.py:2061
  147.2 7.5 %all-gather.7.cloned.1.call-done = bf16[16,128,512]{2,1,0:T(8,128)(2,1)} async-done(((bf16[4,128,512]{2,1,0:T(8,128)(2,1)}), bf16[16,128,512]{2,1,0:T(8,128)(2,1)}) %all-gather.7.cloned.1.call-update) | async-done | bytes 2097168 | tf_op jit(solution)/shard_map/all_gather | solution.py:2416
  162.8 4.0 collective-permute-done
  166.9 4.2 collective-permute-done.1
  172.1 9.0 %shard_map.439 = (bf16[1536,128]{1,0:T(8,128)(2,1)}, f32[1536,1]{1,0:T(8,128)}, bf16[1536,128]{1,0:T(8,128)(2,1)}, bf16[1536,128]{1,0:T(8,128)(2,1)}, bf16[1536,128]{1,0:T(8,128)(2,1)}) custom-call(f32[1536,1024]{1,0:T(8,128)} %fusion.11.proj_ref.before_ref.raw_ref, f32[1536,128]{1,0:T(8,128)} %constant.102.clone.cos_ref, ...), custom_call_target="tpu_custom_call" | custom-call | flops 8099999744 | bytes 27000000 | tf_op jit(solution)/shard_map/pallas_call | solution.py:2290
  183.3 35.4 %shard_map.440 = f32[192,2048]{1,0:T(8,128)} custom-call(bf16[1536,512]{1,0:T(8,128)(2,1)} %copy-done.10, bf16[2048,512]{1,0:T(8,128)(2,1)} %bitcast.90), custom_call_target="tpu_custom_call" | custom-call | flops 31499999232 | bytes 105000000 | tf_op jit(solution)/shard_map/pallas_call | solution.py:1092
  218.7 2.4 multiply_reduce_fusion.2
  221.1 14.8 %all-gather.9.cloned.1.call-done = bf16[16,128,1024]{2,1,0:T(8,128)(2,1)} async-done(((bf16[4,128,1024]{2,1,0:T(8,128)(2,1)}), bf16[16,128,1024]{2,1,0:T(8,128)(2,1)}) %all-gather.9.cloned.1.call-update) | async-done | bytes 4194320 | tf_op jit(solution)/shard_map/all_gather | solution.py:2475
  237.2 38.3 %shard_map.441 = (bf16[8,192,2048]{2,1,0:T(8,128)(2,1)}, f32[1536,1024]{1,0:T(8,128)}, bf16[1536,512]{1,0:T(8,128)(2,1)}) custom-call(bf16[192,2048]{1,0:T(8,128)(2,1)} %multiply_convert_fusion.own_ref, bf16[2048,1024]{1,0:T(8,128)(2,1)} %bitcast.88), custom_call_target="tpu_custom_call" | custom-call | flops 31499999232 | bytes 105000000 | tf_op jit(solution)/shard_map/pallas_call | solution.py:770
  275.5 6.3 all-gather.11.cloned.1.call-done
  281.8 73.4 %shard_map.442 = (bf16[192,2048]{1,0:T(8,128)(2,1)}, f32[192,2048]{1,0:T(8,128)}, bf16[8,192,2048]{2,1,0:T(8,128)(2,1)}, bf16[1536,1024]{1,0:T(8,128)(2,1)}, bf16[2048,512]{1,0:T(8,128)(2,1)}) custom-call(bf16[1536,512]{1,0:T(8,128)(2,1)} %get-tuple-element.137.act_ref, bf16[2048,512]{1,0:T(8,128)(2,1)} %bitcast.92, f32[192,2048]{1,0:T(8,128)} %copy-done.2, ...), custom_call_target="tpu_custom_call" | custom-call | flops 62999998464 | bytes 210000000 | tf_op jit(solution)/shard_map/pallas_call | solution.py:1011
  355.3 41.2 %shard_map.443 = (f32[192,2048]{1,0:T(8,128)}, bf16[2048,1024]{1,0:T(8,128)(2,1)}) custom-call(bf16[1536,1024]{1,0:T(8,128)(2,1)} %get-tuple-element.142.d_both_ref, bf16[2048,1024]{1,0:T(8,128)(2,1)} %bitcast.89, bf16[1536,2048]{1,0:T(8,128)(2,1)} %bitcast.101), custom_call_target="tpu_custom_call" | custom-call | flops 34200000512 | bytes 114000000 | tf_op jit(solution)/shard_map/pallas_call | solution.py:1052
  403.1 35.9 %shard_map.444 = (bf16[8,192,2048]{2,1,0:T(8,128)(2,1)}, f32[1536,384]{1,0:T(8,128)}, bf16[1536,128]{1,0:T(8,128)(2,1)}) custom-call(bf16[192,2048]{1,0:T(8,128)(2,1)} %get-tuple-element.146.own_ref, bf16[2048,512]{1,0:T(8,128)(2,1)} %bitcast.91), custom_call_target="tpu_custom_call" | custom-call | flops 31499999232 | bytes 105000000 | tf_op jit(solution)/shard_map/pallas_call | solution.py:770
  438.9 9.3 %shard_map.445 = (bf16[1536,128]{1,0:T(8,128)(2,1)}, bf16[4,768,128]{2,1,0:T(8,128)(2,1)}) custom-call(bf16[1536,128]{1,0:T(8,128)(2,1)} %get-tuple-element.148.q_ref, bf16[1536,128]{1,0:T(8,128)(2,1)} %get-tuple-element.149.k_ref, bf16[1536,128]{1,0:T(8,128)(2,1)} %get-tuple-element.150.v_ref, f32[1536,128]{1,0:T(8,128)} %constant.102.clone.cos_ref, ...), custom_call_target="tpu_custom_call" | custom-call | flops 8099999744 | bytes 27000000 | tf_op jit(solution)/shard_map/pallas_call | solution.py:2290
  448.2 2.1 dynamic-slice_bitcast_fusion.4
  453.8 7.6 %convolution_convert_fusion.1 = bf16[2048,512]{1,0:T(8,128)(2,1)} fusion(bf16[1536,2048]{1,0:T(8,128)(2,1)} %bitcast.100, bf16[1536,512]{1,0:T(8,128)(2,1)S(1)} %copy-done.11), kind=kOutput, calls=%fused_computation.7 | convolution fusion | flops 3222274048 | bytes 9961472 | tf_op jit(solution)/shard_map/dot_general | solution.py:51
  461.4 14.9 %reduce-scatter.7.cloned.1.call-done = bf16[512,1024]{1,0:T(8,128)(2,1)} async-done(((bf16[2048,1024]{1,0:T(8,128)(2,1)}), bf16[512,1024]{1,0:T(8,128)(2,1)}) %reduce-scatter.7.cloned.1.call-update) | async-done | bytes 1048592 | tf_op jit(solution)/shard_map/reduce_scatter | solution.py:2516
  477.4 36.8 %shard_map.446 = (bf16[1536,1536]{1,0:T(8,128)(2,1)}, f32[8,896]{1,0:T(8,128)}, f32[8,128]{1,0:T(8,128)}, f32[1,384]{1,0:T(1,128)}, f32[1,384]{1,0:T(1,128)}, /*...) custom-call(f32[1536,1024]{1,0:T(8,128)} %fusion.11.proj_ref.before_ref.raw_ref, ...), custom_call_target="tpu_custom_call" | custom-call | flops 43200000000 | bytes 144000000 | tf_op jit(solution)/shard_map/pallas_call | solution.py:2094
  514.2 11.6 %convolution_convert_fusion = bf16[2048,1024]{1,0:T(8,128)(2,1)} fusion(bf16[1536,2048]{1,0:T(8,128)(2,1)} %get-tuple-element.114.refs_0_, bf16[1536,1536]{1,0:T(8,128)(2,1)} %get-tuple-element.165.left_ref), kind=kOutput, calls=%fused_computation | convolution fusion | flops 6444548096 | bytes 13631488 | tf_op jit(solution)/shard_map/dot_general | solution.py:51
  528.3 50.9 %shard_map.447 = (f32[192,2048]{1,0:T(8,128)}, f32[128,1024]{1,0:T(8,128)}) custom-call(bf16[1536,1536]{1,0:T(8,128)(2,1)} %get-tuple-element.165.left_ref, bf16[2048,1024]{1,0:T(8,128)(2,1)} %bitcast.87, bf16[1536,2048]{1,0:T(8,128)(2,1)} %get-tuple-element.114.refs_0_, bf16[2048,512]{1,0:T(8,128)(2,1)} %refs_1_.3), custom_call_target="tpu_custom_call" | custom-call | flops 31499999232 | bytes 105000000 | tf_op jit(solution)/shard_map/pallas_call | solution.py:1092
  579.1 1.8 fusion.6
  581.7 3.0 fusion.5.own_ref
  584.7 14.8 %shard_map.448 = (f32[8,640]{1,0:T(8,128)}, f32[2,192,2048]{2,1,0:T(8,128)}, bf16[2,192,2048]{2,1,0:T(8,128)(2,1)}, bf16[4,128,512]{2,1,0:T(8,128)(2,1)}) custom-call(f32[8,5120]{1,0:T(8,128)} %pad.15.small_ref, f32[192,2048]{1,0:T(8,128)} %fusion.5.own_ref, bf16[192,2048]{1,0:T(8,128)(2,1)} %get-tuple-element.168.out_ref, bf16[4,128,512]{2,1,0:T(8,128)(2,1)} %bitcast.95), custom_call_target="tpu_custom_call" | custom-call | flops 17999998976 | bytes 60000000 | tf_op jit(solution)/shard_map/pallas_call | solution.py:1154
  599.5 2.6 reduce-scatter.11.cloned.1.call-done
  602.1 32.5 %shard_map.449 = (f32[8,8,640]{2,1,0:T(8,128)}, bf16[8,4,32,1024]{3,2,1,0:T(8,128)(2,1)}, bf16[4,128,1024]{2,1,0:T(8,128)(2,1)}) custom-call(f32[8,640]{1,0:T(8,128)} %get-tuple-element.170.piece_ref, f32[128,1024]{1,0:T(8,128)} %get-tuple-element.171.bc_ref, bf16[4,128,1024]{2,1,0:T(8,128)(2,1)} %bitcast.94), custom_call_target="tpu_custom_call" | custom-call | flops 27000000512 | bytes 90000000 | tf_op jit(solution)/shard_map/pallas_call | solution.py:1285
  634.6 10.7 %shard_map.450 = (f32[128,2048]{1,0:T(8,128)}, f32[128,2048]{1,0:T(8,128)}, f32[2048,128]{1,0:T(8,128)}, f32[1536,128]{1,0:T(8,128)}, f32[512,128]{1,0:T(8,128)}...) custom-call(bf16[4,128,1024]{2,1,0:T(8,128)(2,1)} %get-tuple-element, ...), custom_call_target="tpu_custom_call" | custom-call | flops 7200000000 | bytes 24000000 | tf_op jit(solution)/shard_map/pallas_call | solution.py:1430
  (177 shorter events, 40.1 us)
Async XLA Ops:
  7.2 22.5 %copy-start = (bf16[1,384,2048]{2,1,0:T(8,128)(2,1)S(1)}, bf16[1,384,2048]{2,1,0:T(8,128)(2,1)}, u32[]{:S(2)}) copy-start(bf16[1,384,2048]{2,1,0:T(8,128)(2,1)} %param.28) | copy-start | bytes 4718596
  7.2 101.5 %all-gather.5.cloned.1.call-start = ((), (), s32[]{:S(2)}) async-start(), calls=%async_computation.4 | async-start | bytes 5242880 | tf_op jit(solution)/shard_map/all_gather | solution.py:2388
  29.7 125.1 %all-gather.7.cloned.1.call-start = ((), (), s32[]{:S(2)}) async-start(), calls=%async_computation.5 | async-start | bytes 2621440 | tf_op jit(solution)/shard_map/all_gather | solution.py:2416
  33.2 37.2 %copy-start.17 = (bf16[512,128]{1,0:T(8,128)(2,1)S(1)}, bf16[512,128]{1,0:T(8,128)(2,1)}, u32[]{:S(2)}) copy-start(bf16[512,128]{1,0:T(8,128)(2,1)} %param.47) | copy-start | bytes 393220
  33.2 38.0 %copy-start.13 = (bf16[2048,128]{1,0:T(8,128)(2,1)S(1)}, bf16[2048,128]{1,0:T(8,128)(2,1)}, u32[]{:S(2)}) copy-start(bf16[2048,128]{1,0:T(8,128)(2,1)} %param.51) | copy-start | bytes 1572868
  72.2 27.6 %copy-start.22 = (f32[3584]{0:T(1024)S(1)}, f32[3584]{0:T(1024)}, u32[]{:S(2)}) copy-start(f32[3584]{0:T(1024)} %param.38) | copy-start | bytes 43012
  72.3 28.0 %copy-start.27 = (f32[48]{0:T(128)S(1)}, f32[48]{0:T(128)}, u32[]{:S(2)}) copy-start(f32[48]{0:T(128)} %param.40) | copy-start | bytes 580
  72.3 28.0 %copy-start.28 = (f32[48]{0:T(128)S(1)}, f32[48]{0:T(128)}, u32[]{:S(2)}) copy-start(f32[48]{0:T(128)} %param.39) | copy-start | bytes 580
  72.3 28.7 %slice-start.1 = ((f32[3584]{0:T(1024)}), f32[512]{0:T(512)S(1)}, s32[]{:S(2)}) async-start(f32[3584]{0:T(1024)} %param.38), calls=%async_computation.13 | async-start | bytes 4096 | tf_op jit(solution)/shard_map/slice | solution.py:2435
  72.3 28.8 %copy-start.19 = (f32[3584,4]{0,1:T(4,128)S(1)}, f32[3584,4]{0,1:T(4,128)}, u32[]{:S(2)}) copy-start(f32[3584,4]{0,1:T(4,128)} %param.37) | copy-start | bytes 172036
  99.8 12.9 %copy-start.32 = (f32[48]{0:T(128)S(1)}, f32[48]{0:T(128)}, u32[]{:S(2)}) copy-start(f32[48]{0:T(128)} %param.41) | copy-start | bytes 580
  99.9 14.3 %slice-start = ((f32[3584,4]{0,1:T(4,128)}), f32[512,4]{0,1:T(4,128)S(1)}, s32[]{:S(2)}) async-start(f32[3584,4]{0,1:T(4,128)} %param.37), calls=%async_computation.12 | async-start | bytes 16384 | tf_op jit(solution)/shard_map/slice | solution.py:2435
  108.7 127.1 %all-gather.9.cloned.1.call-start = ((), (), s32[]{:S(2)}) async-start(), calls=%async_computation.6 | async-start | bytes 5242880 | tf_op jit(solution)/shard_map/all_gather | solution.py:2475
  128.7 27.3 %copy-start.21 = (s32[4,1536]{1,0:T(4,128)S(1)}, s32[4,1536]{1,0:T(4,128)}, u32[]{:S(2)}) copy-start(s32[4,1536]{1,0:T(4,128)} %param.31) | copy-start | bytes 73732
  128.7 29.4 %copy-start.14 = (bf16[1,384,2048]{2,1,0:T(8,128)(2,1)S(1)}, bf16[1,384,2048]{2,1,0:T(8,128)(2,1)}, u32[]{:S(2)}) copy-start(bf16[1,384,2048]{2,1,0:T(8,128)(2,1)} %param.29) | copy-start | bytes 4718596
  147.2 15.3 %copy-start.9 = (bf16[1536,384]{1,0:T(8,128)(2,1)S(1)}, bf16[1536,384]{1,0:T(8,128)(2,1)}, u32[]{:S(2)}) copy-start(bf16[1536,384]{1,0:T(8,128)(2,1)} %get-tuple-element.129) | copy-start | bytes 3538948
  154.8 127.0 %all-gather.11.cloned.1.call-start = ((), (), s32[]{:S(2)}) async-start(), calls=%async_computation.7 | async-start | bytes 2621440 | tf_op jit(solution)/shard_map/all_gather | solution.py:2476
  159.1 7.8 %collective-permute-start = (bf16[768,128]{1,0:T(8,128)(2,1)S(1)}, bf16[768,128]{1,0:T(8,128)(2,1)S(1)}, u32[]{:S(2)}, u32[]{:S(2)}) collective-permute-start(bf16[768,128]{1,0:T(8,128)(2,1)S(1)} %copy-done.16), channel_id=1, source_target_pairs={{0,2},{2,0},{4,6},{6,4},{1,3},{3,1},{5,7},{7,5},{8,10},{10,8},{12,... | collective-permute-start | bytes 589832 | tf_op jit(solution)/shard_map/ppermute | solution.py:2315
  160.5 10.6 %collective-permute-start.1 = (bf16[768,128]{1,0:T(8,128)(2,1)S(1)}, bf16[768,128]{1,0:T(8,128)(2,1)S(1)}, u32[]{:S(2)}, u32[]{:S(2)}) collective-permute-start(bf16[768,128]{1,0:T(8,128)(2,1)S(1)} %copy-done.16), channel_id=1, source_target_pairs={{0,4},{2,6},{4,0},{6,2},{1,5},{3,7},{5,1},{7,3},{8,12},{10,14},{12... | collective-permute-start | bytes 589832 | tf_op jit(solution)/shard_map/ppermute | solution.py:2315
  162.0 9.2 %collective-permute-start.2 = (bf16[768,128]{1,0:T(8,128)(2,1)S(1)}, bf16[768,128]{1,0:T(8,128)(2,1)S(1)}, u32[]{:S(2)}, u32[]{:S(2)}) collective-permute-start(bf16[768,128]{1,0:T(8,128)(2,1)S(1)} %copy-done.16), channel_id=1, source_target_pairs={{0,6},{2,4},{4,2},{6,0},{1,7},{3,5},{5,3},{7,1},{8,14},{10,12},{12... | collective-permute-start | bytes 589832 | tf_op jit(solution)/shard_map/ppermute | solution.py:2315
  183.3 35.4 %copy-start.4 = (bf16[192,2048]{1,0:T(8,128)(2,1)S(1)}, bf16[192,2048]{1,0:T(8,128)(2,1)}, u32[]{:S(2)}) copy-start(bf16[192,2048]{1,0:T(8,128)(2,1)} %dynamic-slice_bitcast_fusion.1.own_ref) | copy-start | bytes 2359300
  221.1 54.4 %copy-start.2 = (f32[192,2048]{1,0:T(8,128)}, f32[192,2048]{1,0:T(8,128)S(1)}, u32[]{:S(2)}) copy-start(f32[192,2048]{1,0:T(8,128)S(1)} %get-tuple-element.207.middle_ref) | copy-start | bytes 4718596
  235.9 162.0 %reduce-scatter.5.cloned.1.call-start = ((), (), s32[]{:S(2)}) async-start(), calls=%async_computation.8 | async-start | bytes 2621440 | tf_op jit(solution)/shard_map/reduce_scatter | solution.py:2516
  355.2 121.1 %reduce-scatter.7.cloned.1.call-start = ((), (), s32[]{:S(2)}) async-start(), calls=%async_computation.9 | async-start | bytes 5242880 | tf_op jit(solution)/shard_map/reduce_scatter | solution.py:2516
  398.0 127.9 %reduce-scatter.9.cloned.1.call-start = ((), (), s32[]{:S(2)}) async-start(), calls=%async_computation.10 | async-start | bytes 2621440 | tf_op jit(solution)/shard_map/reduce_scatter | solution.py:2516
  450.3 26.3 %collective-permute-start.3 = (bf16[768,128]{1,0:T(8,128)(2,1)S(1)}, bf16[768,128]{1,0:T(8,128)(2,1)S(1)}, u32[]{:S(2)}, u32[]{:S(2)}) collective-permute-start(bf16[768,128]{1,0:T(8,128)(2,1)S(1)} %get-tuple-element.211), channel_id=1, source_target_pairs={{0,2},{2,0},{4,6},{6,4},{1,3},{3,1},{5,7},{7,5},{8,10},{10,8},{12,... | collective-permute-start | bytes 589832 | tf_op jit(solution)/shard_map/ppermute | solution.py:2326
  451.3 25.3 %collective-permute-start.4 = (bf16[768,128]{1,0:T(8,128)(2,1)S(1)}, bf16[768,128]{1,0:T(8,128)(2,1)S(1)}, u32[]{:S(2)}, u32[]{:S(2)}) collective-permute-start(bf16[768,128]{1,0:T(8,128)(2,1)S(1)} %get-tuple-element.210), channel_id=1, source_target_pairs={{0,4},{2,6},{4,0},{6,2},{1,5},{3,7},{5,1},{7,3},{8,12},{10,14},{12... | collective-permute-start | bytes 589832 | tf_op jit(solution)/shard_map/ppermute | solution.py:2326
  452.3 24.4 %collective-permute-start.5 = (bf16[768,128]{1,0:T(8,128)(2,1)S(1)}, bf16[768,128]{1,0:T(8,128)(2,1)S(1)}, u32[]{:S(2)}, u32[]{:S(2)}) collective-permute-start(bf16[768,128]{1,0:T(8,128)(2,1)S(1)} %get-tuple-element.209), channel_id=1, source_target_pairs={{0,6},{2,4},{4,2},{6,0},{1,7},{3,5},{5,3},{7,1},{8,14},{10,12},{12... | collective-permute-start | bytes 589832 | tf_op jit(solution)/shard_map/ppermute | solution.py:2326
  476.3 125.7 %reduce-scatter.11.cloned.1.call-start = ((), (), s32[]{:S(2)}) async-start(), calls=%async_computation.11 | async-start | bytes 5242880 | tf_op jit(solution)/shard_map/reduce_scatter | solution.py:2516
  528.2 50.9 %copy-start.5 = (bf16[192,2048]{1,0:T(8,128)(2,1)S(1)}, bf16[192,2048]{1,0:T(8,128)(2,1)}, u32[]{:S(2)}) copy-start(bf16[192,2048]{1,0:T(8,128)(2,1)} %dynamic-slice_bitcast_fusion.1.own_ref) | copy-start | bytes 2359300
  528.2 50.9 %copy-start.18 = (f32[16,1,128]{2,1,0:T(1,128)S(1)}, f32[16,1,128]{2,1,0:T(1,128)}, u32[]{:S(2)}) copy-start(f32[16,1,128]{2,1,0:T(1,128)} %get-tuple-element.213) | copy-start | bytes 24580
  634.6 12.1 %copy-start.1 = (bf16[1,384,2048]{2,1,0:T(8,128)(2,1)S(1)}, bf16[1,384,2048]{2,1,0:T(8,128)(2,1)}, u32[]{:S(2)}) copy-start(bf16[1,384,2048]{2,1,0:T(8,128)(2,1)} %param.28) | copy-start | bytes 4718596
  (17 other events, 35.6 us)
Sparse Core Ops, SparseCore 0:
  29.8 78.8 all-gather.4
  110.3 44.4 all-gather.6
  156.4 79.4 all-gather.8
  237.3 44.4 all-gather.10
  355.4 42.5 reduce-scatter.4
  400.2 76.0 reduce-scatter.6
  478.6 44.3 reduce-scatter.8
  526.0 76.0 reduce-scatter.10

commit v5 on v4

--- a/solution.py
+++ b/solution.py
@@ -822,7 +822,9 @@
     )
 
 
-def scatter_kernel(count, left_ref, right_ref, *refs, store=None, between=None):
+def scatter_kernel(
+    count, left_ref, right_ref, *refs, store=None, between=None, preparing=None, finishing=None
+):
     data, place, core, along_x, along_y, across = plane_place()
     partner = (data, place, 1 - core)
     to_x, to_y = (data, along_x, core), (data, along_y, core)
@@ -931,7 +933,7 @@
                 if store is None:
                     sum_ref[place_rows] = total
                 else:
-                    store(place_rows, total)
+                    store(at, sum_ref, place_rows, total)
                 return carry
 
             lax.fori_loop(0, half // step, one, 0)
@@ -946,10 +948,14 @@
         one_array(at, parts[at], sums[at], scratch[each * at : each * (at + 1)]) for at in range(count)
     ]
     for stage in range(2):
-        for run in runs:
+        for at, run in enumerate(runs):
+            if at > 0 and stage == 0 and preparing is not None:
+                preparing()
             next(run)
         if between is not None:
             between(stage)
+    if finishing is not None:
+        finishing()
     for run in runs:
         for _ in run:
             pass
@@ -958,22 +964,40 @@
 def down_and_back_kernel(
     act_ref,
     weights_ref,
-    middle_ref,
-    teacher_ref,
     factor_ref,
-    both_ref,
+    middle_hbm,
+    teacher_hbm,
+    both_hbm,
     out_ref,
     d_out_ref,
-    d_mlp_ref,
     d_both_ref,
     grad_ref,
     own_ref,
     grad_sum,
+    d_mlp_ref,
+    middle_ref,
+    teacher_ref,
+    both_ref,
+    load_sems,
     gather_send,
     gather_recv,
     *scratch,
 ):
-    def store(rows, total):
+    loads = []
+    for source, target in (
+        (middle_hbm, middle_ref),
+        (teacher_hbm, teacher_ref),
+        (both_hbm, both_ref),
+    ):
+        copy = pltpu.make_async_copy(source, target, load_sems.at[len(loads)])
+        copy.start()
+        loads.append(copy)
+
+    def loaded():
+        for copy in loads:
+            copy.wait()
+
+    def store(at, target, rows, total):
         out = middle_ref[rows] + total
         out_ref[rows] = out.astype(jnp.bfloat16)
         d_out = factor_ref[rows] * (out - teacher_ref[rows].astype(jnp.float32))
@@ -992,7 +1016,7 @@
         else:
             grad_ref[...] = (grad_sum[...] + part).astype(jnp.bfloat16)
 
-    scatter_kernel(1, act_ref, weights_ref, None, *scratch, store=store)
+    scatter_kernel(1, act_ref, weights_ref, None, *scratch, store=store, finishing=loaded)
     gather_steps(
         apply_down_back,
         own_ref,
@@ -1013,15 +1037,19 @@
         out_shape=[
             shaped((rows, width), jnp.bfloat16),
             shaped((rows, width), jnp.float32),
-            shaped((2 * GROUP, rows, width), jnp.bfloat16),
             shaped(gate_up.shape, jnp.bfloat16),
             shaped(full_down.shape, jnp.bfloat16),
         ],
-        in_specs=vmem_specs(6),
-        out_specs=vmem_specs(5),
+        in_specs=vmem_specs(3) + any_specs(3),
+        out_specs=vmem_specs(4),
         scratch_shapes=[
             pltpu.VMEM((rows, width), jnp.bfloat16),
             pltpu.VMEM(full_down.shape, jnp.float32),
+            pltpu.VMEM((2 * GROUP, rows, width), jnp.bfloat16),
+            pltpu.VMEM(middle.shape, middle.dtype),
+            pltpu.VMEM(teacher_own.shape, teacher_own.dtype),
+            pltpu.VMEM(gate_up.shape, gate_up.dtype),
+            pltpu.SemaphoreType.DMA((3,)),
             pltpu.SemaphoreType.DMA((11,)),
             pltpu.SemaphoreType.DMA((11,)),
         ]
@@ -1030,7 +1058,7 @@
         compiler_params=pltpu.CompilerParams(
             collective_id=10, has_side_effects=True, vmem_limit_bytes=VMEM_BYTES
         ),
-    )(activated, full_down, middle, teacher_own, factor, gate_up)
+    )(activated, full_down, factor, middle, teacher_own, gate_up)
 
 
 def up_back_kernel(d_both_ref, weights_ref, normed_ref, sum_ref, grad_ref, *scratch):
@@ -1063,6 +1091,93 @@
             collective_id=11, has_side_effects=True, vmem_limit_bytes=VMEM_BYTES
         ),
     )(d_gate_up, full_gu, normed_two)
+
+
+def input_back_kernel(
+    left_ref,
+    weights_ref,
+    bc_weights_ref,
+    gain_ref,
+    normed_hbm,
+    hidden_hbm,
+    d_middle_hbm,
+    grad_ref,
+    bc_ref,
+    gain_sum_ref,
+    normed_ref,
+    hidden_ref,
+    d_middle_ref,
+    load_sems,
+    *scratch,
+):
+    loads = []
+    for source, target in (
+        (normed_hbm, normed_ref),
+        (hidden_hbm, hidden_ref),
+        (d_middle_hbm, d_middle_ref),
+    ):
+        copy = pltpu.make_async_copy(source, target, load_sems.at[len(loads)])
+        copy.start()
+        loads.append(copy)
+    gain_sum_ref[...] = jnp.zeros_like(gain_sum_ref)
+
+    def loaded():
+        for copy in loads[1:]:
+            copy.wait()
+
+
+    def store(at, target, rows, total):
+        if at > 0:
+            target[rows] = total
+            return
+        hidden = hidden_ref[rows].astype(jnp.float32)
+        scale = lax.rsqrt(jnp.mean(hidden * hidden, axis=-1, keepdims=True) + EPSILON)
+        scaled = total * gain_ref[...]
+        inner = jnp.mean(scaled * hidden, axis=-1, keepdims=True)
+        grad_ref[rows] = d_middle_ref[rows] + scale * scaled - hidden * (scale**3 * inner)
+        product = total * hidden * scale
+        gain_sum_ref[...] += product[:8] + product[8:]
+
+    scatter_kernel(
+        2,
+        left_ref,
+        weights_ref,
+        normed_ref,
+        bc_weights_ref,
+        None,
+        bc_ref,
+        *scratch,
+        store=store,
+        preparing=loads[0].wait,
+        finishing=loaded,
+    )
+
+
+def input_back(d_projected, full_in, normed, w_bc, hidden_own, d_middle, gain, bc_cols):
+    rows, width = d_middle.shape
+    sizes = [(rows, width), (bc_cols, width // 2)]
+    shaped = jax.ShapeDtypeStruct
+    return pl.pallas_call(
+        input_back_kernel,
+        out_shape=[
+            shaped((rows, width), jnp.float32),
+            shaped(sizes[1], jnp.float32),
+            shaped((8, width), jnp.float32),
+        ],
+        in_specs=vmem_specs(4) + any_specs(3),
+        out_specs=vmem_specs(3),
+        scratch_shapes=[
+            pltpu.VMEM(normed.shape, normed.dtype),
+            pltpu.VMEM(hidden_own.shape, hidden_own.dtype),
+            pltpu.VMEM(d_middle.shape, d_middle.dtype),
+            pltpu.SemaphoreType.DMA((3,)),
+        ]
+        + scatter_scratch(sizes),
+        cost_estimate=lasting(50),
+        compiler_params=pltpu.CompilerParams(
+            collective_id=8, has_side_effects=True, vmem_limit_bytes=VMEM_BYTES
+        ),
+    )(d_projected, full_in, w_bc, gain, normed, hidden_own, d_middle)
 
 
 def scatter_scratch(sizes):
@@ -1307,21 +1422,36 @@
     )(piece, bc_sum, bulk)
 
 
-def unpack_kernel(
+def unpack_early_kernel(
     gu_ref,
     down_ref,
     out_ref,
-    in_ref,
-    bc_ref,
-    misc_ref,
     both_ref,
     both_out,
-    pieces_ref,
     gate_ref,
     up_ref,
     d_ref,
     mo_ref,
     ao_ref,
+    input_ref,
+    output_ref,
+):
+    units, width = down_ref.shape[2], HEADS * HP
+    input_ref[...] = both_ref[0]
+    output_ref[...] = both_out[0]
+    gate_ref[...] = gu_ref[0, :, :units].astype(jnp.float32)
+    up_ref[...] = gu_ref[0, :, units:].astype(jnp.float32)
+    d_ref[...] = down_ref[0].astype(jnp.float32).T
+    turned = out_ref[0].astype(jnp.float32).T
+    mo_ref[...] = turned[:width]
+    ao_ref[...] = turned[width:]
+
+
+def unpack_kernel(
+    in_ref,
+    bc_ref,
+    misc_ref,
+    pieces_ref,
     z_ref,
     x_ref,
     q_ref,
@@ -1337,19 +1467,9 @@
     group_ref,
     one_ref,
     two_ref,
-    input_ref,
-    output_ref,
     sums_ref,
 ):
-    units, width, part = down_ref.shape[2], HEADS * HP, HD // 4
-    input_ref[...] = both_ref[0]
-    output_ref[...] = both_out[0]
-    gate_ref[...] = gu_ref[0, :, :units].astype(jnp.float32)
-    up_ref[...] = gu_ref[0, :, units:].astype(jnp.float32)
-    d_ref[...] = down_ref[0].astype(jnp.float32).T
-    turned = out_ref[0].astype(jnp.float32).T
-    mo_ref[...] = turned[:width]
-    ao_ref[...] = turned[width:]
+    width, part = HEADS * HP, HD // 4
     z_ref[...] = in_ref[0, :, :width].astype(jnp.float32)
     q_ref[...] = in_ref[0, :, width : width + HD].astype(jnp.float32)
     x_ref[...] = in_ref[0, :, width + HD : 2 * width + HD].astype(jnp.float32)
@@ -1402,51 +1522,59 @@
             group_ref[head : head + 1, :] = sums_ref[row : row + 1, lane : lane + HP]
 
 
-def unpack_all(back, bc_all, both, sums, shapes):
-    gu, down, out, in_all = back
-
-    def per_chip(array, rows=1):
-        return pl.BlockSpec((rows,) + array.shape[1:], lambda chip: (chip, 0, 0))
-
-    def across(shape):
-        return pl.BlockSpec((shape[0], shape[1] // GROUP), lambda chip: (0, chip))
-
-    def down_along(shape):
-        return pl.BlockSpec((shape[0] // GROUP, shape[1]), lambda chip: (chip, 0))
-
-    def once(shape):
-        return pl.BlockSpec(shape, lambda chip: (0,) * len(shape))
-
-    misc_block = (GROUP, in_all.shape[1], HD)
-    kinds = [across, across, down_along, down_along, down_along, across, across, across, across]
-    kinds += [once] * (len(shapes) - len(kinds))
-    out_shape = [jax.ShapeDtypeStruct(shape, jnp.float32) for shape in shapes]
+def across_chips(shape):
+    return pl.BlockSpec((shape[0], shape[1] // GROUP), lambda chip: (0, chip))
+
+
+def along_chips(shape):
+    return pl.BlockSpec((shape[0] // GROUP, shape[1]), lambda chip: (chip, 0))
+
+
+def per_chip(array, rows=1):
+    return pl.BlockSpec((rows,) + array.shape[1:], lambda chip: (chip, 0, 0))
+
+
+def unpack_early(gu, down, out, both, shapes):
     rows, width = both[0].shape[1:]
     step = 2 * rows // GROUP
     rows_in = pl.BlockSpec((1, step, width), lambda chip: (chip // 2, lax.rem(chip, 2), 0))
+    kinds = [across_chips, across_chips, along_chips, along_chips, along_chips]
+    out_shape = [jax.ShapeDtypeStruct(shape, jnp.float32) for shape in shapes]
     out_shape += [jax.ShapeDtypeStruct((2 * rows, width), array.dtype) for array in both]
-    out_specs = [kind(shape) for kind, shape in zip(kinds, shapes)]
-    out_specs += [pl.BlockSpec((step, width), lambda chip: (chip, 0))] * 2
+    return pl.pallas_call(
+        unpack_early_kernel,
+        grid=(GROUP,),
+        in_specs=[per_chip(gu), per_chip(down), per_chip(out), rows_in, rows_in],
+        out_specs=[kind(shape) for kind, shape in zip(kinds, shapes)]
+        + [along_chips((2 * rows, width))] * 2,
+        out_shape=out_shape,
+        cost_estimate=lasting(6),
+        compiler_params=pltpu.CompilerParams(vmem_limit_bytes=VMEM_BYTES),
+    )(gu, down, out, *both)
+
+
+def unpack_late(in_all, bc_all, sums, shapes):
+    def once(shape):
+        return pl.BlockSpec(shape, lambda chip: (0,) * len(shape))
+
+    misc_block = (GROUP, in_all.shape[1], HD)
+    kinds = [across_chips] * 4
+    kinds += [once] * (len(shapes) - len(kinds))
     return pl.pallas_call(
         unpack_kernel,
         grid=(GROUP,),
         in_specs=[
-            per_chip(gu),
-            per_chip(down),
-            per_chip(out),
             per_chip(in_all),
             per_chip(bc_all, 2),
             pl.BlockSpec(misc_block, lambda chip: (0, 0, in_all.shape[2] // HD - 1)),
-            rows_in,
-            rows_in,
             once(sums.shape),
         ],
-        out_specs=out_specs,
-        out_shape=out_shape,
+        out_specs=[kind(shape) for kind, shape in zip(kinds, shapes)],
+        out_shape=[jax.ShapeDtypeStruct(shape, jnp.float32) for shape in shapes],
         scratch_shapes=[pltpu.VMEM((8, 2 * GROUP * sums.shape[2]), jnp.float32)],
-        cost_estimate=lasting(8),
+        cost_estimate=lasting(6),
         compiler_params=pltpu.CompilerParams(vmem_limit_bytes=VMEM_BYTES),
-    )(gu, down, out, in_all, bc_all, in_all, *both, sums)
+    )(in_all, bc_all, in_all, sums)
 
 
 def push_moves(moves, sources, targets, local_sems, send_sems, recv_sems, first=0):
@@ -2395,7 +2523,7 @@
         (gain_one[None], w_bc),
         (((length, width), bf16), ((length, 2 * NS), bf16)),
     )
-    hidden_own = hidden_own.astype(jnp.float32)
+    hidden_low, hidden_own = hidden_own, hidden_own.astype(jnp.float32)
     width_out = width_x + HD
     out_slices, gu_slices, down_slices = exchange_plane(
         (
@@ -2508,7 +2636,7 @@
     )
     teacher_own = lax.dynamic_slice(teacher[0], (core * own_rows, 0), (own_rows, width))
     factor = 2.0 * total_tokens / token_count * mask_rows.astype(jnp.float32)[:, None]
-    block_out, d_out, d_mlp, d_gate_up, grad_down = down_and_back(
+    block_out, d_out, d_gate_up, grad_down = down_and_back(
         activated, full_down, middle, teacher_own, factor, gate_up
     )
 
@@ -2579,17 +2707,18 @@
         after(dot_left_t(normed, d_projected[:, :width_in]).astype(bf16), grad_out)
     )
     bc_cols = 2 * NS // GROUP
-    d_normed, bc_sum = scatter_plane(
-        after(d_projected, grad_out), full_in, 8, ((normed, bc_cols, width // 2),), (w_bc,)
-    )
-    scale_own = lax.rsqrt(jnp.mean(hidden_own * hidden_own, axis=-1, keepdims=True) + EPSILON)
-    grad_gain_one = jnp.sum(d_normed * hidden_own * scale_own, axis=0)
-    d_scaled_one = d_normed * gain_one
-    grad_input = (
-        d_middle
-        + scale_own * d_scaled_one
-        - hidden_own * scale_own**3 * jnp.mean(d_scaled_one * hidden_own, axis=-1, keepdims=True)
-    )
+    grad_input, bc_sum, gain_sums = input_back(
+        after(d_projected, grad_out),
+        full_in,
+        normed,
+        w_bc,
+        hidden_low,
+        d_middle,
+        gain_one[None],
+        bc_cols,
+    )
+    grad_gain_one = jnp.sum(gain_sums, axis=0)
+
     taps_all = jnp.concatenate(
         [
             lax.dynamic_update_slice(
@@ -2615,33 +2744,21 @@
     small_width = -(-small.shape[1] // (2 * GROUP * 128)) * 2 * GROUP * 128
     small = jnp.pad(small, ((0, 0), (0, small_width - small.shape[1])))
     piece, both_input, both_output, back_out = plane_sum(small, grad_input, block_out, grad_out)
-    small_all, bc_all, back_in = finish_all(piece, bc_sum, grad_in)
+    grad_gate, grad_up, grad_down, grad_mo, grad_ao, grad_input, block_out = unpack_early(
+        back_gate_up,
+        back_down,
+        back_out,
+        (both_input, both_output),
+        [array.shape for array in (w_gate, w_up, w_down, w_mamba_out, w_attn_out)],
+    )
+    small_all, bc_all, back_in = finish_all(after(piece, grad_input), bc_sum, grad_in)
     bc_all = bc_all.reshape(2 * GROUP, bc_cols, width // 2)
     shapes = [
         array.shape
-        for array in (
-            w_gate,
-            w_up,
-            w_down,
-            w_mamba_out,
-            w_attn_out,
-            w_z,
-            w_x,
-            w_query,
-            w_bc,
-            w_key,
-            w_value,
-            w_dt.T,
-            conv_weight.T,
-        )
+        for array in (w_z, w_x, w_query, w_bc, w_key, w_value, w_dt.T, conv_weight.T)
     ]
     shapes += [(1, conv_bias.shape[0])] + [(1, MH)] * 3 + [(MH, HP)] + [(1, slice_rows)] * 2
     (
-        grad_gate,
-        grad_up,
-        grad_down,
-        grad_mo,
-        grad_ao,
         grad_z,
         grad_x,
         grad_q,
@@ -2657,15 +2774,7 @@
         grad_group,
         grad_one,
         grad_two,
-        grad_input,
-        block_out,
-    ) = unpack_all(
-        (back_gate_up, back_down, back_out, back_in),
-        bc_all,
-        (both_input, both_output),
-        small_all,
-        shapes,
-    )
+    ) = unpack_late(back_in, bc_all, small_all, shapes)
     return (
         block_out[None],
         grad_input[None],

time: 663 us -> 654 us (0.986)
    pallas_call x2 -> x1, Pallas kernels: 86.3 us -> 35.4 us  [scatter_plane(): pl.pallas_call(partial(scatter_kernel, count), out_shape=shapes, in_specs...]
    pallas_call x1 -> x3, Pallas kernels: 10.7 us -> 61.4 us  [the longest x1 49 us: input_back(): pl.pallas_call(input_back_kernel, out_shape=[shaped((rows, width), jnp.fl...]
  transfers between devices with their start and end apart: 14 -> 14, of which waited for: 9 -> 9; matrix products, arithmetic and copies ran while one was open for 10% -> 9% of each run, Pallas kernels for 54% -> 56%
where the time goes in v5:
time: 654 us; the launch traced here: 645 us
  Pallas kernels  489 us (75%)
  waiting for transfers between devices  63.2 us (10%)
  matrix products  31.1 us (5%)
  local copies, waits for them, and re-layouts  26.3 us (4%)
  between operations  15.9 us (2%)
  other arithmetic  10.7 us (2%)
  starting transfers between devices  8.31 us (1%)
    pallas_call x3, Pallas kernels, gather_plane(): pl.pallas_call(partial(gather_kernel, apply, len(inputs), len(outputs)),...  112 us
    pallas_call x1, Pallas kernels, down_and_back(): pl.pallas_call(down_and_back_kernel, out_shape=[shaped((rows, width), jnp...  69 us
    pallas_call x1, Pallas kernels, input_back(): pl.pallas_call(input_back_kernel, out_shape=[shaped((rows, width), jnp.fl...  49 us
    pallas_call x1, Pallas kernels, up_back(): pl.pallas_call(up_back_kernel, out_shape=[jax.ShapeDtypeStruct((rows, wid...  41.2 us
    pallas_call x1, Pallas kernels, ssd_backward(): pl.pallas_call(partial(ssd_backward_kernel, moves), grid=(laps,), in_spec...  36.8 us
    pallas_call x1, Pallas kernels, scatter_plane(): pl.pallas_call(partial(scatter_kernel, count), out_shape=shapes, in_specs...  35.4 us
    pallas_call x1, Pallas kernels, finish_all(): pl.pallas_call(finish_kernel, out_shape=[shaped((places,) + piece.shape,...  32.6 us
    pallas_call x1, Pallas kernels, exchange_plane(): pl.pallas_call(partial(exchange_kernel, moves, len(arrays)), out_shape=[j...  27.5 us
  transfers between devices with their start and end apart: 14, of which 9 were waited for; matrix products, arithmetic and copies ran while one was open for 9% of the time, Pallas kernels for 56%

profile of v5, /device:TPU:0, one launch (start us, length us, event | category | flops | bytes accessed | tf_op | source)
XLA Modules:
  0.0 644.7 jit_solution(6900486435434579227)
XLA Ops:
  7.3 22.4 %shard_map.435 = (bf16[4,128,1024]{2,1,0:T(8,128)(2,1)}, f32[16,8,128]{2,1,0:T(8,128)}) custom-call(bf16[128,1536]{1,0:T(8,128)(2,1)} %z_ref.1, bf16[128,512]{1,0:T(8,128)(2,1)} %q_ref.1, bf16[128,1536]{1,0:T(8,128)(2,1)} %x_ref.1, bf16[128,128]{1,0:T(8,128)(2,1)} %key_ref.1, bf16[128,128]{1,0:T(8,128)(2,1)} %value_ref.1, bf16[24,128]{1,0:T(8,128)(2,1)} %bitcast.94, ...), custom_call_target="tpu_custom_call" | custom-call | flops 17999998976 | bytes 60000000 | tf_op jit(solution)/shard_map/pallas_call | solution.py:1672
  33.2 37.3 %shard_map.436 = (bf16[8,192,2048]{2,1,0:T(8,128)(2,1)}, bf16[1536,2048]{1,0:T(8,128)(2,1)}, bf16[1536,512]{1,0:T(8,128)(2,1)}) custom-call(bf16[192,2048]{1,0:T(8,128)(2,1)} %dynamic-slice_bitcast_fusion.1.own_ref.hidden_hbm, f32[1,2048]{1,0:T(1,128)} %get-tuple-element.215.refs_0_.gain_ref, bf16[2048,512]{1,0:T(8,128)(2,1)} %bc_weights_ref.1), custom_call_target="tpu_custom_call" | custom-call | flops 31499999232 | bytes 105000000 | tf_op jit(solution)/shard_map/pallas_call | solution.py:770
  72.3 27.5 %shard_map.437 = (bf16[4,128,512]{2,1,0:T(8,128)(2,1)}, bf16[4,128,1024]{2,1,0:T(8,128)(2,1)}, bf16[4,128,512]{2,1,0:T(8,128)(2,1)}) custom-call(bf16[128,1536]{1,0:T(8,128)(2,1)} %bitcast.77, bf16[128,512]{1,0:T(8,128)(2,1)} %bitcast.81, bf16[128,2048]{1,0:T(8,128)(2,1)} %refs_2_.1, bf16[128,2048]{1,0:T(8,128)(2,1)} %refs_3_.1, bf16[128,2048]{1,0:T(8,128)(2,1)} %bitcast.74), custom_call_target="tpu_custom_call" | custom-call | flops 22499999744 | bytes 75000000 | tf_op jit(solution)/shard_map/pallas_call | solution.py:1694
  101.3 7.4 %all-gather.5.cloned.1.call-done = bf16[16,128,1024]{2,1,0:T(8,128)(2,1)} async-done(((bf16[4,128,1024]{2,1,0:T(8,128)(2,1)}), bf16[16,128,1024]{2,1,0:T(8,128)(2,1)}) %all-gather.5.cloned.1.call-update) | async-done | bytes 4194320 | tf_op jit(solution)/shard_map/all_gather | solution.py:2516
  114.8 2.1 dynamic-slice_bitcast_fusion.2
  116.9 11.8 %fusion.5.proj_ref.before_ref.raw_ref = f32[1536,1024]{1,0:T(8,128)} fusion(bf16[1536,2048]{1,0:T(8,128)(2,1)} %get-tuple-element.116.normed_hbm, bf16[2048,1024]{1,0:T(8,128)(2,1)} %bitcast.83), kind=kOutput, calls=%fused_computation.59 | convolution fusion | flops 6442450944 | bytes 16777216 | tf_op jit(solution)/shard_map/dot_general | solution.py:47
  128.7 18.5 %shard_map.438 = (bf16[1536,384]{1,0:T(8,128)(2,1)}, f32[1536,384]{1,0:T(8,128)}, f32[12,256,384]{2,1,0:T(8,128)}, bf16[1536,896]{1,0:T(8,128)(2,1)}, f32[1536,896]{1,0:T(8,128)}, /*index=5*/bf16[768,128]{1,0:T(8,128)(2,1)}) custom-call(f32[1536,1024]{1,0:T(8,128)} %fusion.5.proj_ref.before_ref.raw_ref, f32[1536,1024]{1,0:T(8,128)} %fusion.5.proj_ref.before_ref.raw_ref, ...), custom_call_target="tpu_custom_call" | custom-call | flops 5400000000 | bytes 18000000 | tf_op jit(solution)/shard_map/pallas_call | solution.py:2189
  147.2 7.6 %all-gather.7.cloned.1.call-done = bf16[16,128,512]{2,1,0:T(8,128)(2,1)} async-done(((bf16[4,128,512]{2,1,0:T(8,128)(2,1)}), bf16[16,128,512]{2,1,0:T(8,128)(2,1)}) %all-gather.7.cloned.1.call-update) | async-done | bytes 2097168 | tf_op jit(solution)/shard_map/all_gather | solution.py:2544
  162.8 4.0 collective-permute-done
  166.9 4.2 collective-permute-done.1
  172.1 8.9 %shard_map.439 = (bf16[1536,128]{1,0:T(8,128)(2,1)}, f32[1536,1]{1,0:T(8,128)}, bf16[1536,128]{1,0:T(8,128)(2,1)}, bf16[1536,128]{1,0:T(8,128)(2,1)}, bf16[1536,128]{1,0:T(8,128)(2,1)}) custom-call(f32[1536,1024]{1,0:T(8,128)} %fusion.5.proj_ref.before_ref.raw_ref, f32[1536,128]{1,0:T(8,128)} %constant.100.clone.cos_ref, ...), custom_call_target="tpu_custom_call" | custom-call | flops 8099999744 | bytes 27000000 | tf_op jit(solution)/shard_map/pallas_call | solution.py:2418
  183.3 35.4 %shard_map.440 = f32[192,2048]{1,0:T(8,128)} custom-call(bf16[1536,512]{1,0:T(8,128)(2,1)} %copy-done.8, bf16[2048,512]{1,0:T(8,128)(2,1)} %bitcast.87), custom_call_target="tpu_custom_call" | custom-call | flops 31499999232 | bytes 105000000 | tf_op jit(solution)/shard_map/pallas_call | solution.py:1207
  218.7 1.7 multiply_reduce_fusion.2
  220.4 15.4 %all-gather.9.cloned.1.call-done = bf16[16,128,1024]{2,1,0:T(8,128)(2,1)} async-done(((bf16[4,128,1024]{2,1,0:T(8,128)(2,1)}), bf16[16,128,1024]{2,1,0:T(8,128)(2,1)}) %all-gather.9.cloned.1.call-update) | async-done | bytes 4194320 | tf_op jit(solution)/shard_map/all_gather | solution.py:2603
  237.2 38.3 %shard_map.441 = (bf16[8,192,2048]{2,1,0:T(8,128)(2,1)}, f32[1536,1024]{1,0:T(8,128)}, bf16[1536,512]{1,0:T(8,128)(2,1)}) custom-call(bf16[192,2048]{1,0:T(8,128)(2,1)} %multiply_convert_fusion.own_ref, bf16[2048,1024]{1,0:T(8,128)(2,1)} %bitcast.85), custom_call_target="tpu_custom_call" | custom-call | flops 31499999232 | bytes 105000000 | tf_op jit(solution)/shard_map/pallas_call | solution.py:770
  275.5 6.3 all-gather.11.cloned.1.call-done
  281.8 69.0 %shard_map.442 = (bf16[192,2048]{1,0:T(8,128)(2,1)}, f32[192,2048]{1,0:T(8,128)}, bf16[1536,1024]{1,0:T(8,128)(2,1)}, bf16[2048,512]{1,0:T(8,128)(2,1)}) custom-call(bf16[1536,512]{1,0:T(8,128)(2,1)} %get-tuple-element.139.act_ref, bf16[2048,512]{1,0:T(8,128)(2,1)} %bitcast.89, f32[192,1]{1,0:T(8,128)} %copy.86.factor_ref, f32[192,2048]{1,0:T(8,128)} %copy-done.2, ...), custom_call_target="tpu_custom_call" | custom-call | flops 62999998464 | bytes 210000000 | tf_op jit(solution)/shard_map/pallas_call | solution.py:1035
  350.9 41.2 %shard_map.443 = (f32[192,2048]{1,0:T(8,128)}, bf16[2048,1024]{1,0:T(8,128)(2,1)}) custom-call(bf16[1536,1024]{1,0:T(8,128)(2,1)} %get-tuple-element.144.d_both_ref, bf16[2048,1024]{1,0:T(8,128)(2,1)} %bitcast.86, bf16[1536,2048]{1,0:T(8,128)(2,1)} %bitcast.98), custom_call_target="tpu_custom_call" | custom-call | flops 34200000512 | bytes 114000000 | tf_op jit(solution)/shard_map/pallas_call | solution.py:1080
  396.9 1.9 fusion.3
  398.8 36.0 %shard_map.444 = (bf16[8,192,2048]{2,1,0:T(8,128)(2,1)}, f32[1536,384]{1,0:T(8,128)}, bf16[1536,128]{1,0:T(8,128)(2,1)}) custom-call(bf16[192,2048]{1,0:T(8,128)(2,1)} %get-tuple-element.148.own_ref, bf16[2048,512]{1,0:T(8,128)(2,1)} %bitcast.88), custom_call_target="tpu_custom_call" | custom-call | flops 31499999232 | bytes 105000000 | tf_op jit(solution)/shard_map/pallas_call | solution.py:770
  434.8 9.3 %shard_map.445 = (bf16[1536,128]{1,0:T(8,128)(2,1)}, bf16[4,768,128]{2,1,0:T(8,128)(2,1)}) custom-call(bf16[1536,128]{1,0:T(8,128)(2,1)} %get-tuple-element.150.q_ref, bf16[1536,128]{1,0:T(8,128)(2,1)} %get-tuple-element.151.k_ref, bf16[1536,128]{1,0:T(8,128)(2,1)} %get-tuple-element.152.v_ref, f32[1536,128]{1,0:T(8,128)} %constant.100.clone.cos_ref, ...), custom_call_target="tpu_custom_call" | custom-call | flops 8099999744 | bytes 27000000 | tf_op jit(solution)/shard_map/pallas_call | solution.py:2418
  444.0 2.1 dynamic-slice_bitcast_fusion.4
  449.6 7.7 %convolution_convert_fusion.1 = bf16[2048,512]{1,0:T(8,128)(2,1)} fusion(bf16[1536,2048]{1,0:T(8,128)(2,1)} %bitcast.97, bf16[1536,512]{1,0:T(8,128)(2,1)S(1)} %copy-done.9), kind=kOutput, calls=%fused_computation.2 | convolution fusion | flops 3222274048 | bytes 9961472 | tf_op jit(solution)/shard_map/dot_general | solution.py:51
  457.3 14.6 %reduce-scatter.7.cloned.1.call-done = bf16[512,1024]{1,0:T(8,128)(2,1)} async-done(((bf16[2048,1024]{1,0:T(8,128)(2,1)}), bf16[512,1024]{1,0:T(8,128)(2,1)}) %reduce-scatter.7.cloned.1.call-update) | async-done | bytes 1048592 | tf_op jit(solution)/shard_map/reduce_scatter | solution.py:2644
  473.0 36.8 %shard_map.446 = (bf16[1536,1536]{1,0:T(8,128)(2,1)}, f32[8,896]{1,0:T(8,128)}, f32[8,128]{1,0:T(8,128)}, f32[1,384]{1,0:T(1,128)}, f32[1,384]{1,0:T(1,128)}, /*...) custom-call(f32[1536,1024]{1,0:T(8,128)} %fusion.5.proj_ref.before_ref.raw_ref, ...), custom_call_target="tpu_custom_call" | custom-call | flops 43200000000 | bytes 144000000 | tf_op jit(solution)/shard_map/pallas_call | solution.py:2222
  509.9 11.6 %convolution_convert_fusion = bf16[2048,1024]{1,0:T(8,128)(2,1)} fusion(bf16[1536,2048]{1,0:T(8,128)(2,1)} %get-tuple-element.116.normed_hbm, bf16[1536,1536]{1,0:T(8,128)(2,1)} %get-tuple-element.167.left_ref), kind=kOutput, calls=%fused_computation | convolution fusion | flops 6444548096 | bytes 13631488 | tf_op jit(solution)/shard_map/dot_general | solution.py:51
  523.8 49.0 %shard_map.447 = (f32[192,2048]{1,0:T(8,128)}, f32[128,1024]{1,0:T(8,128)}, f32[8,2048]{1,0:T(8,128)}) custom-call(bf16[1536,1536]{1,0:T(8,128)(2,1)} %get-tuple-element.167.left_ref, bf16[2048,1024]{1,0:T(8,128)(2,1)} %bitcast.84, bf16[2048,512]{1,0:T(8,128)(2,1)} %bc_weights_ref.1, f32[1,2048]{1,0:T(1,128)} %get-tuple-element.215.refs_0_.gain_ref, ...), custom_call_target="tpu_custom_call" | custom-call | flops 44999999488 | bytes 150000000 | tf_op jit(solution)/shard_map/pallas_call | solution.py:1160
  574.4 14.5 %shard_map.448 = (f32[8,640]{1,0:T(8,128)}, f32[2,192,2048]{2,1,0:T(8,128)}, bf16[2,192,2048]{2,1,0:T(8,128)(2,1)}, bf16[4,128,512]{2,1,0:T(8,128)(2,1)}) custom-call(f32[8,5120]{1,0:T(8,128)} %pad.15.small_ref, f32[192,2048]{1,0:T(8,128)} %get-tuple-element.170.own_ref, bf16[192,2048]{1,0:T(8,128)(2,1)} %get-tuple-element.171.out_ref, ...), custom_call_target="tpu_custom_call" | custom-call | flops 17999998976 | bytes 60000000 | tf_op jit(solution)/shard_map/pallas_call | solution.py:1269
  589.0 6.6 %shard_map.449 = (f32[128,2048]{1,0:T(8,128)}, f32[128,2048]{1,0:T(8,128)}, f32[2048,128]{1,0:T(8,128)}, f32[1536,128]{1,0:T(8,128)}, f32[512,128]{1,0:T(8,128)}...) custom-call(bf16[4,128,1024]{2,1,0:T(8,128)(2,1)} %get-tuple-element.159.gu_ref, ...), custom_call_target="tpu_custom_call" | custom-call | flops 5400000000 | bytes 18000000 | tf_op jit(solution)/shard_map/pallas_call | solution.py:1544
  595.6 2.1 reduce-scatter.11.cloned.1.call-done
  597.7 32.6 %shard_map.450 = (f32[8,8,640]{2,1,0:T(8,128)}, bf16[8,4,32,1024]{3,2,1,0:T(8,128)(2,1)}, bf16[4,128,1024]{2,1,0:T(8,128)(2,1)}) custom-call(f32[8,640]{1,0:T(8,128)} %get-tuple-element.178.piece_ref, f32[128,1024]{1,0:T(8,128)} %get-tuple-element.179.bc_ref, bf16[4,128,1024]{2,1,0:T(8,128)(2,1)} %bitcast.91), custom_call_target="tpu_custom_call" | custom-call | flops 27000000512 | bytes 90000000 | tf_op jit(solution)/shard_map/pallas_call | solution.py:1400
  630.3 5.7 shard_map.451
  (167 shorter events, 39.1 us)
Async XLA Ops:
  7.2 22.5 %copy-start = (bf16[1,384,2048]{2,1,0:T(8,128)(2,1)S(1)}, bf16[1,384,2048]{2,1,0:T(8,128)(2,1)}, u32[]{:S(2)}) copy-start(bf16[1,384,2048]{2,1,0:T(8,128)(2,1)} %param.28) | copy-start | bytes 4718596
  7.2 101.5 %all-gather.5.cloned.1.call-start = ((), (), s32[]{:S(2)}) async-start(), calls=%async_computation.4 | async-start | bytes 5242880 | tf_op jit(solution)/shard_map/all_gather | solution.py:2516
  29.7 125.1 %all-gather.7.cloned.1.call-start = ((), (), s32[]{:S(2)}) async-start(), calls=%async_computation.5 | async-start | bytes 2621440 | tf_op jit(solution)/shard_map/all_gather | solution.py:2544
  33.2 37.3 %copy-start.15 = (bf16[512,128]{1,0:T(8,128)(2,1)S(1)}, bf16[512,128]{1,0:T(8,128)(2,1)}, u32[]{:S(2)}) copy-start(bf16[512,128]{1,0:T(8,128)(2,1)} %param.47) | copy-start | bytes 393220
  33.2 38.1 %copy-start.11 = (bf16[2048,128]{1,0:T(8,128)(2,1)S(1)}, bf16[2048,128]{1,0:T(8,128)(2,1)}, u32[]{:S(2)}) copy-start(bf16[2048,128]{1,0:T(8,128)(2,1)} %param.51) | copy-start | bytes 1572868
  72.3 27.6 %copy-start.19 = (f32[3584]{0:T(1024)S(1)}, f32[3584]{0:T(1024)}, u32[]{:S(2)}) copy-start(f32[3584]{0:T(1024)} %param.38) | copy-start | bytes 43012
  72.3 28.0 %copy-start.23 = (f32[48]{0:T(128)S(1)}, f32[48]{0:T(128)}, u32[]{:S(2)}) copy-start(f32[48]{0:T(128)} %param.40) | copy-start | bytes 580
  72.3 28.0 %copy-start.24 = (f32[48]{0:T(128)S(1)}, f32[48]{0:T(128)}, u32[]{:S(2)}) copy-start(f32[48]{0:T(128)} %param.39) | copy-start | bytes 580
  72.3 28.7 %slice-start.1 = ((f32[3584]{0:T(1024)}), f32[512]{0:T(512)S(1)}, s32[]{:S(2)}) async-start(f32[3584]{0:T(1024)} %param.38), calls=%async_computation.13 | async-start | bytes 4096 | tf_op jit(solution)/shard_map/slice | solution.py:2563
  72.3 28.7 %copy-start.16 = (f32[3584,4]{0,1:T(4,128)S(1)}, f32[3584,4]{0,1:T(4,128)}, u32[]{:S(2)}) copy-start(f32[3584,4]{0,1:T(4,128)} %param.37) | copy-start | bytes 172036
  99.8 12.9 %copy-start.28 = (f32[48]{0:T(128)S(1)}, f32[48]{0:T(128)}, u32[]{:S(2)}) copy-start(f32[48]{0:T(128)} %param.41) | copy-start | bytes 580
  99.9 14.3 %slice-start = ((f32[3584,4]{0,1:T(4,128)}), f32[512,4]{0,1:T(4,128)S(1)}, s32[]{:S(2)}) async-start(f32[3584,4]{0,1:T(4,128)} %param.37), calls=%async_computation.12 | async-start | bytes 16384 | tf_op jit(solution)/shard_map/slice | solution.py:2563
  108.7 127.1 %all-gather.9.cloned.1.call-start = ((), (), s32[]{:S(2)}) async-start(), calls=%async_computation.6 | async-start | bytes 5242880 | tf_op jit(solution)/shard_map/all_gather | solution.py:2603
  128.7 27.2 %copy-start.18 = (s32[4,1536]{1,0:T(4,128)S(1)}, s32[4,1536]{1,0:T(4,128)}, u32[]{:S(2)}) copy-start(s32[4,1536]{1,0:T(4,128)} %param.31) | copy-start | bytes 73732
  128.7 29.4 %copy-start.12 = (bf16[1,384,2048]{2,1,0:T(8,128)(2,1)S(1)}, bf16[1,384,2048]{2,1,0:T(8,128)(2,1)}, u32[]{:S(2)}) copy-start(bf16[1,384,2048]{2,1,0:T(8,128)(2,1)} %param.29) | copy-start | bytes 4718596
  147.2 11.9 %copy-start.14 = (bf16[768,128]{1,0:T(8,128)(2,1)S(1)}, bf16[768,128]{1,0:T(8,128)(2,1)}, u32[]{:S(2)}) copy-start(bf16[768,128]{1,0:T(8,128)(2,1)} %get-tuple-element.132) | copy-start | bytes 589828
  147.2 15.4 %copy-start.7 = (bf16[1536,384]{1,0:T(8,128)(2,1)S(1)}, bf16[1536,384]{1,0:T(8,128)(2,1)}, u32[]{:S(2)}) copy-start(bf16[1536,384]{1,0:T(8,128)(2,1)} %get-tuple-element.131) | copy-start | bytes 3538948
  154.8 127.0 %all-gather.11.cloned.1.call-start = ((), (), s32[]{:S(2)}) async-start(), calls=%async_computation.7 | async-start | bytes 2621440 | tf_op jit(solution)/shard_map/all_gather | solution.py:2604
  159.1 7.8 %collective-permute-start = (bf16[768,128]{1,0:T(8,128)(2,1)S(1)}, bf16[768,128]{1,0:T(8,128)(2,1)S(1)}, u32[]{:S(2)}, u32[]{:S(2)}) collective-permute-start(bf16[768,128]{1,0:T(8,128)(2,1)S(1)} %copy-done.14), channel_id=1, source_target_pairs={{0,2},{2,0},{4,6},{6,4},{1,3},{3,1},{5,7},{7,5},{8,10},{10,8},{12,... | collective-permute-start | bytes 589832 | tf_op jit(solution)/shard_map/ppermute | solution.py:2443
  160.5 10.6 %collective-permute-start.1 = (bf16[768,128]{1,0:T(8,128)(2,1)S(1)}, bf16[768,128]{1,0:T(8,128)(2,1)S(1)}, u32[]{:S(2)}, u32[]{:S(2)}) collective-permute-start(bf16[768,128]{1,0:T(8,128)(2,1)S(1)} %copy-done.14), channel_id=1, source_target_pairs={{0,4},{2,6},{4,0},{6,2},{1,5},{3,7},{5,1},{7,3},{8,12},{10,14},{12... | collective-permute-start | bytes 589832 | tf_op jit(solution)/shard_map/ppermute | solution.py:2443
  162.0 9.2 %collective-permute-start.2 = (bf16[768,128]{1,0:T(8,128)(2,1)S(1)}, bf16[768,128]{1,0:T(8,128)(2,1)S(1)}, u32[]{:S(2)}, u32[]{:S(2)}) collective-permute-start(bf16[768,128]{1,0:T(8,128)(2,1)S(1)} %copy-done.14), channel_id=1, source_target_pairs={{0,6},{2,4},{4,2},{6,0},{1,7},{3,5},{5,3},{7,1},{8,14},{10,12},{12... | collective-permute-start | bytes 589832 | tf_op jit(solution)/shard_map/ppermute | solution.py:2443
  183.3 35.4 %copy-start.5 = (bf16[192,2048]{1,0:T(8,128)(2,1)S(1)}, bf16[192,2048]{1,0:T(8,128)(2,1)}, u32[]{:S(2)}) copy-start(bf16[192,2048]{1,0:T(8,128)(2,1)} %dynamic-slice_bitcast_fusion.1.own_ref.hidden_hbm) | copy-start | bytes 2359300
  220.4 55.1 %copy-start.2 = (f32[192,2048]{1,0:T(8,128)}, f32[192,2048]{1,0:T(8,128)S(1)}, u32[]{:S(2)}) copy-start(f32[192,2048]{1,0:T(8,128)S(1)} %get-tuple-element.209.middle_hbm) | copy-start | bytes 4718596
  235.9 157.7 %reduce-scatter.5.cloned.1.call-start = ((), (), s32[]{:S(2)}) async-start(), calls=%async_computation.8 | async-start | bytes 2621440 | tf_op jit(solution)/shard_map/reduce_scatter | solution.py:2644
  350.8 121.1 %reduce-scatter.7.cloned.1.call-start = ((), (), s32[]{:S(2)}) async-start(), calls=%async_computation.9 | async-start | bytes 5242880 | tf_op jit(solution)/shard_map/reduce_scatter | solution.py:2644
  393.6 127.8 %reduce-scatter.9.cloned.1.call-start = ((), (), s32[]{:S(2)}) async-start(), calls=%async_computation.10 | async-start | bytes 2621440 | tf_op jit(solution)/shard_map/reduce_scatter | solution.py:2644
  444.0 5.6 copy-start.9
  446.1 26.1 %collective-permute-start.3 = (bf16[768,128]{1,0:T(8,128)(2,1)S(1)}, bf16[768,128]{1,0:T(8,128)(2,1)S(1)}, u32[]{:S(2)}, u32[]{:S(2)}) collective-permute-start(bf16[768,128]{1,0:T(8,128)(2,1)S(1)} %get-tuple-element.212), channel_id=1, source_target_pairs={{0,2},{2,0},{4,6},{6,4},{1,3},{3,1},{5,7},{7,5},{8,10},{10,8},{12,... | collective-permute-start | bytes 589832 | tf_op jit(solution)/shard_map/ppermute | solution.py:2454
  447.2 25.0 %collective-permute-start.4 = (bf16[768,128]{1,0:T(8,128)(2,1)S(1)}, bf16[768,128]{1,0:T(8,128)(2,1)S(1)}, u32[]{:S(2)}, u32[]{:S(2)}) collective-permute-start(bf16[768,128]{1,0:T(8,128)(2,1)S(1)} %get-tuple-element.211), channel_id=1, source_target_pairs={{0,4},{2,6},{4,0},{6,2},{1,5},{3,7},{5,1},{7,3},{8,12},{10,14},{12... | collective-permute-start | bytes 589832 | tf_op jit(solution)/shard_map/ppermute | solution.py:2454
  448.0 24.2 %collective-permute-start.5 = (bf16[768,128]{1,0:T(8,128)(2,1)S(1)}, bf16[768,128]{1,0:T(8,128)(2,1)S(1)}, u32[]{:S(2)}, u32[]{:S(2)}) collective-permute-start(bf16[768,128]{1,0:T(8,128)(2,1)S(1)} %get-tuple-element.210), channel_id=1, source_target_pairs={{0,6},{2,4},{4,2},{6,0},{1,7},{3,5},{5,3},{7,1},{8,14},{10,12},{12... | collective-permute-start | bytes 589832 | tf_op jit(solution)/shard_map/ppermute | solution.py:2454
  472.0 125.8 %reduce-scatter.11.cloned.1.call-start = ((), (), s32[]{:S(2)}) async-start(), calls=%async_computation.11 | async-start | bytes 5242880 | tf_op jit(solution)/shard_map/reduce_scatter | solution.py:2644
  630.3 7.1 %copy-start.1 = (bf16[1,384,2048]{2,1,0:T(8,128)(2,1)S(1)}, bf16[1,384,2048]{2,1,0:T(8,128)(2,1)}, u32[]{:S(2)}) copy-start(bf16[1,384,2048]{2,1,0:T(8,128)(2,1)} %param.28) | copy-start | bytes 4718596
  (13 other events, 15.5 us)
Sparse Core Ops, SparseCore 0:
  29.8 78.8 all-gather.4
  110.3 44.4 all-gather.6
  156.3 79.4 all-gather.8
  237.3 44.4 all-gather.10
  351.0 42.5 reduce-scatter.4
  395.8 76.0 reduce-scatter.6
  474.2 44.3 reduce-scatter.8
  521.6 76.0 reduce-scatter.10

commit v6 on v5

--- a/solution.py
+++ b/solution.py
@@ -744,11 +744,13 @@
     over_x.wait_recv()
     pair_b = push(10, block(across, 1), block(across, 1), partner)
     work(across, core)
+    if ready is not None:
+        ready(across, 3, core)
     pair_a.wait_recv()
     pair_b.wait_recv()
     work(across, 1 - core)
     if ready is not None:
-        ready(across, 3)
+        ready(across, 4, 1 - core)
     for copy in (
         x_first,
         y_second,
@@ -968,10 +970,14 @@
     middle_hbm,
     teacher_hbm,
     both_hbm,
+    out_hbm,
+    d_out_hbm,
+    d_both_hbm,
+    grad_ref,
     out_ref,
     d_out_ref,
     d_both_ref,
-    grad_ref,
+    store_sems,
     own_ref,
     grad_sum,
     d_mlp_ref,
@@ -1004,19 +1010,34 @@
         d_out_ref[rows] = d_out
         own_ref[rows] = d_out.astype(jnp.bfloat16)
 
-    def ready(chip, turn_at):
-        blocks = d_mlp_ref[pl.ds(2 * chip, 2)]
+    stores = []
+
+    def leave(source, target):
+        copy = pltpu.make_async_copy(source, target, store_sems.at[len(stores)])
+        copy.start()
+        stores.append(copy)
+
+    def ready(chip, turn_at, side=None):
+        if side is None:
+            blocks = d_mlp_ref[pl.ds(2 * chip, 2)]
+            first = 2 * chip
+        else:
+            blocks = d_mlp_ref[pl.ds(2 * chip + side, 1)]
+            first = 2 * chip + side
         height = blocks.shape[0] * blocks.shape[1]
-        rows = pl.ds(pl.multiple_of(chip * height, 16), height)
+        rows = pl.ds(pl.multiple_of(first * blocks.shape[1], 16), height)
+        leave(d_both_ref.at[rows], d_both_hbm.at[rows])
         part = dot_f32(blocks.reshape(height, blocks.shape[2]), act_ref[rows], 0, 0)
         if turn_at == 0:
             grad_sum[...] = part
-        elif turn_at < GROUP - 1:
+        elif turn_at < GROUP:
             grad_sum[...] += part
         else:
             grad_ref[...] = (grad_sum[...] + part).astype(jnp.bfloat16)
 
     scatter_kernel(1, act_ref, weights_ref, None, *scratch, store=store, finishing=loaded)
+    leave(out_ref, out_hbm)
+    leave(d_out_ref, d_out_hbm)
     gather_steps(
         apply_down_back,
         own_ref,
@@ -1027,6 +1048,8 @@
         gather_recv,
         ready,
     )
+    for copy in stores:
+        copy.wait()
 
 
 def down_and_back(activated, full_down, middle, teacher_own, factor, gate_up):
@@ -1041,8 +1064,12 @@
             shaped(full_down.shape, jnp.bfloat16),
         ],
         in_specs=vmem_specs(3) + any_specs(3),
-        out_specs=vmem_specs(4),
+        out_specs=any_specs(3) + vmem_specs(1),
         scratch_shapes=[
+            pltpu.VMEM((rows, width), jnp.bfloat16),
+            pltpu.VMEM((rows, width), jnp.float32),
+            pltpu.VMEM(gate_up.shape, jnp.bfloat16),
+            pltpu.SemaphoreType.DMA((GROUP + 3,)),
             pltpu.VMEM((rows, width), jnp.bfloat16),
             pltpu.VMEM(full_down.shape, jnp.float32),
             pltpu.VMEM((2 * GROUP, rows, width), jnp.bfloat16),
@@ -1056,7 +1083,7 @@
         + scatter_scratch([(rows, width)]),
         cost_estimate=lasting(70),
         compiler_params=pltpu.CompilerParams(
-            collective_id=10, has_side_effects=True, vmem_limit_bytes=VMEM_BYTES
+            collective_id=10, has_side_effects=True, vmem_limit_bytes=VMEM_BYTES + 3 * 1024 * 1024
         ),
     )(activated, full_down, factor, middle, teacher_own, gate_up)
 
@@ -1496,9 +1523,10 @@
         dt_ref[...] = jnp.concatenate(
             [values[:, DT_LANE : DT_LANE + HEADS] for values in held], axis=1
         ).T
-        taps = bias_ref.shape[1]
+        taps = conv_ref.shape[1]
         conv_ref[...] = sums_ref[:KC, :taps]
-        bias_ref[...] = sums_ref[KC : KC + 1, :taps]
+        for row in range(bias_ref.shape[0]):
+            bias_ref[row : row + 1] = sums_ref[KC : KC + 1, 128 * row : 128 * (row + 1)]
         dtb_ref[...] = sums_ref[0:1, taps : taps + MH]
         alog_ref[...] = sums_ref[1:2, taps : taps + MH]
         skip_ref[...] = sums_ref[2:3, taps : taps + MH]
@@ -1634,7 +1662,6 @@
     for turn_by in range(1, places):
         other = lax.rem(mine + turn_by, places)
         devices.append((other // GROUP, lax.rem(other, GROUP), core))
-    meet(devices)
     half, part = HD // 2, HD // 4
     keys, values = key_ref[...], value_ref[...]
     steps = dt_ref[...].astype(jnp.float32).T.astype(keys.dtype)
@@ -1651,6 +1678,7 @@
     gains[...] = jnp.zeros_like(gains)
     gains[0:1] = one_ref[...].astype(jnp.float32)
     gains[1:2] = two_ref[...].astype(jnp.float32)
+    meet(devices)
     sources = (z_ref, q_ref, x_ref, misc)
     copies = push_moves(moves, sources, (in_ref,), local_sems, send_sems, recv_sems)
     for index, device in enumerate(devices):
@@ -2757,7 +2785,7 @@
         array.shape
         for array in (w_z, w_x, w_query, w_bc, w_key, w_value, w_dt.T, conv_weight.T)
     ]
-    shapes += [(1, conv_bias.shape[0])] + [(1, MH)] * 3 + [(MH, HP)] + [(1, slice_rows)] * 2
+    shapes += [(conv_bias.shape[0] // 128, 128)] + [(1, MH)] * 3 + [(MH, HP)] + [(1, slice_rows)] * 2
     (
         grad_z,
         grad_x,

time: 654 us -> 650 us (level)
  no operation moved by 1% of the time
where the time goes in v6:
time: 650 us; the launch traced here: 641 us
  Pallas kernels  487 us (75%)
  waiting for transfers between devices  63.4 us (10%)
  matrix products  31.1 us (5%)
  local copies, waits for them, and re-layouts  26.2 us (4%)
  between operations  16 us (2%)
  other arithmetic  9.35 us (1%)
  starting transfers between devices  8.31 us (1%)
    pallas_call x3, Pallas kernels, gather_plane(): pl.pallas_call(partial(gather_kernel, apply, len(inputs), len(outputs)),...  112 us
    pallas_call x1, Pallas kernels, down_and_back(): pl.pallas_call(down_and_back_kernel, out_shape=[shaped((rows, width), jnp...  66.9 us
    pallas_call x1, Pallas kernels, input_back(): pl.pallas_call(input_back_kernel, out_shape=[shaped((rows, width), jnp.fl...  49 us
    pallas_call x1, Pallas kernels, up_back(): pl.pallas_call(up_back_kernel, out_shape=[jax.ShapeDtypeStruct((rows, wid...  41.1 us
    pallas_call x1, Pallas kernels, ssd_backward(): pl.pallas_call(partial(ssd_backward_kernel, moves), grid=(laps,), in_spec...  36.8 us
    pallas_call x1, Pallas kernels, scatter_plane(): pl.pallas_call(partial(scatter_kernel, count), out_shape=shapes, in_specs...  35.4 us
    pallas_call x1, Pallas kernels, finish_all(): pl.pallas_call(finish_kernel, out_shape=[shaped((places,) + piece.shape,...  32.6 us
    pallas_call x1, Pallas kernels, exchange_plane(): pl.pallas_call(partial(exchange_kernel, moves, len(arrays)), out_shape=[j...  27.6 us
  transfers between devices with their start and end apart: 14, of which 9 were waited for; matrix products, arithmetic and copies ran while one was open for 9% of the time, Pallas kernels for 56%

profile of v6, /device:TPU:0, one launch (start us, length us, event | category | flops | bytes accessed | tf_op | source)
XLA Modules:
  0.0 641.3 jit_solution(3156815208446387780)
XLA Ops:
  7.3 22.4 %shard_map.435 = (bf16[4,128,1024]{2,1,0:T(8,128)(2,1)}, f32[16,8,128]{2,1,0:T(8,128)}) custom-call(bf16[128,1536]{1,0:T(8,128)(2,1)} %z_ref.1, bf16[128,512]{1,0:T(8,128)(2,1)} %q_ref.1, bf16[128,1536]{1,0:T(8,128)(2,1)} %x_ref.1, bf16[128,128]{1,0:T(8,128)(2,1)} %key_ref.1, bf16[128,128]{1,0:T(8,128)(2,1)} %value_ref.1, bf16[24,128]{1,0:T(8,128)(2,1)} %bitcast.95, ...), custom_call_target="tpu_custom_call" | custom-call | flops 17999998976 | bytes 60000000 | tf_op jit(solution)/shard_map/pallas_call | solution.py:1700
  33.2 37.2 %shard_map.436 = (bf16[8,192,2048]{2,1,0:T(8,128)(2,1)}, bf16[1536,2048]{1,0:T(8,128)(2,1)}, bf16[1536,512]{1,0:T(8,128)(2,1)}) custom-call(bf16[192,2048]{1,0:T(8,128)(2,1)} %dynamic-slice_bitcast_fusion.1.own_ref.hidden_hbm, f32[1,2048]{1,0:T(1,128)} %get-tuple-element.215.refs_0_.gain_ref, bf16[2048,512]{1,0:T(8,128)(2,1)} %bc_weights_ref.1), custom_call_target="tpu_custom_call" | custom-call | flops 31499999232 | bytes 105000000 | tf_op jit(solution)/shard_map/pallas_call | solution.py:772
  72.3 27.6 %shard_map.437 = (bf16[4,128,512]{2,1,0:T(8,128)(2,1)}, bf16[4,128,1024]{2,1,0:T(8,128)(2,1)}, bf16[4,128,512]{2,1,0:T(8,128)(2,1)}) custom-call(bf16[128,1536]{1,0:T(8,128)(2,1)} %bitcast.78, bf16[128,512]{1,0:T(8,128)(2,1)} %bitcast.82, bf16[128,2048]{1,0:T(8,128)(2,1)} %refs_2_.1, bf16[128,2048]{1,0:T(8,128)(2,1)} %refs_3_.1, bf16[128,2048]{1,0:T(8,128)(2,1)} %bitcast.75), custom_call_target="tpu_custom_call" | custom-call | flops 22499999744 | bytes 75000000 | tf_op jit(solution)/shard_map/pallas_call | solution.py:1722
  101.3 7.4 %all-gather.5.cloned.1.call-done = bf16[16,128,1024]{2,1,0:T(8,128)(2,1)} async-done(((bf16[4,128,1024]{2,1,0:T(8,128)(2,1)}), bf16[16,128,1024]{2,1,0:T(8,128)(2,1)}) %all-gather.5.cloned.1.call-update) | async-done | bytes 4194320 | tf_op jit(solution)/shard_map/all_gather | solution.py:2544
  114.8 2.1 dynamic-slice_bitcast_fusion.2
  116.9 11.8 %fusion.5.proj_ref.before_ref.raw_ref = f32[1536,1024]{1,0:T(8,128)} fusion(bf16[1536,2048]{1,0:T(8,128)(2,1)} %get-tuple-element.116.normed_hbm, bf16[2048,1024]{1,0:T(8,128)(2,1)} %bitcast.84), kind=kOutput, calls=%fused_computation.59 | convolution fusion | flops 6442450944 | bytes 16777216 | tf_op jit(solution)/shard_map/dot_general | solution.py:47
  128.7 18.5 %shard_map.438 = (bf16[1536,384]{1,0:T(8,128)(2,1)}, f32[1536,384]{1,0:T(8,128)}, f32[12,256,384]{2,1,0:T(8,128)}, bf16[1536,896]{1,0:T(8,128)(2,1)}, f32[1536,896]{1,0:T(8,128)}, /*index=5*/bf16[768,128]{1,0:T(8,128)(2,1)}) custom-call(f32[1536,1024]{1,0:T(8,128)} %fusion.5.proj_ref.before_ref.raw_ref, f32[1536,1024]{1,0:T(8,128)} %fusion.5.proj_ref.before_ref.raw_ref, ...), custom_call_target="tpu_custom_call" | custom-call | flops 5400000000 | bytes 18000000 | tf_op jit(solution)/shard_map/pallas_call | solution.py:2217
  147.3 7.6 %all-gather.7.cloned.1.call-done = bf16[16,128,512]{2,1,0:T(8,128)(2,1)} async-done(((bf16[4,128,512]{2,1,0:T(8,128)(2,1)}), bf16[16,128,512]{2,1,0:T(8,128)(2,1)}) %all-gather.7.cloned.1.call-update) | async-done | bytes 2097168 | tf_op jit(solution)/shard_map/all_gather | solution.py:2572
  162.9 4.0 collective-permute-done
  166.9 4.2 collective-permute-done.1
  172.1 9.0 %shard_map.439 = (bf16[1536,128]{1,0:T(8,128)(2,1)}, f32[1536,1]{1,0:T(8,128)}, bf16[1536,128]{1,0:T(8,128)(2,1)}, bf16[1536,128]{1,0:T(8,128)(2,1)}, bf16[1536,128]{1,0:T(8,128)(2,1)}) custom-call(f32[1536,1024]{1,0:T(8,128)} %fusion.5.proj_ref.before_ref.raw_ref, f32[1536,128]{1,0:T(8,128)} %constant.100.clone.cos_ref, ...), custom_call_target="tpu_custom_call" | custom-call | flops 8099999744 | bytes 27000000 | tf_op jit(solution)/shard_map/pallas_call | solution.py:2446
  183.3 35.4 %shard_map.440 = f32[192,2048]{1,0:T(8,128)} custom-call(bf16[1536,512]{1,0:T(8,128)(2,1)} %copy-done.8, bf16[2048,512]{1,0:T(8,128)(2,1)} %bitcast.88), custom_call_target="tpu_custom_call" | custom-call | flops 31499999232 | bytes 105000000 | tf_op jit(solution)/shard_map/pallas_call | solution.py:1234
  218.7 1.7 multiply_reduce_fusion.2
  220.5 15.5 %all-gather.9.cloned.1.call-done = bf16[16,128,1024]{2,1,0:T(8,128)(2,1)} async-done(((bf16[4,128,1024]{2,1,0:T(8,128)(2,1)}), bf16[16,128,1024]{2,1,0:T(8,128)(2,1)}) %all-gather.9.cloned.1.call-update) | async-done | bytes 4194320 | tf_op jit(solution)/shard_map/all_gather | solution.py:2631
  237.2 38.3 %shard_map.441 = (bf16[8,192,2048]{2,1,0:T(8,128)(2,1)}, f32[1536,1024]{1,0:T(8,128)}, bf16[1536,512]{1,0:T(8,128)(2,1)}) custom-call(bf16[192,2048]{1,0:T(8,128)(2,1)} %multiply_convert_fusion.own_ref, bf16[2048,1024]{1,0:T(8,128)(2,1)} %bitcast.86), custom_call_target="tpu_custom_call" | custom-call | flops 31499999232 | bytes 105000000 | tf_op jit(solution)/shard_map/pallas_call | solution.py:772
  275.6 6.3 all-gather.11.cloned.1.call-done
  281.8 66.9 %shard_map.442 = (bf16[192,2048]{1,0:T(8,128)(2,1)}, f32[192,2048]{1,0:T(8,128)}, bf16[1536,1024]{1,0:T(8,128)(2,1)}, bf16[2048,512]{1,0:T(8,128)(2,1)}) custom-call(bf16[1536,512]{1,0:T(8,128)(2,1)} %get-tuple-element.139.act_ref, bf16[2048,512]{1,0:T(8,128)(2,1)} %bitcast.90, f32[192,1]{1,0:T(8,128)} %copy.86.factor_ref, f32[192,2048]{1,0:T(8,128)} %copy-done.2, ...), custom_call_target="tpu_custom_call" | custom-call | flops 62999998464 | bytes 210000000 | tf_op jit(solution)/shard_map/pallas_call | solution.py:1058
  348.9 41.1 %shard_map.443 = (f32[192,2048]{1,0:T(8,128)}, bf16[2048,1024]{1,0:T(8,128)(2,1)}) custom-call(bf16[1536,1024]{1,0:T(8,128)(2,1)} %get-tuple-element.144.d_both_ref, bf16[2048,1024]{1,0:T(8,128)(2,1)} %bitcast.87, bf16[1536,2048]{1,0:T(8,128)(2,1)} %bitcast.99), custom_call_target="tpu_custom_call" | custom-call | flops 34200000512 | bytes 114000000 | tf_op jit(solution)/shard_map/pallas_call | solution.py:1107
  394.7 1.9 fusion.3
  396.6 36.0 %shard_map.444 = (bf16[8,192,2048]{2,1,0:T(8,128)(2,1)}, f32[1536,384]{1,0:T(8,128)}, bf16[1536,128]{1,0:T(8,128)(2,1)}) custom-call(bf16[192,2048]{1,0:T(8,128)(2,1)} %get-tuple-element.148.own_ref, bf16[2048,512]{1,0:T(8,128)(2,1)} %bitcast.89), custom_call_target="tpu_custom_call" | custom-call | flops 31499999232 | bytes 105000000 | tf_op jit(solution)/shard_map/pallas_call | solution.py:772
  432.6 9.3 %shard_map.445 = (bf16[1536,128]{1,0:T(8,128)(2,1)}, bf16[4,768,128]{2,1,0:T(8,128)(2,1)}) custom-call(bf16[1536,128]{1,0:T(8,128)(2,1)} %get-tuple-element.150.q_ref, bf16[1536,128]{1,0:T(8,128)(2,1)} %get-tuple-element.151.k_ref, bf16[1536,128]{1,0:T(8,128)(2,1)} %get-tuple-element.152.v_ref, f32[1536,128]{1,0:T(8,128)} %constant.100.clone.cos_ref, ...), custom_call_target="tpu_custom_call" | custom-call | flops 8099999744 | bytes 27000000 | tf_op jit(solution)/shard_map/pallas_call | solution.py:2446
  441.9 2.1 dynamic-slice_bitcast_fusion.4
  447.4 7.7 %convolution_convert_fusion.1 = bf16[2048,512]{1,0:T(8,128)(2,1)} fusion(bf16[1536,2048]{1,0:T(8,128)(2,1)} %bitcast.98, bf16[1536,512]{1,0:T(8,128)(2,1)S(1)} %copy-done.9), kind=kOutput, calls=%fused_computation.2 | convolution fusion | flops 3222274048 | bytes 9961472 | tf_op jit(solution)/shard_map/dot_general | solution.py:51
  455.1 14.7 %reduce-scatter.7.cloned.1.call-done = bf16[512,1024]{1,0:T(8,128)(2,1)} async-done(((bf16[2048,1024]{1,0:T(8,128)(2,1)}), bf16[512,1024]{1,0:T(8,128)(2,1)}) %reduce-scatter.7.cloned.1.call-update) | async-done | bytes 1048592 | tf_op jit(solution)/shard_map/reduce_scatter | solution.py:2672
  470.9 36.8 %shard_map.446 = (bf16[1536,1536]{1,0:T(8,128)(2,1)}, f32[8,896]{1,0:T(8,128)}, f32[8,128]{1,0:T(8,128)}, f32[1,384]{1,0:T(1,128)}, f32[1,384]{1,0:T(1,128)}, /*...) custom-call(f32[1536,1024]{1,0:T(8,128)} %fusion.5.proj_ref.before_ref.raw_ref, ...), custom_call_target="tpu_custom_call" | custom-call | flops 43200000000 | bytes 144000000 | tf_op jit(solution)/shard_map/pallas_call | solution.py:2250
  507.7 11.6 %convolution_convert_fusion = bf16[2048,1024]{1,0:T(8,128)(2,1)} fusion(bf16[1536,2048]{1,0:T(8,128)(2,1)} %get-tuple-element.116.normed_hbm, bf16[1536,1536]{1,0:T(8,128)(2,1)} %get-tuple-element.167.left_ref), kind=kOutput, calls=%fused_computation | convolution fusion | flops 6444548096 | bytes 13631488 | tf_op jit(solution)/shard_map/dot_general | solution.py:51
  521.7 49.0 %shard_map.447 = (f32[192,2048]{1,0:T(8,128)}, f32[128,1024]{1,0:T(8,128)}, f32[8,2048]{1,0:T(8,128)}) custom-call(bf16[1536,1536]{1,0:T(8,128)(2,1)} %get-tuple-element.167.left_ref, bf16[2048,1024]{1,0:T(8,128)(2,1)} %bitcast.85, bf16[2048,512]{1,0:T(8,128)(2,1)} %bc_weights_ref.1, f32[1,2048]{1,0:T(1,128)} %get-tuple-element.215.refs_0_.gain_ref, ...), custom_call_target="tpu_custom_call" | custom-call | flops 44999999488 | bytes 150000000 | tf_op jit(solution)/shard_map/pallas_call | solution.py:1187
  572.3 14.6 %shard_map.448 = (f32[8,640]{1,0:T(8,128)}, f32[2,192,2048]{2,1,0:T(8,128)}, bf16[2,192,2048]{2,1,0:T(8,128)(2,1)}, bf16[4,128,512]{2,1,0:T(8,128)(2,1)}) custom-call(f32[8,5120]{1,0:T(8,128)} %pad.15.small_ref, f32[192,2048]{1,0:T(8,128)} %get-tuple-element.170.own_ref, bf16[192,2048]{1,0:T(8,128)(2,1)} %get-tuple-element.171.out_ref, ...), custom_call_target="tpu_custom_call" | custom-call | flops 17999998976 | bytes 60000000 | tf_op jit(solution)/shard_map/pallas_call | solution.py:1296
  586.9 6.6 %shard_map.449 = (f32[128,2048]{1,0:T(8,128)}, f32[128,2048]{1,0:T(8,128)}, f32[2048,128]{1,0:T(8,128)}, f32[1536,128]{1,0:T(8,128)}, f32[512,128]{1,0:T(8,128)}...) custom-call(bf16[4,128,1024]{2,1,0:T(8,128)(2,1)} %get-tuple-element.159.gu_ref, ...), custom_call_target="tpu_custom_call" | custom-call | flops 5400000000 | bytes 18000000 | tf_op jit(solution)/shard_map/pallas_call | solution.py:1572
  593.5 2.1 reduce-scatter.11.cloned.1.call-done
  595.6 32.6 %shard_map.450 = (f32[8,8,640]{2,1,0:T(8,128)}, bf16[8,4,32,1024]{3,2,1,0:T(8,128)(2,1)}, bf16[4,128,1024]{2,1,0:T(8,128)(2,1)}) custom-call(f32[8,640]{1,0:T(8,128)} %get-tuple-element.178.piece_ref, f32[128,1024]{1,0:T(8,128)} %get-tuple-element.179.bc_ref, bf16[4,128,1024]{2,1,0:T(8,128)(2,1)} %bitcast.91), custom_call_target="tpu_custom_call" | custom-call | flops 27000000512 | bytes 90000000 | tf_op jit(solution)/shard_map/pallas_call | solution.py:1427
  628.2 5.7 shard_map.451
  (166 shorter events, 37.7 us)
Async XLA Ops:
  7.2 22.6 %copy-start = (bf16[1,384,2048]{2,1,0:T(8,128)(2,1)S(1)}, bf16[1,384,2048]{2,1,0:T(8,128)(2,1)}, u32[]{:S(2)}) copy-start(bf16[1,384,2048]{2,1,0:T(8,128)(2,1)} %param.28) | copy-start | bytes 4718596
  7.2 101.5 %all-gather.5.cloned.1.call-start = ((), (), s32[]{:S(2)}) async-start(), calls=%async_computation.4 | async-start | bytes 5242880 | tf_op jit(solution)/shard_map/all_gather | solution.py:2544
  29.7 125.1 %all-gather.7.cloned.1.call-start = ((), (), s32[]{:S(2)}) async-start(), calls=%async_computation.5 | async-start | bytes 2621440 | tf_op jit(solution)/shard_map/all_gather | solution.py:2572
  33.2 37.2 %copy-start.15 = (bf16[512,128]{1,0:T(8,128)(2,1)S(1)}, bf16[512,128]{1,0:T(8,128)(2,1)}, u32[]{:S(2)}) copy-start(bf16[512,128]{1,0:T(8,128)(2,1)} %param.47) | copy-start | bytes 393220
  33.2 38.0 %copy-start.11 = (bf16[2048,128]{1,0:T(8,128)(2,1)S(1)}, bf16[2048,128]{1,0:T(8,128)(2,1)}, u32[]{:S(2)}) copy-start(bf16[2048,128]{1,0:T(8,128)(2,1)} %param.51) | copy-start | bytes 1572868
  72.2 27.6 %copy-start.19 = (f32[3584]{0:T(1024)S(1)}, f32[3584]{0:T(1024)}, u32[]{:S(2)}) copy-start(f32[3584]{0:T(1024)} %param.38) | copy-start | bytes 43012
  72.2 28.0 %copy-start.23 = (f32[48]{0:T(128)S(1)}, f32[48]{0:T(128)}, u32[]{:S(2)}) copy-start(f32[48]{0:T(128)} %param.40) | copy-start | bytes 580
  72.2 28.0 %copy-start.24 = (f32[48]{0:T(128)S(1)}, f32[48]{0:T(128)}, u32[]{:S(2)}) copy-start(f32[48]{0:T(128)} %param.39) | copy-start | bytes 580
  72.2 28.8 %slice-start.1 = ((f32[3584]{0:T(1024)}), f32[512]{0:T(512)S(1)}, s32[]{:S(2)}) async-start(f32[3584]{0:T(1024)} %param.38), calls=%async_computation.13 | async-start | bytes 4096 | tf_op jit(solution)/shard_map/slice | solution.py:2591
  72.3 28.8 %copy-start.16 = (f32[3584,4]{0,1:T(4,128)S(1)}, f32[3584,4]{0,1:T(4,128)}, u32[]{:S(2)}) copy-start(f32[3584,4]{0,1:T(4,128)} %param.37) | copy-start | bytes 172036
  99.8 12.9 %copy-start.28 = (f32[48]{0:T(128)S(1)}, f32[48]{0:T(128)}, u32[]{:S(2)}) copy-start(f32[48]{0:T(128)} %param.41) | copy-start | bytes 580
  99.9 14.3 %slice-start = ((f32[3584,4]{0,1:T(4,128)}), f32[512,4]{0,1:T(4,128)S(1)}, s32[]{:S(2)}) async-start(f32[3584,4]{0,1:T(4,128)} %param.37), calls=%async_computation.12 | async-start | bytes 16384 | tf_op jit(solution)/shard_map/slice | solution.py:2591
  108.8 127.1 %all-gather.9.cloned.1.call-start = ((), (), s32[]{:S(2)}) async-start(), calls=%async_computation.6 | async-start | bytes 5242880 | tf_op jit(solution)/shard_map/all_gather | solution.py:2631
  128.7 27.2 %copy-start.18 = (s32[4,1536]{1,0:T(4,128)S(1)}, s32[4,1536]{1,0:T(4,128)}, u32[]{:S(2)}) copy-start(s32[4,1536]{1,0:T(4,128)} %param.31) | copy-start | bytes 73732
  128.7 29.4 %copy-start.12 = (bf16[1,384,2048]{2,1,0:T(8,128)(2,1)S(1)}, bf16[1,384,2048]{2,1,0:T(8,128)(2,1)}, u32[]{:S(2)}) copy-start(bf16[1,384,2048]{2,1,0:T(8,128)(2,1)} %param.29) | copy-start | bytes 4718596
  147.2 11.9 %copy-start.14 = (bf16[768,128]{1,0:T(8,128)(2,1)S(1)}, bf16[768,128]{1,0:T(8,128)(2,1)}, u32[]{:S(2)}) copy-start(bf16[768,128]{1,0:T(8,128)(2,1)} %get-tuple-element.132) | copy-start | bytes 589828
  147.3 15.3 %copy-start.7 = (bf16[1536,384]{1,0:T(8,128)(2,1)S(1)}, bf16[1536,384]{1,0:T(8,128)(2,1)}, u32[]{:S(2)}) copy-start(bf16[1536,384]{1,0:T(8,128)(2,1)} %get-tuple-element.131) | copy-start | bytes 3538948
  154.9 127.0 %all-gather.11.cloned.1.call-start = ((), (), s32[]{:S(2)}) async-start(), calls=%async_computation.7 | async-start | bytes 2621440 | tf_op jit(solution)/shard_map/all_gather | solution.py:2632
  159.1 7.8 %collective-permute-start = (bf16[768,128]{1,0:T(8,128)(2,1)S(1)}, bf16[768,128]{1,0:T(8,128)(2,1)S(1)}, u32[]{:S(2)}, u32[]{:S(2)}) collective-permute-start(bf16[768,128]{1,0:T(8,128)(2,1)S(1)} %copy-done.14), channel_id=1, source_target_pairs={{0,2},{2,0},{4,6},{6,4},{1,3},{3,1},{5,7},{7,5},{8,10},{10,8},{12,... | collective-permute-start | bytes 589832 | tf_op jit(solution)/shard_map/ppermute | solution.py:2471
  160.6 10.6 %collective-permute-start.1 = (bf16[768,128]{1,0:T(8,128)(2,1)S(1)}, bf16[768,128]{1,0:T(8,128)(2,1)S(1)}, u32[]{:S(2)}, u32[]{:S(2)}) collective-permute-start(bf16[768,128]{1,0:T(8,128)(2,1)S(1)} %copy-done.14), channel_id=1, source_target_pairs={{0,4},{2,6},{4,0},{6,2},{1,5},{3,7},{5,1},{7,3},{8,12},{10,14},{12... | collective-permute-start | bytes 589832 | tf_op jit(solution)/shard_map/ppermute | solution.py:2471
  162.0 9.2 %collective-permute-start.2 = (bf16[768,128]{1,0:T(8,128)(2,1)S(1)}, bf16[768,128]{1,0:T(8,128)(2,1)S(1)}, u32[]{:S(2)}, u32[]{:S(2)}) collective-permute-start(bf16[768,128]{1,0:T(8,128)(2,1)S(1)} %copy-done.14), channel_id=1, source_target_pairs={{0,6},{2,4},{4,2},{6,0},{1,7},{3,5},{5,3},{7,1},{8,14},{10,12},{12... | collective-permute-start | bytes 589832 | tf_op jit(solution)/shard_map/ppermute | solution.py:2471
  183.3 35.4 %copy-start.5 = (bf16[192,2048]{1,0:T(8,128)(2,1)S(1)}, bf16[192,2048]{1,0:T(8,128)(2,1)}, u32[]{:S(2)}) copy-start(bf16[192,2048]{1,0:T(8,128)(2,1)} %dynamic-slice_bitcast_fusion.1.own_ref.hidden_hbm) | copy-start | bytes 2359300
  220.4 55.1 %copy-start.2 = (f32[192,2048]{1,0:T(8,128)}, f32[192,2048]{1,0:T(8,128)S(1)}, u32[]{:S(2)}) copy-start(f32[192,2048]{1,0:T(8,128)S(1)} %get-tuple-element.209.middle_hbm) | copy-start | bytes 4718596
  235.9 155.5 %reduce-scatter.5.cloned.1.call-start = ((), (), s32[]{:S(2)}) async-start(), calls=%async_computation.8 | async-start | bytes 2621440 | tf_op jit(solution)/shard_map/reduce_scatter | solution.py:2672
  348.8 121.0 %reduce-scatter.7.cloned.1.call-start = ((), (), s32[]{:S(2)}) async-start(), calls=%async_computation.9 | async-start | bytes 5242880 | tf_op jit(solution)/shard_map/reduce_scatter | solution.py:2672
  391.5 127.8 %reduce-scatter.9.cloned.1.call-start = ((), (), s32[]{:S(2)}) async-start(), calls=%async_computation.10 | async-start | bytes 2621440 | tf_op jit(solution)/shard_map/reduce_scatter | solution.py:2672
  441.9 5.6 copy-start.9
  443.9 26.1 %collective-permute-start.3 = (bf16[768,128]{1,0:T(8,128)(2,1)S(1)}, bf16[768,128]{1,0:T(8,128)(2,1)S(1)}, u32[]{:S(2)}, u32[]{:S(2)}) collective-permute-start(bf16[768,128]{1,0:T(8,128)(2,1)S(1)} %get-tuple-element.212), channel_id=1, source_target_pairs={{0,2},{2,0},{4,6},{6,4},{1,3},{3,1},{5,7},{7,5},{8,10},{10,8},{12,... | collective-permute-start | bytes 589832 | tf_op jit(solution)/shard_map/ppermute | solution.py:2482
  445.0 25.1 %collective-permute-start.4 = (bf16[768,128]{1,0:T(8,128)(2,1)S(1)}, bf16[768,128]{1,0:T(8,128)(2,1)S(1)}, u32[]{:S(2)}, u32[]{:S(2)}) collective-permute-start(bf16[768,128]{1,0:T(8,128)(2,1)S(1)} %get-tuple-element.211), channel_id=1, source_target_pairs={{0,4},{2,6},{4,0},{6,2},{1,5},{3,7},{5,1},{7,3},{8,12},{10,14},{12... | collective-permute-start | bytes 589832 | tf_op jit(solution)/shard_map/ppermute | solution.py:2482
  445.9 24.2 %collective-permute-start.5 = (bf16[768,128]{1,0:T(8,128)(2,1)S(1)}, bf16[768,128]{1,0:T(8,128)(2,1)S(1)}, u32[]{:S(2)}, u32[]{:S(2)}) collective-permute-start(bf16[768,128]{1,0:T(8,128)(2,1)S(1)} %get-tuple-element.210), channel_id=1, source_target_pairs={{0,6},{2,4},{4,2},{6,0},{1,7},{3,5},{5,3},{7,1},{8,14},{10,12},{12... | collective-permute-start | bytes 589832 | tf_op jit(solution)/shard_map/ppermute | solution.py:2482
  469.8 125.8 %reduce-scatter.11.cloned.1.call-start = ((), (), s32[]{:S(2)}) async-start(), calls=%async_computation.11 | async-start | bytes 5242880 | tf_op jit(solution)/shard_map/reduce_scatter | solution.py:2672
  628.2 5.8 copy-start.1
  (13 other events, 15.6 us)
Sparse Core Ops, SparseCore 0:
  29.8 78.9 all-gather.4
  110.3 44.4 all-gather.6
  156.4 79.4 all-gather.8
  237.3 44.4 all-gather.10
  348.9 42.4 reduce-scatter.4
  393.7 76.0 reduce-scatter.6
  472.1 44.3 reduce-scatter.8
  519.5 76.1 reduce-scatter.10

commit v7 on v6

--- a/solution.py
+++ b/solution.py
@@ -1468,8 +1468,8 @@
     output_ref[...] = both_out[0]
     gate_ref[...] = gu_ref[0, :, :units].astype(jnp.float32)
     up_ref[...] = gu_ref[0, :, units:].astype(jnp.float32)
-    d_ref[...] = down_ref[0].astype(jnp.float32).T
-    turned = out_ref[0].astype(jnp.float32).T
+    d_ref[...] = down_ref[0].T.astype(jnp.float32)
+    turned = out_ref[0].T.astype(jnp.float32)
     mo_ref[...] = turned[:width]
     ao_ref[...] = turned[width:]
 
@@ -1502,7 +1502,7 @@
     x_ref[...] = in_ref[0, :, width + HD : 2 * width + HD].astype(jnp.float32)
     wide = bc_ref.shape[2]
     for core in range(2):
-        grad_bc_ref[wide * core : wide * (core + 1)] = bc_ref[core].astype(jnp.float32).T
+        grad_bc_ref[wide * core : wide * (core + 1)] = bc_ref[core].T.astype(jnp.float32)
 
     @pl.when(pl.program_id(0) == 0)
     def _():

time: 650 us -> 650 us (level)
  no operation moved by 1% of the time
where the time goes in v7:
time: 650 us; the launch traced here: 641 us
  Pallas kernels  487 us (75%)
  waiting for transfers between devices  63.4 us (10%)
  matrix products  31.1 us (5%)
  local copies, waits for them, and re-layouts  26.2 us (4%)
  between operations  16 us (2%)
  other arithmetic  9.35 us (1%)
  starting transfers between devices  8.31 us (1%)
    pallas_call x3, Pallas kernels, gather_plane(): pl.pallas_call(partial(gather_kernel, apply, len(inputs), len(outputs)),...  112 us
    pallas_call x1, Pallas kernels, down_and_back(): pl.pallas_call(down_and_back_kernel, out_shape=[shaped((rows, width), jnp...  66.9 us
    pallas_call x1, Pallas kernels, input_back(): pl.pallas_call(input_back_kernel, out_shape=[shaped((rows, width), jnp.fl...  49 us
    pallas_call x1, Pallas kernels, up_back(): pl.pallas_call(up_back_kernel, out_shape=[jax.ShapeDtypeStruct((rows, wid...  41.1 us
    pallas_call x1, Pallas kernels, ssd_backward(): pl.pallas_call(partial(ssd_backward_kernel, moves), grid=(laps,), in_spec...  36.8 us
    pallas_call x1, Pallas kernels, scatter_plane(): pl.pallas_call(partial(scatter_kernel, count), out_shape=shapes, in_specs...  35.4 us
    pallas_call x1, Pallas kernels, finish_all(): pl.pallas_call(finish_kernel, out_shape=[shaped((places,) + piece.shape,...  32.6 us
    pallas_call x1, Pallas kernels, exchange_plane(): pl.pallas_call(partial(exchange_kernel, moves, len(arrays)), out_shape=[j...  27.6 us
  transfers between devices with their start and end apart: 14, of which 9 were waited for; matrix products, arithmetic and copies ran while one was open for 9% of the time, Pallas kernels for 56%

profile of v7, /device:TPU:0, one launch (start us, length us, event | category | flops | bytes accessed | tf_op | source)
XLA Modules:
  0.0 641.2 jit_solution(11835599559491491888)
XLA Ops:
  7.3 22.4 %shard_map.435 = (bf16[4,128,1024]{2,1,0:T(8,128)(2,1)}, f32[16,8,128]{2,1,0:T(8,128)}) custom-call(bf16[128,1536]{1,0:T(8,128)(2,1)} %z_ref.1, bf16[128,512]{1,0:T(8,128)(2,1)} %q_ref.1, bf16[128,1536]{1,0:T(8,128)(2,1)} %x_ref.1, bf16[128,128]{1,0:T(8,128)(2,1)} %key_ref.1, bf16[128,128]{1,0:T(8,128)(2,1)} %value_ref.1, bf16[24,128]{1,0:T(8,128)(2,1)} %bitcast.95, ...), custom_call_target="tpu_custom_call" | custom-call | flops 17999998976 | bytes 60000000 | tf_op jit(solution)/shard_map/pallas_call | solution.py:1700
  33.2 37.2 %shard_map.436 = (bf16[8,192,2048]{2,1,0:T(8,128)(2,1)}, bf16[1536,2048]{1,0:T(8,128)(2,1)}, bf16[1536,512]{1,0:T(8,128)(2,1)}) custom-call(bf16[192,2048]{1,0:T(8,128)(2,1)} %dynamic-slice_bitcast_fusion.1.own_ref.hidden_hbm, f32[1,2048]{1,0:T(1,128)} %get-tuple-element.215.refs_0_.gain_ref, bf16[2048,512]{1,0:T(8,128)(2,1)} %bc_weights_ref.1), custom_call_target="tpu_custom_call" | custom-call | flops 31499999232 | bytes 105000000 | tf_op jit(solution)/shard_map/pallas_call | solution.py:772
  72.3 27.6 %shard_map.437 = (bf16[4,128,512]{2,1,0:T(8,128)(2,1)}, bf16[4,128,1024]{2,1,0:T(8,128)(2,1)}, bf16[4,128,512]{2,1,0:T(8,128)(2,1)}) custom-call(bf16[128,1536]{1,0:T(8,128)(2,1)} %bitcast.78, bf16[128,512]{1,0:T(8,128)(2,1)} %bitcast.82, bf16[128,2048]{1,0:T(8,128)(2,1)} %refs_2_.1, bf16[128,2048]{1,0:T(8,128)(2,1)} %refs_3_.1, bf16[128,2048]{1,0:T(8,128)(2,1)} %bitcast.75), custom_call_target="tpu_custom_call" | custom-call | flops 22499999744 | bytes 75000000 | tf_op jit(solution)/shard_map/pallas_call | solution.py:1722
  101.3 7.4 %all-gather.5.cloned.1.call-done = bf16[16,128,1024]{2,1,0:T(8,128)(2,1)} async-done(((bf16[4,128,1024]{2,1,0:T(8,128)(2,1)}), bf16[16,128,1024]{2,1,0:T(8,128)(2,1)}) %all-gather.5.cloned.1.call-update) | async-done | bytes 4194320 | tf_op jit(solution)/shard_map/all_gather | solution.py:2544
  114.8 2.1 dynamic-slice_bitcast_fusion.2
  116.9 11.8 %fusion.5.proj_ref.before_ref.raw_ref = f32[1536,1024]{1,0:T(8,128)} fusion(bf16[1536,2048]{1,0:T(8,128)(2,1)} %get-tuple-element.116.normed_hbm, bf16[2048,1024]{1,0:T(8,128)(2,1)} %bitcast.84), kind=kOutput, calls=%fused_computation.59 | convolution fusion | flops 6442450944 | bytes 16777216 | tf_op jit(solution)/shard_map/dot_general | solution.py:47
  128.7 18.5 %shard_map.438 = (bf16[1536,384]{1,0:T(8,128)(2,1)}, f32[1536,384]{1,0:T(8,128)}, f32[12,256,384]{2,1,0:T(8,128)}, bf16[1536,896]{1,0:T(8,128)(2,1)}, f32[1536,896]{1,0:T(8,128)}, /*index=5*/bf16[768,128]{1,0:T(8,128)(2,1)}) custom-call(f32[1536,1024]{1,0:T(8,128)} %fusion.5.proj_ref.before_ref.raw_ref, f32[1536,1024]{1,0:T(8,128)} %fusion.5.proj_ref.before_ref.raw_ref, ...), custom_call_target="tpu_custom_call" | custom-call | flops 5400000000 | bytes 18000000 | tf_op jit(solution)/shard_map/pallas_call | solution.py:2217
  147.3 7.6 %all-gather.7.cloned.1.call-done = bf16[16,128,512]{2,1,0:T(8,128)(2,1)} async-done(((bf16[4,128,512]{2,1,0:T(8,128)(2,1)}), bf16[16,128,512]{2,1,0:T(8,128)(2,1)}) %all-gather.7.cloned.1.call-update) | async-done | bytes 2097168 | tf_op jit(solution)/shard_map/all_gather | solution.py:2572
  162.9 4.0 collective-permute-done
  166.9 4.2 collective-permute-done.1
  172.1 9.0 %shard_map.439 = (bf16[1536,128]{1,0:T(8,128)(2,1)}, f32[1536,1]{1,0:T(8,128)}, bf16[1536,128]{1,0:T(8,128)(2,1)}, bf16[1536,128]{1,0:T(8,128)(2,1)}, bf16[1536,128]{1,0:T(8,128)(2,1)}) custom-call(f32[1536,1024]{1,0:T(8,128)} %fusion.5.proj_ref.before_ref.raw_ref, f32[1536,128]{1,0:T(8,128)} %constant.100.clone.cos_ref, ...), custom_call_target="tpu_custom_call" | custom-call | flops 8099999744 | bytes 27000000 | tf_op jit(solution)/shard_map/pallas_call | solution.py:2446
  183.3 35.4 %shard_map.440 = f32[192,2048]{1,0:T(8,128)} custom-call(bf16[1536,512]{1,0:T(8,128)(2,1)} %copy-done.8, bf16[2048,512]{1,0:T(8,128)(2,1)} %bitcast.88), custom_call_target="tpu_custom_call" | custom-call | flops 31499999232 | bytes 105000000 | tf_op jit(solution)/shard_map/pallas_call | solution.py:1234
  218.7 1.7 multiply_reduce_fusion.2
  220.5 15.5 %all-gather.9.cloned.1.call-done = bf16[16,128,1024]{2,1,0:T(8,128)(2,1)} async-done(((bf16[4,128,1024]{2,1,0:T(8,128)(2,1)}), bf16[16,128,1024]{2,1,0:T(8,128)(2,1)}) %all-gather.9.cloned.1.call-update) | async-done | bytes 4194320 | tf_op jit(solution)/shard_map/all_gather | solution.py:2631
  237.2 38.3 %shard_map.441 = (bf16[8,192,2048]{2,1,0:T(8,128)(2,1)}, f32[1536,1024]{1,0:T(8,128)}, bf16[1536,512]{1,0:T(8,128)(2,1)}) custom-call(bf16[192,2048]{1,0:T(8,128)(2,1)} %multiply_convert_fusion.own_ref, bf16[2048,1024]{1,0:T(8,128)(2,1)} %bitcast.86), custom_call_target="tpu_custom_call" | custom-call | flops 31499999232 | bytes 105000000 | tf_op jit(solution)/shard_map/pallas_call | solution.py:772
  275.6 6.3 all-gather.11.cloned.1.call-done
  281.8 66.9 %shard_map.442 = (bf16[192,2048]{1,0:T(8,128)(2,1)}, f32[192,2048]{1,0:T(8,128)}, bf16[1536,1024]{1,0:T(8,128)(2,1)}, bf16[2048,512]{1,0:T(8,128)(2,1)}) custom-call(bf16[1536,512]{1,0:T(8,128)(2,1)} %get-tuple-element.139.act_ref, bf16[2048,512]{1,0:T(8,128)(2,1)} %bitcast.90, f32[192,1]{1,0:T(8,128)} %copy.86.factor_ref, f32[192,2048]{1,0:T(8,128)} %copy-done.2, ...), custom_call_target="tpu_custom_call" | custom-call | flops 62999998464 | bytes 210000000 | tf_op jit(solution)/shard_map/pallas_call | solution.py:1058
  348.9 41.1 %shard_map.443 = (f32[192,2048]{1,0:T(8,128)}, bf16[2048,1024]{1,0:T(8,128)(2,1)}) custom-call(bf16[1536,1024]{1,0:T(8,128)(2,1)} %get-tuple-element.144.d_both_ref, bf16[2048,1024]{1,0:T(8,128)(2,1)} %bitcast.87, bf16[1536,2048]{1,0:T(8,128)(2,1)} %bitcast.99), custom_call_target="tpu_custom_call" | custom-call | flops 34200000512 | bytes 114000000 | tf_op jit(solution)/shard_map/pallas_call | solution.py:1107
  394.7 1.9 fusion.3
  396.6 36.0 %shard_map.444 = (bf16[8,192,2048]{2,1,0:T(8,128)(2,1)}, f32[1536,384]{1,0:T(8,128)}, bf16[1536,128]{1,0:T(8,128)(2,1)}) custom-call(bf16[192,2048]{1,0:T(8,128)(2,1)} %get-tuple-element.148.own_ref, bf16[2048,512]{1,0:T(8,128)(2,1)} %bitcast.89), custom_call_target="tpu_custom_call" | custom-call | flops 31499999232 | bytes 105000000 | tf_op jit(solution)/shard_map/pallas_call | solution.py:772
  432.6 9.3 %shard_map.445 = (bf16[1536,128]{1,0:T(8,128)(2,1)}, bf16[4,768,128]{2,1,0:T(8,128)(2,1)}) custom-call(bf16[1536,128]{1,0:T(8,128)(2,1)} %get-tuple-element.150.q_ref, bf16[1536,128]{1,0:T(8,128)(2,1)} %get-tuple-element.151.k_ref, bf16[1536,128]{1,0:T(8,128)(2,1)} %get-tuple-element.152.v_ref, f32[1536,128]{1,0:T(8,128)} %constant.100.clone.cos_ref, ...), custom_call_target="tpu_custom_call" | custom-call | flops 8099999744 | bytes 27000000 | tf_op jit(solution)/shard_map/pallas_call | solution.py:2446
  441.9 2.1 dynamic-slice_bitcast_fusion.4
  447.4 7.7 %convolution_convert_fusion.1 = bf16[2048,512]{1,0:T(8,128)(2,1)} fusion(bf16[1536,2048]{1,0:T(8,128)(2,1)} %bitcast.98, bf16[1536,512]{1,0:T(8,128)(2,1)S(1)} %copy-done.9), kind=kOutput, calls=%fused_computation.2 | convolution fusion | flops 3222274048 | bytes 9961472 | tf_op jit(solution)/shard_map/dot_general | solution.py:51
  455.1 14.7 %reduce-scatter.7.cloned.1.call-done = bf16[512,1024]{1,0:T(8,128)(2,1)} async-done(((bf16[2048,1024]{1,0:T(8,128)(2,1)}), bf16[512,1024]{1,0:T(8,128)(2,1)}) %reduce-scatter.7.cloned.1.call-update) | async-done | bytes 1048592 | tf_op jit(solution)/shard_map/reduce_scatter | solution.py:2672
  470.9 36.8 %shard_map.446 = (bf16[1536,1536]{1,0:T(8,128)(2,1)}, f32[8,896]{1,0:T(8,128)}, f32[8,128]{1,0:T(8,128)}, f32[1,384]{1,0:T(1,128)}, f32[1,384]{1,0:T(1,128)}, /*...) custom-call(f32[1536,1024]{1,0:T(8,128)} %fusion.5.proj_ref.before_ref.raw_ref, ...), custom_call_target="tpu_custom_call" | custom-call | flops 43200000000 | bytes 144000000 | tf_op jit(solution)/shard_map/pallas_call | solution.py:2250
  507.7 11.6 %convolution_convert_fusion = bf16[2048,1024]{1,0:T(8,128)(2,1)} fusion(bf16[1536,2048]{1,0:T(8,128)(2,1)} %get-tuple-element.116.normed_hbm, bf16[1536,1536]{1,0:T(8,128)(2,1)} %get-tuple-element.167.left_ref), kind=kOutput, calls=%fused_computation | convolution fusion | flops 6444548096 | bytes 13631488 | tf_op jit(solution)/shard_map/dot_general | solution.py:51
  521.7 49.0 %shard_map.447 = (f32[192,2048]{1,0:T(8,128)}, f32[128,1024]{1,0:T(8,128)}, f32[8,2048]{1,0:T(8,128)}) custom-call(bf16[1536,1536]{1,0:T(8,128)(2,1)} %get-tuple-element.167.left_ref, bf16[2048,1024]{1,0:T(8,128)(2,1)} %bitcast.85, bf16[2048,512]{1,0:T(8,128)(2,1)} %bc_weights_ref.1, f32[1,2048]{1,0:T(1,128)} %get-tuple-element.215.refs_0_.gain_ref, ...), custom_call_target="tpu_custom_call" | custom-call | flops 44999999488 | bytes 150000000 | tf_op jit(solution)/shard_map/pallas_call | solution.py:1187
  572.3 14.6 %shard_map.448 = (f32[8,640]{1,0:T(8,128)}, f32[2,192,2048]{2,1,0:T(8,128)}, bf16[2,192,2048]{2,1,0:T(8,128)(2,1)}, bf16[4,128,512]{2,1,0:T(8,128)(2,1)}) custom-call(f32[8,5120]{1,0:T(8,128)} %pad.15.small_ref, f32[192,2048]{1,0:T(8,128)} %get-tuple-element.170.own_ref, bf16[192,2048]{1,0:T(8,128)(2,1)} %get-tuple-element.171.out_ref, ...), custom_call_target="tpu_custom_call" | custom-call | flops 17999998976 | bytes 60000000 | tf_op jit(solution)/shard_map/pallas_call | solution.py:1296
  586.9 6.6 %shard_map.449 = (f32[128,2048]{1,0:T(8,128)}, f32[128,2048]{1,0:T(8,128)}, f32[2048,128]{1,0:T(8,128)}, f32[1536,128]{1,0:T(8,128)}, f32[512,128]{1,0:T(8,128)}...) custom-call(bf16[4,128,1024]{2,1,0:T(8,128)(2,1)} %get-tuple-element.159.gu_ref, ...), custom_call_target="tpu_custom_call" | custom-call | flops 5400000000 | bytes 18000000 | tf_op jit(solution)/shard_map/pallas_call | solution.py:1572
  593.4 2.2 reduce-scatter.11.cloned.1.call-done
  595.6 32.6 %shard_map.450 = (f32[8,8,640]{2,1,0:T(8,128)}, bf16[8,4,32,1024]{3,2,1,0:T(8,128)(2,1)}, bf16[4,128,1024]{2,1,0:T(8,128)(2,1)}) custom-call(f32[8,640]{1,0:T(8,128)} %get-tuple-element.178.piece_ref, f32[128,1024]{1,0:T(8,128)} %get-tuple-element.179.bc_ref, bf16[4,128,1024]{2,1,0:T(8,128)(2,1)} %bitcast.91), custom_call_target="tpu_custom_call" | custom-call | flops 27000000512 | bytes 90000000 | tf_op jit(solution)/shard_map/pallas_call | solution.py:1427
  628.2 5.7 shard_map.451
  (166 shorter events, 37.7 us)
Async XLA Ops:
  7.2 22.6 %copy-start = (bf16[1,384,2048]{2,1,0:T(8,128)(2,1)S(1)}, bf16[1,384,2048]{2,1,0:T(8,128)(2,1)}, u32[]{:S(2)}) copy-start(bf16[1,384,2048]{2,1,0:T(8,128)(2,1)} %param.28) | copy-start | bytes 4718596
  7.2 101.5 %all-gather.5.cloned.1.call-start = ((), (), s32[]{:S(2)}) async-start(), calls=%async_computation.4 | async-start | bytes 5242880 | tf_op jit(solution)/shard_map/all_gather | solution.py:2544
  29.7 125.1 %all-gather.7.cloned.1.call-start = ((), (), s32[]{:S(2)}) async-start(), calls=%async_computation.5 | async-start | bytes 2621440 | tf_op jit(solution)/shard_map/all_gather | solution.py:2572
  33.2 37.2 %copy-start.15 = (bf16[512,128]{1,0:T(8,128)(2,1)S(1)}, bf16[512,128]{1,0:T(8,128)(2,1)}, u32[]{:S(2)}) copy-start(bf16[512,128]{1,0:T(8,128)(2,1)} %param.47) | copy-start | bytes 393220
  33.2 38.0 %copy-start.11 = (bf16[2048,128]{1,0:T(8,128)(2,1)S(1)}, bf16[2048,128]{1,0:T(8,128)(2,1)}, u32[]{:S(2)}) copy-start(bf16[2048,128]{1,0:T(8,128)(2,1)} %param.51) | copy-start | bytes 1572868
  72.2 27.6 %copy-start.19 = (f32[3584]{0:T(1024)S(1)}, f32[3584]{0:T(1024)}, u32[]{:S(2)}) copy-start(f32[3584]{0:T(1024)} %param.38) | copy-start | bytes 43012
  72.2 28.0 %copy-start.23 = (f32[48]{0:T(128)S(1)}, f32[48]{0:T(128)}, u32[]{:S(2)}) copy-start(f32[48]{0:T(128)} %param.40) | copy-start | bytes 580
  72.2 28.0 %copy-start.24 = (f32[48]{0:T(128)S(1)}, f32[48]{0:T(128)}, u32[]{:S(2)}) copy-start(f32[48]{0:T(128)} %param.39) | copy-start | bytes 580
  72.2 28.8 %slice-start.1 = ((f32[3584]{0:T(1024)}), f32[512]{0:T(512)S(1)}, s32[]{:S(2)}) async-start(f32[3584]{0:T(1024)} %param.38), calls=%async_computation.13 | async-start | bytes 4096 | tf_op jit(solution)/shard_map/slice | solution.py:2591
  72.3 28.8 %copy-start.16 = (f32[3584,4]{0,1:T(4,128)S(1)}, f32[3584,4]{0,1:T(4,128)}, u32[]{:S(2)}) copy-start(f32[3584,4]{0,1:T(4,128)} %param.37) | copy-start | bytes 172036
  99.8 12.9 %copy-start.28 = (f32[48]{0:T(128)S(1)}, f32[48]{0:T(128)}, u32[]{:S(2)}) copy-start(f32[48]{0:T(128)} %param.41) | copy-start | bytes 580
  99.9 14.3 %slice-start = ((f32[3584,4]{0,1:T(4,128)}), f32[512,4]{0,1:T(4,128)S(1)}, s32[]{:S(2)}) async-start(f32[3584,4]{0,1:T(4,128)} %param.37), calls=%async_computation.12 | async-start | bytes 16384 | tf_op jit(solution)/shard_map/slice | solution.py:2591
  108.8 127.1 %all-gather.9.cloned.1.call-start = ((), (), s32[]{:S(2)}) async-start(), calls=%async_computation.6 | async-start | bytes 5242880 | tf_op jit(solution)/shard_map/all_gather | solution.py:2631
  128.7 27.2 %copy-start.18 = (s32[4,1536]{1,0:T(4,128)S(1)}, s32[4,1536]{1,0:T(4,128)}, u32[]{:S(2)}) copy-start(s32[4,1536]{1,0:T(4,128)} %param.31) | copy-start | bytes 73732
  128.7 29.4 %copy-start.12 = (bf16[1,384,2048]{2,1,0:T(8,128)(2,1)S(1)}, bf16[1,384,2048]{2,1,0:T(8,128)(2,1)}, u32[]{:S(2)}) copy-start(bf16[1,384,2048]{2,1,0:T(8,128)(2,1)} %param.29) | copy-start | bytes 4718596
  147.2 11.9 %copy-start.14 = (bf16[768,128]{1,0:T(8,128)(2,1)S(1)}, bf16[768,128]{1,0:T(8,128)(2,1)}, u32[]{:S(2)}) copy-start(bf16[768,128]{1,0:T(8,128)(2,1)} %get-tuple-element.132) | copy-start | bytes 589828
  147.3 15.3 %copy-start.7 = (bf16[1536,384]{1,0:T(8,128)(2,1)S(1)}, bf16[1536,384]{1,0:T(8,128)(2,1)}, u32[]{:S(2)}) copy-start(bf16[1536,384]{1,0:T(8,128)(2,1)} %get-tuple-element.131) | copy-start | bytes 3538948
  154.9 127.0 %all-gather.11.cloned.1.call-start = ((), (), s32[]{:S(2)}) async-start(), calls=%async_computation.7 | async-start | bytes 2621440 | tf_op jit(solution)/shard_map/all_gather | solution.py:2632
  159.1 7.8 %collective-permute-start = (bf16[768,128]{1,0:T(8,128)(2,1)S(1)}, bf16[768,128]{1,0:T(8,128)(2,1)S(1)}, u32[]{:S(2)}, u32[]{:S(2)}) collective-permute-start(bf16[768,128]{1,0:T(8,128)(2,1)S(1)} %copy-done.14), channel_id=1, source_target_pairs={{0,2},{2,0},{4,6},{6,4},{1,3},{3,1},{5,7},{7,5},{8,10},{10,8},{12,... | collective-permute-start | bytes 589832 | tf_op jit(solution)/shard_map/ppermute | solution.py:2471
  160.6 10.6 %collective-permute-start.1 = (bf16[768,128]{1,0:T(8,128)(2,1)S(1)}, bf16[768,128]{1,0:T(8,128)(2,1)S(1)}, u32[]{:S(2)}, u32[]{:S(2)}) collective-permute-start(bf16[768,128]{1,0:T(8,128)(2,1)S(1)} %copy-done.14), channel_id=1, source_target_pairs={{0,4},{2,6},{4,0},{6,2},{1,5},{3,7},{5,1},{7,3},{8,12},{10,14},{12... | collective-permute-start | bytes 589832 | tf_op jit(solution)/shard_map/ppermute | solution.py:2471
  162.0 9.2 %collective-permute-start.2 = (bf16[768,128]{1,0:T(8,128)(2,1)S(1)}, bf16[768,128]{1,0:T(8,128)(2,1)S(1)}, u32[]{:S(2)}, u32[]{:S(2)}) collective-permute-start(bf16[768,128]{1,0:T(8,128)(2,1)S(1)} %copy-done.14), channel_id=1, source_target_pairs={{0,6},{2,4},{4,2},{6,0},{1,7},{3,5},{5,3},{7,1},{8,14},{10,12},{12... | collective-permute-start | bytes 589832 | tf_op jit(solution)/shard_map/ppermute | solution.py:2471
  183.3 35.4 %copy-start.5 = (bf16[192,2048]{1,0:T(8,128)(2,1)S(1)}, bf16[192,2048]{1,0:T(8,128)(2,1)}, u32[]{:S(2)}) copy-start(bf16[192,2048]{1,0:T(8,128)(2,1)} %dynamic-slice_bitcast_fusion.1.own_ref.hidden_hbm) | copy-start | bytes 2359300
  220.4 55.1 %copy-start.2 = (f32[192,2048]{1,0:T(8,128)}, f32[192,2048]{1,0:T(8,128)S(1)}, u32[]{:S(2)}) copy-start(f32[192,2048]{1,0:T(8,128)S(1)} %get-tuple-element.209.middle_hbm) | copy-start | bytes 4718596
  235.9 155.5 %reduce-scatter.5.cloned.1.call-start = ((), (), s32[]{:S(2)}) async-start(), calls=%async_computation.8 | async-start | bytes 2621440 | tf_op jit(solution)/shard_map/reduce_scatter | solution.py:2672
  348.8 121.0 %reduce-scatter.7.cloned.1.call-start = ((), (), s32[]{:S(2)}) async-start(), calls=%async_computation.9 | async-start | bytes 5242880 | tf_op jit(solution)/shard_map/reduce_scatter | solution.py:2672
  391.5 127.8 %reduce-scatter.9.cloned.1.call-start = ((), (), s32[]{:S(2)}) async-start(), calls=%async_computation.10 | async-start | bytes 2621440 | tf_op jit(solution)/shard_map/reduce_scatter | solution.py:2672
  441.9 5.6 copy-start.9
  443.9 26.1 %collective-permute-start.3 = (bf16[768,128]{1,0:T(8,128)(2,1)S(1)}, bf16[768,128]{1,0:T(8,128)(2,1)S(1)}, u32[]{:S(2)}, u32[]{:S(2)}) collective-permute-start(bf16[768,128]{1,0:T(8,128)(2,1)S(1)} %get-tuple-element.212), channel_id=1, source_target_pairs={{0,2},{2,0},{4,6},{6,4},{1,3},{3,1},{5,7},{7,5},{8,10},{10,8},{12,... | collective-permute-start | bytes 589832 | tf_op jit(solution)/shard_map/ppermute | solution.py:2482
  445.0 25.1 %collective-permute-start.4 = (bf16[768,128]{1,0:T(8,128)(2,1)S(1)}, bf16[768,128]{1,0:T(8,128)(2,1)S(1)}, u32[]{:S(2)}, u32[]{:S(2)}) collective-permute-start(bf16[768,128]{1,0:T(8,128)(2,1)S(1)} %get-tuple-element.211), channel_id=1, source_target_pairs={{0,4},{2,6},{4,0},{6,2},{1,5},{3,7},{5,1},{7,3},{8,12},{10,14},{12... | collective-permute-start | bytes 589832 | tf_op jit(solution)/shard_map/ppermute | solution.py:2482
  445.9 24.2 %collective-permute-start.5 = (bf16[768,128]{1,0:T(8,128)(2,1)S(1)}, bf16[768,128]{1,0:T(8,128)(2,1)S(1)}, u32[]{:S(2)}, u32[]{:S(2)}) collective-permute-start(bf16[768,128]{1,0:T(8,128)(2,1)S(1)} %get-tuple-element.210), channel_id=1, source_target_pairs={{0,6},{2,4},{4,2},{6,0},{1,7},{3,5},{5,3},{7,1},{8,14},{10,12},{12... | collective-permute-start | bytes 589832 | tf_op jit(solution)/shard_map/ppermute | solution.py:2482
  469.8 125.8 %reduce-scatter.11.cloned.1.call-start = ((), (), s32[]{:S(2)}) async-start(), calls=%async_computation.11 | async-start | bytes 5242880 | tf_op jit(solution)/shard_map/reduce_scatter | solution.py:2672
  628.2 5.7 copy-start.1
  (13 other events, 15.6 us)
Sparse Core Ops, SparseCore 0:
  29.8 78.9 all-gather.4
  110.3 44.4 all-gather.6
  156.4 79.4 all-gather.8
  237.3 44.4 all-gather.10
  348.9 42.4 reduce-scatter.4
  393.7 76.0 reduce-scatter.6
  472.1 44.3 reduce-scatter.8
  519.5 76.1 reduce-scatter.10
